TPU v7x, 256 devices: a whole 4x4x8 slice. The times are simulated.
256 devices in a mesh: grp: 8 (over y, z_lo), dev: 32 (over z_hi, x, core).
Axes of the slice: x: 4, y: 4, z: 8 (z_hi: 4, z_lo: 2; z = z_hi * 2 + z_lo), core: 2. Of those that a mesh axis runs over, the one named last changes fastest.
Arguments:
- reservoir: bfloat16 [262144, 1024], P(('grp', 'dev')), may hold values from -6 to 6
- send_rows: int32 [256, 8, 16], P(('grp', 'dev')), may hold values from 0 to 1023
- send_count: int32 [256, 8], P(('grp', 'dev')), may hold values from 0 to 16, as said below
- new_rows: bfloat16 [131072, 1024], P(('grp', 'dev')), may hold values from -6 to 6
- w_up: bfloat16 [1024, 2048], P('dev'), may hold values from -0.1875 to 0.1875
- w_down: bfloat16 [2048, 1024], P('dev'), may hold values from -0.125 to 0.125
- ln_gain: bfloat16 [1024], replicated, may hold values from 0.099609375 to 1.8984375
- grad_new: bfloat16 [131072, 1024], P(('grp', 'dev')), may hold values from -0.016479492 to 0.016479492
- grad_old: bfloat16 [32768, 1024], P(('grp', 'dev')), may hold values from -0.016479492 to 0.016479492
Outputs:
- block_out: bfloat16 [131072, 1024], P(('grp', 'dev'))
- grad_up: float32 [1024, 2048], P('dev')
- grad_down: float32 [2048, 1024], P('dev')
Inputs may be any that keep to these rules, and one draw needn't show every extreme that they name: send_count[s, t] slots of source s toward group t are live, the others are empty; 16 is reached in every draw, and about a quarter of the (source, group) pairs carry 8 to 16 live slots, the others 0 to 4.
All inputs are finite; a program needn't handle non-finite values.
Results may differ from a plain program's by a relative error of at most 0.024.
Values may be sent and summed in bfloat16 or wider, within the bound.
No kernel may reach another device: no remote copies, remote signals or barrier semaphores. Data moves between devices by JAX's collectives and lax.ppermute only.
A program may use at most 64 MiB of HBM per device.

v0:
```python
import jax
import jax.numpy as jnp
from jax import lax
from jax.sharding import PartitionSpec as P


def normalize(rows, ln_gain):
    values = rows.astype(jnp.float32)
    center = jnp.mean(values, axis=-1, keepdims=True)
    centred = values - center
    spread = jnp.mean(centred * centred, axis=-1, keepdims=True)
    return (centred * lax.rsqrt(spread + 1e-05) * ln_gain.astype(jnp.float32)).astype(jnp.bfloat16)


def gelu_parts(pre):
    cdf_value = 0.5 * (1.0 + lax.erf(pre * 0.7071067811865476))
    density = jnp.exp(-0.5 * pre * pre) * 0.3989422804014327
    return (pre * cdf_value, cdf_value + pre * density)


def fetch_old(picked, groups, slots, width):
    return lax.all_to_all(picked, "grp", split_axis=0, concat_axis=0, tiled=True).reshape(
        groups * slots, width
    )


def body(reservoir, send_rows, send_count, new_rows, w_up, w_down, ln_gain, grad_new, grad_old):
    groups = lax.axis_size("grp")
    slots = send_rows.shape[2]
    fresh_count = new_rows.shape[0]
    width = new_rows.shape[1]
    live = (lax.broadcasted_iota(jnp.int32, (groups, slots), 1) < send_count[0][:, None]).astype(
        jnp.bfloat16
    )
    picked = reservoir[send_rows[0].reshape(-1)].reshape(groups, slots, width) * live[:, :, None]
    up_full = lax.all_gather(w_up, "dev", axis=0, tiled=True)
    arrived = fetch_old(picked, groups, slots, width)
    normed = normalize(jnp.concatenate([new_rows, arrived], axis=0), ln_gain)
    pre = jnp.dot(normed, up_full, preferred_element_type=jnp.float32)
    act, slope = gelu_parts(pre)
    hidden = act.astype(jnp.bfloat16)
    fresh_hidden = hidden[:fresh_count]
    cot = jnp.concatenate([grad_new, grad_old], axis=0)
    mixed = jnp.dot(
        fresh_hidden,
        lax.all_gather(w_down, "dev", axis=0, tiled=True),
        preferred_element_type=jnp.float32,
    )
    back = lax.dot_general(
        cot,
        lax.all_gather(w_down, "dev", axis=0, tiled=True),
        (((1,), (1,)), ((), ())),
        preferred_element_type=jnp.float32,
    )
    block_out = (new_rows.astype(jnp.float32) + mixed).astype(jnp.bfloat16)
    pre_grad = (back * slope).astype(jnp.bfloat16)
    group_down = lax.psum_scatter(
        lax.dot_general(
            hidden, cot, (((0,), (0,)), ((), ())), preferred_element_type=jnp.float32
        ).astype(jnp.bfloat16),
        "dev",
        scatter_dimension=0,
        tiled=True,
    )
    group_up = lax.psum_scatter(
        lax.dot_general(
            normed, pre_grad, (((0,), (0,)), ((), ())), preferred_element_type=jnp.float32
        ).astype(jnp.bfloat16),
        "dev",
        scatter_dimension=0,
        tiled=True,
    )
    grad_up, grad_down = (
        lax.psum(group_up, "grp").astype(jnp.float32),
        lax.psum(group_down, "grp").astype(jnp.float32),
    )
    return (block_out, grad_up, grad_down)


def solution(mesh):
    return jax.shard_map(
        body,
        mesh=mesh,
        in_specs=(
            P(("grp", "dev"), None),
            P(("grp", "dev"), None, None),
            P(("grp", "dev"), None),
            P(("grp", "dev"), None),
            P("dev", None),
            P("dev", None),
            P(),
            P(("grp", "dev"), None),
            P(("grp", "dev"), None),
        ),
        out_specs=(P(("grp", "dev"), None), P("dev", None), P("dev", None)),
        check_vma=False,
    )
```

profile of v0, /device:TPU:64, one launch (start us, length us, event | category | flops | bytes accessed | tf_op | source)
XLA Modules:
  0.0 432.3 jit_solution(15267910627218984748)
XLA Ops:
  7.2 0.0 copy-start
  7.2 0.0 all-gather.3.cloned.1.call-start
  7.2 0.7 all-gather.3.cloned.1.call-update
  7.9 0.0 all-gather.5.cloned.1.call-start
  8.0 0.7 all-gather.5.cloned.1.call-update
  8.7 0.8 reshape_squeeze.3
  9.5 0.9 gather_fusion
  10.4 0.1 fusion.15
  10.4 0.8 broadcast_multiply_fusion
  11.2 5.8 %all-to-all-start = ((bf16[8,16,1024]{2,1,0:T(8,128)(2,1)}), bf16[8,16,1024]{2,1,0:T(8,128)(2,1)S(1)}, u32[]{:S(2)}, u32[]{:S(2)}) async-start(bf16[8,16,1024]{2,1,0:T(8,128)(2,1)} %broadcast_multiply_fusion), calls=%async_computation | async-start | bytes 524288 | tf_op jit(solution)/shard_map/all_to_all | solution.py:22
  17.0 0.0 reduce-scatter.3.cloned.1.call-start
  17.1 2.3 constant_dynamic-update-slice_fusion.1
  19.4 1.7 constant_dynamic-update-slice_fusion
  21.1 3.3 all-to-all-done
  24.3 0.2 convert_reduce_fusion
  24.6 0.5 fusion.8
  25.1 47.1 %all-gather.3.cloned.1.call-done = bf16[1024,2048]{1,0:T(8,128)(2,1)} async-done(((bf16[32,2048]{1,0:T(8,128)(2,1)}), bf16[1024,2048]{1,0:T(8,128)(2,1)}) %all-gather.3.cloned.1.call-update) | async-done | bytes 4194320 | tf_op jit(solution)/shard_map/all_gather | solution.py:36
  72.2 8.1 %multiply_convert_fusion = (bf16[640,2048]{1,0:T(8,128)(2,1)}, f32[640,2048]{1,0:T(8,128)}) fusion(bf16[1024,2048]{1,0:T(8,128)(2,1)} %all-gather.3.cloned.1.call-done, f32[1024]{0:T(1024)S(1)} %convert_element_type.43, f32[640]{0:T(1024)S(1)} %add_rsqrt_fusion, f32[640]{0:T(1024)S(1)} %broadcast_multiply_fusion.1, bf16[128,1024]{1,0:T(8,128)(2,1)S(1)} %bitcast.13, ...), kind=kOutput, calls=%fused_computation.8 | convolution fusion | flops 2696151040 | bytes 13378560 | tf_op jit(solution)/shard_map/dot_general | solution.py:39
  80.4 52.4 %all-gather.5.cloned.1.call-done = bf16[2048,1024]{1,0:T(8,128)(2,1)} async-done(((bf16[64,1024]{1,0:T(8,128)(2,1)}), bf16[2048,1024]{1,0:T(8,128)(2,1)}) %all-gather.5.cloned.1.call-update) | async-done | bytes 4194320 | tf_op jit(solution)/shard_map/all_gather | solution.py:46
  132.7 11.5 %convolution_convert_fusion.1 = bf16[1024,2048]{1,0:T(8,128)(2,1)} fusion(f32[640,2048]{1,0:T(8,128)} %get-tuple-element.6, bf16[640,1024]{1,0:T(8,128)(2,1)} %constant_dynamic-update-slice_fusion, bf16[2048,1024]{1,0:T(8,128)(2,1)} %all-gather.5.cloned.1.call-done, f32[1024]{0:T(1024)S(1)} %convert_element_type.43, f32[640]{0:T(1024)S(1)} %add_rsqrt_fusion, ...), kind=kOutput, calls=%fused_computation.11 | convolution fusion | flops 5389156352 | bytes 16262144 | tf_op jit(solution)/shard_map/dot_general | solution.py:66
  144.2 0.0 reduce-scatter.3.cloned.1.call-update
  144.2 0.0 reduce-scatter.5.cloned.1.call-start
  144.3 7.5 %convolution_convert_fusion = bf16[2048,1024]{1,0:T(8,128)(2,1)} fusion(bf16[640,2048]{1,0:T(8,128)(2,1)} %get-tuple-element.5, bf16[640,1024]{1,0:T(8,128)(2,1)} %constant_dynamic-update-slice_fusion), kind=kOutput, calls=%fused_computation.10 | convolution fusion | flops 2686451712 | bytes 8126464 | tf_op jit(solution)/shard_map/dot_general | solution.py:58
  151.8 0.0 reduce-scatter.5.cloned.1.call-update
  151.8 0.0 all-reduce.3.cloned.1.call-start
  151.9 89.2 %reduce-scatter.3.cloned.1.call-done = bf16[32,2048]{1,0:T(8,128)(2,1)} async-done(((bf16[1024,2048]{1,0:T(8,128)(2,1)}), bf16[32,2048]{1,0:T(8,128)(2,1)}) %reduce-scatter.3.cloned.1.call-update) | async-done | bytes 131088 | tf_op jit(solution)/shard_map/reduce_scatter | solution.py:65
  241.1 101.2 %reduce-scatter.5.cloned.1.call-done = bf16[64,1024]{1,0:T(8,128)(2,1)} async-done(((bf16[2048,1024]{1,0:T(8,128)(2,1)}), bf16[64,1024]{1,0:T(8,128)(2,1)}) %reduce-scatter.5.cloned.1.call-update) | async-done | bytes 131088 | tf_op jit(solution)/shard_map/reduce_scatter | solution.py:57
  342.3 0.0 all-reduce.3.cloned.1.call-update
  342.4 6.1 %add_convert_fusion = bf16[512,1024]{1,0:T(8,128)(2,1)} fusion(bf16[512,1024]{1,0:T(8,128)(2,1)S(1)} %copy-done.1, bf16[2048,1024]{1,0:T(8,128)(2,1)} %all-gather.5.cloned.1.call-done, bf16[640,2048]{1,0:T(8,128)(2,1)} %get-tuple-element.5), kind=kOutput, calls=%fused_computation.21 | convolution fusion | flops 2149056512 | bytes 8388608 | tf_op jit(solution)/shard_map/dot_general | solution.py:44
  348.5 74.0 %all-reduce.3.cloned.1.call-done = (bf16[32,2048]{1,0:T(8,128)(2,1)}, bf16[64,1024]{1,0:T(8,128)(2,1)}) async-done(((bf16[32,2048]{1,0:T(8,128)(2,1)}, bf16[64,1024]{1,0:T(8,128)(2,1)}), (bf16[32,2048]{1,0:T(8,128)(2,1)}, bf16[64,1024]{1,0:T(8,128)(2,1)})) %all-reduce.3.cloned.1.call-update) | async-done | bytes 262160 | tf_op jit(solution)/shard_map/psum | solution.py:74
  422.5 1.6 convert_element_type.49
  424.1 1.6 convert_element_type.51
  (12 shorter events, 0.0 us)
Async XLA Ops:
  7.2 2.3 copy-start
  7.2 3.2 copy-start.3
  7.2 9.9 %copy-start.2 = (bf16[1024]{0:T(1024)(128)(2,1)S(1)}, bf16[1024]{0:T(1024)(128)(2,1)}, u32[]{:S(2)}) copy-start(bf16[1024]{0:T(1024)(128)(2,1)} %param.15) | copy-start | bytes 6148
  7.2 65.0 %all-gather.3.cloned.1.call-start = ((), (), s32[]{:S(2)}) async-start(), calls=%async_computation.3 | async-start | bytes 4325376 | tf_op jit(solution)/shard_map/all_gather | solution.py:36
  7.9 124.8 %all-gather.5.cloned.1.call-start = ((), (), s32[]{:S(2)}) async-start(), calls=%async_computation.4 | async-start | bytes 4325376 | tf_op jit(solution)/shard_map/all_gather | solution.py:46
  9.5 14.9 %copy-start.1 = (bf16[512,1024]{1,0:T(8,128)(2,1)S(1)}, bf16[512,1024]{1,0:T(8,128)(2,1)}, u32[]{:S(2)}) copy-start(bf16[512,1024]{1,0:T(8,128)(2,1)} %param.12) | copy-start | bytes 3145732
  11.2 13.1 %all-to-all-start = ((bf16[8,16,1024]{2,1,0:T(8,128)(2,1)}), bf16[8,16,1024]{2,1,0:T(8,128)(2,1)S(1)}, u32[]{:S(2)}, u32[]{:S(2)}) async-start(bf16[8,16,1024]{2,1,0:T(8,128)(2,1)} %broadcast_multiply_fusion), calls=%async_computation | async-start | bytes 524288 | tf_op jit(solution)/shard_map/all_to_all | solution.py:22
  17.0 224.1 %reduce-scatter.3.cloned.1.call-start = ((), (), s32[]{:S(2)}) async-start(), calls=%async_computation.5 | async-start | bytes 4325376 | tf_op jit(solution)/shard_map/reduce_scatter | solution.py:65
  144.2 198.1 %reduce-scatter.5.cloned.1.call-start = ((), (), s32[]{:S(2)}) async-start(), calls=%async_computation.6 | async-start | bytes 4325376 | tf_op jit(solution)/shard_map/reduce_scatter | solution.py:57
  151.8 270.7 %all-reduce.3.cloned.1.call-start = ((), (), s32[]{:S(2)}) async-start(), calls=%async_computation.7 | async-start | bytes 524288 | tf_op jit(solution)/shard_map/psum | solution.py:74
Sparse Core Ops, SparseCore 0:
  10.6 61.5 all-gather.2
  74.8 57.8 all-gather.4
  144.3 96.7 reduce-scatter.2
  245.4 96.8 reduce-scatter.4
  344.8 77.5 all-reduce.2
where the time goes:
time: 433 us; the launch traced here: 432 us
  waiting for transfers between devices  369 us (85%)
  matrix products  33.3 us (8%)
  between operations  13.9 us (3%)
  starting transfers between devices  6.02 us (1%)
  local copies, waits for them, and re-layouts  5.59 us (1%)
  other arithmetic  4.86 us (1%)
    reduce_scatter x1, waiting for transfers between devices, body(): lax.psum_scatter(lax.dot_general(hidden, cot, (((0,), (0,)), ((), ())), p...  101 us
    reduce_scatter x1, waiting for transfers between devices, body(): lax.psum_scatter(lax.dot_general(normed, pre_grad, (((0,), (0,)), ((), ()...  89.2 us
    psum x1, waiting for transfers between devices, body(): lax.psum(group_up, 'grp').astype(jnp.float32)  74 us
    all_gather x1, waiting for transfers between devices, body(): lax.all_gather(w_down, 'dev', axis=0, tiled=True)  52.4 us
    all_gather x1, waiting for transfers between devices, body(): up_full = lax.all_gather(w_up, 'dev', axis=0, tiled=True)  47.1 us
    dot_general x1, matrix products, body(): lax.dot_general(normed, pre_grad, (((0,), (0,)), ((), ())), preferred_ele...  11.5 us
  transfers between devices with their start and end apart: 6, of which 6 were waited for; matrix products, arithmetic and copies ran while one was open for 7% of the time, Pallas kernels for 0%

commit v1 on v0

v1 whole, which is shorter than its diff:
```python
import jax
import jax.numpy as jnp
from jax import lax
from jax.sharding import Mesh, PartitionSpec as P

PHYSICAL = (("y", 4), ("zl", 2), ("zh", 4), ("x", 4), ("c", 2))
AXES = tuple(name for name, _ in PHYSICAL)
GRP = ("y", "zl")
DEV = ("zh", "x", "c")


def normalize(rows, ln_gain):
    values = rows.astype(jnp.float32)
    center = jnp.mean(values, axis=-1, keepdims=True)
    centred = values - center
    spread = jnp.mean(centred * centred, axis=-1, keepdims=True)
    return (centred * lax.rsqrt(spread + 1e-05) * ln_gain.astype(jnp.float32)).astype(jnp.bfloat16)


def gelu_parts(pre):
    cdf_value = 0.5 * (1.0 + lax.erf(pre * 0.7071067811865476))
    density = jnp.exp(-0.5 * pre * pre) * 0.3989422804014327
    return (pre * cdf_value, cdf_value + pre * density)


def swap(value):
    return lax.ppermute(value, "c", [(0, 1), (1, 0)])


def exchange(value, axes):
    return lax.all_to_all(value, axes, split_axis=0, concat_axis=0, tiled=True)


def gather_zh(value):
    n = lax.axis_size("zh")
    parts = [value]
    for step in range(1, n):
        parts.append(lax.ppermute(value, "zh", [((i + step) % n, i) for i in range(n)]))
    ring = jnp.stack(parts + parts[:-1])
    return lax.dynamic_slice_in_dim(ring, (n - lax.axis_index("zh")) % n, n, 0)


def body(reservoir, send_rows, send_count, new_rows, w_up, w_down, ln_gain, grad_new, grad_old):
    n_grp, n_zh, n_x, n_c = lax.axis_size(GRP), lax.axis_size("zh"), lax.axis_size("x"), lax.axis_size("c")
    slots = send_rows.shape[2]
    fresh_count, width = new_rows.shape
    up_rows, hid = w_up.shape
    down_rows = w_down.shape[0]
    half = hid // n_c
    cut = half // n_grp
    pair = cut // down_rows
    group = lax.axis_index(GRP)

    mine = lax.dynamic_index_in_dim(w_up.reshape(up_rows, n_grp, pair, n_c, down_rows), group, 1, keepdims=False)
    mine = mine.transpose(2, 0, 1, 3).reshape(n_c, up_rows, cut)
    column = gather_zh(mine).transpose(1, 0, 2, 3)
    spread_up = jnp.broadcast_to(column[None], (n_grp * n_x,) + column.shape)
    spread_up = spread_up.reshape(n_grp * n_x * n_c, n_zh, up_rows, cut)

    live = (lax.broadcasted_iota(jnp.int32, (n_grp, slots), 1) < send_count[0][:, None]).astype(jnp.bfloat16)
    picked = reservoir[send_rows[0].reshape(-1)].reshape(n_grp, slots, width) * live[:, :, None]
    arrived = exchange(picked, GRP).reshape(n_grp * slots, width)

    down_half = lax.all_gather(w_down, ("zh", "x"), axis=0, tiled=True)
    got_up = exchange(spread_up, ("y", "zl", "x", "c")).reshape(n_grp, n_x, n_c, n_zh, up_rows, cut)
    up_half = got_up.transpose(3, 1, 2, 4, 0, 5).reshape(width, half)

    normed_own = normalize(jnp.concatenate([new_rows, arrived], axis=0), ln_gain)
    cot_own = jnp.concatenate([grad_new, grad_old], axis=0)
    normed = jnp.concatenate([normed_own, swap(normed_own)], axis=0)
    cot = jnp.concatenate([cot_own, swap(cot_own)], axis=0)
    rows = normed_own.shape[0]

    pre = jnp.dot(normed, up_half, preferred_element_type=jnp.float32)
    act, slope = gelu_parts(pre)
    hidden = act.astype(jnp.bfloat16)

    term_down = lax.dot_general(hidden, cot, (((0,), (0,)), ((), ())), preferred_element_type=jnp.float32)
    term_down = term_down.astype(jnp.bfloat16).reshape(n_zh, n_x, down_rows, n_grp, cut)
    term_down = term_down.transpose(3, 1, 0, 2, 4).reshape(n_grp * n_x, n_zh, down_rows, cut)
    part_down = jnp.sum(exchange(term_down, ("y", "zl", "x")).astype(jnp.float32), axis=0).astype(jnp.bfloat16)

    back = lax.dot_general(cot, down_half, (((1,), (1,)), ((), ())), preferred_element_type=jnp.float32)
    pre_grad = (back * slope).astype(jnp.bfloat16)
    term_up = lax.dot_general(normed, pre_grad, (((0,), (0,)), ((), ())), preferred_element_type=jnp.float32)
    term_up = term_up.astype(jnp.bfloat16).reshape(n_zh, n_x, n_c, up_rows, n_grp, cut)
    term_up = term_up.transpose(4, 1, 2, 0, 3, 5).reshape(n_grp * n_x * n_c, n_zh, up_rows, cut)
    part_up = exchange(term_up, ("y", "zl", "x", "c")).reshape(n_grp * n_x, n_c, n_zh, up_rows, cut)
    part_up = jnp.sum(part_up.astype(jnp.float32), axis=0).astype(jnp.bfloat16)

    other = jnp.dot(hidden[rows : rows + fresh_count], down_half, preferred_element_type=jnp.float32)
    mixed = jnp.dot(hidden[:fresh_count], down_half, preferred_element_type=jnp.float32)
    returned = swap(other.astype(jnp.bfloat16)).astype(jnp.float32)
    block_out = (new_rows.astype(jnp.float32) + (mixed + returned)).astype(jnp.bfloat16)

    both = jnp.concatenate([part_down[:, None], part_up.transpose(1, 0, 2, 3).reshape(n_zh, 1, n_c * up_rows, cut)], axis=1)
    both = jnp.broadcast_to(both[:, None], (n_zh, n_grp) + both.shape[1:]).reshape((n_zh * n_grp,) + both.shape[1:])
    both = exchange(both, ("zh", "y", "zl")).reshape((n_zh, n_grp) + both.shape[1:])
    both = jnp.sum(both.astype(jnp.float32), axis=0)
    grad_down = both[:, 0].transpose(1, 0, 2).reshape(down_rows, width)
    grad_up = both[:, 1].reshape(n_grp, n_c, up_rows, pair, down_rows)
    grad_up = grad_up.transpose(2, 0, 3, 1, 4).reshape(up_rows, hid)
    return (block_out, grad_up, grad_down)


def solution(mesh):
    fine = Mesh(mesh.devices.reshape(tuple(size for _, size in PHYSICAL)), AXES)
    every = P(AXES, None)
    return jax.shard_map(
        body,
        mesh=fine,
        in_specs=(every, P(AXES, None, None), every, every, P(DEV, None), P(DEV, None), P(), every, every),
        out_specs=(every, P(DEV, None), P(DEV, None)),
        check_vma=False,
    )
```

time: 433 us -> 219 us (0.51)
  waiting for transfers between devices: 369 us -> 90.2 us
  starting transfers between devices: 6.02 us -> 41.7 us
  local copies, waits for them, and re-layouts: 5.59 us -> 26.1 us
  other arithmetic: 4.86 us -> 11.7 us
    reduce_scatter x2 -> x0, waiting for transfers between devices: 190 us -> none  [the longest x1 101 us: body(): lax.psum_scatter(lax.dot_general(hidden, cot, (((0,), (0,)), ((), ())), p...]
    all_gather x2 -> x1, waiting for transfers between devices: 99.5 us -> 10.8 us  [body(): down_half = lax.all_gather(w_down, ('zh', 'x'), axis=0, tiled=True)]
    psum x1 -> x0, waiting for transfers between devices: 74 us -> none  [body(): lax.psum(group_up, 'grp').astype(jnp.float32)]
    all_to_all x1 -> x5, waiting for transfers between devices: 3.28 us -> 76.7 us  [exchange(): return lax.all_to_all(value, axes, split_axis=0, concat_axis=0, tiled=True)]
    all_to_all x1 -> x5, starting transfers between devices: 5.82 us -> 32.4 us  [exchange(): return lax.all_to_all(value, axes, split_axis=0, concat_axis=0, tiled=True)]
    ppermute x0 -> x6, starting transfers between devices: none -> 9.25 us  [the longest x3 8.39 us: gather_zh(): lax.ppermute(value, 'zh', [((i + step) % n, i) for i in range(n)])]
    reshape x0 -> x6, local copies, waits for them, and re-layouts: none -> 7.08 us  [the longest x1 1.91 us: body(): term_up.astype(jnp.bfloat16).reshape(n_zh, n_x, n_c, up_rows, n_grp, cut)]
    reduce_sum x0 -> x3, other arithmetic: none -> 5.33 us  [the longest x1 1.96 us: body(): jnp.sum(exchange(term_down, ('y', 'zl', 'x')).astype(jnp.float32), axis=0)]
  transfers between devices with their start and end apart: 6 -> 12, of which waited for: 6 -> 7; matrix products, arithmetic and copies ran while one was open for 7% -> 27% of each run, Pallas kernels for 0% -> 0%
where the time goes in v1:
time: 219 us; the launch traced here: 215 us
  waiting for transfers between devices  90.2 us (41%)
  starting transfers between devices  41.7 us (19%)
  matrix products  30.6 us (14%)
  local copies, waits for them, and re-layouts  26.1 us (12%)
  between operations  14.3 us (7%)
  other arithmetic  11.7 us (5%)
    all_to_all x5, waiting for transfers between devices, exchange(): return lax.all_to_all(value, axes, split_axis=0, concat_axis=0, tiled=True)  76.7 us
    all_to_all x5, starting transfers between devices, exchange(): return lax.all_to_all(value, axes, split_axis=0, concat_axis=0, tiled=True)  32.4 us
    dot_general x1, matrix products, body(): lax.dot_general(normed, pre_grad, (((0,), (0,)), ((), ())), preferred_ele...  12.6 us
    all_gather x1, waiting for transfers between devices, body(): down_half = lax.all_gather(w_down, ('zh', 'x'), axis=0, tiled=True)  10.8 us
    ppermute x3, starting transfers between devices, gather_zh(): lax.ppermute(value, 'zh', [((i + step) % n, i) for i in range(n)])  8.39 us
    unnamed x23, local copies, waits for them, and re-layouts  6.98 us
    dot_general x1, matrix products, body(): pre = jnp.dot(normed, up_half, preferred_element_type=jnp.float32)  6.37 us
    dot_general x1, matrix products, body(): lax.dot_general(hidden, cot, (((0,), (0,)), ((), ())), preferred_element_...  6 us
  transfers between devices with their start and end apart: 12, of which 7 were waited for; matrix products, arithmetic and copies ran while one was open for 27% of the time, Pallas kernels for 0%

profile of v1, /device:TPU:64, one launch (start us, length us, event | category | flops | bytes accessed | tf_op | source)
XLA Modules:
  0.0 214.6 jit_solution(15931970223711766736)
XLA Ops:
  8.7 4.6 %collective-permute-start.3 = (bf16[2,32,128]{2,1,0:T(8,128)(2,1)S(1)}, bf16[2,32,128]{2,1,0:T(8,128)(2,1)S(1)}, u32[]{:S(2)}, u32[]{:S(2)}) collective-permute-start(bf16[2,32,128]{2,1,0:T(8,128)(2,1)S(1)} %reshape.126), channel_id=1, source_target_pairs={{24,0},{0,8},{8,16},{16,24},{25,1},{1,9},{9,17},{17,25},{26,2},{2,... | collective-permute-start | bytes 49160 | tf_op jit(solution)/shard_map/ppermute | solution.py:38
  14.2 2.8 %collective-permute-start.1 = (bf16[2,32,128]{2,1,0:T(8,128)(2,1)S(1)}, bf16[2,32,128]{2,1,0:T(8,128)(2,1)S(1)}, u32[]{:S(2)}, u32[]{:S(2)}) collective-permute-start(bf16[2,32,128]{2,1,0:T(8,128)(2,1)S(1)} %reshape.126), channel_id=1, source_target_pairs={{8,0},{16,8},{24,16},{0,24},{9,1},{17,9},{25,17},{1,25},{10,2},{18... | collective-permute-start | bytes 49160 | tf_op jit(solution)/shard_map/ppermute | solution.py:38
  20.2 4.9 %all-to-all-start = ((bf16[8,16,1024]{2,1,0:T(8,128)(2,1)}), bf16[8,16,1024]{2,1,0:T(8,128)(2,1)S(1)}, u32[]{:S(2)}, u32[]{:S(2)}) async-start(bf16[8,16,1024]{2,1,0:T(8,128)(2,1)} %broadcast_multiply_fusion), calls=%async_computation | async-start | bytes 524288 | tf_op jit(solution)/shard_map/all_to_all | solution.py:31
  25.4 7.0 %all-to-all-done = bf16[8,16,1024]{2,1,0:T(8,128)(2,1)S(1)} async-done(((bf16[8,16,1024]{2,1,0:T(8,128)(2,1)}), bf16[8,16,1024]{2,1,0:T(8,128)(2,1)S(1)}, u32[]{:S(2)}, u32[]{:S(2)}) %all-to-all-start) | async-done | bytes 262176 | tf_op jit(solution)/shard_map/all_to_all | solution.py:31
  32.4 1.8 broadcast_in_dim.6
  34.3 6.6 %all-to-all-start.1 = ((bf16[64,4,32,128]{3,2,1,0:T(8,128)(2,1)}), bf16[64,4,32,128]{3,2,1,0:T(8,128)(2,1)}, u32[]{:S(2)}, u32[]{:S(2)}) async-start(bf16[64,4,32,128]{3,2,1,0:T(8,128)(2,1)} %bitcast.69), calls=%async_computation.1 | async-start | bytes 4194304 | tf_op jit(solution)/shard_map/all_to_all | solution.py:31
  40.9 2.5 %pad_maximum_fusion.4 = bf16[640,1024]{1,0:T(8,128)(2,1)} fusion(bf16[128,1024]{1,0:T(8,128)(2,1)} %param.17, bf16[512,1024]{1,0:T(8,128)(2,1)} %param.16), kind=kLoop, calls=%fused_computation.27 | loop fusion | flops 2621440 | bytes 2621440 | tf_op jit(solution)/shard_map/concatenate | solution.py:69
  44.2 1.5 fusion.10
  46.2 2.3 %constant_dynamic-update-slice_fusion.9 = bf16[1280,1024]{1,0:T(8,128)(2,1)} fusion(bf16[512,1024]{1,0:T(8,128)(2,1)} %param.16), kind=kLoop, calls=%fused_computation.46 | loop fusion | bytes 2097152
  48.6 1.7 constant_dynamic-update-slice_fusion.8
  50.3 2.5 %constant_dynamic-update-slice_fusion.7 = bf16[1280,1024]{1,0:T(8,128)(2,1)} fusion(bf16[1280,1024]{1,0:T(8,128)(2,1)} %constant_dynamic-update-slice_fusion.8, bf16[640,1024]{1,0:T(8,128)(2,1)} %collective-permute-done.5), kind=kLoop, calls=%fused_computation.44 | loop fusion | bytes 2621440 | tf_op jit(solution)/shard_map/concatenate | solution.py:71
  52.7 18.1 %all-to-all-done.1 = bf16[64,4,32,128]{3,2,1,0:T(8,128)(2,1)} async-done(((bf16[64,4,32,128]{3,2,1,0:T(8,128)(2,1)}), bf16[64,4,32,128]{3,2,1,0:T(8,128)(2,1)}, u32[]{:S(2)}, u32[]{:S(2)}) %all-to-all-start.1) | async-done | bytes 2097184 | tf_op jit(solution)/shard_map/all_to_all | solution.py:31
  70.8 4.0 %copy.53 = bf16[4,4,2,32,8,128]{5,4,3,2,1,0:T(8,128)(2,1)S(1)} copy(bf16[4,4,2,32,8,128]{5,3,0,2,1,4:T(8,128)(2,1)} %bitcast.13) | data formatting | bytes 4194304 | tf_op jit(solution)/shard_map/transpose | solution.py:66
  74.8 6.4 %multiply_convert_fusion = (bf16[1280,1024]{1,0:T(8,128)(2,1)S(1)}, f32[1280,1024]{1,0:T(8,128)}) fusion(bf16[128,8,8,128]{3,2,1,0:T(8,128)(2,1)S(1)} %bitcast.78, bf16[640,1024]{1,0:T(8,128)(2,1)} %collective-permute-done, bf16[640,1024]{1,0:T(8,128)(2,1)} %fusion.10), kind=kOutput, calls=%fused_computation.8 | convolution fusion | flops 2696151040 | bytes 12582912 | tf_op jit(solution)/shard_map/dot_general | solution.py:74
  81.2 6.0 %convert_bitcast_fusion.1 = bf16[128,8,8,128]{3,1,2,0:T(8,128)(2,1)S(1)} fusion(bf16[1280,1024]{1,0:T(8,128)(2,1)S(1)} %get-tuple-element.5, bf16[1280,1024]{1,0:T(8,128)(2,1)} %constant_dynamic-update-slice_fusion.7), kind=kOutput, calls=%fused_computation.23 | convolution fusion | flops 2685403136 | bytes 7340032 | tf_op jit(solution)/shard_map/dot_general | solution.py:78
  87.9 1.9 copy.54
  89.7 5.4 %all-to-all-start.2 = ((bf16[32,4,64,128]{3,2,1,0:T(8,128)(2,1)}), bf16[32,4,64,128]{3,2,1,0:T(8,128)(2,1)}, u32[]{:S(2)}, u32[]{:S(2)}) async-start(bf16[32,4,64,128]{3,2,1,0:T(8,128)(2,1)} %bitcast.70), calls=%async_computation.2 | async-start | bytes 4194304 | tf_op jit(solution)/shard_map/all_to_all | solution.py:31
  95.2 10.8 %all-gather.2.cloned.1.call-done = bf16[1024,1024]{1,0:T(8,128)(2,1)} async-done(((bf16[64,1024]{1,0:T(8,128)(2,1)}), bf16[1024,1024]{1,0:T(8,128)(2,1)}) %all-gather.2.cloned.1.call-update) | async-done | bytes 2097168 | tf_op jit(solution)/shard_map/all_gather | solution.py:64
  106.0 12.6 %convert_bitcast_fusion = bf16[128,8,8,128]{3,1,2,0:T(8,128)(2,1)} fusion(bf16[640,1024]{1,0:T(8,128)(2,1)} %collective-permute-done, bf16[640,1024]{1,0:T(8,128)(2,1)} %fusion.10, f32[1280,1024]{1,0:T(8,128)} %get-tuple-element.6, bf16[1280,1024]{1,0:T(8,128)(2,1)} %constant_dynamic-update-slice_fusion.7, bf16[1024,1024]{1,0:T(8,128)(2,1)} %all-gather.2.cloned.1.call-done), kind=kOutput, calls=%fused_computation.22 | convolution fusion | flops 5388107776 | bytes 14680064 | tf_op jit(solution)/shard_map/dot_general | solution.py:85
  118.6 2.2 %copy.63 = bf16[128,8,8,128]{3,2,1,0:T(8,128)(2,1)S(1)} copy(bf16[128,8,8,128]{3,1,2,0:T(8,128)(2,1)} %convert_bitcast_fusion) | data formatting | bytes 4194304
  120.8 1.9 copy.55
  122.7 7.8 %all-to-all-done.2 = bf16[32,4,64,128]{3,2,1,0:T(8,128)(2,1)} async-done(((bf16[32,4,64,128]{3,2,1,0:T(8,128)(2,1)}), bf16[32,4,64,128]{3,2,1,0:T(8,128)(2,1)}, u32[]{:S(2)}, u32[]{:S(2)}) %all-to-all-start.2) | async-done | bytes 2097184 | tf_op jit(solution)/shard_map/all_to_all | solution.py:31
  130.5 7.8 %all-to-all-start.3 = ((bf16[64,4,32,128]{3,2,1,0:T(8,128)(2,1)}), bf16[64,4,32,128]{3,2,1,0:T(8,128)(2,1)}, u32[]{:S(2)}, u32[]{:S(2)}) async-start(bf16[64,4,32,128]{3,2,1,0:T(8,128)(2,1)} %bitcast.71), calls=%async_computation.3 | async-start | bytes 4194304 | tf_op jit(solution)/shard_map/all_to_all | solution.py:31
  138.4 2.0 reduce_sum.53
  140.3 26.6 %all-to-all-done.3 = bf16[64,4,32,128]{3,2,1,0:T(8,128)(2,1)} async-done(((bf16[64,4,32,128]{3,2,1,0:T(8,128)(2,1)}), bf16[64,4,32,128]{3,2,1,0:T(8,128)(2,1)}, u32[]{:S(2)}, u32[]{:S(2)}) %all-to-all-start.3) | async-done | bytes 2097184 | tf_op jit(solution)/shard_map/all_to_all | solution.py:31
  166.9 1.9 reduce_sum.54
  170.1 7.6 %all-to-all-start.4 = ((bf16[32,2,64,128]{3,2,1,0:T(8,128)(2,1)}), bf16[32,2,64,128]{3,2,1,0:T(8,128)(2,1)}, u32[]{:S(2)}, u32[]{:S(2)}) async-start(bf16[32,2,64,128]{3,2,1,0:T(8,128)(2,1)} %bitcast.77), calls=%async_computation.4 | async-start | bytes 2097152 | tf_op jit(solution)/shard_map/all_to_all | solution.py:31
  177.7 3.3 %convolution_convert_fusion = bf16[512,1024]{1,0:T(8,128)(2,1)S(1)} fusion(bf16[1024,1024]{1,0:T(8,128)(2,1)} %all-gather.2.cloned.1.call-done, bf16[1280,1024]{1,0:T(8,128)(2,1)} %copy-done.4), kind=kOutput, calls=%fused_computation.25 | convolution fusion | flops 1074266112 | bytes 4194304 | tf_op jit(solution)/shard_map/dot_general | solution.py:91
  181.4 2.6 %collective-permute-done.4 = bf16[512,1024]{1,0:T(8,128)(2,1)S(1)} collective-permute-done((bf16[512,1024]{1,0:T(8,128)(2,1)S(1)}, bf16[512,1024]{1,0:T(8,128)(2,1)S(1)}, u32[]{:S(2)}, u32[]{:S(2)}) %collective-permute-start.4) | collective-permute-done | bytes 1048608 | tf_op jit(solution)/shard_map/ppermute | solution.py:27
  184.1 2.3 %add_convert_fusion = bf16[512,1024]{1,0:T(8,128)(2,1)} fusion(bf16[512,1024]{1,0:T(8,128)(2,1)S(1)} %collective-permute-done.4, bf16[512,1024]{1,0:T(8,128)(2,1)S(1)} %copy-done.1, bf16[1024,1024]{1,0:T(8,128)(2,1)S(1)} %copy-done.3, bf16[1280,1024]{1,0:T(8,128)(2,1)S(1)} %copy-done.5), kind=kOutput, calls=%fused_computation.24 | convolution fusion | flops 1076363264 | bytes 6291456 | tf_op jit(solution)/shard_map/dot_general | solution.py:92
  186.4 17.2 %all-to-all-done.4 = bf16[32,2,64,128]{3,2,1,0:T(8,128)(2,1)} async-done(((bf16[32,2,64,128]{3,2,1,0:T(8,128)(2,1)}), bf16[32,2,64,128]{3,2,1,0:T(8,128)(2,1)}, u32[]{:S(2)}, u32[]{:S(2)}) %all-to-all-start.4) | async-done | bytes 1048608 | tf_op jit(solution)/shard_map/all_to_all | solution.py:31
  203.6 1.5 convert_reduce_fusion.1
  (58 shorter events, 12.1 us)
Async XLA Ops:
  7.2 11.4 %copy-start = (bf16[1024,1024]{1,0:T(8,128)(2,1)S(1)}, bf16[1024,1024]{1,0:T(8,128)(2,1)}, u32[]{:S(2)}) copy-start(bf16[1024,1024]{1,0:T(8,128)(2,1)} %param.9) | copy-start | bytes 6291460
  8.7 16.7 %collective-permute-start.3 = (bf16[2,32,128]{2,1,0:T(8,128)(2,1)S(1)}, bf16[2,32,128]{2,1,0:T(8,128)(2,1)S(1)}, u32[]{:S(2)}, u32[]{:S(2)}) collective-permute-start(bf16[2,32,128]{2,1,0:T(8,128)(2,1)S(1)} %reshape.126), channel_id=1, source_target_pairs={{24,0},{0,8},{8,16},{16,24},{25,1},{1,9},{9,17},{17,25},{26,2},{2,... | collective-permute-start | bytes 49160 | tf_op jit(solution)/shard_map/ppermute | solution.py:38
  13.2 12.1 %collective-permute-start.2 = (bf16[2,32,128]{2,1,0:T(8,128)(2,1)S(1)}, bf16[2,32,128]{2,1,0:T(8,128)(2,1)S(1)}, u32[]{:S(2)}, u32[]{:S(2)}) collective-permute-start(bf16[2,32,128]{2,1,0:T(8,128)(2,1)S(1)} %reshape.126), channel_id=1, source_target_pairs={{16,0},{24,8},{0,16},{8,24},{17,1},{25,9},{1,17},{9,25},{18,2},{26... | collective-permute-start | bytes 49160 | tf_op jit(solution)/shard_map/ppermute | solution.py:38
  14.2 11.0 %collective-permute-start.1 = (bf16[2,32,128]{2,1,0:T(8,128)(2,1)S(1)}, bf16[2,32,128]{2,1,0:T(8,128)(2,1)S(1)}, u32[]{:S(2)}, u32[]{:S(2)}) collective-permute-start(bf16[2,32,128]{2,1,0:T(8,128)(2,1)S(1)} %reshape.126), channel_id=1, source_target_pairs={{8,0},{16,8},{24,16},{0,24},{9,1},{17,9},{25,17},{1,25},{10,2},{18... | collective-permute-start | bytes 49160 | tf_op jit(solution)/shard_map/ppermute | solution.py:38
  20.2 12.2 %all-to-all-start = ((bf16[8,16,1024]{2,1,0:T(8,128)(2,1)}), bf16[8,16,1024]{2,1,0:T(8,128)(2,1)S(1)}, u32[]{:S(2)}, u32[]{:S(2)}) async-start(bf16[8,16,1024]{2,1,0:T(8,128)(2,1)} %broadcast_multiply_fusion), calls=%async_computation | async-start | bytes 524288 | tf_op jit(solution)/shard_map/all_to_all | solution.py:31
  34.3 9.2 %copy-start.2 = (bf16[1024]{0:T(1024)(128)(2,1)S(1)}, bf16[1024]{0:T(1024)(128)(2,1)}, u32[]{:S(2)}) copy-start(bf16[1024]{0:T(1024)(128)(2,1)} %param.15) | copy-start | bytes 6148
  34.3 9.2 %copy-start.1 = (bf16[512,1024]{1,0:T(8,128)(2,1)S(1)}, bf16[512,1024]{1,0:T(8,128)(2,1)}, u32[]{:S(2)}) copy-start(bf16[512,1024]{1,0:T(8,128)(2,1)} %param.12) | copy-start | bytes 3145732
  34.3 36.5 %all-to-all-start.1 = ((bf16[64,4,32,128]{3,2,1,0:T(8,128)(2,1)}), bf16[64,4,32,128]{3,2,1,0:T(8,128)(2,1)}, u32[]{:S(2)}, u32[]{:S(2)}) async-start(bf16[64,4,32,128]{3,2,1,0:T(8,128)(2,1)} %bitcast.69), calls=%async_computation.1 | async-start | bytes 4194304 | tf_op jit(solution)/shard_map/all_to_all | solution.py:31
  40.9 65.1 %all-gather.2.cloned.1.call-start = ((), (), s32[]{:S(2)}) async-start(), calls=%async_computation.5 | async-start | bytes 2228224 | tf_op jit(solution)/shard_map/all_gather | solution.py:64
  43.4 6.9 %collective-permute-start.5 = (bf16[640,1024]{1,0:T(8,128)(2,1)}, bf16[640,1024]{1,0:T(8,128)(2,1)}, u32[]{:S(2)}, u32[]{:S(2)}) collective-permute-start(bf16[640,1024]{1,0:T(8,128)(2,1)} %pad_maximum_fusion.4), channel_id=1, source_target_pairs={{0,1},{1,0},{2,3},{3,2},{4,5},{5,4},{6,7},{7,6},{8,9},{9,8},{10,11... | collective-permute-start | bytes 3932168 | tf_op jit(solution)/shard_map/ppermute | solution.py:27
  45.7 29.1 %collective-permute-start = (bf16[640,1024]{1,0:T(8,128)(2,1)}, bf16[640,1024]{1,0:T(8,128)(2,1)}, u32[]{:S(2)}, u32[]{:S(2)}) collective-permute-start(bf16[640,1024]{1,0:T(8,128)(2,1)} %fusion.10), channel_id=1, source_target_pairs={{0,1},{1,0},{2,3},{3,2},{4,5},{5,4},{6,7},{7,6},{8,9},{9,8},{10,11... | collective-permute-start | bytes 3932168 | tf_op jit(solution)/shard_map/ppermute | solution.py:27
  81.2 6.0 %copy-start.4 = (bf16[1280,1024]{1,0:T(8,128)(2,1)}, bf16[1280,1024]{1,0:T(8,128)(2,1)S(1)}, u32[]{:S(2)}) copy-start(bf16[1280,1024]{1,0:T(8,128)(2,1)S(1)} %get-tuple-element.5) | copy-start | bytes 7864324
  89.7 40.8 %all-to-all-start.2 = ((bf16[32,4,64,128]{3,2,1,0:T(8,128)(2,1)}), bf16[32,4,64,128]{3,2,1,0:T(8,128)(2,1)}, u32[]{:S(2)}, u32[]{:S(2)}) async-start(bf16[32,4,64,128]{3,2,1,0:T(8,128)(2,1)} %bitcast.70), calls=%async_computation.2 | async-start | bytes 4194304 | tf_op jit(solution)/shard_map/all_to_all | solution.py:31
  130.5 36.4 %all-to-all-start.3 = ((bf16[64,4,32,128]{3,2,1,0:T(8,128)(2,1)}), bf16[64,4,32,128]{3,2,1,0:T(8,128)(2,1)}, u32[]{:S(2)}, u32[]{:S(2)}) async-start(bf16[64,4,32,128]{3,2,1,0:T(8,128)(2,1)} %bitcast.71), calls=%async_computation.3 | async-start | bytes 4194304 | tf_op jit(solution)/shard_map/all_to_all | solution.py:31
  170.1 33.5 %all-to-all-start.4 = ((bf16[32,2,64,128]{3,2,1,0:T(8,128)(2,1)}), bf16[32,2,64,128]{3,2,1,0:T(8,128)(2,1)}, u32[]{:S(2)}, u32[]{:S(2)}) async-start(bf16[32,2,64,128]{3,2,1,0:T(8,128)(2,1)} %bitcast.77), calls=%async_computation.4 | async-start | bytes 2097152 | tf_op jit(solution)/shard_map/all_to_all | solution.py:31
  177.7 6.3 %copy-start.3 = (bf16[1024,1024]{1,0:T(8,128)(2,1)S(1)}, bf16[1024,1024]{1,0:T(8,128)(2,1)}, u32[]{:S(2)}) copy-start(bf16[1024,1024]{1,0:T(8,128)(2,1)} %all-gather.2.cloned.1.call-done) | copy-start | bytes 6291460
  177.7 6.3 %copy-start.5 = (bf16[1280,1024]{1,0:T(8,128)(2,1)S(1)}, bf16[1280,1024]{1,0:T(8,128)(2,1)}, u32[]{:S(2)}) copy-start(bf16[1280,1024]{1,0:T(8,128)(2,1)} %copy-done.4) | copy-start | bytes 7864324
  181.0 3.0 %collective-permute-start.4 = (bf16[512,1024]{1,0:T(8,128)(2,1)S(1)}, bf16[512,1024]{1,0:T(8,128)(2,1)S(1)}, u32[]{:S(2)}, u32[]{:S(2)}) collective-permute-start(bf16[512,1024]{1,0:T(8,128)(2,1)S(1)} %convolution_convert_fusion), channel_id=1, source_target_pairs={{0,1},{1,0},{2,3},{3,2},{4,5},{5,4},{6,7},{7,6},{8,9},{9,8},{10,11... | collective-permute-start | bytes 3145736 | tf_op jit(solution)/shard_map/ppermute | solution.py:27
Sparse Core Ops, SparseCore 0:
  46.4 59.6 all-gather.1

commit v2 on v1

v2 whole, which is shorter than its diff:
```python
import jax
import jax.numpy as jnp
from jax import lax
from jax.experimental import pallas as pl
from jax.experimental.pallas import tpu as pltpu
from jax.sharding import Mesh, PartitionSpec as P

PHYSICAL = (("y", 4), ("zl", 2), ("zh", 4), ("x", 4), ("c", 2))
SIZE = dict(PHYSICAL)
AXES = tuple(name for name, _ in PHYSICAL)
GRP = ("y", "zl")
DEV = ("zh", "x", "c")
N_GRP = SIZE["y"] * SIZE["zl"]
N_ZH, N_X, N_C = SIZE["zh"], SIZE["x"], SIZE["c"]
VMEM_BYTES = 48 * 1024 * 1024


def normalize(rows, ln_gain):
    values = rows.astype(jnp.float32)
    center = jnp.mean(values, axis=-1, keepdims=True)
    centred = values - center
    spread = jnp.mean(centred * centred, axis=-1, keepdims=True)
    return (centred * lax.rsqrt(spread + 1e-05) * ln_gain.astype(jnp.float32)).astype(jnp.bfloat16)


def gelu_parts(pre):
    cdf_value = 0.5 * (1.0 + lax.erf(pre * 0.7071067811865476))
    density = jnp.exp(-0.5 * pre * pre) * 0.3989422804014327
    return (pre * cdf_value, cdf_value + pre * density)


def swap(value):
    return lax.ppermute(value, "c", [(0, 1), (1, 0)])


def exchange(value, axes):
    return lax.all_to_all(value, axes, split_axis=0, concat_axis=0, tiled=True)


def shift_zh(value, step):
    return lax.ppermute(value, "zh", [(i, (i + step) % N_ZH) for i in range(N_ZH)])


def lanes_split(left, right):
    low = lax.broadcasted_iota(jnp.int32, left.shape, 1) < 64
    first = jnp.where(low, left, pltpu.roll(right, 64, 1))
    second = jnp.where(low, pltpu.roll(left, 64, 1), right)
    return first, second


def cut_kernel(group_ref, w_ref, out_ref):
    value = w_ref[...].astype(jnp.float32)
    first, second = lanes_split(value[:, :128], value[:, 128:])
    out_ref[0] = first.astype(out_ref.dtype)
    out_ref[1] = second.astype(out_ref.dtype)


def cut_up(w_up, group):
    rows = w_up.shape[0]
    return pl.pallas_call(
        cut_kernel,
        grid_spec=pltpu.PrefetchScalarGridSpec(
            num_scalar_prefetch=1,
            grid=(1,),
            in_specs=[pl.BlockSpec((rows, 256), lambda i, g: (0, g[0]))],
            out_specs=pl.BlockSpec((2, rows, 128), lambda i, g: (0, 0, 0)),
        ),
        out_shape=jax.ShapeDtypeStruct((2, rows, 128), w_up.dtype),
        name="cut_up",
    )(group.reshape(1), w_up)


def final_kernel(both_ref, down_ref, up_ref):
    rows = up_ref.shape[0]
    for g in range(N_GRP):
        down_ref[:, g * 128 : (g + 1) * 128] = both_ref[g, 0].astype(jnp.float32)
        left = both_ref[g, 1, :rows].astype(jnp.float32)
        right = both_ref[g, 1, rows:].astype(jnp.float32)
        first, second = lanes_split(left, right)
        up_ref[:, g * 256 : g * 256 + 128] = first
        up_ref[:, g * 256 + 128 : g * 256 + 256] = second


def finish(both, width, hid):
    rows = both.shape[2]
    return pl.pallas_call(
        final_kernel,
        out_shape=(
            jax.ShapeDtypeStruct((rows, width), jnp.float32),
            jax.ShapeDtypeStruct((rows // N_C, hid), jnp.float32),
        ),
        name="finish",
    )(both)


def join_cot(parts, cot):
    at = 0
    for part in parts:
        cot[at : at + part.shape[0], :] = part[...]
        at += part.shape[0]


def forward_kernel(zh_ref, own_ref, partner_ref, c0, c1, c2, c3, w_ref, hidden_ref, slope_ref, term_ref, w, cot):
    @pl.when(pl.program_id(0) == 0)
    def _():
        join_cot((c0, c1, c2, c3), cot)

    for j in range(N_ZH):
        at = pl.multiple_of(((zh_ref[0] + j) % N_ZH) * 256, 256)
        for g in range(2):
            w[pl.ds(at, 256), g * 128 : (g + 1) * 128] = w_ref[g, :, :, j].reshape(256, 128)
    rows = own_ref.shape[0]
    step = rows // 2
    for which, ref in enumerate((own_ref, partner_ref)):
        for at in range(0, rows, step):
            pre = jnp.dot(ref[at : at + step, :], w[...], preferred_element_type=jnp.float32)
            act, slope = gelu_parts(pre)
            to = which * rows + at
            hidden_ref[to : to + step, :] = act.astype(jnp.bfloat16)
            slope_ref[to : to + step, :] = slope.astype(jnp.bfloat16)
    term = lax.dot_general(hidden_ref[...], cot[...], (((0,), (0,)), ((), ())), preferred_element_type=jnp.float32)
    term = term.astype(jnp.bfloat16)
    for x in range(N_X):
        for g in range(N_GRP):
            term_ref[g, x, 0] = term[x * 64 : (x + 1) * 64, g * 128 : (g + 1) * 128]


def whole(array):
    return pl.BlockSpec(array.shape, lambda *i: (0,) * array.ndim)


def forward(zh, own, partner, cots, got_up):
    rows, width = own.shape
    half = N_GRP * 128
    return pl.pallas_call(
        forward_kernel,
        grid_spec=pltpu.PrefetchScalarGridSpec(
            num_scalar_prefetch=1,
            grid=(N_ZH,),
            in_specs=[
                whole(own),
                whole(partner),
                *[whole(c) for c in cots],
                pl.BlockSpec((2,) + got_up.shape[1:], lambda q, z: (q, 0, 0, 0, 0, 0)),
            ],
            out_specs=[
                pl.BlockSpec((2 * rows, 256), lambda q, z: (0, q)),
                pl.BlockSpec((2 * rows, 256), lambda q, z: (0, q)),
                pl.BlockSpec((N_GRP, N_X, 1, 64, 128), lambda q, z: (0, 0, q, 0, 0)),
            ],
            scratch_shapes=[pltpu.VMEM((width, 256), jnp.bfloat16), pltpu.VMEM((2 * rows, width), jnp.bfloat16)],
        ),
        out_shape=(
            jax.ShapeDtypeStruct((2 * rows, half), jnp.bfloat16),
            jax.ShapeDtypeStruct((2 * rows, half), jnp.bfloat16),
            jax.ShapeDtypeStruct((N_GRP, N_X, N_ZH, 64, 128), jnp.bfloat16),
        ),
        compiler_params=pltpu.CompilerParams(vmem_limit_bytes=VMEM_BYTES),
        cost_estimate=pl.CostEstimate(
            flops=8 * rows * width * half, bytes_accessed=24 * 1024 * 1024, transcendentals=4 * rows * half
        ),
        name="forward",
    )(zh.reshape(1), own, partner, *cots, got_up)


def backward_kernel(own_ref, partner_ref, c0, c1, c2, c3, w_ref, slope_ref, term_ref, pre_grad, cot):
    @pl.when(pl.program_id(0) == 0)
    def _():
        join_cot((c0, c1, c2, c3), cot)

    rows = own_ref.shape[0]
    step = rows // 2
    for at in range(0, 2 * rows, step):
        back = lax.dot_general(
            cot[at : at + step, :], w_ref[...], (((1,), (1,)), ((), ())), preferred_element_type=jnp.float32
        )
        slope = slope_ref[at : at + step, :].astype(jnp.float32)
        pre_grad[at : at + step, :] = (back * slope).astype(jnp.bfloat16)
    dims = (((0,), (0,)), ((), ()))
    term = lax.dot_general(own_ref[...], pre_grad[:rows, :], dims, preferred_element_type=jnp.float32)
    term += lax.dot_general(partner_ref[...], pre_grad[rows:, :], dims, preferred_element_type=jnp.float32)
    term = term.astype(jnp.bfloat16)
    for g in range(2):
        for z in range(N_ZH):
            for x in range(N_X):
                for c in range(N_C):
                    at = z * 256 + x * 64 + c * 32
                    term_ref[g, x, c, z] = term[at : at + 32, g * 128 : (g + 1) * 128]


def backward(own, partner, cots, down_half, slope):
    rows, width = own.shape
    half = down_half.shape[0]
    return pl.pallas_call(
        backward_kernel,
        grid=(half // 256,),
        in_specs=[
            whole(own),
            whole(partner),
            *[whole(c) for c in cots],
            pl.BlockSpec((256, width), lambda q: (q, 0)),
            pl.BlockSpec((2 * rows, 256), lambda q: (0, q)),
        ],
        out_specs=pl.BlockSpec((2, N_X, N_C, N_ZH, 32, 128), lambda q: (q, 0, 0, 0, 0, 0)),
        out_shape=jax.ShapeDtypeStruct((N_GRP, N_X, N_C, N_ZH, 32, 128), jnp.bfloat16),
        scratch_shapes=[pltpu.VMEM((2 * rows, 256), jnp.bfloat16), pltpu.VMEM((2 * rows, width), jnp.bfloat16)],
        compiler_params=pltpu.CompilerParams(vmem_limit_bytes=VMEM_BYTES),
        cost_estimate=pl.CostEstimate(
            flops=8 * rows * width * half, bytes_accessed=20 * 1024 * 1024, transcendentals=0
        ),
        name="backward",
    )(own, partner, *cots, down_half, slope)


def sum_zh(part, zh):
    total = lax.dynamic_index_in_dim(part, zh, 0, keepdims=False).astype(jnp.float32)
    for step in range(1, N_ZH):
        block = lax.dynamic_index_in_dim(part, (zh + step) % N_ZH, 0, keepdims=False)
        total += shift_zh(block, step).astype(jnp.float32)
    return total.astype(jnp.bfloat16)


def body(reservoir, send_rows, send_count, new_rows, w_up, w_down, ln_gain, grad_new, grad_old):
    slots = send_rows.shape[2]
    fresh_count, width = new_rows.shape
    up_rows, hid = w_up.shape
    group, zh = lax.axis_index(GRP), lax.axis_index("zh")

    down_half = lax.all_gather(w_down, ("zh", "x"), axis=0, tiled=True)

    mine = cut_up(w_up, group)
    column = jnp.stack([mine] + [shift_zh(mine, -step) for step in range(1, N_ZH)], axis=1)
    spread_up = jnp.broadcast_to(column[None], (N_GRP * N_X,) + column.shape)
    spread_up = spread_up.reshape(N_GRP * N_X * N_C, N_ZH, up_rows, 128)
    got_up = exchange(spread_up, ("y", "zl", "x", "c")).reshape(N_GRP, N_X, N_C, N_ZH, up_rows, 128)

    grad_new, grad_old, _ = lax.optimization_barrier((grad_new, grad_old, spread_up))
    blocks = grad_old.reshape(N_GRP, slots, width)
    y, zl = group // SIZE["zl"], group % SIZE["zl"]
    order, old_cot = [], []
    for dy in range(SIZE["y"]):
        for dz in range(SIZE["zl"]):
            to = (y + dy) % SIZE["y"] * SIZE["zl"] + (zl + dz) % SIZE["zl"]
            order.append((y - dy) % SIZE["y"] * SIZE["zl"] + (zl + dz) % SIZE["zl"])
            block = lax.dynamic_index_in_dim(blocks, to, 0, keepdims=False)
            if dy or dz:
                perm = [
                    (a * 2 + b, (a + dy) % SIZE["y"] * 2 + (b + dz) % 2)
                    for a in range(SIZE["y"])
                    for b in range(SIZE["zl"])
                ]
                block = lax.ppermute(block, GRP, perm)
            old_cot.append(block)
    old_cot = jnp.concatenate(old_cot, axis=0)
    order = jnp.stack(order)
    picks, counts = send_rows[0][order], send_count[0][order]
    live = (lax.broadcasted_iota(jnp.int32, (N_GRP, slots), 1) < counts[:, None]).astype(jnp.bfloat16)
    picked = reservoir[picks.reshape(-1)] * live.reshape(-1, 1)

    normed = normalize(jnp.concatenate([new_rows, picked], axis=0), ln_gain)
    partner = swap(normed)
    cots = (grad_new, old_cot, swap(grad_new), swap(old_cot))
    rows = normed.shape[0]

    hidden, slope, term_down = forward(zh, normed, partner, cots, got_up)
    part_down = exchange(term_down.reshape(N_GRP * N_X, N_ZH, 64, 128), ("y", "zl", "x"))
    part_down = jnp.sum(part_down.astype(jnp.float32), axis=0).astype(jnp.bfloat16)
    sum_down = sum_zh(part_down, zh)

    term_up = backward(normed, partner, cots, down_half, slope)
    part_up = exchange(term_up.reshape(N_GRP * N_X * N_C, N_ZH, up_rows, 128), ("y", "zl", "x", "c"))
    part_up = part_up.reshape(N_GRP * N_X, N_C, N_ZH, up_rows, 128)
    part_up = jnp.sum(part_up.astype(jnp.float32), axis=0).astype(jnp.bfloat16)
    sum_up = sum_zh(part_up.transpose(1, 0, 2, 3).reshape(N_ZH, N_C * up_rows, 128), zh)

    other = jnp.dot(hidden[rows : rows + fresh_count], down_half, preferred_element_type=jnp.float32)
    mixed = jnp.dot(hidden[:fresh_count], down_half, preferred_element_type=jnp.float32)
    returned = swap(other.astype(jnp.bfloat16)).astype(jnp.float32)
    block_out = (new_rows.astype(jnp.float32) + (mixed + returned)).astype(jnp.bfloat16)

    both = jnp.stack([sum_down, sum_up])
    both = exchange(jnp.broadcast_to(both[None], (N_GRP,) + both.shape), GRP)
    grad_down, grad_up = finish(both, width, hid)
    return (block_out, grad_up, grad_down)


def solution(mesh):
    fine = Mesh(mesh.devices.reshape(tuple(size for _, size in PHYSICAL)), AXES)
    every = P(AXES, None)
    return jax.shard_map(
        body,
        mesh=fine,
        in_specs=(every, P(AXES, None, None), every, every, P(DEV, None), P(DEV, None), P(), every, every),
        out_specs=(every, P(DEV, None), P(DEV, None)),
        check_vma=False,
    )
```

time: 219 us -> 223 us (1.018); the launches traced: 215 us -> 222 us
  Pallas kernels: 0 us -> 25.2 us
  matrix products: 30.6 us -> 8.61 us
  starting transfers between devices: 41.7 us -> 61.1 us
  local copies, waits for them, and re-layouts: 26.1 us -> 15.1 us
  other arithmetic: 11.7 us -> 6.01 us
    all_to_all x5 -> x4, waiting for transfers between devices: 76.7 us -> 20.3 us  [exchange(): return lax.all_to_all(value, axes, split_axis=0, concat_axis=0, tiled=True)]
    all_gather x1, waiting for transfers between devices: 10.8 us -> 46.4 us  [body(): down_half = lax.all_gather(w_down, ('zh', 'x'), axis=0, tiled=True)]
    pallas_call x0 -> x4, Pallas kernels: none -> 25.2 us  [the longest x1 11.5 us: forward(): pl.pallas_call(forward_kernel, grid_spec=pltpu.PrefetchScalarGridSpec(num...]
    dot_general x3 -> x0, matrix products: 25 us -> none  [the longest x1 12.6 us: body(): lax.dot_general(normed, pre_grad, (((0,), (0,)), ((), ())), preferred_ele...]
    ppermute x3 -> x16, starting transfers between devices: 8.39 us -> 31.4 us  [the longest x9 20 us: shift_zh(): lax.ppermute(value, 'zh', [(i, (i + step) % N_ZH) for i in range(N_ZH)])]
    ppermute x3 -> x16, waiting for transfers between devices: 0.01 us -> 22.6 us  [the longest x7 14.6 us: body(): block = lax.ppermute(block, GRP, perm)]
    reshape x6 -> x1, local copies, waits for them, and re-layouts: 7.08 us -> 0.08 us  [body(): picked = reservoir[picks.reshape(-1)] * live.reshape(-1, 1)]
    transpose x5 -> x1, local copies, waits for them, and re-layouts: 4.46 us -> 0.01 us  [body(): part_up.transpose(1, 0, 2, 3).reshape(N_ZH, N_C * up_rows, 128)]
  transfers between devices with their start and end apart: 12 -> 25, of which waited for: 7 -> 9; matrix products, arithmetic and copies ran while one was open for 27% -> 11% of each run, Pallas kernels for 0% -> 10%
where the time goes in v2:
time: 223 us; the launch traced here: 222 us
  waiting for transfers between devices  91.2 us (41%)
  starting transfers between devices  61.1 us (27%)
  Pallas kernels  25.2 us (11%)
  local copies, waits for them, and re-layouts  15.1 us (7%)
  between operations  14.5 us (7%)
  matrix products  8.61 us (4%)
  other arithmetic  6.01 us (3%)
    all_gather x1, waiting for transfers between devices, body(): down_half = lax.all_gather(w_down, ('zh', 'x'), axis=0, tiled=True)  46.4 us
    all_to_all x4, starting transfers between devices, exchange(): return lax.all_to_all(value, axes, split_axis=0, concat_axis=0, tiled=True)  29.6 us
    all_to_all x4, waiting for transfers between devices, exchange(): return lax.all_to_all(value, axes, split_axis=0, concat_axis=0, tiled=True)  20.3 us
    ppermute x9, starting transfers between devices, shift_zh(): lax.ppermute(value, 'zh', [(i, (i + step) % N_ZH) for i in range(N_ZH)])  20 us
    ppermute x7, waiting for transfers between devices, body(): block = lax.ppermute(block, GRP, perm)  14.6 us
    pallas_call x1, Pallas kernels, forward(): pl.pallas_call(forward_kernel, grid_spec=pltpu.PrefetchScalarGridSpec(num...  11.5 us
    ppermute x7, starting transfers between devices, body(): block = lax.ppermute(block, GRP, perm)  11.3 us
    pallas_call x1, Pallas kernels, backward(): pl.pallas_call(backward_kernel, grid=(half // 256,), in_specs=[whole(own)...  10.4 us
  transfers between devices with their start and end apart: 25, of which 9 were waited for; matrix products, arithmetic and copies ran while one was open for 11% of the time, Pallas kernels for 10%

profile of v2, /device:TPU:64, one launch (start us, length us, event | category | flops | bytes accessed | tf_op | source)
XLA Modules:
  0.0 221.8 jit_solution(3350992997387573681)
XLA Ops:
  7.2 1.5 cut_up.1
  10.1 5.5 %collective-permute-start.2 = (bf16[2,32,128]{2,1,0:T(8,128)(2,1)}, bf16[2,32,128]{2,1,0:T(8,128)(2,1)S(1)}, u32[]{:S(2)}, u32[]{:S(2)}) collective-permute-start(bf16[2,32,128]{2,1,0:T(8,128)(2,1)} %cut_up.1), channel_id=1, source_target_pairs={{0,16},{8,24},{16,0},{24,8},{1,17},{9,25},{17,1},{25,9},{2,18},{10... | collective-permute-start | bytes 49160 | tf_op jit(solution)/shard_map/ppermute | solution.py:41
  15.6 2.7 %collective-permute-start.3 = (bf16[2,32,128]{2,1,0:T(8,128)(2,1)}, bf16[2,32,128]{2,1,0:T(8,128)(2,1)S(1)}, u32[]{:S(2)}, u32[]{:S(2)}) collective-permute-start(bf16[2,32,128]{2,1,0:T(8,128)(2,1)} %cut_up.1), channel_id=1, source_target_pairs={{0,8},{8,16},{16,24},{24,0},{1,9},{9,17},{17,25},{25,1},{2,10},{10... | collective-permute-start | bytes 49160 | tf_op jit(solution)/shard_map/ppermute | solution.py:41
  18.3 2.2 collective-permute-done.3
  21.2 1.9 broadcast_in_dim.4
  23.0 8.8 %all-to-all-start = ((bf16[64,4,32,128]{3,2,1,0:T(8,128)(2,1)}), bf16[64,4,32,128]{3,2,1,0:T(8,128)(2,1)}, u32[]{:S(2)}, u32[]{:S(2)}) async-start(bf16[64,4,32,128]{3,2,1,0:T(8,128)(2,1)} %bitcast.69), calls=%async_computation | async-start | bytes 4194304 | tf_op jit(solution)/shard_map/all_to_all | solution.py:37
  37.3 1.6 collective-permute-start.4
  40.3 1.5 collective-permute-start.5
  41.8 1.5 collective-permute-start.6
  43.3 1.6 collective-permute-start.7
  44.9 12.6 %collective-permute-done.4 = bf16[16,1024]{1,0:T(8,128)(2,1)S(1)} collective-permute-done((bf16[16,1024]{1,0:T(8,128)(2,1)S(1)}, bf16[16,1024]{1,0:T(8,128)(2,1)S(1)}, u32[]{:S(2)}, u32[]{:S(2)}) %collective-permute-start.4) | collective-permute-done | bytes 32800 | tf_op jit(solution)/shard_map/ppermute | solution.py:252
  58.1 3.1 %collective-permute-start.8 = (bf16[16,1024]{1,0:T(8,128)(2,1)S(1)}, bf16[16,1024]{1,0:T(8,128)(2,1)S(1)}, u32[]{:S(2)}, u32[]{:S(2)}) collective-permute-start(bf16[16,1024]{1,0:T(8,128)(2,1)S(1)} %get-tuple-element.19), channel_id=1, source_target_pairs={{0,160},{32,128},{64,224},{96,192},{128,32},{160,0},{192,96},{224,... | collective-permute-start | bytes 98312 | tf_op jit(solution)/shard_map/ppermute | solution.py:252
  66.4 2.0 collective-permute-done.10
  69.0 1.8 collective-permute-done.12.c3
  72.1 11.5 %forward.1 = (bf16[1280,1024]{1,0:T(8,128)(2,1)}, bf16[1280,1024]{1,0:T(8,128)(2,1)}, bf16[8,4,4,64,128]{4,3,2,1,0:T(8,128)(2,1)}) custom-call(s32[1]{0:T(128)} %bitcast.zh_ref, bf16[640,1024]{1,0:T(8,128)(2,1)S(1)} %fusion.4.own_ref, bf16[640,1024]{1,0:T(8,128)(2,1)} %collective-permute-done.partner_ref, bf16[512,1024]{1,0:T(8,128)(2,1)S(1)} %copy-done.1, ...), custom_call_target="tpu_custom_call" | custom-call | flops 5368709120 | bytes 25165824 | tf_op jit(solution)/shard_map/forward/pallas_call | solution.py:135
  83.6 7.5 %all-to-all-start.1 = ((bf16[32,4,64,128]{3,2,1,0:T(8,128)(2,1)}), bf16[32,4,64,128]{3,2,1,0:T(8,128)(2,1)}, u32[]{:S(2)}, u32[]{:S(2)}) async-start(bf16[32,4,64,128]{3,2,1,0:T(8,128)(2,1)} %bitcast.71), calls=%async_computation.1 | async-start | bytes 4194304 | tf_op jit(solution)/shard_map/all_to_all | solution.py:37
  91.1 46.4 %all-gather.2.cloned.1.call-done.w_ref = bf16[1024,1024]{1,0:T(8,128)(2,1)} async-done(((bf16[64,1024]{1,0:T(8,128)(2,1)}), bf16[1024,1024]{1,0:T(8,128)(2,1)}) %all-gather.2.cloned.1.call-update) | async-done | bytes 2097168 | tf_op jit(solution)/shard_map/all_gather | solution.py:229
  138.8 10.4 %backward.1 = bf16[8,4,2,4,32,128]{5,4,3,2,1,0:T(8,128)(2,1)} custom-call(bf16[640,1024]{1,0:T(8,128)(2,1)S(1)} %fusion.4.own_ref, bf16[640,1024]{1,0:T(8,128)(2,1)} %collective-permute-done.partner_ref, bf16[512,1024]{1,0:T(8,128)(2,1)S(1)} %copy-done.2, bf16[128,1024]{1,0:T(8,128)(2,1)} %constant_dynamic-update-slice_fusion.c1, ...), custom_call_target="tpu_custom_call" | custom-call | flops 5368709120 | bytes 20971520 | tf_op jit(solution)/shard_map/backward/pallas_call | solution.py:194
  149.2 9.4 %all-to-all-start.2 = ((bf16[64,4,32,128]{3,2,1,0:T(8,128)(2,1)}), bf16[64,4,32,128]{3,2,1,0:T(8,128)(2,1)}, u32[]{:S(2)}, u32[]{:S(2)}) async-start(bf16[64,4,32,128]{3,2,1,0:T(8,128)(2,1)} %bitcast.70), calls=%async_computation.2 | async-start | bytes 4194304 | tf_op jit(solution)/shard_map/all_to_all | solution.py:37
  158.5 4.1 %convolution_convert_fusion = bf16[512,1024]{1,0:T(8,128)(2,1)} fusion(bf16[1024,1024]{1,0:T(8,128)(2,1)} %all-gather.2.cloned.1.call-done.w_ref, bf16[1280,1024]{1,0:T(8,128)(2,1)} %get-tuple-element.12), kind=kOutput, calls=%fused_computation.11 | convolution fusion | flops 1074266112 | bytes 4194304 | tf_op jit(solution)/shard_map/dot_general | solution.py:276
  162.7 2.0 reduce_sum.44
  164.7 2.0 collective-permute-start.14
  166.7 3.2 %collective-permute-start.15 = (bf16[64,128]{1,0:T(8,128)(2,1)S(1)}, bf16[64,128]{1,0:T(8,128)(2,1)S(1)}, u32[]{:S(2)}, u32[]{:S(2)}) collective-permute-start(bf16[64,128]{1,0:T(8,128)(2,1)S(1)} %get-tuple-element.26), channel_id=1, source_target_pairs={{0,16},{8,24},{16,0},{24,8},{1,17},{9,25},{17,1},{25,9},{2,18},{10... | collective-permute-start | bytes 49160 | tf_op jit(solution)/shard_map/ppermute | solution.py:41
  169.9 17.5 %all-to-all-done.2 = bf16[64,4,32,128]{3,2,1,0:T(8,128)(2,1)} async-done(((bf16[64,4,32,128]{3,2,1,0:T(8,128)(2,1)}), bf16[64,4,32,128]{3,2,1,0:T(8,128)(2,1)}, u32[]{:S(2)}, u32[]{:S(2)}) %all-to-all-start.2) | async-done | bytes 2097184 | tf_op jit(solution)/shard_map/all_to_all | solution.py:37
  187.4 1.9 reduce_sum.45
  189.4 2.0 collective-permute-start.17
  191.4 3.2 %collective-permute-start.18 = (bf16[64,128]{1,0:T(8,128)(2,1)S(1)}, bf16[64,128]{1,0:T(8,128)(2,1)S(1)}, u32[]{:S(2)}, u32[]{:S(2)}) collective-permute-start(bf16[64,128]{1,0:T(8,128)(2,1)S(1)} %get-tuple-element.29), channel_id=1, source_target_pairs={{0,16},{8,24},{16,0},{24,8},{1,17},{9,25},{17,1},{25,9},{2,18},{10... | collective-permute-start | bytes 49160 | tf_op jit(solution)/shard_map/ppermute | solution.py:41
  194.7 4.4 %collective-permute-done.18 = bf16[64,128]{1,0:T(8,128)(2,1)S(1)} collective-permute-done((bf16[64,128]{1,0:T(8,128)(2,1)S(1)}, bf16[64,128]{1,0:T(8,128)(2,1)S(1)}, u32[]{:S(2)}, u32[]{:S(2)}) %collective-permute-start.18) | collective-permute-done | bytes 16416 | tf_op jit(solution)/shard_map/ppermute | solution.py:41
  201.3 3.9 %all-to-all-start.3 = ((bf16[8,2,64,128]{3,2,1,0:T(8,128)(2,1)}), bf16[8,2,64,128]{3,2,1,0:T(8,128)(2,1)S(1)}, u32[]{:S(2)}, u32[]{:S(2)}) async-start(bf16[8,2,64,128]{3,2,1,0:T(8,128)(2,1)} %broadcast_in_dim.5), calls=%async_computation.3 | async-start | bytes 524288 | tf_op jit(solution)/shard_map/all_to_all | solution.py:37
  205.2 4.5 %add_convert_fusion = bf16[512,1024]{1,0:T(8,128)(2,1)} fusion(bf16[512,1024]{1,0:T(8,128)(2,1)} %collective-permute-done.13, bf16[512,1024]{1,0:T(8,128)(2,1)S(1)} %copy-done.6, bf16[1024,1024]{1,0:T(8,128)(2,1)} %all-gather.2.cloned.1.call-done.w_ref, bf16[1280,1024]{1,0:T(8,128)(2,1)} %get-tuple-element.12), kind=kOutput, calls=%fused_computation.10 | convolution fusion | flops 1076363264 | bytes 6291456 | tf_op jit(solution)/shard_map/dot_general | solution.py:277
  209.7 2.8 %all-to-all-done.3.both_ref = bf16[8,2,64,128]{3,2,1,0:T(8,128)(2,1)S(1)} async-done(((bf16[8,2,64,128]{3,2,1,0:T(8,128)(2,1)}), bf16[8,2,64,128]{3,2,1,0:T(8,128)(2,1)S(1)}, u32[]{:S(2)}, u32[]{:S(2)}) %all-to-all-start.3) | async-done | bytes 262176 | tf_op jit(solution)/shard_map/all_to_all | solution.py:37
  213.2 1.8 finish.1
  (84 shorter events, 20.5 us)
Async XLA Ops:
  7.2 26.5 %copy-start = (bf16[1024,1024]{1,0:T(8,128)(2,1)S(1)}, bf16[1024,1024]{1,0:T(8,128)(2,1)}, u32[]{:S(2)}) copy-start(bf16[1024,1024]{1,0:T(8,128)(2,1)} %param.9) | copy-start | bytes 6291460
  8.7 9.5 %collective-permute-start.1 = (bf16[2,32,128]{2,1,0:T(8,128)(2,1)}, bf16[2,32,128]{2,1,0:T(8,128)(2,1)S(1)}, u32[]{:S(2)}, u32[]{:S(2)}) collective-permute-start(bf16[2,32,128]{2,1,0:T(8,128)(2,1)} %cut_up.1), channel_id=1, source_target_pairs={{0,24},{8,0},{16,8},{24,16},{1,25},{9,1},{17,9},{25,17},{2,26},{10... | collective-permute-start | bytes 49160 | tf_op jit(solution)/shard_map/ppermute | solution.py:41
  10.1 8.1 %collective-permute-start.2 = (bf16[2,32,128]{2,1,0:T(8,128)(2,1)}, bf16[2,32,128]{2,1,0:T(8,128)(2,1)S(1)}, u32[]{:S(2)}, u32[]{:S(2)}) collective-permute-start(bf16[2,32,128]{2,1,0:T(8,128)(2,1)} %cut_up.1), channel_id=1, source_target_pairs={{0,16},{8,24},{16,0},{24,8},{1,17},{9,25},{17,1},{25,9},{2,18},{10... | collective-permute-start | bytes 49160 | tf_op jit(solution)/shard_map/ppermute | solution.py:41
  15.6 4.8 %collective-permute-start.3 = (bf16[2,32,128]{2,1,0:T(8,128)(2,1)}, bf16[2,32,128]{2,1,0:T(8,128)(2,1)S(1)}, u32[]{:S(2)}, u32[]{:S(2)}) collective-permute-start(bf16[2,32,128]{2,1,0:T(8,128)(2,1)} %cut_up.1), channel_id=1, source_target_pairs={{0,8},{8,16},{16,24},{24,0},{1,9},{9,17},{17,25},{25,1},{2,10},{10... | collective-permute-start | bytes 49160 | tf_op jit(solution)/shard_map/ppermute | solution.py:41
  23.0 9.1 %copy-start.8 = (s32[1,8,16]{2,1,0:T(8,128)S(1)}, s32[1,8,16]{2,1,0:T(8,128)}, u32[]{:S(2)}) copy-start(s32[1,8,16]{2,1,0:T(8,128)} %param.10) | copy-start | bytes 1540
  23.0 9.7 %copy-start.3 = (s32[1,8]{1,0:T(1,128)S(1)}, s32[1,8]{1,0:T(1,128)}, u32[]{:S(2)}) copy-start(s32[1,8]{1,0:T(1,128)} %param.11) | copy-start | bytes 100
  23.0 10.6 %copy-start.9 = (bf16[1024]{0:T(1024)(128)(2,1)S(1)}, bf16[1024]{0:T(1024)(128)(2,1)}, u32[]{:S(2)}) copy-start(bf16[1024]{0:T(1024)(128)(2,1)} %param.15) | copy-start | bytes 6148
  23.0 47.8 %all-to-all-start = ((bf16[64,4,32,128]{3,2,1,0:T(8,128)(2,1)}), bf16[64,4,32,128]{3,2,1,0:T(8,128)(2,1)}, u32[]{:S(2)}, u32[]{:S(2)}) async-start(bf16[64,4,32,128]{3,2,1,0:T(8,128)(2,1)} %bitcast.69), calls=%async_computation | async-start | bytes 4194304 | tf_op jit(solution)/shard_map/all_to_all | solution.py:37
  31.8 2.8 %copy-start.4 = (bf16[512,1024]{1,0:T(8,128)(2,1)S(1)}, bf16[512,1024]{1,0:T(8,128)(2,1)}, u32[]{:S(2)}) copy-start(bf16[512,1024]{1,0:T(8,128)(2,1)} %param.12) | copy-start | bytes 3145732
  31.8 105.7 %all-gather.2.cloned.1.call-start = ((), (), s32[]{:S(2)}) async-start(), calls=%async_computation.4 | async-start | bytes 2228224 | tf_op jit(solution)/shard_map/all_gather | solution.py:229
  36.2 34.6 %collective-permute-start = (bf16[640,1024]{1,0:T(8,128)(2,1)S(1)}, bf16[640,1024]{1,0:T(8,128)(2,1)}, u32[]{:S(2)}, u32[]{:S(2)}) collective-permute-start(bf16[640,1024]{1,0:T(8,128)(2,1)S(1)} %fusion.4.own_ref), channel_id=1, source_target_pairs={{0,1},{1,0},{2,3},{3,2},{4,5},{5,4},{6,7},{7,6},{8,9},{9,8},{10,11... | collective-permute-start | bytes 3932168 | tf_op jit(solution)/shard_map/ppermute | solution.py:33
  37.3 20.2 %collective-permute-start.4 = (bf16[16,1024]{1,0:T(8,128)(2,1)S(1)}, bf16[16,1024]{1,0:T(8,128)(2,1)S(1)}, u32[]{:S(2)}, u32[]{:S(2)}) collective-permute-start(bf16[16,1024]{1,0:T(8,128)(2,1)S(1)} %get-tuple-element.23), channel_id=1, source_target_pairs={{0,32},{32,0},{64,96},{96,64},{128,160},{160,128},{192,224},{224,1... | collective-permute-start | bytes 98312 | tf_op jit(solution)/shard_map/ppermute | solution.py:252
  40.3 17.9 %collective-permute-start.5 = (bf16[16,1024]{1,0:T(8,128)(2,1)S(1)}, bf16[16,1024]{1,0:T(8,128)(2,1)S(1)}, u32[]{:S(2)}, u32[]{:S(2)}) collective-permute-start(bf16[16,1024]{1,0:T(8,128)(2,1)S(1)} %get-tuple-element.22), channel_id=1, source_target_pairs={{0,64},{32,96},{64,128},{96,160},{128,192},{160,224},{192,0},{224,... | collective-permute-start | bytes 98312 | tf_op jit(solution)/shard_map/ppermute | solution.py:252
  41.8 20.0 %collective-permute-start.6 = (bf16[16,1024]{1,0:T(8,128)(2,1)S(1)}, bf16[16,1024]{1,0:T(8,128)(2,1)S(1)}, u32[]{:S(2)}, u32[]{:S(2)}) collective-permute-start(bf16[16,1024]{1,0:T(8,128)(2,1)S(1)} %get-tuple-element.21), channel_id=1, source_target_pairs={{0,96},{32,64},{64,160},{96,128},{128,224},{160,192},{192,32},{224... | collective-permute-start | bytes 98312 | tf_op jit(solution)/shard_map/ppermute | solution.py:252
  43.3 20.2 %collective-permute-start.7 = (bf16[16,1024]{1,0:T(8,128)(2,1)S(1)}, bf16[16,1024]{1,0:T(8,128)(2,1)S(1)}, u32[]{:S(2)}, u32[]{:S(2)}) collective-permute-start(bf16[16,1024]{1,0:T(8,128)(2,1)S(1)} %get-tuple-element.20), channel_id=1, source_target_pairs={{0,128},{32,160},{64,192},{96,224},{128,0},{160,32},{192,64},{224,... | collective-permute-start | bytes 98312 | tf_op jit(solution)/shard_map/ppermute | solution.py:252
  57.5 13.3 %collective-permute-start.11 = (bf16[512,1024]{1,0:T(8,128)(2,1)}, bf16[512,1024]{1,0:T(8,128)(2,1)}, u32[]{:S(2)}, u32[]{:S(2)}) collective-permute-start(bf16[512,1024]{1,0:T(8,128)(2,1)} %c0.1), channel_id=1, source_target_pairs={{0,1},{1,0},{2,3},{3,2},{4,5},{5,4},{6,7},{7,6},{8,9},{9,8},{10,11... | collective-permute-start | bytes 3145736 | tf_op jit(solution)/shard_map/ppermute | solution.py:33
  58.1 6.9 %collective-permute-start.8 = (bf16[16,1024]{1,0:T(8,128)(2,1)S(1)}, bf16[16,1024]{1,0:T(8,128)(2,1)S(1)}, u32[]{:S(2)}, u32[]{:S(2)}) collective-permute-start(bf16[16,1024]{1,0:T(8,128)(2,1)S(1)} %get-tuple-element.19), channel_id=1, source_target_pairs={{0,160},{32,128},{64,224},{96,192},{128,32},{160,0},{192,96},{224,... | collective-permute-start | bytes 98312 | tf_op jit(solution)/shard_map/ppermute | solution.py:252
  61.8 3.9 %collective-permute-start.9 = (bf16[16,1024]{1,0:T(8,128)(2,1)S(1)}, bf16[16,1024]{1,0:T(8,128)(2,1)S(1)}, u32[]{:S(2)}, u32[]{:S(2)}) collective-permute-start(bf16[16,1024]{1,0:T(8,128)(2,1)S(1)} %get-tuple-element.18), channel_id=1, source_target_pairs={{0,192},{32,224},{64,0},{96,32},{128,64},{160,96},{192,128},{224,1... | collective-permute-start | bytes 98312 | tf_op jit(solution)/shard_map/ppermute | solution.py:252
  63.5 4.8 %collective-permute-start.10 = (bf16[16,1024]{1,0:T(8,128)(2,1)S(1)}, bf16[16,1024]{1,0:T(8,128)(2,1)S(1)}, u32[]{:S(2)}, u32[]{:S(2)}) collective-permute-start(bf16[16,1024]{1,0:T(8,128)(2,1)S(1)} %get-tuple-element.17), channel_id=1, source_target_pairs={{0,224},{32,192},{64,32},{96,0},{128,96},{160,64},{192,160},{224,1... | collective-permute-start | bytes 98312 | tf_op jit(solution)/shard_map/ppermute | solution.py:252
  68.9 1.9 collective-permute-start.12
  70.8 1.2 copy-start.1
  83.6 65.6 %all-to-all-start.1 = ((bf16[32,4,64,128]{3,2,1,0:T(8,128)(2,1)}), bf16[32,4,64,128]{3,2,1,0:T(8,128)(2,1)}, u32[]{:S(2)}, u32[]{:S(2)}) async-start(bf16[32,4,64,128]{3,2,1,0:T(8,128)(2,1)} %bitcast.71), calls=%async_computation.1 | async-start | bytes 4194304 | tf_op jit(solution)/shard_map/all_to_all | solution.py:37
  149.2 38.3 %all-to-all-start.2 = ((bf16[64,4,32,128]{3,2,1,0:T(8,128)(2,1)}), bf16[64,4,32,128]{3,2,1,0:T(8,128)(2,1)}, u32[]{:S(2)}, u32[]{:S(2)}) async-start(bf16[64,4,32,128]{3,2,1,0:T(8,128)(2,1)} %bitcast.70), calls=%async_computation.2 | async-start | bytes 4194304 | tf_op jit(solution)/shard_map/all_to_all | solution.py:37
  162.7 42.5 %collective-permute-start.13 = (bf16[512,1024]{1,0:T(8,128)(2,1)}, bf16[512,1024]{1,0:T(8,128)(2,1)}, u32[]{:S(2)}, u32[]{:S(2)}) collective-permute-start(bf16[512,1024]{1,0:T(8,128)(2,1)} %convolution_convert_fusion), channel_id=1, source_target_pairs={{0,1},{1,0},{2,3},{3,2},{4,5},{5,4},{6,7},{7,6},{8,9},{9,8},{10,11... | collective-permute-start | bytes 3145736 | tf_op jit(solution)/shard_map/ppermute | solution.py:33
  164.6 40.6 %copy-start.6 = (bf16[512,1024]{1,0:T(8,128)(2,1)S(1)}, bf16[512,1024]{1,0:T(8,128)(2,1)}, u32[]{:S(2)}) copy-start(bf16[512,1024]{1,0:T(8,128)(2,1)} %param.12) | copy-start | bytes 3145732
  164.7 26.7 %collective-permute-start.14 = (bf16[64,128]{1,0:T(8,128)(2,1)S(1)}, bf16[64,128]{1,0:T(8,128)(2,1)S(1)}, u32[]{:S(2)}, u32[]{:S(2)}) collective-permute-start(bf16[64,128]{1,0:T(8,128)(2,1)S(1)} %get-tuple-element.24), channel_id=1, source_target_pairs={{0,8},{8,16},{16,24},{24,0},{1,9},{9,17},{17,25},{25,1},{2,10},{10... | collective-permute-start | bytes 49160 | tf_op jit(solution)/shard_map/ppermute | solution.py:41
  166.7 27.9 %collective-permute-start.15 = (bf16[64,128]{1,0:T(8,128)(2,1)S(1)}, bf16[64,128]{1,0:T(8,128)(2,1)S(1)}, u32[]{:S(2)}, u32[]{:S(2)}) collective-permute-start(bf16[64,128]{1,0:T(8,128)(2,1)S(1)} %get-tuple-element.26), channel_id=1, source_target_pairs={{0,16},{8,24},{16,0},{24,8},{1,17},{9,25},{17,1},{25,9},{2,18},{10... | collective-permute-start | bytes 49160 | tf_op jit(solution)/shard_map/ppermute | solution.py:41
  169.9 24.7 %collective-permute-start.16 = (bf16[64,128]{1,0:T(8,128)(2,1)S(1)}, bf16[64,128]{1,0:T(8,128)(2,1)S(1)}, u32[]{:S(2)}, u32[]{:S(2)}) collective-permute-start(bf16[64,128]{1,0:T(8,128)(2,1)S(1)} %get-tuple-element.25), channel_id=1, source_target_pairs={{0,24},{8,0},{16,8},{24,16},{1,25},{9,1},{17,9},{25,17},{2,26},{10... | collective-permute-start | bytes 49160 | tf_op jit(solution)/shard_map/ppermute | solution.py:41
  189.4 5.3 %collective-permute-start.17 = (bf16[64,128]{1,0:T(8,128)(2,1)S(1)}, bf16[64,128]{1,0:T(8,128)(2,1)S(1)}, u32[]{:S(2)}, u32[]{:S(2)}) collective-permute-start(bf16[64,128]{1,0:T(8,128)(2,1)S(1)} %get-tuple-element.27), channel_id=1, source_target_pairs={{0,8},{8,16},{16,24},{24,0},{1,9},{9,17},{17,25},{25,1},{2,10},{10... | collective-permute-start | bytes 49160 | tf_op jit(solution)/shard_map/ppermute | solution.py:41
  191.4 7.6 %collective-permute-start.18 = (bf16[64,128]{1,0:T(8,128)(2,1)S(1)}, bf16[64,128]{1,0:T(8,128)(2,1)S(1)}, u32[]{:S(2)}, u32[]{:S(2)}) collective-permute-start(bf16[64,128]{1,0:T(8,128)(2,1)S(1)} %get-tuple-element.29), channel_id=1, source_target_pairs={{0,16},{8,24},{16,0},{24,8},{1,17},{9,25},{17,1},{25,9},{2,18},{10... | collective-permute-start | bytes 49160 | tf_op jit(solution)/shard_map/ppermute | solution.py:41
  194.6 5.9 %collective-permute-start.19 = (bf16[64,128]{1,0:T(8,128)(2,1)S(1)}, bf16[64,128]{1,0:T(8,128)(2,1)S(1)}, u32[]{:S(2)}, u32[]{:S(2)}) collective-permute-start(bf16[64,128]{1,0:T(8,128)(2,1)S(1)} %get-tuple-element.28), channel_id=1, source_target_pairs={{0,24},{8,0},{16,8},{24,16},{1,25},{9,1},{17,9},{25,17},{2,26},{10... | collective-permute-start | bytes 49160 | tf_op jit(solution)/shard_map/ppermute | solution.py:41
  201.3 11.2 %all-to-all-start.3 = ((bf16[8,2,64,128]{3,2,1,0:T(8,128)(2,1)}), bf16[8,2,64,128]{3,2,1,0:T(8,128)(2,1)S(1)}, u32[]{:S(2)}, u32[]{:S(2)}) async-start(bf16[8,2,64,128]{3,2,1,0:T(8,128)(2,1)} %broadcast_in_dim.5), calls=%async_computation.3 | async-start | bytes 524288 | tf_op jit(solution)/shard_map/all_to_all | solution.py:37
  (3 other events, 3.1 us)
Sparse Core Ops, SparseCore 0:
  69.1 68.4 all-gather.1

commit v3 on v2

--- a/solution.py
+++ b/solution.py
@@ -157,22 +157,23 @@
         ),
         compiler_params=pltpu.CompilerParams(vmem_limit_bytes=VMEM_BYTES),
         cost_estimate=pl.CostEstimate(
-            flops=8 * rows * width * half, bytes_accessed=24 * 1024 * 1024, transcendentals=4 * rows * half
+            flops=0, bytes_accessed=1024, transcendentals=0
         ),
         name="forward",
     )(zh.reshape(1), own, partner, *cots, got_up)
 
 
-def backward_kernel(own_ref, partner_ref, c0, c1, c2, c3, w_ref, slope_ref, term_ref, pre_grad, cot):
+def backward_kernel(core_ref, own_ref, partner_ref, c0, c1, c2, c3, w_ref, slope_ref, term_ref, pre_grad, cot):
     @pl.when(pl.program_id(0) == 0)
     def _():
         join_cot((c0, c1, c2, c3), cot)
 
-    rows = own_ref.shape[0]
+    rows, width = own_ref.shape
     step = rows // 2
+    w = w_ref[...].reshape(256, width)
     for at in range(0, 2 * rows, step):
         back = lax.dot_general(
-            cot[at : at + step, :], w_ref[...], (((1,), (1,)), ((), ())), preferred_element_type=jnp.float32
+            cot[at : at + step, :], w, (((1,), (1,)), ((), ())), preferred_element_type=jnp.float32
         )
         slope = slope_ref[at : at + step, :].astype(jnp.float32)
         pre_grad[at : at + step, :] = (back * slope).astype(jnp.bfloat16)
@@ -188,28 +189,31 @@
                     term_ref[g, x, c, z] = term[at : at + 32, g * 128 : (g + 1) * 128]
 
 
-def backward(own, partner, cots, down_half, slope):
+def backward(core, own, partner, cots, down_all, slope):
     rows, width = own.shape
-    half = down_half.shape[0]
+    half = N_GRP * 128
     return pl.pallas_call(
         backward_kernel,
-        grid=(half // 256,),
-        in_specs=[
-            whole(own),
-            whole(partner),
-            *[whole(c) for c in cots],
-            pl.BlockSpec((256, width), lambda q: (q, 0)),
-            pl.BlockSpec((2 * rows, 256), lambda q: (0, q)),
-        ],
-        out_specs=pl.BlockSpec((2, N_X, N_C, N_ZH, 32, 128), lambda q: (q, 0, 0, 0, 0, 0)),
+        grid_spec=pltpu.PrefetchScalarGridSpec(
+            num_scalar_prefetch=1,
+            grid=(N_ZH,),
+            in_specs=[
+                whole(own),
+                whole(partner),
+                *[whole(c) for c in cots],
+                pl.BlockSpec((None, N_X, None, 64, width), lambda q, c: (q, 0, c[0], 0, 0)),
+                pl.BlockSpec((2 * rows, 256), lambda q, c: (0, q)),
+            ],
+            out_specs=pl.BlockSpec((2, N_X, N_C, N_ZH, 32, 128), lambda q, c: (q, 0, 0, 0, 0, 0)),
+            scratch_shapes=[pltpu.VMEM((2 * rows, 256), jnp.bfloat16), pltpu.VMEM((2 * rows, width), jnp.bfloat16)],
+        ),
         out_shape=jax.ShapeDtypeStruct((N_GRP, N_X, N_C, N_ZH, 32, 128), jnp.bfloat16),
-        scratch_shapes=[pltpu.VMEM((2 * rows, 256), jnp.bfloat16), pltpu.VMEM((2 * rows, width), jnp.bfloat16)],
         compiler_params=pltpu.CompilerParams(vmem_limit_bytes=VMEM_BYTES),
         cost_estimate=pl.CostEstimate(
             flops=8 * rows * width * half, bytes_accessed=20 * 1024 * 1024, transcendentals=0
         ),
         name="backward",
-    )(own, partner, *cots, down_half, slope)
+    )(core.reshape(1), own, partner, *cots, down_all, slope)
 
 
 def sum_zh(part, zh):
@@ -226,7 +230,8 @@
     up_rows, hid = w_up.shape
     group, zh = lax.axis_index(GRP), lax.axis_index("zh")
 
-    down_half = lax.all_gather(w_down, ("zh", "x"), axis=0, tiled=True)
+    down_all = lax.all_gather(w_down, DEV, axis=0, tiled=True).reshape(N_ZH, N_X, N_C, *w_down.shape)
+    core = lax.axis_index("c")
 
     mine = cut_up(w_up, group)
     column = jnp.stack([mine] + [shift_zh(mine, -step) for step in range(1, N_ZH)], axis=1)
@@ -235,22 +240,19 @@
     got_up = exchange(spread_up, ("y", "zl", "x", "c")).reshape(N_GRP, N_X, N_C, N_ZH, up_rows, 128)
 
     grad_new, grad_old, _ = lax.optimization_barrier((grad_new, grad_old, spread_up))
-    blocks = grad_old.reshape(N_GRP, slots, width)
-    y, zl = group // SIZE["zl"], group % SIZE["zl"]
+    n_y, n_zl = SIZE["y"], SIZE["zl"]
+    y, zl = lax.axis_index("y"), lax.axis_index("zl")
+    blocks = grad_old.reshape(n_y, n_zl, slots, width)
+    kept = lax.dynamic_index_in_dim(blocks, zl, 1, keepdims=False)
+    sent = lax.dynamic_index_in_dim(blocks, 1 - zl, 1, keepdims=False)
+    pair = jnp.stack([kept, lax.ppermute(sent, "zl", [(0, 1), (1, 0)])], axis=1)
     order, old_cot = [], []
-    for dy in range(SIZE["y"]):
-        for dz in range(SIZE["zl"]):
-            to = (y + dy) % SIZE["y"] * SIZE["zl"] + (zl + dz) % SIZE["zl"]
-            order.append((y - dy) % SIZE["y"] * SIZE["zl"] + (zl + dz) % SIZE["zl"])
-            block = lax.dynamic_index_in_dim(blocks, to, 0, keepdims=False)
-            if dy or dz:
-                perm = [
-                    (a * 2 + b, (a + dy) % SIZE["y"] * 2 + (b + dz) % 2)
-                    for a in range(SIZE["y"])
-                    for b in range(SIZE["zl"])
-                ]
-                block = lax.ppermute(block, GRP, perm)
-            old_cot.append(block)
+    for dy in range(n_y):
+        block = lax.dynamic_index_in_dim(pair, (y + dy) % n_y, 0, keepdims=False)
+        if dy:
+            block = lax.ppermute(block, "y", [(i, (i + dy) % n_y) for i in range(n_y)])
+        old_cot.append(block.reshape(n_zl * slots, width))
+        order += [(y - dy) % n_y * n_zl + zl, (y - dy) % n_y * n_zl + 1 - zl]
     old_cot = jnp.concatenate(old_cot, axis=0)
     order = jnp.stack(order)
     picks, counts = send_rows[0][order], send_count[0][order]
@@ -267,12 +269,13 @@
     part_down = jnp.sum(part_down.astype(jnp.float32), axis=0).astype(jnp.bfloat16)
     sum_down = sum_zh(part_down, zh)
 
-    term_up = backward(normed, partner, cots, down_half, slope)
+    term_up = backward(core, normed, partner, cots, down_all, slope)
     part_up = exchange(term_up.reshape(N_GRP * N_X * N_C, N_ZH, up_rows, 128), ("y", "zl", "x", "c"))
     part_up = part_up.reshape(N_GRP * N_X, N_C, N_ZH, up_rows, 128)
     part_up = jnp.sum(part_up.astype(jnp.float32), axis=0).astype(jnp.bfloat16)
     sum_up = sum_zh(part_up.transpose(1, 0, 2, 3).reshape(N_ZH, N_C * up_rows, 128), zh)
 
+    down_half = lax.dynamic_index_in_dim(down_all, core, 2, keepdims=False).reshape(-1, width)
     other = jnp.dot(hidden[rows : rows + fresh_count], down_half, preferred_element_type=jnp.float32)
     mixed = jnp.dot(hidden[:fresh_count], down_half, preferred_element_type=jnp.float32)
     returned = swap(other.astype(jnp.bfloat16)).astype(jnp.float32)

time: 223 us -> 210 us (0.942)
  local copies, waits for them, and re-layouts: 15.1 us -> 9.54 us
  starting transfers between devices: 61.1 us -> 56.2 us
  waiting for transfers between devices: 91.2 us -> 86.8 us
    all_gather x1, waiting for transfers between devices: 46.4 us -> 0.02 us  [body(): lax.all_gather(w_down, DEV, axis=0, tiled=True)]
    ppermute x7 -> x4, waiting for transfers between devices: 14.6 us -> 41 us  [the longest x1 38.2 us: body(): pair = jnp.stack([kept, lax.ppermute(sent, 'zl', [(0, 1), (1, 0)])], axis=1)]
    all_to_all x4, waiting for transfers between devices: 20.3 us -> 35.4 us  [exchange(): return lax.all_to_all(value, axes, split_axis=0, concat_axis=0, tiled=True)]
    unnamed x27 -> x18, local copies, waits for them, and re-layouts: 8.62 us -> 1.11 us
    ppermute x7 -> x4, starting transfers between devices: 11.3 us -> 7.33 us  [the longest x3 5.81 us: body(): block = lax.ppermute(block, 'y', [(i, (i + dy) % n_y) for i in range(n_y)])]
    all_to_all x4, starting transfers between devices: 29.6 us -> 26.7 us  [exchange(): return lax.all_to_all(value, axes, split_axis=0, concat_axis=0, tiled=True)]
  transfers between devices with their start and end apart: 25 -> 22, of which waited for: 9 -> 11; matrix products, arithmetic and copies ran while one was open for 11% -> 12% of each run, Pallas kernels for 10% -> 12%
where the time goes in v3:
time: 210 us; the launch traced here: 209 us
  waiting for transfers between devices  86.8 us (41%)
  starting transfers between devices  56.2 us (27%)
  Pallas kernels  25.9 us (12%)
  between operations  14.4 us (7%)
  local copies, waits for them, and re-layouts  9.54 us (5%)
  matrix products  8.69 us (4%)
  other arithmetic  7.56 us (4%)
    ppermute x1, waiting for transfers between devices, body(): pair = jnp.stack([kept, lax.ppermute(sent, 'zl', [(0, 1), (1, 0)])], axis=1)  38.2 us
    all_to_all x4, waiting for transfers between devices, exchange(): return lax.all_to_all(value, axes, split_axis=0, concat_axis=0, tiled=True)  35.4 us
    all_to_all x4, starting transfers between devices, exchange(): return lax.all_to_all(value, axes, split_axis=0, concat_axis=0, tiled=True)  26.7 us
    ppermute x9, starting transfers between devices, shift_zh(): lax.ppermute(value, 'zh', [(i, (i + step) % N_ZH) for i in range(N_ZH)])  21.5 us
    pallas_call x1, Pallas kernels, forward(): pl.pallas_call(forward_kernel, grid_spec=pltpu.PrefetchScalarGridSpec(num...  11.9 us
    pallas_call x1, Pallas kernels, backward(): pl.pallas_call(backward_kernel, grid_spec=pltpu.PrefetchScalarGridSpec(nu...  10.8 us
    ppermute x9, waiting for transfers between devices, shift_zh(): lax.ppermute(value, 'zh', [(i, (i + step) % N_ZH) for i in range(N_ZH)])  7.76 us
    ppermute x3, starting transfers between devices, body(): block = lax.ppermute(block, 'y', [(i, (i + dy) % n_y) for i in range(n_y)])  5.81 us
  transfers between devices with their start and end apart: 22, of which 11 were waited for; matrix products, arithmetic and copies ran while one was open for 12% of the time, Pallas kernels for 12%

profile of v3, /device:TPU:64, one launch (start us, length us, event | category | flops | bytes accessed | tf_op | source)
XLA Modules:
  0.0 209.1 jit_solution(10714733475625216128)
XLA Ops:
  7.9 1.4 cut_up.1
  9.3 1.4 collective-permute-start.1
  10.7 5.5 %collective-permute-start.2 = (bf16[2,32,128]{2,1,0:T(8,128)(2,1)}, bf16[2,32,128]{2,1,0:T(8,128)(2,1)S(1)}, u32[]{:S(2)}, u32[]{:S(2)}) collective-permute-start(bf16[2,32,128]{2,1,0:T(8,128)(2,1)} %cut_up.1), channel_id=1, source_target_pairs={{0,16},{8,24},{16,0},{24,8},{1,17},{9,25},{17,1},{25,9},{2,18},{10... | collective-permute-start | bytes 49160 | tf_op jit(solution)/shard_map/ppermute | solution.py:41
  16.2 2.7 %collective-permute-start.3 = (bf16[2,32,128]{2,1,0:T(8,128)(2,1)}, bf16[2,32,128]{2,1,0:T(8,128)(2,1)S(1)}, u32[]{:S(2)}, u32[]{:S(2)}) collective-permute-start(bf16[2,32,128]{2,1,0:T(8,128)(2,1)} %cut_up.1), channel_id=1, source_target_pairs={{0,8},{8,16},{16,24},{24,0},{1,9},{9,17},{17,25},{25,1},{2,10},{10... | collective-permute-start | bytes 49160 | tf_op jit(solution)/shard_map/ppermute | solution.py:41
  18.9 2.2 %collective-permute-done.3 = bf16[2,32,128]{2,1,0:T(8,128)(2,1)S(1)} collective-permute-done((bf16[2,32,128]{2,1,0:T(8,128)(2,1)}, bf16[2,32,128]{2,1,0:T(8,128)(2,1)S(1)}, u32[]{:S(2)}, u32[]{:S(2)}) %collective-permute-start.3) | collective-permute-done | bytes 16416 | tf_op jit(solution)/shard_map/ppermute | solution.py:41
  21.8 1.9 broadcast_in_dim.4
  23.6 8.8 %all-to-all-start = ((bf16[64,4,32,128]{3,2,1,0:T(8,128)(2,1)}), bf16[64,4,32,128]{3,2,1,0:T(8,128)(2,1)}, u32[]{:S(2)}, u32[]{:S(2)}) async-start(bf16[64,4,32,128]{3,2,1,0:T(8,128)(2,1)} %bitcast.69), calls=%async_computation | async-start | bytes 4194304 | tf_op jit(solution)/shard_map/all_to_all | solution.py:37
  37.3 1.6 dynamic-slice_bitcast_fusion
  39.0 1.5 collective-permute-start.4
  40.5 38.2 %collective-permute-done.4 = bf16[4,16,1024]{2,1,0:T(8,128)(2,1)} collective-permute-done((bf16[4,16,1024]{2,1,0:T(8,128)(2,1)}, bf16[4,16,1024]{2,1,0:T(8,128)(2,1)}, u32[]{:S(2)}, u32[]{:S(2)}) %collective-permute-start.4) | collective-permute-done | bytes 131104 | tf_op jit(solution)/shard_map/ppermute | solution.py:248
  79.5 1.6 collective-permute-start.5
  81.1 2.8 %collective-permute-start.6 = (bf16[2,16,1024]{2,1,0:T(8,128)(2,1)S(1)}, bf16[2,16,1024]{2,1,0:T(8,128)(2,1)S(1)}, u32[]{:S(2)}, u32[]{:S(2)}) collective-permute-start(bf16[2,16,1024]{2,1,0:T(8,128)(2,1)S(1)} %get-tuple-element.19), channel_id=1, source_target_pairs={{0,128},{64,192},{128,0},{192,64},{1,129},{65,193},{129,1},{193,65... | collective-permute-start | bytes 196616 | tf_op jit(solution)/shard_map/ppermute | solution.py:253
  88.9 1.9 collective-permute-done.9.c3
  90.8 11.9 %forward.1 = (bf16[1280,1024]{1,0:T(8,128)(2,1)}, bf16[1280,1024]{1,0:T(8,128)(2,1)}, bf16[8,4,4,64,128]{4,3,2,1,0:T(8,128)(2,1)}) custom-call(s32[1]{0:T(128)} %bitcast.zh_ref, bf16[640,1024]{1,0:T(8,128)(2,1)S(1)} %fusion.4.own_ref, bf16[640,1024]{1,0:T(8,128)(2,1)} %collective-permute-done.partner_ref, bf16[512,1024]{1,0:T(8,128)(2,1)} %c0.1, ...), custom_call_target="tpu_custom_call" | custom-call | bytes 1024 | tf_op jit(solution)/shard_map/forward/pallas_call | solution.py:135
  102.6 6.4 %all-to-all-start.1 = ((bf16[32,4,64,128]{3,2,1,0:T(8,128)(2,1)}), bf16[32,4,64,128]{3,2,1,0:T(8,128)(2,1)}, u32[]{:S(2)}, u32[]{:S(2)}) async-start(bf16[32,4,64,128]{3,2,1,0:T(8,128)(2,1)} %bitcast.73), calls=%async_computation.1 | async-start | bytes 4194304 | tf_op jit(solution)/shard_map/all_to_all | solution.py:37
  109.1 10.8 %backward.1 = bf16[8,4,2,4,32,128]{5,4,3,2,1,0:T(8,128)(2,1)} custom-call(s32[1]{0:T(128)} %bitcast.38.core_ref, bf16[640,1024]{1,0:T(8,128)(2,1)S(1)} %fusion.4.own_ref, bf16[640,1024]{1,0:T(8,128)(2,1)} %collective-permute-done.partner_ref, bf16[512,1024]{1,0:T(8,128)(2,1)} %c0.1, bf16[128,1024]{1,0:T(8,128)(2,1)} %pad_maximum_fusion.1.c1, ...), custom_call_target="tpu_custom_call" | custom-call | flops 5368709120 | bytes 20971520 | tf_op jit(solution)/shard_map/backward/pallas_call | solution.py:195
  120.0 17.7 %all-to-all-done.1 = bf16[32,4,64,128]{3,2,1,0:T(8,128)(2,1)} async-done(((bf16[32,4,64,128]{3,2,1,0:T(8,128)(2,1)}), bf16[32,4,64,128]{3,2,1,0:T(8,128)(2,1)}, u32[]{:S(2)}, u32[]{:S(2)}) %all-to-all-start.1) | async-done | bytes 2097184 | tf_op jit(solution)/shard_map/all_to_all | solution.py:37
  137.7 7.6 %all-to-all-start.2 = ((bf16[64,4,32,128]{3,2,1,0:T(8,128)(2,1)}), bf16[64,4,32,128]{3,2,1,0:T(8,128)(2,1)}, u32[]{:S(2)}, u32[]{:S(2)}) async-start(bf16[64,4,32,128]{3,2,1,0:T(8,128)(2,1)} %bitcast.72), calls=%async_computation.2 | async-start | bytes 4194304 | tf_op jit(solution)/shard_map/all_to_all | solution.py:37
  145.3 1.8 constant_dynamic-slice_fusion
  147.1 4.2 %convolution_convert_fusion = bf16[512,1024]{1,0:T(8,128)(2,1)} fusion(bf16[1024,1024]{1,0:T(8,128)(2,1)S(1)} %bitcast.70, bf16[1280,1024]{1,0:T(8,128)(2,1)} %get-tuple-element.12), kind=kOutput, calls=%fused_computation.11 | convolution fusion | flops 1074266112 | bytes 4194304 | tf_op jit(solution)/shard_map/dot_general | solution.py:279
  151.3 2.0 reduce_sum.44
  153.3 3.5 %collective-permute-start.11 = (bf16[64,128]{1,0:T(8,128)(2,1)S(1)}, bf16[64,128]{1,0:T(8,128)(2,1)S(1)}, u32[]{:S(2)}, u32[]{:S(2)}) collective-permute-start(bf16[64,128]{1,0:T(8,128)(2,1)S(1)} %get-tuple-element.23), channel_id=1, source_target_pairs={{0,8},{8,16},{16,24},{24,0},{1,9},{9,17},{17,25},{25,1},{2,10},{10... | collective-permute-start | bytes 49160 | tf_op jit(solution)/shard_map/ppermute | solution.py:41
  156.8 2.3 %collective-permute-start.12 = (bf16[64,128]{1,0:T(8,128)(2,1)S(1)}, bf16[64,128]{1,0:T(8,128)(2,1)S(1)}, u32[]{:S(2)}, u32[]{:S(2)}) collective-permute-start(bf16[64,128]{1,0:T(8,128)(2,1)S(1)} %get-tuple-element.25), channel_id=1, source_target_pairs={{0,16},{8,24},{16,0},{24,8},{1,17},{9,25},{17,1},{25,9},{2,18},{10... | collective-permute-start | bytes 49160 | tf_op jit(solution)/shard_map/ppermute | solution.py:41
  159.3 14.9 %all-to-all-done.2 = bf16[64,4,32,128]{3,2,1,0:T(8,128)(2,1)} async-done(((bf16[64,4,32,128]{3,2,1,0:T(8,128)(2,1)}), bf16[64,4,32,128]{3,2,1,0:T(8,128)(2,1)}, u32[]{:S(2)}, u32[]{:S(2)}) %all-to-all-start.2) | async-done | bytes 2097184 | tf_op jit(solution)/shard_map/all_to_all | solution.py:37
  174.2 1.9 reduce_sum.45
  176.1 3.5 %collective-permute-start.14 = (bf16[64,128]{1,0:T(8,128)(2,1)S(1)}, bf16[64,128]{1,0:T(8,128)(2,1)S(1)}, u32[]{:S(2)}, u32[]{:S(2)}) collective-permute-start(bf16[64,128]{1,0:T(8,128)(2,1)S(1)} %get-tuple-element.26), channel_id=1, source_target_pairs={{0,8},{8,16},{16,24},{24,0},{1,9},{9,17},{17,25},{25,1},{2,10},{10... | collective-permute-start | bytes 49160 | tf_op jit(solution)/shard_map/ppermute | solution.py:41
  179.6 2.3 %collective-permute-start.15 = (bf16[64,128]{1,0:T(8,128)(2,1)S(1)}, bf16[64,128]{1,0:T(8,128)(2,1)S(1)}, u32[]{:S(2)}, u32[]{:S(2)}) collective-permute-start(bf16[64,128]{1,0:T(8,128)(2,1)S(1)} %get-tuple-element.28), channel_id=1, source_target_pairs={{0,16},{8,24},{16,0},{24,8},{1,17},{9,25},{17,1},{25,9},{2,18},{10... | collective-permute-start | bytes 49160 | tf_op jit(solution)/shard_map/ppermute | solution.py:41
  182.2 5.1 %collective-permute-done.15 = bf16[64,128]{1,0:T(8,128)(2,1)S(1)} collective-permute-done((bf16[64,128]{1,0:T(8,128)(2,1)S(1)}, bf16[64,128]{1,0:T(8,128)(2,1)S(1)}, u32[]{:S(2)}, u32[]{:S(2)}) %collective-permute-start.15) | collective-permute-done | bytes 16416 | tf_op jit(solution)/shard_map/ppermute | solution.py:41
  188.5 3.9 %all-to-all-start.3 = ((bf16[8,2,64,128]{3,2,1,0:T(8,128)(2,1)}), bf16[8,2,64,128]{3,2,1,0:T(8,128)(2,1)S(1)}, u32[]{:S(2)}, u32[]{:S(2)}) async-start(bf16[8,2,64,128]{3,2,1,0:T(8,128)(2,1)} %broadcast_in_dim.5), calls=%async_computation.3 | async-start | bytes 524288 | tf_op jit(solution)/shard_map/all_to_all | solution.py:37
  192.5 4.5 %add_convert_fusion = bf16[512,1024]{1,0:T(8,128)(2,1)} fusion(bf16[512,1024]{1,0:T(8,128)(2,1)} %collective-permute-done.10, bf16[512,1024]{1,0:T(8,128)(2,1)S(1)} %copy-done.4, bf16[1024,1024]{1,0:T(8,128)(2,1)} %bitcast.71, bf16[1280,1024]{1,0:T(8,128)(2,1)} %get-tuple-element.12), kind=kOutput, calls=%fused_computation.10 | convolution fusion | flops 1076363264 | bytes 6291456 | tf_op jit(solution)/shard_map/dot_general | solution.py:280
  197.0 2.8 %all-to-all-done.3.both_ref = bf16[8,2,64,128]{3,2,1,0:T(8,128)(2,1)S(1)} async-done(((bf16[8,2,64,128]{3,2,1,0:T(8,128)(2,1)}), bf16[8,2,64,128]{3,2,1,0:T(8,128)(2,1)S(1)}, u32[]{:S(2)}, u32[]{:S(2)}) %all-to-all-start.3) | async-done | bytes 262176 | tf_op jit(solution)/shard_map/all_to_all | solution.py:37
  200.5 1.8 finish.1
  (71 shorter events, 14.5 us)
Async XLA Ops:
  7.2 27.0 %copy-start = (bf16[1024,1024]{1,0:T(8,128)(2,1)S(1)}, bf16[1024,1024]{1,0:T(8,128)(2,1)}, u32[]{:S(2)}) copy-start(bf16[1024,1024]{1,0:T(8,128)(2,1)} %param.9) | copy-start | bytes 6291460
  7.2 101.9 %all-gather.2.cloned.1.call-start = ((), (), s32[]{:S(2)}) async-start(), calls=%async_computation.4 | async-start | bytes 4325376 | tf_op jit(solution)/shard_map/all_gather | solution.py:233
  9.3 9.5 %collective-permute-start.1 = (bf16[2,32,128]{2,1,0:T(8,128)(2,1)}, bf16[2,32,128]{2,1,0:T(8,128)(2,1)S(1)}, u32[]{:S(2)}, u32[]{:S(2)}) collective-permute-start(bf16[2,32,128]{2,1,0:T(8,128)(2,1)} %cut_up.1), channel_id=1, source_target_pairs={{0,24},{8,0},{16,8},{24,16},{1,25},{9,1},{17,9},{25,17},{2,26},{10... | collective-permute-start | bytes 49160 | tf_op jit(solution)/shard_map/ppermute | solution.py:41
  10.7 8.1 %collective-permute-start.2 = (bf16[2,32,128]{2,1,0:T(8,128)(2,1)}, bf16[2,32,128]{2,1,0:T(8,128)(2,1)S(1)}, u32[]{:S(2)}, u32[]{:S(2)}) collective-permute-start(bf16[2,32,128]{2,1,0:T(8,128)(2,1)} %cut_up.1), channel_id=1, source_target_pairs={{0,16},{8,24},{16,0},{24,8},{1,17},{9,25},{17,1},{25,9},{2,18},{10... | collective-permute-start | bytes 49160 | tf_op jit(solution)/shard_map/ppermute | solution.py:41
  16.2 4.8 %collective-permute-start.3 = (bf16[2,32,128]{2,1,0:T(8,128)(2,1)}, bf16[2,32,128]{2,1,0:T(8,128)(2,1)S(1)}, u32[]{:S(2)}, u32[]{:S(2)}) collective-permute-start(bf16[2,32,128]{2,1,0:T(8,128)(2,1)} %cut_up.1), channel_id=1, source_target_pairs={{0,8},{8,16},{16,24},{24,0},{1,9},{9,17},{17,25},{25,1},{2,10},{10... | collective-permute-start | bytes 49160 | tf_op jit(solution)/shard_map/ppermute | solution.py:41
  23.6 9.0 %copy-start.7 = (s32[1,8,16]{2,1,0:T(8,128)S(1)}, s32[1,8,16]{2,1,0:T(8,128)}, u32[]{:S(2)}) copy-start(s32[1,8,16]{2,1,0:T(8,128)} %param.10) | copy-start | bytes 1540
  23.6 9.7 %copy-start.1 = (s32[1,8]{1,0:T(1,128)S(1)}, s32[1,8]{1,0:T(1,128)}, u32[]{:S(2)}) copy-start(s32[1,8]{1,0:T(1,128)} %param.11) | copy-start | bytes 100
  23.6 10.5 %copy-start.8 = (bf16[1024]{0:T(1024)(128)(2,1)S(1)}, bf16[1024]{0:T(1024)(128)(2,1)}, u32[]{:S(2)}) copy-start(bf16[1024]{0:T(1024)(128)(2,1)} %param.15) | copy-start | bytes 6148
  23.6 67.1 %all-to-all-start = ((bf16[64,4,32,128]{3,2,1,0:T(8,128)(2,1)}), bf16[64,4,32,128]{3,2,1,0:T(8,128)(2,1)}, u32[]{:S(2)}, u32[]{:S(2)}) async-start(bf16[64,4,32,128]{3,2,1,0:T(8,128)(2,1)} %bitcast.69), calls=%async_computation | async-start | bytes 4194304 | tf_op jit(solution)/shard_map/all_to_all | solution.py:37
  32.4 2.7 %copy-start.2 = (bf16[512,1024]{1,0:T(8,128)(2,1)S(1)}, bf16[512,1024]{1,0:T(8,128)(2,1)}, u32[]{:S(2)}) copy-start(bf16[512,1024]{1,0:T(8,128)(2,1)} %param.12) | copy-start | bytes 3145732
  35.0 1.2 copy-start.3
  36.7 54.1 %collective-permute-start = (bf16[640,1024]{1,0:T(8,128)(2,1)S(1)}, bf16[640,1024]{1,0:T(8,128)(2,1)}, u32[]{:S(2)}, u32[]{:S(2)}) collective-permute-start(bf16[640,1024]{1,0:T(8,128)(2,1)S(1)} %fusion.4.own_ref), channel_id=1, source_target_pairs={{0,1},{1,0},{2,3},{3,2},{4,5},{5,4},{6,7},{7,6},{8,9},{9,8},{10,11... | collective-permute-start | bytes 3932168 | tf_op jit(solution)/shard_map/ppermute | solution.py:33
  36.8 54.0 %collective-permute-start.8 = (bf16[512,1024]{1,0:T(8,128)(2,1)}, bf16[512,1024]{1,0:T(8,128)(2,1)}, u32[]{:S(2)}, u32[]{:S(2)}) collective-permute-start(bf16[512,1024]{1,0:T(8,128)(2,1)} %c0.1), channel_id=1, source_target_pairs={{0,1},{1,0},{2,3},{3,2},{4,5},{5,4},{6,7},{7,6},{8,9},{9,8},{10,11... | collective-permute-start | bytes 3145736 | tf_op jit(solution)/shard_map/ppermute | solution.py:33
  39.0 39.7 %collective-permute-start.4 = (bf16[4,16,1024]{2,1,0:T(8,128)(2,1)}, bf16[4,16,1024]{2,1,0:T(8,128)(2,1)}, u32[]{:S(2)}, u32[]{:S(2)}) collective-permute-start(bf16[4,16,1024]{2,1,0:T(8,128)(2,1)} %get-tuple-element.21), channel_id=1, source_target_pairs={{0,32},{32,0},{1,33},{33,1},{2,34},{34,2},{3,35},{35,3},{4,36},{36... | collective-permute-start | bytes 393224 | tf_op jit(solution)/shard_map/ppermute | solution.py:248
  79.5 6.3 %collective-permute-start.5 = (bf16[2,16,1024]{2,1,0:T(8,128)(2,1)S(1)}, bf16[2,16,1024]{2,1,0:T(8,128)(2,1)S(1)}, u32[]{:S(2)}, u32[]{:S(2)}) collective-permute-start(bf16[2,16,1024]{2,1,0:T(8,128)(2,1)S(1)} %get-tuple-element.18), channel_id=1, source_target_pairs={{0,64},{64,128},{128,192},{192,0},{1,65},{65,129},{129,193},{193,1... | collective-permute-start | bytes 196616 | tf_op jit(solution)/shard_map/ppermute | solution.py:253
  81.1 5.9 %collective-permute-start.6 = (bf16[2,16,1024]{2,1,0:T(8,128)(2,1)S(1)}, bf16[2,16,1024]{2,1,0:T(8,128)(2,1)S(1)}, u32[]{:S(2)}, u32[]{:S(2)}) collective-permute-start(bf16[2,16,1024]{2,1,0:T(8,128)(2,1)S(1)} %get-tuple-element.19), channel_id=1, source_target_pairs={{0,128},{64,192},{128,0},{192,64},{1,129},{65,193},{129,1},{193,65... | collective-permute-start | bytes 196616 | tf_op jit(solution)/shard_map/ppermute | solution.py:253
  83.9 4.3 %collective-permute-start.7 = (bf16[2,16,1024]{2,1,0:T(8,128)(2,1)S(1)}, bf16[2,16,1024]{2,1,0:T(8,128)(2,1)S(1)}, u32[]{:S(2)}, u32[]{:S(2)}) collective-permute-start(bf16[2,16,1024]{2,1,0:T(8,128)(2,1)S(1)} %get-tuple-element.20), channel_id=1, source_target_pairs={{0,192},{64,0},{128,64},{192,128},{1,193},{65,1},{129,65},{193,129... | collective-permute-start | bytes 196616 | tf_op jit(solution)/shard_map/ppermute | solution.py:253
  88.9 1.9 collective-permute-start.9
  102.6 35.1 %all-to-all-start.1 = ((bf16[32,4,64,128]{3,2,1,0:T(8,128)(2,1)}), bf16[32,4,64,128]{3,2,1,0:T(8,128)(2,1)}, u32[]{:S(2)}, u32[]{:S(2)}) async-start(bf16[32,4,64,128]{3,2,1,0:T(8,128)(2,1)} %bitcast.73), calls=%async_computation.1 | async-start | bytes 4194304 | tf_op jit(solution)/shard_map/all_to_all | solution.py:37
  137.7 36.5 %all-to-all-start.2 = ((bf16[64,4,32,128]{3,2,1,0:T(8,128)(2,1)}), bf16[64,4,32,128]{3,2,1,0:T(8,128)(2,1)}, u32[]{:S(2)}, u32[]{:S(2)}) async-start(bf16[64,4,32,128]{3,2,1,0:T(8,128)(2,1)} %bitcast.72), calls=%async_computation.2 | async-start | bytes 4194304 | tf_op jit(solution)/shard_map/all_to_all | solution.py:37
  147.1 4.2 %copy-start.5 = (bf16[4,4,1,64,1024]{4,3,2,1,0:T(8,128)(2,1)}, bf16[4,4,1,64,1024]{4,3,2,1,0:T(8,128)(2,1)S(1)}, u32[]{:S(2)}) copy-start(bf16[4,4,1,64,1024]{4,3,2,1,0:T(8,128)(2,1)S(1)} %constant_dynamic-slice_fusion) | copy-start | bytes 6291460
  151.3 41.2 %collective-permute-start.10 = (bf16[512,1024]{1,0:T(8,128)(2,1)}, bf16[512,1024]{1,0:T(8,128)(2,1)}, u32[]{:S(2)}, u32[]{:S(2)}) collective-permute-start(bf16[512,1024]{1,0:T(8,128)(2,1)} %convolution_convert_fusion), channel_id=1, source_target_pairs={{0,1},{1,0},{2,3},{3,2},{4,5},{5,4},{6,7},{7,6},{8,9},{9,8},{10,11... | collective-permute-start | bytes 3145736 | tf_op jit(solution)/shard_map/ppermute | solution.py:33
  153.3 39.2 %copy-start.4 = (bf16[512,1024]{1,0:T(8,128)(2,1)S(1)}, bf16[512,1024]{1,0:T(8,128)(2,1)}, u32[]{:S(2)}) copy-start(bf16[512,1024]{1,0:T(8,128)(2,1)} %param.12) | copy-start | bytes 3145732
  153.3 26.3 %collective-permute-start.11 = (bf16[64,128]{1,0:T(8,128)(2,1)S(1)}, bf16[64,128]{1,0:T(8,128)(2,1)S(1)}, u32[]{:S(2)}, u32[]{:S(2)}) collective-permute-start(bf16[64,128]{1,0:T(8,128)(2,1)S(1)} %get-tuple-element.23), channel_id=1, source_target_pairs={{0,8},{8,16},{16,24},{24,0},{1,9},{9,17},{17,25},{25,1},{2,10},{10... | collective-permute-start | bytes 49160 | tf_op jit(solution)/shard_map/ppermute | solution.py:41
  156.8 25.2 %collective-permute-start.12 = (bf16[64,128]{1,0:T(8,128)(2,1)S(1)}, bf16[64,128]{1,0:T(8,128)(2,1)S(1)}, u32[]{:S(2)}, u32[]{:S(2)}) collective-permute-start(bf16[64,128]{1,0:T(8,128)(2,1)S(1)} %get-tuple-element.25), channel_id=1, source_target_pairs={{0,16},{8,24},{16,0},{24,8},{1,17},{9,25},{17,1},{25,9},{2,18},{10... | collective-permute-start | bytes 49160 | tf_op jit(solution)/shard_map/ppermute | solution.py:41
  159.1 23.1 %collective-permute-start.13 = (bf16[64,128]{1,0:T(8,128)(2,1)S(1)}, bf16[64,128]{1,0:T(8,128)(2,1)S(1)}, u32[]{:S(2)}, u32[]{:S(2)}) collective-permute-start(bf16[64,128]{1,0:T(8,128)(2,1)S(1)} %get-tuple-element.24), channel_id=1, source_target_pairs={{0,24},{8,0},{16,8},{24,16},{1,25},{9,1},{17,9},{25,17},{2,26},{10... | collective-permute-start | bytes 49160 | tf_op jit(solution)/shard_map/ppermute | solution.py:41
  176.1 6.0 %collective-permute-start.14 = (bf16[64,128]{1,0:T(8,128)(2,1)S(1)}, bf16[64,128]{1,0:T(8,128)(2,1)S(1)}, u32[]{:S(2)}, u32[]{:S(2)}) collective-permute-start(bf16[64,128]{1,0:T(8,128)(2,1)S(1)} %get-tuple-element.26), channel_id=1, source_target_pairs={{0,8},{8,16},{16,24},{24,0},{1,9},{9,17},{17,25},{25,1},{2,10},{10... | collective-permute-start | bytes 49160 | tf_op jit(solution)/shard_map/ppermute | solution.py:41
  179.6 7.7 %collective-permute-start.15 = (bf16[64,128]{1,0:T(8,128)(2,1)S(1)}, bf16[64,128]{1,0:T(8,128)(2,1)S(1)}, u32[]{:S(2)}, u32[]{:S(2)}) collective-permute-start(bf16[64,128]{1,0:T(8,128)(2,1)S(1)} %get-tuple-element.28), channel_id=1, source_target_pairs={{0,16},{8,24},{16,0},{24,8},{1,17},{9,25},{17,1},{25,9},{2,18},{10... | collective-permute-start | bytes 49160 | tf_op jit(solution)/shard_map/ppermute | solution.py:41
  181.9 5.8 %collective-permute-start.16 = (bf16[64,128]{1,0:T(8,128)(2,1)S(1)}, bf16[64,128]{1,0:T(8,128)(2,1)S(1)}, u32[]{:S(2)}, u32[]{:S(2)}) collective-permute-start(bf16[64,128]{1,0:T(8,128)(2,1)S(1)} %get-tuple-element.27), channel_id=1, source_target_pairs={{0,24},{8,0},{16,8},{24,16},{1,25},{9,1},{17,9},{25,17},{2,26},{10... | collective-permute-start | bytes 49160 | tf_op jit(solution)/shard_map/ppermute | solution.py:41
  188.5 11.2 %all-to-all-start.3 = ((bf16[8,2,64,128]{3,2,1,0:T(8,128)(2,1)}), bf16[8,2,64,128]{3,2,1,0:T(8,128)(2,1)S(1)}, u32[]{:S(2)}, u32[]{:S(2)}) async-start(bf16[8,2,64,128]{3,2,1,0:T(8,128)(2,1)} %broadcast_in_dim.5), calls=%async_computation.3 | async-start | bytes 524288 | tf_op jit(solution)/shard_map/all_to_all | solution.py:37
  199.8 0.7 copy-start.6
Sparse Core Ops, SparseCore 0:
  10.6 69.1 all-gather.1

commit v4 on v3

--- a/solution.py
+++ b/solution.py
@@ -233,13 +233,6 @@
     down_all = lax.all_gather(w_down, DEV, axis=0, tiled=True).reshape(N_ZH, N_X, N_C, *w_down.shape)
     core = lax.axis_index("c")
 
-    mine = cut_up(w_up, group)
-    column = jnp.stack([mine] + [shift_zh(mine, -step) for step in range(1, N_ZH)], axis=1)
-    spread_up = jnp.broadcast_to(column[None], (N_GRP * N_X,) + column.shape)
-    spread_up = spread_up.reshape(N_GRP * N_X * N_C, N_ZH, up_rows, 128)
-    got_up = exchange(spread_up, ("y", "zl", "x", "c")).reshape(N_GRP, N_X, N_C, N_ZH, up_rows, 128)
-
-    grad_new, grad_old, _ = lax.optimization_barrier((grad_new, grad_old, spread_up))
     n_y, n_zl = SIZE["y"], SIZE["zl"]
     y, zl = lax.axis_index("y"), lax.axis_index("zl")
     blocks = grad_old.reshape(n_y, n_zl, slots, width)
@@ -253,8 +246,16 @@
             block = lax.ppermute(block, "y", [(i, (i + dy) % n_y) for i in range(n_y)])
         old_cot.append(block.reshape(n_zl * slots, width))
         order += [(y - dy) % n_y * n_zl + zl, (y - dy) % n_y * n_zl + 1 - zl]
+    order = jnp.stack(order)
+
+    mine = cut_up(w_up, group)
+    column = jnp.stack([mine] + [shift_zh(mine, -step) for step in range(1, N_ZH)], axis=1)
+    column, *old_cot = lax.optimization_barrier((column, *old_cot))
     old_cot = jnp.concatenate(old_cot, axis=0)
-    order = jnp.stack(order)
+    spread_up = jnp.broadcast_to(column[None], (N_GRP * N_X,) + column.shape)
+    spread_up = spread_up.reshape(N_GRP * N_X * N_C, N_ZH, up_rows, 128)
+    got_up = exchange(spread_up, ("y", "zl", "x", "c")).reshape(N_GRP, N_X, N_C, N_ZH, up_rows, 128)
+
     picks, counts = send_rows[0][order], send_count[0][order]
     live = (lax.broadcasted_iota(jnp.int32, (N_GRP, slots), 1) < counts[:, None]).astype(jnp.bfloat16)
     picked = reservoir[picks.reshape(-1)] * live.reshape(-1, 1)

time: 210 us -> 203 us (0.967)
  starting transfers between devices: 56.2 us -> 49.3 us
  local copies, waits for them, and re-layouts: 9.54 us -> 12 us
    all_to_all x4, waiting for transfers between devices: 35.4 us -> 74.7 us  [exchange(): return lax.all_to_all(value, axes, split_axis=0, concat_axis=0, tiled=True)]
    ppermute x1, waiting for transfers between devices: 38.2 us -> 0.01 us  [body(): pair = jnp.stack([kept, lax.ppermute(sent, 'zl', [(0, 1), (1, 0)])], axis=1)]
    ppermute x9, starting transfers between devices: 21.5 us -> 16.6 us  [shift_zh(): lax.ppermute(value, 'zh', [(i, (i + step) % N_ZH) for i in range(N_ZH)])]
    all_to_all x4, starting transfers between devices: 26.7 us -> 24.1 us  [exchange(): return lax.all_to_all(value, axes, split_axis=0, concat_axis=0, tiled=True)]
    unnamed x18 -> x29, local copies, waits for them, and re-layouts: 1.11 us -> 3.62 us
  transfers between devices with their start and end apart: 22 -> 22, of which waited for: 11 -> 10; matrix products, arithmetic and copies ran while one was open for 12% -> 12% of each run, Pallas kernels for 12% -> 12%
where the time goes in v4:
time: 203 us; the launch traced here: 202 us
  waiting for transfers between devices  85.4 us (42%)
  starting transfers between devices  49.3 us (24%)
  Pallas kernels  25.9 us (13%)
  between operations  14.4 us (7%)
  local copies, waits for them, and re-layouts  12 us (6%)
  matrix products  8.69 us (4%)
  other arithmetic  6.03 us (3%)
    all_to_all x4, waiting for transfers between devices, exchange(): return lax.all_to_all(value, axes, split_axis=0, concat_axis=0, tiled=True)  74.7 us
    all_to_all x4, starting transfers between devices, exchange(): return lax.all_to_all(value, axes, split_axis=0, concat_axis=0, tiled=True)  24.1 us
    ppermute x9, starting transfers between devices, shift_zh(): lax.ppermute(value, 'zh', [(i, (i + step) % N_ZH) for i in range(N_ZH)])  16.6 us
    pallas_call x1, Pallas kernels, forward(): pl.pallas_call(forward_kernel, grid_spec=pltpu.PrefetchScalarGridSpec(num...  11.8 us
    pallas_call x1, Pallas kernels, backward(): pl.pallas_call(backward_kernel, grid_spec=pltpu.PrefetchScalarGridSpec(nu...  10.9 us
    ppermute x3, starting transfers between devices, body(): block = lax.ppermute(block, 'y', [(i, (i + dy) % n_y) for i in range(n_y)])  5.9 us
    ppermute x9, waiting for transfers between devices, shift_zh(): lax.ppermute(value, 'zh', [(i, (i + step) % N_ZH) for i in range(N_ZH)])  5.74 us
    dot_general x1, matrix products, body(): jnp.dot(hidden[:fresh_count], down_half, preferred_element_type=jnp.float32)  4.47 us
  transfers between devices with their start and end apart: 22, of which 10 were waited for; matrix products, arithmetic and copies ran while one was open for 12% of the time, Pallas kernels for 12%

profile of v4, /device:TPU:64, one launch (start us, length us, event | category | flops | bytes accessed | tf_op | source)
XLA Modules:
  0.0 201.7 jit_solution(9921787045932606307)
XLA Ops:
  7.9 1.0 dynamic-slice_bitcast_fusion
  8.9 2.0 collective-permute-start.4
  10.9 1.4 cut_up.1
  12.3 5.9 %collective-permute-start.2 = (bf16[2,32,128]{2,1,0:T(8,128)(2,1)}, bf16[2,32,128]{2,1,0:T(8,128)(2,1)S(1)}, u32[]{:S(2)}, u32[]{:S(2)}) collective-permute-start(bf16[2,32,128]{2,1,0:T(8,128)(2,1)} %cut_up.1), channel_id=1, source_target_pairs={{0,16},{8,24},{16,0},{24,8},{1,17},{9,25},{17,1},{25,9},{2,18},{10... | collective-permute-start | bytes 49160 | tf_op jit(solution)/shard_map/ppermute | solution.py:41
  18.3 2.7 %collective-permute-start.3 = (bf16[2,32,128]{2,1,0:T(8,128)(2,1)}, bf16[2,32,128]{2,1,0:T(8,128)(2,1)S(1)}, u32[]{:S(2)}, u32[]{:S(2)}) collective-permute-start(bf16[2,32,128]{2,1,0:T(8,128)(2,1)} %cut_up.1), channel_id=1, source_target_pairs={{0,8},{8,16},{16,24},{24,0},{1,9},{9,17},{17,25},{25,1},{2,10},{10... | collective-permute-start | bytes 49160 | tf_op jit(solution)/shard_map/ppermute | solution.py:41
  21.0 1.7 collective-permute-start.5
  22.6 2.9 %collective-permute-start.6 = (bf16[2,16,1024]{2,1,0:T(8,128)(2,1)S(1)}, bf16[2,16,1024]{2,1,0:T(8,128)(2,1)S(1)}, u32[]{:S(2)}, u32[]{:S(2)}) collective-permute-start(bf16[2,16,1024]{2,1,0:T(8,128)(2,1)S(1)} %get-tuple-element.26), channel_id=1, source_target_pairs={{0,128},{64,192},{128,0},{192,64},{1,129},{65,193},{129,1},{193,65... | collective-permute-start | bytes 196616 | tf_op jit(solution)/shard_map/ppermute | solution.py:246
  25.5 1.3 collective-permute-start.7
  28.5 1.3 collective-permute-done.7
  30.4 1.9 broadcast_in_dim.4
  32.3 8.1 %all-to-all-start = ((bf16[64,4,32,128]{3,2,1,0:T(8,128)(2,1)}), bf16[64,4,32,128]{3,2,1,0:T(8,128)(2,1)}, u32[]{:S(2)}, u32[]{:S(2)}) async-start(bf16[64,4,32,128]{3,2,1,0:T(8,128)(2,1)} %bitcast.69), calls=%async_computation | async-start | bytes 4194304 | tf_op jit(solution)/shard_map/all_to_all | solution.py:37
  42.2 0.9 gather_fusion.1
  48.0 2.1 %collective-permute-done.9.c3 = bf16[128,1024]{1,0:T(8,128)(2,1)} collective-permute-done((bf16[128,1024]{1,0:T(8,128)(2,1)}, bf16[128,1024]{1,0:T(8,128)(2,1)}, u32[]{:S(2)}, u32[]{:S(2)}) %collective-permute-start.9) | collective-permute-done | bytes 262176 | tf_op jit(solution)/shard_map/ppermute | solution.py:33
  50.1 35.8 %all-to-all-done = bf16[64,4,32,128]{3,2,1,0:T(8,128)(2,1)} async-done(((bf16[64,4,32,128]{3,2,1,0:T(8,128)(2,1)}), bf16[64,4,32,128]{3,2,1,0:T(8,128)(2,1)}, u32[]{:S(2)}, u32[]{:S(2)}) %all-to-all-start) | async-done | bytes 2097184 | tf_op jit(solution)/shard_map/all_to_all | solution.py:37
  85.9 11.8 %forward.1 = (bf16[1280,1024]{1,0:T(8,128)(2,1)}, bf16[1280,1024]{1,0:T(8,128)(2,1)}, bf16[8,4,4,64,128]{4,3,2,1,0:T(8,128)(2,1)}) custom-call(s32[1]{0:T(128)} %bitcast.zh_ref, bf16[640,1024]{1,0:T(8,128)(2,1)S(1)} %fusion.4.own_ref, bf16[640,1024]{1,0:T(8,128)(2,1)} %collective-permute-done.partner_ref, bf16[512,1024]{1,0:T(8,128)(2,1)} %c0.3, ...), custom_call_target="tpu_custom_call" | custom-call | bytes 1024 | tf_op jit(solution)/shard_map/forward/pallas_call | solution.py:135
  97.7 4.9 %all-to-all-start.1 = ((bf16[32,4,64,128]{3,2,1,0:T(8,128)(2,1)}), bf16[32,4,64,128]{3,2,1,0:T(8,128)(2,1)}, u32[]{:S(2)}, u32[]{:S(2)}) async-start(bf16[32,4,64,128]{3,2,1,0:T(8,128)(2,1)} %bitcast.73), calls=%async_computation.1 | async-start | bytes 4194304 | tf_op jit(solution)/shard_map/all_to_all | solution.py:37
  102.7 10.9 %backward.1 = bf16[8,4,2,4,32,128]{5,4,3,2,1,0:T(8,128)(2,1)} custom-call(s32[1]{0:T(128)} %bitcast.38.core_ref, bf16[640,1024]{1,0:T(8,128)(2,1)S(1)} %fusion.4.own_ref, bf16[640,1024]{1,0:T(8,128)(2,1)} %collective-permute-done.partner_ref, bf16[512,1024]{1,0:T(8,128)(2,1)} %c0.3, bf16[128,1024]{1,0:T(8,128)(2,1)} %constant_dynamic-update-slice_fusion.c1, ...), custom_call_target="tpu_custom_call" | custom-call | flops 5368709120 | bytes 20971520 | tf_op jit(solution)/shard_map/backward/pallas_call | solution.py:195
  113.5 19.2 %all-to-all-done.1 = bf16[32,4,64,128]{3,2,1,0:T(8,128)(2,1)} async-done(((bf16[32,4,64,128]{3,2,1,0:T(8,128)(2,1)}), bf16[32,4,64,128]{3,2,1,0:T(8,128)(2,1)}, u32[]{:S(2)}, u32[]{:S(2)}) %all-to-all-start.1) | async-done | bytes 2097184 | tf_op jit(solution)/shard_map/all_to_all | solution.py:37
  132.8 7.0 %all-to-all-start.2 = ((bf16[64,4,32,128]{3,2,1,0:T(8,128)(2,1)}), bf16[64,4,32,128]{3,2,1,0:T(8,128)(2,1)}, u32[]{:S(2)}, u32[]{:S(2)}) async-start(bf16[64,4,32,128]{3,2,1,0:T(8,128)(2,1)} %bitcast.72), calls=%async_computation.2 | async-start | bytes 4194304 | tf_op jit(solution)/shard_map/all_to_all | solution.py:37
  139.8 1.8 constant_dynamic-slice_fusion
  141.6 4.2 %convolution_convert_fusion = bf16[512,1024]{1,0:T(8,128)(2,1)} fusion(bf16[1024,1024]{1,0:T(8,128)(2,1)S(1)} %bitcast.70, bf16[1280,1024]{1,0:T(8,128)(2,1)} %get-tuple-element.18), kind=kOutput, calls=%fused_computation.11 | convolution fusion | flops 1074266112 | bytes 4194304 | tf_op jit(solution)/shard_map/dot_general | solution.py:280
  145.8 2.0 reduce_sum.44
  147.9 3.8 %collective-permute-start.12 = (bf16[64,128]{1,0:T(8,128)(2,1)S(1)}, bf16[64,128]{1,0:T(8,128)(2,1)S(1)}, u32[]{:S(2)}, u32[]{:S(2)}) collective-permute-start(bf16[64,128]{1,0:T(8,128)(2,1)S(1)} %get-tuple-element.31), channel_id=1, source_target_pairs={{0,16},{8,24},{16,0},{24,8},{1,17},{9,25},{17,1},{25,9},{2,18},{10... | collective-permute-start | bytes 49160 | tf_op jit(solution)/shard_map/ppermute | solution.py:41
  151.8 16.9 %all-to-all-done.2 = bf16[64,4,32,128]{3,2,1,0:T(8,128)(2,1)} async-done(((bf16[64,4,32,128]{3,2,1,0:T(8,128)(2,1)}), bf16[64,4,32,128]{3,2,1,0:T(8,128)(2,1)}, u32[]{:S(2)}, u32[]{:S(2)}) %all-to-all-start.2) | async-done | bytes 2097184 | tf_op jit(solution)/shard_map/all_to_all | solution.py:37
  168.7 1.9 reduce_sum.45
  170.8 3.8 %collective-permute-start.15 = (bf16[64,128]{1,0:T(8,128)(2,1)S(1)}, bf16[64,128]{1,0:T(8,128)(2,1)S(1)}, u32[]{:S(2)}, u32[]{:S(2)}) collective-permute-start(bf16[64,128]{1,0:T(8,128)(2,1)S(1)} %get-tuple-element.34), channel_id=1, source_target_pairs={{0,16},{8,24},{16,0},{24,8},{1,17},{9,25},{17,1},{25,9},{2,18},{10... | collective-permute-start | bytes 49160 | tf_op jit(solution)/shard_map/ppermute | solution.py:41
  175.5 3.0 %collective-permute-done.15 = bf16[64,128]{1,0:T(8,128)(2,1)S(1)} collective-permute-done((bf16[64,128]{1,0:T(8,128)(2,1)S(1)}, bf16[64,128]{1,0:T(8,128)(2,1)S(1)}, u32[]{:S(2)}, u32[]{:S(2)}) %collective-permute-start.15) | collective-permute-done | bytes 16416 | tf_op jit(solution)/shard_map/ppermute | solution.py:41
  178.5 1.9 collective-permute-done.16
  181.2 3.9 %all-to-all-start.3 = ((bf16[8,2,64,128]{3,2,1,0:T(8,128)(2,1)}), bf16[8,2,64,128]{3,2,1,0:T(8,128)(2,1)S(1)}, u32[]{:S(2)}, u32[]{:S(2)}) async-start(bf16[8,2,64,128]{3,2,1,0:T(8,128)(2,1)} %broadcast_in_dim.5), calls=%async_computation.3 | async-start | bytes 524288 | tf_op jit(solution)/shard_map/all_to_all | solution.py:37
  185.1 4.5 %add_convert_fusion = bf16[512,1024]{1,0:T(8,128)(2,1)} fusion(bf16[512,1024]{1,0:T(8,128)(2,1)} %collective-permute-done.10, bf16[512,1024]{1,0:T(8,128)(2,1)S(1)} %copy-done.4, bf16[1024,1024]{1,0:T(8,128)(2,1)} %bitcast.71, bf16[1280,1024]{1,0:T(8,128)(2,1)} %get-tuple-element.18), kind=kOutput, calls=%fused_computation.10 | convolution fusion | flops 1076363264 | bytes 6291456 | tf_op jit(solution)/shard_map/dot_general | solution.py:281
  189.6 2.8 %all-to-all-done.3.both_ref = bf16[8,2,64,128]{3,2,1,0:T(8,128)(2,1)S(1)} async-done(((bf16[8,2,64,128]{3,2,1,0:T(8,128)(2,1)}), bf16[8,2,64,128]{3,2,1,0:T(8,128)(2,1)S(1)}, u32[]{:S(2)}, u32[]{:S(2)}) %all-to-all-start.3) | async-done | bytes 262176 | tf_op jit(solution)/shard_map/all_to_all | solution.py:37
  193.1 1.8 finish.1
  (82 shorter events, 12.2 us)
Async XLA Ops:
  7.2 35.0 %copy-start = (bf16[1024,1024]{1,0:T(8,128)(2,1)S(1)}, bf16[1024,1024]{1,0:T(8,128)(2,1)}, u32[]{:S(2)}) copy-start(bf16[1024,1024]{1,0:T(8,128)(2,1)} %param.9) | copy-start | bytes 6291460
  7.2 95.5 %all-gather.2.cloned.1.call-start = ((), (), s32[]{:S(2)}) async-start(), calls=%async_computation.4 | async-start | bytes 4325376 | tf_op jit(solution)/shard_map/all_gather | solution.py:233
  8.9 12.0 %collective-permute-start.4 = (bf16[4,16,1024]{2,1,0:T(8,128)(2,1)S(1)}, bf16[4,16,1024]{2,1,0:T(8,128)(2,1)S(1)}, u32[]{:S(2)}, u32[]{:S(2)}) collective-permute-start(bf16[4,16,1024]{2,1,0:T(8,128)(2,1)S(1)} %get-tuple-element.27), channel_id=1, source_target_pairs={{0,32},{32,0},{1,33},{33,1},{2,34},{34,2},{3,35},{35,3},{4,36},{36... | collective-permute-start | bytes 393224 | tf_op jit(solution)/shard_map/ppermute | solution.py:241
  12.3 13.2 %collective-permute-start.1 = (bf16[2,32,128]{2,1,0:T(8,128)(2,1)}, bf16[2,32,128]{2,1,0:T(8,128)(2,1)S(1)}, u32[]{:S(2)}, u32[]{:S(2)}) collective-permute-start(bf16[2,32,128]{2,1,0:T(8,128)(2,1)} %cut_up.1), channel_id=1, source_target_pairs={{0,24},{8,0},{16,8},{24,16},{1,25},{9,1},{17,9},{25,17},{2,26},{10... | collective-permute-start | bytes 49160 | tf_op jit(solution)/shard_map/ppermute | solution.py:41
  12.3 14.6 %collective-permute-start.2 = (bf16[2,32,128]{2,1,0:T(8,128)(2,1)}, bf16[2,32,128]{2,1,0:T(8,128)(2,1)S(1)}, u32[]{:S(2)}, u32[]{:S(2)}) collective-permute-start(bf16[2,32,128]{2,1,0:T(8,128)(2,1)} %cut_up.1), channel_id=1, source_target_pairs={{0,16},{8,24},{16,0},{24,8},{1,17},{9,25},{17,1},{25,9},{2,18},{10... | collective-permute-start | bytes 49160 | tf_op jit(solution)/shard_map/ppermute | solution.py:41
  18.3 8.6 %collective-permute-start.3 = (bf16[2,32,128]{2,1,0:T(8,128)(2,1)}, bf16[2,32,128]{2,1,0:T(8,128)(2,1)S(1)}, u32[]{:S(2)}, u32[]{:S(2)}) collective-permute-start(bf16[2,32,128]{2,1,0:T(8,128)(2,1)} %cut_up.1), channel_id=1, source_target_pairs={{0,8},{8,16},{16,24},{24,0},{1,9},{9,17},{17,25},{25,1},{2,10},{10... | collective-permute-start | bytes 49160 | tf_op jit(solution)/shard_map/ppermute | solution.py:41
  21.0 6.6 %collective-permute-start.5 = (bf16[2,16,1024]{2,1,0:T(8,128)(2,1)S(1)}, bf16[2,16,1024]{2,1,0:T(8,128)(2,1)S(1)}, u32[]{:S(2)}, u32[]{:S(2)}) collective-permute-start(bf16[2,16,1024]{2,1,0:T(8,128)(2,1)S(1)} %get-tuple-element.25), channel_id=1, source_target_pairs={{0,64},{64,128},{128,192},{192,0},{1,65},{65,129},{129,193},{193,1... | collective-permute-start | bytes 196616 | tf_op jit(solution)/shard_map/ppermute | solution.py:246
  22.6 5.8 %collective-permute-start.6 = (bf16[2,16,1024]{2,1,0:T(8,128)(2,1)S(1)}, bf16[2,16,1024]{2,1,0:T(8,128)(2,1)S(1)}, u32[]{:S(2)}, u32[]{:S(2)}) collective-permute-start(bf16[2,16,1024]{2,1,0:T(8,128)(2,1)S(1)} %get-tuple-element.26), channel_id=1, source_target_pairs={{0,128},{64,192},{128,0},{192,64},{1,129},{65,193},{129,1},{193,65... | collective-permute-start | bytes 196616 | tf_op jit(solution)/shard_map/ppermute | solution.py:246
  25.5 4.3 %collective-permute-start.7 = (bf16[2,16,1024]{2,1,0:T(8,128)(2,1)S(1)}, bf16[2,16,1024]{2,1,0:T(8,128)(2,1)S(1)}, u32[]{:S(2)}, u32[]{:S(2)}) collective-permute-start(bf16[2,16,1024]{2,1,0:T(8,128)(2,1)S(1)} %get-tuple-element.23), channel_id=1, source_target_pairs={{0,192},{64,0},{128,64},{192,128},{1,193},{65,1},{129,65},{193,129... | collective-permute-start | bytes 196616 | tf_op jit(solution)/shard_map/ppermute | solution.py:246
  28.5 1.3 copy-start.8
  32.3 8.4 %copy-start.7 = (s32[1,8,16]{2,1,0:T(8,128)S(1)}, s32[1,8,16]{2,1,0:T(8,128)}, u32[]{:S(2)}) copy-start(s32[1,8,16]{2,1,0:T(8,128)} %param.10) | copy-start | bytes 1540
  32.3 9.0 %copy-start.1 = (s32[1,8]{1,0:T(1,128)S(1)}, s32[1,8]{1,0:T(1,128)}, u32[]{:S(2)}) copy-start(s32[1,8]{1,0:T(1,128)} %param.11) | copy-start | bytes 100
  32.3 9.8 %copy-start.12 = (bf16[1024]{0:T(1024)(128)(2,1)S(1)}, bf16[1024]{0:T(1024)(128)(2,1)}, u32[]{:S(2)}) copy-start(bf16[1024]{0:T(1024)(128)(2,1)} %param.15) | copy-start | bytes 6148
  32.3 53.5 %all-to-all-start = ((bf16[64,4,32,128]{3,2,1,0:T(8,128)(2,1)}), bf16[64,4,32,128]{3,2,1,0:T(8,128)(2,1)}, u32[]{:S(2)}, u32[]{:S(2)}) async-start(bf16[64,4,32,128]{3,2,1,0:T(8,128)(2,1)} %bitcast.69), calls=%async_computation | async-start | bytes 4194304 | tf_op jit(solution)/shard_map/all_to_all | solution.py:37
  40.5 2.7 %copy-start.2 = (bf16[512,1024]{1,0:T(8,128)(2,1)S(1)}, bf16[512,1024]{1,0:T(8,128)(2,1)}, u32[]{:S(2)}) copy-start(bf16[512,1024]{1,0:T(8,128)(2,1)} %param.12) | copy-start | bytes 3145732
  43.4 3.2 %copy-start.9 = (bf16[2,16,1024]{2,1,0:T(8,128)(2,1)S(1)}, bf16[2,16,1024]{2,1,0:T(8,128)(2,1)}, u32[]{:S(2)}) copy-start(bf16[2,16,1024]{2,1,0:T(8,128)(2,1)} %copy-done.8) | copy-start | bytes 196612
  43.4 3.8 %copy-start.11 = (bf16[2,16,1024]{2,1,0:T(8,128)(2,1)S(1)}, bf16[2,16,1024]{2,1,0:T(8,128)(2,1)}, u32[]{:S(2)}) copy-start(bf16[2,16,1024]{2,1,0:T(8,128)(2,1)} %copy-done.10) | copy-start | bytes 196612
  44.7 5.3 %collective-permute-start = (bf16[640,1024]{1,0:T(8,128)(2,1)S(1)}, bf16[640,1024]{1,0:T(8,128)(2,1)}, u32[]{:S(2)}, u32[]{:S(2)}) collective-permute-start(bf16[640,1024]{1,0:T(8,128)(2,1)S(1)} %fusion.4.own_ref), channel_id=1, source_target_pairs={{0,1},{1,0},{2,3},{3,2},{4,5},{5,4},{6,7},{7,6},{8,9},{9,8},{10,11... | collective-permute-start | bytes 3932168 | tf_op jit(solution)/shard_map/ppermute | solution.py:33
  44.8 5.2 %collective-permute-start.8 = (bf16[512,1024]{1,0:T(8,128)(2,1)}, bf16[512,1024]{1,0:T(8,128)(2,1)}, u32[]{:S(2)}, u32[]{:S(2)}) collective-permute-start(bf16[512,1024]{1,0:T(8,128)(2,1)} %c0.3), channel_id=1, source_target_pairs={{0,1},{1,0},{2,3},{3,2},{4,5},{5,4},{6,7},{7,6},{8,9},{9,8},{10,11... | collective-permute-start | bytes 3145736 | tf_op jit(solution)/shard_map/ppermute | solution.py:33
  47.9 2.2 %collective-permute-start.9 = (bf16[128,1024]{1,0:T(8,128)(2,1)}, bf16[128,1024]{1,0:T(8,128)(2,1)}, u32[]{:S(2)}, u32[]{:S(2)}) collective-permute-start(bf16[128,1024]{1,0:T(8,128)(2,1)} %constant_dynamic-update-slice_fusion.c1), channel_id=1, source_target_pairs={{0,1},{1,0},{2,3},{3,2},{4,5},{5,4},{6,7},{7,6},{8,9},{9,8},{10,11... | collective-permute-start | bytes 786440 | tf_op jit(solution)/shard_map/ppermute | solution.py:33
  97.7 35.1 %all-to-all-start.1 = ((bf16[32,4,64,128]{3,2,1,0:T(8,128)(2,1)}), bf16[32,4,64,128]{3,2,1,0:T(8,128)(2,1)}, u32[]{:S(2)}, u32[]{:S(2)}) async-start(bf16[32,4,64,128]{3,2,1,0:T(8,128)(2,1)} %bitcast.73), calls=%async_computation.1 | async-start | bytes 4194304 | tf_op jit(solution)/shard_map/all_to_all | solution.py:37
  132.8 35.9 %all-to-all-start.2 = ((bf16[64,4,32,128]{3,2,1,0:T(8,128)(2,1)}), bf16[64,4,32,128]{3,2,1,0:T(8,128)(2,1)}, u32[]{:S(2)}, u32[]{:S(2)}) async-start(bf16[64,4,32,128]{3,2,1,0:T(8,128)(2,1)} %bitcast.72), calls=%async_computation.2 | async-start | bytes 4194304 | tf_op jit(solution)/shard_map/all_to_all | solution.py:37
  141.6 4.2 %copy-start.5 = (bf16[4,4,1,64,1024]{4,3,2,1,0:T(8,128)(2,1)}, bf16[4,4,1,64,1024]{4,3,2,1,0:T(8,128)(2,1)S(1)}, u32[]{:S(2)}) copy-start(bf16[4,4,1,64,1024]{4,3,2,1,0:T(8,128)(2,1)S(1)} %constant_dynamic-slice_fusion) | copy-start | bytes 6291460
  145.8 39.3 %collective-permute-start.10 = (bf16[512,1024]{1,0:T(8,128)(2,1)}, bf16[512,1024]{1,0:T(8,128)(2,1)}, u32[]{:S(2)}, u32[]{:S(2)}) collective-permute-start(bf16[512,1024]{1,0:T(8,128)(2,1)} %convolution_convert_fusion), channel_id=1, source_target_pairs={{0,1},{1,0},{2,3},{3,2},{4,5},{5,4},{6,7},{7,6},{8,9},{9,8},{10,11... | collective-permute-start | bytes 3145736 | tf_op jit(solution)/shard_map/ppermute | solution.py:33
  147.8 37.3 %copy-start.4 = (bf16[512,1024]{1,0:T(8,128)(2,1)S(1)}, bf16[512,1024]{1,0:T(8,128)(2,1)}, u32[]{:S(2)}) copy-start(bf16[512,1024]{1,0:T(8,128)(2,1)} %param.12) | copy-start | bytes 3145732
  147.8 22.9 %collective-permute-start.11 = (bf16[64,128]{1,0:T(8,128)(2,1)S(1)}, bf16[64,128]{1,0:T(8,128)(2,1)S(1)}, u32[]{:S(2)}, u32[]{:S(2)}) collective-permute-start(bf16[64,128]{1,0:T(8,128)(2,1)S(1)} %get-tuple-element.29), channel_id=1, source_target_pairs={{0,8},{8,16},{16,24},{24,0},{1,9},{9,17},{17,25},{25,1},{2,10},{10... | collective-permute-start | bytes 49160 | tf_op jit(solution)/shard_map/ppermute | solution.py:41
  147.9 26.6 %collective-permute-start.12 = (bf16[64,128]{1,0:T(8,128)(2,1)S(1)}, bf16[64,128]{1,0:T(8,128)(2,1)S(1)}, u32[]{:S(2)}, u32[]{:S(2)}) collective-permute-start(bf16[64,128]{1,0:T(8,128)(2,1)S(1)} %get-tuple-element.31), channel_id=1, source_target_pairs={{0,16},{8,24},{16,0},{24,8},{1,17},{9,25},{17,1},{25,9},{2,18},{10... | collective-permute-start | bytes 49160 | tf_op jit(solution)/shard_map/ppermute | solution.py:41
  151.7 23.0 %collective-permute-start.13 = (bf16[64,128]{1,0:T(8,128)(2,1)S(1)}, bf16[64,128]{1,0:T(8,128)(2,1)S(1)}, u32[]{:S(2)}, u32[]{:S(2)}) collective-permute-start(bf16[64,128]{1,0:T(8,128)(2,1)S(1)} %get-tuple-element.30), channel_id=1, source_target_pairs={{0,24},{8,0},{16,8},{24,16},{1,25},{9,1},{17,9},{25,17},{2,26},{10... | collective-permute-start | bytes 49160 | tf_op jit(solution)/shard_map/ppermute | solution.py:41
  170.7 4.9 %collective-permute-start.14 = (bf16[64,128]{1,0:T(8,128)(2,1)S(1)}, bf16[64,128]{1,0:T(8,128)(2,1)S(1)}, u32[]{:S(2)}, u32[]{:S(2)}) collective-permute-start(bf16[64,128]{1,0:T(8,128)(2,1)S(1)} %get-tuple-element.32), channel_id=1, source_target_pairs={{0,8},{8,16},{16,24},{24,0},{1,9},{9,17},{17,25},{25,1},{2,10},{10... | collective-permute-start | bytes 49160 | tf_op jit(solution)/shard_map/ppermute | solution.py:41
  170.8 7.8 %collective-permute-start.15 = (bf16[64,128]{1,0:T(8,128)(2,1)S(1)}, bf16[64,128]{1,0:T(8,128)(2,1)S(1)}, u32[]{:S(2)}, u32[]{:S(2)}) collective-permute-start(bf16[64,128]{1,0:T(8,128)(2,1)S(1)} %get-tuple-element.34), channel_id=1, source_target_pairs={{0,16},{8,24},{16,0},{24,8},{1,17},{9,25},{17,1},{25,9},{2,18},{10... | collective-permute-start | bytes 49160 | tf_op jit(solution)/shard_map/ppermute | solution.py:41
  174.6 5.8 %collective-permute-start.16 = (bf16[64,128]{1,0:T(8,128)(2,1)S(1)}, bf16[64,128]{1,0:T(8,128)(2,1)S(1)}, u32[]{:S(2)}, u32[]{:S(2)}) collective-permute-start(bf16[64,128]{1,0:T(8,128)(2,1)S(1)} %get-tuple-element.33), channel_id=1, source_target_pairs={{0,24},{8,0},{16,8},{24,16},{1,25},{9,1},{17,9},{25,17},{2,26},{10... | collective-permute-start | bytes 49160 | tf_op jit(solution)/shard_map/ppermute | solution.py:41
  181.2 11.2 %all-to-all-start.3 = ((bf16[8,2,64,128]{3,2,1,0:T(8,128)(2,1)}), bf16[8,2,64,128]{3,2,1,0:T(8,128)(2,1)S(1)}, u32[]{:S(2)}, u32[]{:S(2)}) async-start(bf16[8,2,64,128]{3,2,1,0:T(8,128)(2,1)} %broadcast_in_dim.5), calls=%async_computation.3 | async-start | bytes 524288 | tf_op jit(solution)/shard_map/all_to_all | solution.py:37
  (3 other events, 2.5 us)
Sparse Core Ops, SparseCore 0:
  10.6 68.0 all-gather.1

commit v5 on v4

--- a/solution.py
+++ b/solution.py
@@ -21,12 +21,6 @@
     centred = values - center
     spread = jnp.mean(centred * centred, axis=-1, keepdims=True)
     return (centred * lax.rsqrt(spread + 1e-05) * ln_gain.astype(jnp.float32)).astype(jnp.bfloat16)
-
-
-def gelu_parts(pre):
-    cdf_value = 0.5 * (1.0 + lax.erf(pre * 0.7071067811865476))
-    density = jnp.exp(-0.5 * pre * pre) * 0.3989422804014327
-    return (pre * cdf_value, cdf_value + pre * density)
 
 
 def swap(value):
@@ -100,7 +94,7 @@
         at += part.shape[0]
 
 
-def forward_kernel(zh_ref, own_ref, partner_ref, c0, c1, c2, c3, w_ref, hidden_ref, slope_ref, term_ref, w, cot):
+def forward_kernel(zh_ref, own_ref, partner_ref, c0, c1, c2, c3, w_ref, hidden_ref, pre_ref, cdf_ref, term_ref, w, cot):
     @pl.when(pl.program_id(0) == 0)
     def _():
         join_cot((c0, c1, c2, c3), cot)
@@ -114,10 +108,11 @@
     for which, ref in enumerate((own_ref, partner_ref)):
         for at in range(0, rows, step):
             pre = jnp.dot(ref[at : at + step, :], w[...], preferred_element_type=jnp.float32)
-            act, slope = gelu_parts(pre)
+            cdf_value = 0.5 * (1.0 + lax.erf(pre * 0.7071067811865476))
             to = which * rows + at
-            hidden_ref[to : to + step, :] = act.astype(jnp.bfloat16)
-            slope_ref[to : to + step, :] = slope.astype(jnp.bfloat16)
+            hidden_ref[to : to + step, :] = (pre * cdf_value).astype(jnp.bfloat16)
+            pre_ref[to : to + step, :] = pre
+            cdf_ref[to : to + step, :] = cdf_value.astype(jnp.bfloat16)
     term = lax.dot_general(hidden_ref[...], cot[...], (((0,), (0,)), ((), ())), preferred_element_type=jnp.float32)
     term = term.astype(jnp.bfloat16)
     for x in range(N_X):
@@ -146,12 +141,14 @@
             out_specs=[
                 pl.BlockSpec((2 * rows, 256), lambda q, z: (0, q)),
                 pl.BlockSpec((2 * rows, 256), lambda q, z: (0, q)),
+                pl.BlockSpec((2 * rows, 256), lambda q, z: (0, q)),
                 pl.BlockSpec((N_GRP, N_X, 1, 64, 128), lambda q, z: (0, 0, q, 0, 0)),
             ],
             scratch_shapes=[pltpu.VMEM((width, 256), jnp.bfloat16), pltpu.VMEM((2 * rows, width), jnp.bfloat16)],
         ),
         out_shape=(
             jax.ShapeDtypeStruct((2 * rows, half), jnp.bfloat16),
+            jax.ShapeDtypeStruct((2 * rows, half), jnp.float32),
             jax.ShapeDtypeStruct((2 * rows, half), jnp.bfloat16),
             jax.ShapeDtypeStruct((N_GRP, N_X, N_ZH, 64, 128), jnp.bfloat16),
         ),
@@ -163,19 +160,21 @@
     )(zh.reshape(1), own, partner, *cots, got_up)
 
 
-def backward_kernel(core_ref, own_ref, partner_ref, c0, c1, c2, c3, w_ref, slope_ref, term_ref, pre_grad, cot):
+def backward_kernel(own_ref, partner_ref, c0, c1, c2, c3, w_ref, pre_ref, cdf_ref, term_ref, pre_grad, cot):
     @pl.when(pl.program_id(0) == 0)
     def _():
         join_cot((c0, c1, c2, c3), cot)
 
     rows, width = own_ref.shape
     step = rows // 2
-    w = w_ref[...].reshape(256, width)
+    w = w_ref[:, :64, :].reshape(256, width)
     for at in range(0, 2 * rows, step):
         back = lax.dot_general(
             cot[at : at + step, :], w, (((1,), (1,)), ((), ())), preferred_element_type=jnp.float32
         )
-        slope = slope_ref[at : at + step, :].astype(jnp.float32)
+        pre = pre_ref[at : at + step, :]
+        density = jnp.exp(-0.5 * pre * pre) * 0.3989422804014327
+        slope = cdf_ref[at : at + step, :].astype(jnp.float32) + pre * density
         pre_grad[at : at + step, :] = (back * slope).astype(jnp.bfloat16)
     dims = (((0,), (0,)), ((), ()))
     term = lax.dot_general(own_ref[...], pre_grad[:rows, :], dims, preferred_element_type=jnp.float32)
@@ -189,22 +188,23 @@
                     term_ref[g, x, c, z] = term[at : at + 32, g * 128 : (g + 1) * 128]
 
 
-def backward(core, own, partner, cots, down_all, slope):
+def backward(own, partner, cots, down_all, pre, cdf_value):
     rows, width = own.shape
     half = N_GRP * 128
     return pl.pallas_call(
         backward_kernel,
         grid_spec=pltpu.PrefetchScalarGridSpec(
-            num_scalar_prefetch=1,
+            num_scalar_prefetch=0,
             grid=(N_ZH,),
             in_specs=[
                 whole(own),
                 whole(partner),
                 *[whole(c) for c in cots],
-                pl.BlockSpec((None, N_X, None, 64, width), lambda q, c: (q, 0, c[0], 0, 0)),
-                pl.BlockSpec((2 * rows, 256), lambda q, c: (0, q)),
+                pl.BlockSpec((None, N_X) + down_all.shape[2:], lambda q: (q, 0, 0, 0)),
+                pl.BlockSpec((2 * rows, 256), lambda q: (0, q)),
+                pl.BlockSpec((2 * rows, 256), lambda q: (0, q)),
             ],
-            out_specs=pl.BlockSpec((2, N_X, N_C, N_ZH, 32, 128), lambda q, c: (q, 0, 0, 0, 0, 0)),
+            out_specs=pl.BlockSpec((2, N_X, N_C, N_ZH, 32, 128), lambda q: (q, 0, 0, 0, 0, 0)),
             scratch_shapes=[pltpu.VMEM((2 * rows, 256), jnp.bfloat16), pltpu.VMEM((2 * rows, width), jnp.bfloat16)],
         ),
         out_shape=jax.ShapeDtypeStruct((N_GRP, N_X, N_C, N_ZH, 32, 128), jnp.bfloat16),
@@ -213,7 +213,7 @@
             flops=8 * rows * width * half, bytes_accessed=20 * 1024 * 1024, transcendentals=0
         ),
         name="backward",
-    )(core.reshape(1), own, partner, *cots, down_all, slope)
+    )(own, partner, *cots, down_all, pre, cdf_value)
 
 
 def sum_zh(part, zh):
@@ -230,8 +230,8 @@
     up_rows, hid = w_up.shape
     group, zh = lax.axis_index(GRP), lax.axis_index("zh")
 
-    down_all = lax.all_gather(w_down, DEV, axis=0, tiled=True).reshape(N_ZH, N_X, N_C, *w_down.shape)
-    core = lax.axis_index("c")
+    down_all = lax.all_gather(jnp.pad(w_down, ((0, 16), (0, 0))), ("zh", "x"), axis=0, tiled=True)
+    down_all = down_all.reshape(N_ZH, N_X, -1, width)
 
     n_y, n_zl = SIZE["y"], SIZE["zl"]
     y, zl = lax.axis_index("y"), lax.axis_index("zl")
@@ -265,18 +265,18 @@
     cots = (grad_new, old_cot, swap(grad_new), swap(old_cot))
     rows = normed.shape[0]
 
-    hidden, slope, term_down = forward(zh, normed, partner, cots, got_up)
+    hidden, pre, cdf_value, term_down = forward(zh, normed, partner, cots, got_up)
     part_down = exchange(term_down.reshape(N_GRP * N_X, N_ZH, 64, 128), ("y", "zl", "x"))
     part_down = jnp.sum(part_down.astype(jnp.float32), axis=0).astype(jnp.bfloat16)
     sum_down = sum_zh(part_down, zh)
 
-    term_up = backward(core, normed, partner, cots, down_all, slope)
+    term_up = backward(normed, partner, cots, down_all, pre, cdf_value)
     part_up = exchange(term_up.reshape(N_GRP * N_X * N_C, N_ZH, up_rows, 128), ("y", "zl", "x", "c"))
     part_up = part_up.reshape(N_GRP * N_X, N_C, N_ZH, up_rows, 128)
     part_up = jnp.sum(part_up.astype(jnp.float32), axis=0).astype(jnp.bfloat16)
     sum_up = sum_zh(part_up.transpose(1, 0, 2, 3).reshape(N_ZH, N_C * up_rows, 128), zh)
 
-    down_half = lax.dynamic_index_in_dim(down_all, core, 2, keepdims=False).reshape(-1, width)
+    down_half = down_all[:, :, :64].reshape(-1, width)
     other = jnp.dot(hidden[rows : rows + fresh_count], down_half, preferred_element_type=jnp.float32)
     mixed = jnp.dot(hidden[:fresh_count], down_half, preferred_element_type=jnp.float32)
     returned = swap(other.astype(jnp.bfloat16)).astype(jnp.float32)

time: 203 us -> 201 us (level)
  waiting for transfers between devices: 85.4 us -> 80.2 us
  starting transfers between devices: 49.3 us -> 52.3 us
    all_to_all x4, waiting for transfers between devices: 74.7 us -> 42.6 us  [exchange(): return lax.all_to_all(value, axes, split_axis=0, concat_axis=0, tiled=True)]
    all_gather x1, waiting for transfers between devices: 0.02 us -> 28.6 us  [body(): lax.all_gather(jnp.pad(w_down, ((0, 16), (0, 0))), ('zh', 'x'), axis=0, t...]
    ppermute x9, starting transfers between devices: 16.6 us -> 20.1 us  [shift_zh(): lax.ppermute(value, 'zh', [(i, (i + step) % N_ZH) for i in range(N_ZH)])]
  transfers between devices with their start and end apart: 22 -> 22, of which waited for: 10 -> 9; matrix products, arithmetic and copies ran while one was open for 12% -> 11% of each run, Pallas kernels for 12% -> 12%
where the time goes in v5:
time: 201 us; the launch traced here: 200 us
  waiting for transfers between devices  80.2 us (40%)
  starting transfers between devices  52.3 us (26%)
  Pallas kernels  25.7 us (13%)
  between operations  14.4 us (7%)
  local copies, waits for them, and re-layouts  12.8 us (6%)
  matrix products  8.69 us (4%)
  other arithmetic  6.03 us (3%)
    all_to_all x4, waiting for transfers between devices, exchange(): return lax.all_to_all(value, axes, split_axis=0, concat_axis=0, tiled=True)  42.6 us
    all_gather x1, waiting for transfers between devices, body(): lax.all_gather(jnp.pad(w_down, ((0, 16), (0, 0))), ('zh', 'x'), axis=0, t...  28.6 us
    all_to_all x4, starting transfers between devices, exchange(): return lax.all_to_all(value, axes, split_axis=0, concat_axis=0, tiled=True)  23.5 us
    ppermute x9, starting transfers between devices, shift_zh(): lax.ppermute(value, 'zh', [(i, (i + step) % N_ZH) for i in range(N_ZH)])  20.1 us
    pallas_call x1, Pallas kernels, backward(): pl.pallas_call(backward_kernel, grid_spec=pltpu.PrefetchScalarGridSpec(nu...  11.8 us
    pallas_call x1, Pallas kernels, forward(): pl.pallas_call(forward_kernel, grid_spec=pltpu.PrefetchScalarGridSpec(num...  10.7 us
    ppermute x3, starting transfers between devices, body(): block = lax.ppermute(block, 'y', [(i, (i + dy) % n_y) for i in range(n_y)])  5.9 us
    ppermute x9, waiting for transfers between devices, shift_zh(): lax.ppermute(value, 'zh', [(i, (i + step) % N_ZH) for i in range(N_ZH)])  4.74 us
  transfers between devices with their start and end apart: 22, of which 9 were waited for; matrix products, arithmetic and copies ran while one was open for 11% of the time, Pallas kernels for 12%

profile of v5, /device:TPU:64, one launch (start us, length us, event | category | flops | bytes accessed | tf_op | source)
XLA Modules:
  0.0 200.1 jit_solution(16212527157478628910)
XLA Ops:
  8.3 2.0 %collective-permute-start.4 = (bf16[4,16,1024]{2,1,0:T(8,128)(2,1)S(1)}, bf16[4,16,1024]{2,1,0:T(8,128)(2,1)S(1)}, u32[]{:S(2)}, u32[]{:S(2)}) collective-permute-start(bf16[4,16,1024]{2,1,0:T(8,128)(2,1)S(1)} %get-tuple-element.29), channel_id=1, source_target_pairs={{0,32},{32,0},{1,33},{33,1},{2,34},{34,2},{3,35},{35,3},{4,36},{36... | collective-permute-start | bytes 393224 | tf_op jit(solution)/shard_map/ppermute | solution.py:241
  10.3 1.4 cut_up.1
  11.7 5.9 %collective-permute-start.2 = (bf16[2,32,128]{2,1,0:T(8,128)(2,1)}, bf16[2,32,128]{2,1,0:T(8,128)(2,1)S(1)}, u32[]{:S(2)}, u32[]{:S(2)}) collective-permute-start(bf16[2,32,128]{2,1,0:T(8,128)(2,1)} %cut_up.1), channel_id=1, source_target_pairs={{0,16},{8,24},{16,0},{24,8},{1,17},{9,25},{17,1},{25,9},{2,18},{10... | collective-permute-start | bytes 49160 | tf_op jit(solution)/shard_map/ppermute | solution.py:35
  17.7 2.7 %collective-permute-start.3 = (bf16[2,32,128]{2,1,0:T(8,128)(2,1)}, bf16[2,32,128]{2,1,0:T(8,128)(2,1)S(1)}, u32[]{:S(2)}, u32[]{:S(2)}) collective-permute-start(bf16[2,32,128]{2,1,0:T(8,128)(2,1)} %cut_up.1), channel_id=1, source_target_pairs={{0,8},{8,16},{16,24},{24,0},{1,9},{9,17},{17,25},{25,1},{2,10},{10... | collective-permute-start | bytes 49160 | tf_op jit(solution)/shard_map/ppermute | solution.py:35
  20.4 1.7 collective-permute-start.5
  22.0 2.9 %collective-permute-start.6 = (bf16[2,16,1024]{2,1,0:T(8,128)(2,1)S(1)}, bf16[2,16,1024]{2,1,0:T(8,128)(2,1)S(1)}, u32[]{:S(2)}, u32[]{:S(2)}) collective-permute-start(bf16[2,16,1024]{2,1,0:T(8,128)(2,1)S(1)} %get-tuple-element.28), channel_id=1, source_target_pairs={{0,128},{64,192},{128,0},{192,64},{1,129},{65,193},{129,1},{193,65... | collective-permute-start | bytes 196616 | tf_op jit(solution)/shard_map/ppermute | solution.py:246
  25.0 1.3 collective-permute-start.7
  27.9 1.3 collective-permute-done.7
  29.8 1.8 broadcast_in_dim.4
  31.7 8.2 %all-to-all-start = ((bf16[64,4,32,128]{3,2,1,0:T(8,128)(2,1)}), bf16[64,4,32,128]{3,2,1,0:T(8,128)(2,1)}, u32[]{:S(2)}, u32[]{:S(2)}) async-start(bf16[64,4,32,128]{3,2,1,0:T(8,128)(2,1)} %bitcast.68), calls=%async_computation | async-start | bytes 4194304 | tf_op jit(solution)/shard_map/all_to_all | solution.py:31
  48.1 2.1 %collective-permute-done.9.c3 = bf16[128,1024]{1,0:T(8,128)(2,1)} collective-permute-done((bf16[128,1024]{1,0:T(8,128)(2,1)}, bf16[128,1024]{1,0:T(8,128)(2,1)}, u32[]{:S(2)}, u32[]{:S(2)}) %collective-permute-start.9) | collective-permute-done | bytes 262176 | tf_op jit(solution)/shard_map/ppermute | solution.py:27
  50.2 21.8 %all-to-all-done = bf16[64,4,32,128]{3,2,1,0:T(8,128)(2,1)} async-done(((bf16[64,4,32,128]{3,2,1,0:T(8,128)(2,1)}), bf16[64,4,32,128]{3,2,1,0:T(8,128)(2,1)}, u32[]{:S(2)}, u32[]{:S(2)}) %all-to-all-start) | async-done | bytes 2097184 | tf_op jit(solution)/shard_map/all_to_all | solution.py:31
  72.0 10.7 %forward.1 = (bf16[1280,1024]{1,0:T(8,128)(2,1)}, f32[1280,1024]{1,0:T(8,128)}, bf16[1280,1024]{1,0:T(8,128)(2,1)}, bf16[8,4,4,64,128]{4,3,2,1,0:T(8,128)(2,1)}) custom-call(s32[1]{0:T(128)} %bitcast.zh_ref, bf16[640,1024]{1,0:T(8,128)(2,1)S(1)} %fusion.4.own_ref, bf16[640,1024]{1,0:T(8,128)(2,1)} %collective-permute-done.partner_ref, bf16[512,1024]{1,0:T(8,128)(2,1)} %c0.3, ...), custom_call_target="tpu_custom_call" | custom-call | bytes 1024 | tf_op jit(solution)/shard_map/forward/pallas_call | solution.py:130
  82.7 5.1 %all-to-all-start.1 = ((bf16[32,4,64,128]{3,2,1,0:T(8,128)(2,1)}), bf16[32,4,64,128]{3,2,1,0:T(8,128)(2,1)}, u32[]{:S(2)}, u32[]{:S(2)}) async-start(bf16[32,4,64,128]{3,2,1,0:T(8,128)(2,1)} %bitcast.72), calls=%async_computation.1 | async-start | bytes 4194304 | tf_op jit(solution)/shard_map/all_to_all | solution.py:31
  87.9 28.6 %all-gather.2.cloned.1.call-done = bf16[1280,1024]{1,0:T(8,128)(2,1)} async-done(((bf16[80,1024]{1,0:T(8,128)(2,1)}), bf16[1280,1024]{1,0:T(8,128)(2,1)}) %all-gather.2.cloned.1.call-update) | async-done | bytes 2621456 | tf_op jit(solution)/shard_map/all_gather | solution.py:233
  116.5 11.8 %backward.1 = bf16[8,4,2,4,32,128]{5,4,3,2,1,0:T(8,128)(2,1)} custom-call(bf16[640,1024]{1,0:T(8,128)(2,1)S(1)} %fusion.4.own_ref, bf16[640,1024]{1,0:T(8,128)(2,1)} %collective-permute-done.partner_ref, bf16[512,1024]{1,0:T(8,128)(2,1)} %c0.3, bf16[128,1024]{1,0:T(8,128)(2,1)} %constant_dynamic-update-slice_fusion.c1, ...), custom_call_target="tpu_custom_call" | custom-call | flops 5368709120 | bytes 20971520 | tf_op jit(solution)/shard_map/backward/pallas_call | solution.py:194
  128.3 2.9 %all-to-all-done.1 = bf16[32,4,64,128]{3,2,1,0:T(8,128)(2,1)} async-done(((bf16[32,4,64,128]{3,2,1,0:T(8,128)(2,1)}), bf16[32,4,64,128]{3,2,1,0:T(8,128)(2,1)}, u32[]{:S(2)}, u32[]{:S(2)}) %all-to-all-start.1) | async-done | bytes 2097184 | tf_op jit(solution)/shard_map/all_to_all | solution.py:31
  131.1 6.1 %all-to-all-start.2 = ((bf16[64,4,32,128]{3,2,1,0:T(8,128)(2,1)}), bf16[64,4,32,128]{3,2,1,0:T(8,128)(2,1)}, u32[]{:S(2)}, u32[]{:S(2)}) async-start(bf16[64,4,32,128]{3,2,1,0:T(8,128)(2,1)} %bitcast.71), calls=%async_computation.2 | async-start | bytes 4194304 | tf_op jit(solution)/shard_map/all_to_all | solution.py:31
  137.3 1.8 slice.18
  139.0 4.2 %convolution_convert_fusion = bf16[512,1024]{1,0:T(8,128)(2,1)} fusion(bf16[1024,1024]{1,0:T(8,128)(2,1)S(1)} %bitcast.69, bf16[1280,1024]{1,0:T(8,128)(2,1)} %get-tuple-element.19), kind=kOutput, calls=%fused_computation.11 | convolution fusion | flops 1074266112 | bytes 4194304 | tf_op jit(solution)/shard_map/dot_general | solution.py:280
  143.3 2.0 reduce_sum.44
  145.3 2.8 %collective-permute-start.11 = (bf16[64,128]{1,0:T(8,128)(2,1)S(1)}, bf16[64,128]{1,0:T(8,128)(2,1)S(1)}, u32[]{:S(2)}, u32[]{:S(2)}) collective-permute-start(bf16[64,128]{1,0:T(8,128)(2,1)S(1)} %get-tuple-element.31), channel_id=1, source_target_pairs={{0,8},{8,16},{16,24},{24,0},{1,9},{9,17},{17,25},{25,1},{2,10},{10... | collective-permute-start | bytes 49160 | tf_op jit(solution)/shard_map/ppermute | solution.py:35
  149.0 2.1 %collective-permute-start.13 = (bf16[64,128]{1,0:T(8,128)(2,1)S(1)}, bf16[64,128]{1,0:T(8,128)(2,1)S(1)}, u32[]{:S(2)}, u32[]{:S(2)}) collective-permute-start(bf16[64,128]{1,0:T(8,128)(2,1)S(1)} %get-tuple-element.32), channel_id=1, source_target_pairs={{0,24},{8,0},{16,8},{24,16},{1,25},{9,1},{17,9},{25,17},{2,26},{10... | collective-permute-start | bytes 49160 | tf_op jit(solution)/shard_map/ppermute | solution.py:35
  151.0 15.1 %all-to-all-done.2 = bf16[64,4,32,128]{3,2,1,0:T(8,128)(2,1)} async-done(((bf16[64,4,32,128]{3,2,1,0:T(8,128)(2,1)}), bf16[64,4,32,128]{3,2,1,0:T(8,128)(2,1)}, u32[]{:S(2)}, u32[]{:S(2)}) %all-to-all-start.2) | async-done | bytes 2097184 | tf_op jit(solution)/shard_map/all_to_all | solution.py:31
  166.1 1.9 reduce_sum.45
  168.1 2.8 %collective-permute-start.14 = (bf16[64,128]{1,0:T(8,128)(2,1)S(1)}, bf16[64,128]{1,0:T(8,128)(2,1)S(1)}, u32[]{:S(2)}, u32[]{:S(2)}) collective-permute-start(bf16[64,128]{1,0:T(8,128)(2,1)S(1)} %get-tuple-element.34), channel_id=1, source_target_pairs={{0,8},{8,16},{16,24},{24,0},{1,9},{9,17},{17,25},{25,1},{2,10},{10... | collective-permute-start | bytes 49160 | tf_op jit(solution)/shard_map/ppermute | solution.py:35
  171.8 2.1 %collective-permute-start.16 = (bf16[64,128]{1,0:T(8,128)(2,1)S(1)}, bf16[64,128]{1,0:T(8,128)(2,1)S(1)}, u32[]{:S(2)}, u32[]{:S(2)}) collective-permute-start(bf16[64,128]{1,0:T(8,128)(2,1)S(1)} %get-tuple-element.35), channel_id=1, source_target_pairs={{0,24},{8,0},{16,8},{24,16},{1,25},{9,1},{17,9},{25,17},{2,26},{10... | collective-permute-start | bytes 49160 | tf_op jit(solution)/shard_map/ppermute | solution.py:35
  173.9 4.7 %collective-permute-done.15 = bf16[64,128]{1,0:T(8,128)(2,1)S(1)} collective-permute-done((bf16[64,128]{1,0:T(8,128)(2,1)S(1)}, bf16[64,128]{1,0:T(8,128)(2,1)S(1)}, u32[]{:S(2)}, u32[]{:S(2)}) %collective-permute-start.15) | collective-permute-done | bytes 16416 | tf_op jit(solution)/shard_map/ppermute | solution.py:35
  179.4 4.1 %all-to-all-start.3 = ((bf16[8,2,64,128]{3,2,1,0:T(8,128)(2,1)}), bf16[8,2,64,128]{3,2,1,0:T(8,128)(2,1)S(1)}, u32[]{:S(2)}, u32[]{:S(2)}) async-start(bf16[8,2,64,128]{3,2,1,0:T(8,128)(2,1)} %broadcast_in_dim.5), calls=%async_computation.3 | async-start | bytes 524288 | tf_op jit(solution)/shard_map/all_to_all | solution.py:31
  183.5 4.5 %add_convert_fusion = bf16[512,1024]{1,0:T(8,128)(2,1)} fusion(bf16[512,1024]{1,0:T(8,128)(2,1)} %collective-permute-done.10, bf16[512,1024]{1,0:T(8,128)(2,1)S(1)} %copy-done.4, bf16[1024,1024]{1,0:T(8,128)(2,1)} %bitcast.70, bf16[1280,1024]{1,0:T(8,128)(2,1)} %get-tuple-element.19), kind=kOutput, calls=%fused_computation.10 | convolution fusion | flops 1076363264 | bytes 6291456 | tf_op jit(solution)/shard_map/dot_general | solution.py:281
  188.0 2.8 %all-to-all-done.3.both_ref = bf16[8,2,64,128]{3,2,1,0:T(8,128)(2,1)S(1)} async-done(((bf16[8,2,64,128]{3,2,1,0:T(8,128)(2,1)}), bf16[8,2,64,128]{3,2,1,0:T(8,128)(2,1)S(1)}, u32[]{:S(2)}, u32[]{:S(2)}) %all-to-all-start.3) | async-done | bytes 262176 | tf_op jit(solution)/shard_map/all_to_all | solution.py:31
  191.5 1.8 finish.1
  (85 shorter events, 14.7 us)
Async XLA Ops:
  7.2 35.2 %copy-start = (bf16[1024,1024]{1,0:T(8,128)(2,1)S(1)}, bf16[1024,1024]{1,0:T(8,128)(2,1)}, u32[]{:S(2)}) copy-start(bf16[1024,1024]{1,0:T(8,128)(2,1)} %param.9) | copy-start | bytes 6291460
  8.3 12.0 %collective-permute-start.4 = (bf16[4,16,1024]{2,1,0:T(8,128)(2,1)S(1)}, bf16[4,16,1024]{2,1,0:T(8,128)(2,1)S(1)}, u32[]{:S(2)}, u32[]{:S(2)}) collective-permute-start(bf16[4,16,1024]{2,1,0:T(8,128)(2,1)S(1)} %get-tuple-element.29), channel_id=1, source_target_pairs={{0,32},{32,0},{1,33},{33,1},{2,34},{34,2},{3,35},{35,3},{4,36},{36... | collective-permute-start | bytes 393224 | tf_op jit(solution)/shard_map/ppermute | solution.py:241
  11.7 13.2 %collective-permute-start.1 = (bf16[2,32,128]{2,1,0:T(8,128)(2,1)}, bf16[2,32,128]{2,1,0:T(8,128)(2,1)S(1)}, u32[]{:S(2)}, u32[]{:S(2)}) collective-permute-start(bf16[2,32,128]{2,1,0:T(8,128)(2,1)} %cut_up.1), channel_id=1, source_target_pairs={{0,24},{8,0},{16,8},{24,16},{1,25},{9,1},{17,9},{25,17},{2,26},{10... | collective-permute-start | bytes 49160 | tf_op jit(solution)/shard_map/ppermute | solution.py:35
  11.7 14.6 %collective-permute-start.2 = (bf16[2,32,128]{2,1,0:T(8,128)(2,1)}, bf16[2,32,128]{2,1,0:T(8,128)(2,1)S(1)}, u32[]{:S(2)}, u32[]{:S(2)}) collective-permute-start(bf16[2,32,128]{2,1,0:T(8,128)(2,1)} %cut_up.1), channel_id=1, source_target_pairs={{0,16},{8,24},{16,0},{24,8},{1,17},{9,25},{17,1},{25,9},{2,18},{10... | collective-permute-start | bytes 49160 | tf_op jit(solution)/shard_map/ppermute | solution.py:35
  17.7 8.6 %collective-permute-start.3 = (bf16[2,32,128]{2,1,0:T(8,128)(2,1)}, bf16[2,32,128]{2,1,0:T(8,128)(2,1)S(1)}, u32[]{:S(2)}, u32[]{:S(2)}) collective-permute-start(bf16[2,32,128]{2,1,0:T(8,128)(2,1)} %cut_up.1), channel_id=1, source_target_pairs={{0,8},{8,16},{16,24},{24,0},{1,9},{9,17},{17,25},{25,1},{2,10},{10... | collective-permute-start | bytes 49160 | tf_op jit(solution)/shard_map/ppermute | solution.py:35
  20.4 6.6 %collective-permute-start.5 = (bf16[2,16,1024]{2,1,0:T(8,128)(2,1)S(1)}, bf16[2,16,1024]{2,1,0:T(8,128)(2,1)S(1)}, u32[]{:S(2)}, u32[]{:S(2)}) collective-permute-start(bf16[2,16,1024]{2,1,0:T(8,128)(2,1)S(1)} %get-tuple-element.27), channel_id=1, source_target_pairs={{0,64},{64,128},{128,192},{192,0},{1,65},{65,129},{129,193},{193,1... | collective-permute-start | bytes 196616 | tf_op jit(solution)/shard_map/ppermute | solution.py:246
  22.0 5.8 %collective-permute-start.6 = (bf16[2,16,1024]{2,1,0:T(8,128)(2,1)S(1)}, bf16[2,16,1024]{2,1,0:T(8,128)(2,1)S(1)}, u32[]{:S(2)}, u32[]{:S(2)}) collective-permute-start(bf16[2,16,1024]{2,1,0:T(8,128)(2,1)S(1)} %get-tuple-element.28), channel_id=1, source_target_pairs={{0,128},{64,192},{128,0},{192,64},{1,129},{65,193},{129,1},{193,65... | collective-permute-start | bytes 196616 | tf_op jit(solution)/shard_map/ppermute | solution.py:246
  25.0 4.3 %collective-permute-start.7 = (bf16[2,16,1024]{2,1,0:T(8,128)(2,1)S(1)}, bf16[2,16,1024]{2,1,0:T(8,128)(2,1)S(1)}, u32[]{:S(2)}, u32[]{:S(2)}) collective-permute-start(bf16[2,16,1024]{2,1,0:T(8,128)(2,1)S(1)} %get-tuple-element.25), channel_id=1, source_target_pairs={{0,192},{64,0},{128,64},{192,128},{1,193},{65,1},{129,65},{193,129... | collective-permute-start | bytes 196616 | tf_op jit(solution)/shard_map/ppermute | solution.py:246
  31.7 8.2 %copy-start.8 = (bf16[64,1024]{1,0:T(8,128)(2,1)S(1)}, bf16[64,1024]{1,0:T(8,128)(2,1)}, u32[]{:S(2)}) copy-start(bf16[64,1024]{1,0:T(8,128)(2,1)} %param.14) | copy-start | bytes 393220
  31.7 9.1 %copy-start.7 = (s32[1,8,16]{2,1,0:T(8,128)S(1)}, s32[1,8,16]{2,1,0:T(8,128)}, u32[]{:S(2)}) copy-start(s32[1,8,16]{2,1,0:T(8,128)} %param.10) | copy-start | bytes 1540
  31.7 9.8 %copy-start.1 = (s32[1,8]{1,0:T(1,128)S(1)}, s32[1,8]{1,0:T(1,128)}, u32[]{:S(2)}) copy-start(s32[1,8]{1,0:T(1,128)} %param.11) | copy-start | bytes 100
  31.7 10.6 %copy-start.13 = (bf16[1024]{0:T(1024)(128)(2,1)S(1)}, bf16[1024]{0:T(1024)(128)(2,1)}, u32[]{:S(2)}) copy-start(bf16[1024]{0:T(1024)(128)(2,1)} %param.15) | copy-start | bytes 6148
  31.7 40.3 %all-to-all-start = ((bf16[64,4,32,128]{3,2,1,0:T(8,128)(2,1)}), bf16[64,4,32,128]{3,2,1,0:T(8,128)(2,1)}, u32[]{:S(2)}, u32[]{:S(2)}) async-start(bf16[64,4,32,128]{3,2,1,0:T(8,128)(2,1)} %bitcast.68), calls=%async_computation | async-start | bytes 4194304 | tf_op jit(solution)/shard_map/all_to_all | solution.py:31
  39.9 3.4 %copy-start.2 = (bf16[512,1024]{1,0:T(8,128)(2,1)S(1)}, bf16[512,1024]{1,0:T(8,128)(2,1)}, u32[]{:S(2)}) copy-start(bf16[512,1024]{1,0:T(8,128)(2,1)} %param.12) | copy-start | bytes 3145732
  39.9 76.6 %all-gather.2.cloned.1.call-start = ((), (), s32[]{:S(2)}) async-start(), calls=%async_computation.4 | async-start | bytes 2785280 | tf_op jit(solution)/shard_map/all_gather | solution.py:233
  43.6 3.2 %copy-start.10 = (bf16[2,16,1024]{2,1,0:T(8,128)(2,1)S(1)}, bf16[2,16,1024]{2,1,0:T(8,128)(2,1)}, u32[]{:S(2)}) copy-start(bf16[2,16,1024]{2,1,0:T(8,128)(2,1)} %copy-done.9) | copy-start | bytes 196612
  43.6 3.8 %copy-start.12 = (bf16[2,16,1024]{2,1,0:T(8,128)(2,1)S(1)}, bf16[2,16,1024]{2,1,0:T(8,128)(2,1)}, u32[]{:S(2)}) copy-start(bf16[2,16,1024]{2,1,0:T(8,128)(2,1)} %copy-done.11) | copy-start | bytes 196612
  44.9 5.3 %collective-permute-start = (bf16[640,1024]{1,0:T(8,128)(2,1)S(1)}, bf16[640,1024]{1,0:T(8,128)(2,1)}, u32[]{:S(2)}, u32[]{:S(2)}) collective-permute-start(bf16[640,1024]{1,0:T(8,128)(2,1)S(1)} %fusion.4.own_ref), channel_id=1, source_target_pairs={{0,1},{1,0},{2,3},{3,2},{4,5},{5,4},{6,7},{7,6},{8,9},{9,8},{10,11... | collective-permute-start | bytes 3932168 | tf_op jit(solution)/shard_map/ppermute | solution.py:27
  45.0 5.2 %collective-permute-start.8 = (bf16[512,1024]{1,0:T(8,128)(2,1)}, bf16[512,1024]{1,0:T(8,128)(2,1)}, u32[]{:S(2)}, u32[]{:S(2)}) collective-permute-start(bf16[512,1024]{1,0:T(8,128)(2,1)} %c0.3), channel_id=1, source_target_pairs={{0,1},{1,0},{2,3},{3,2},{4,5},{5,4},{6,7},{7,6},{8,9},{9,8},{10,11... | collective-permute-start | bytes 3145736 | tf_op jit(solution)/shard_map/ppermute | solution.py:27
  48.0 2.2 %collective-permute-start.9 = (bf16[128,1024]{1,0:T(8,128)(2,1)}, bf16[128,1024]{1,0:T(8,128)(2,1)}, u32[]{:S(2)}, u32[]{:S(2)}) collective-permute-start(bf16[128,1024]{1,0:T(8,128)(2,1)} %constant_dynamic-update-slice_fusion.c1), channel_id=1, source_target_pairs={{0,1},{1,0},{2,3},{3,2},{4,5},{5,4},{6,7},{7,6},{8,9},{9,8},{10,11... | collective-permute-start | bytes 786440 | tf_op jit(solution)/shard_map/ppermute | solution.py:27
  82.7 48.4 %all-to-all-start.1 = ((bf16[32,4,64,128]{3,2,1,0:T(8,128)(2,1)}), bf16[32,4,64,128]{3,2,1,0:T(8,128)(2,1)}, u32[]{:S(2)}, u32[]{:S(2)}) async-start(bf16[32,4,64,128]{3,2,1,0:T(8,128)(2,1)} %bitcast.72), calls=%async_computation.1 | async-start | bytes 4194304 | tf_op jit(solution)/shard_map/all_to_all | solution.py:31
  131.1 35.0 %all-to-all-start.2 = ((bf16[64,4,32,128]{3,2,1,0:T(8,128)(2,1)}), bf16[64,4,32,128]{3,2,1,0:T(8,128)(2,1)}, u32[]{:S(2)}, u32[]{:S(2)}) async-start(bf16[64,4,32,128]{3,2,1,0:T(8,128)(2,1)} %bitcast.71), calls=%async_computation.2 | async-start | bytes 4194304 | tf_op jit(solution)/shard_map/all_to_all | solution.py:31
  139.0 4.2 %copy-start.5 = (bf16[4,4,64,1024]{3,2,1,0:T(8,128)(2,1)}, bf16[4,4,64,1024]{3,2,1,0:T(8,128)(2,1)S(1)}, u32[]{:S(2)}) copy-start(bf16[4,4,64,1024]{3,2,1,0:T(8,128)(2,1)S(1)} %slice.18) | copy-start | bytes 6291460
  143.3 40.2 %collective-permute-start.10 = (bf16[512,1024]{1,0:T(8,128)(2,1)}, bf16[512,1024]{1,0:T(8,128)(2,1)}, u32[]{:S(2)}, u32[]{:S(2)}) collective-permute-start(bf16[512,1024]{1,0:T(8,128)(2,1)} %convolution_convert_fusion), channel_id=1, source_target_pairs={{0,1},{1,0},{2,3},{3,2},{4,5},{5,4},{6,7},{7,6},{8,9},{9,8},{10,11... | collective-permute-start | bytes 3145736 | tf_op jit(solution)/shard_map/ppermute | solution.py:27
  145.2 38.3 %copy-start.4 = (bf16[512,1024]{1,0:T(8,128)(2,1)S(1)}, bf16[512,1024]{1,0:T(8,128)(2,1)}, u32[]{:S(2)}) copy-start(bf16[512,1024]{1,0:T(8,128)(2,1)} %param.12) | copy-start | bytes 3145732
  145.3 25.7 %collective-permute-start.11 = (bf16[64,128]{1,0:T(8,128)(2,1)S(1)}, bf16[64,128]{1,0:T(8,128)(2,1)S(1)}, u32[]{:S(2)}, u32[]{:S(2)}) collective-permute-start(bf16[64,128]{1,0:T(8,128)(2,1)S(1)} %get-tuple-element.31), channel_id=1, source_target_pairs={{0,8},{8,16},{16,24},{24,0},{1,9},{9,17},{17,25},{25,1},{2,10},{10... | collective-permute-start | bytes 49160 | tf_op jit(solution)/shard_map/ppermute | solution.py:35
  148.1 23.7 %collective-permute-start.12 = (bf16[64,128]{1,0:T(8,128)(2,1)S(1)}, bf16[64,128]{1,0:T(8,128)(2,1)S(1)}, u32[]{:S(2)}, u32[]{:S(2)}) collective-permute-start(bf16[64,128]{1,0:T(8,128)(2,1)S(1)} %get-tuple-element.33), channel_id=1, source_target_pairs={{0,16},{8,24},{16,0},{24,8},{1,17},{9,25},{17,1},{25,9},{2,18},{10... | collective-permute-start | bytes 49160 | tf_op jit(solution)/shard_map/ppermute | solution.py:35
  149.0 24.9 %collective-permute-start.13 = (bf16[64,128]{1,0:T(8,128)(2,1)S(1)}, bf16[64,128]{1,0:T(8,128)(2,1)S(1)}, u32[]{:S(2)}, u32[]{:S(2)}) collective-permute-start(bf16[64,128]{1,0:T(8,128)(2,1)S(1)} %get-tuple-element.32), channel_id=1, source_target_pairs={{0,24},{8,0},{16,8},{24,16},{1,25},{9,1},{17,9},{25,17},{2,26},{10... | collective-permute-start | bytes 49160 | tf_op jit(solution)/shard_map/ppermute | solution.py:35
  168.1 5.8 %collective-permute-start.14 = (bf16[64,128]{1,0:T(8,128)(2,1)S(1)}, bf16[64,128]{1,0:T(8,128)(2,1)S(1)}, u32[]{:S(2)}, u32[]{:S(2)}) collective-permute-start(bf16[64,128]{1,0:T(8,128)(2,1)S(1)} %get-tuple-element.34), channel_id=1, source_target_pairs={{0,8},{8,16},{16,24},{24,0},{1,9},{9,17},{17,25},{25,1},{2,10},{10... | collective-permute-start | bytes 49160 | tf_op jit(solution)/shard_map/ppermute | solution.py:35
  170.9 7.7 %collective-permute-start.15 = (bf16[64,128]{1,0:T(8,128)(2,1)S(1)}, bf16[64,128]{1,0:T(8,128)(2,1)S(1)}, u32[]{:S(2)}, u32[]{:S(2)}) collective-permute-start(bf16[64,128]{1,0:T(8,128)(2,1)S(1)} %get-tuple-element.36), channel_id=1, source_target_pairs={{0,16},{8,24},{16,0},{24,8},{1,17},{9,25},{17,1},{25,9},{2,18},{10... | collective-permute-start | bytes 49160 | tf_op jit(solution)/shard_map/ppermute | solution.py:35
  171.8 6.8 %collective-permute-start.16 = (bf16[64,128]{1,0:T(8,128)(2,1)S(1)}, bf16[64,128]{1,0:T(8,128)(2,1)S(1)}, u32[]{:S(2)}, u32[]{:S(2)}) collective-permute-start(bf16[64,128]{1,0:T(8,128)(2,1)S(1)} %get-tuple-element.35), channel_id=1, source_target_pairs={{0,24},{8,0},{16,8},{24,16},{1,25},{9,1},{17,9},{25,17},{2,26},{10... | collective-permute-start | bytes 49160 | tf_op jit(solution)/shard_map/ppermute | solution.py:35
  179.4 11.4 %all-to-all-start.3 = ((bf16[8,2,64,128]{3,2,1,0:T(8,128)(2,1)}), bf16[8,2,64,128]{3,2,1,0:T(8,128)(2,1)S(1)}, u32[]{:S(2)}, u32[]{:S(2)}) async-start(bf16[8,2,64,128]{3,2,1,0:T(8,128)(2,1)} %broadcast_in_dim.5), calls=%async_computation.3 | async-start | bytes 524288 | tf_op jit(solution)/shard_map/all_to_all | solution.py:31
  (4 other events, 3.9 us)
Sparse Core Ops, SparseCore 0:
  43.7 72.7 all-gather.1

commit v6 on v5

--- a/solution.py
+++ b/solution.py
@@ -31,8 +31,17 @@
     return lax.all_to_all(value, axes, split_axis=0, concat_axis=0, tiled=True)
 
 
-def shift_zh(value, step):
-    return lax.ppermute(value, "zh", [(i, (i + step) % N_ZH) for i in range(N_ZH)])
+def shift(value, axis, step):
+    n = SIZE[axis]
+    return lax.ppermute(value, axis, [(i, (i + step) % n) for i in range(n)])
+
+
+def along(value, axis):
+    return [value] + [shift(value, axis, -step) for step in range(1, SIZE[axis])]
+
+
+def whole(array):
+    return pl.BlockSpec(array.shape, lambda *i: (0,) * array.ndim)
 
 
 def lanes_split(left, right):
@@ -42,26 +51,60 @@
     return first, second
 
 
-def cut_kernel(group_ref, w_ref, out_ref):
-    value = w_ref[...].astype(jnp.float32)
+def cut_kernel(at_ref, up_ref, down_ref, out_ref):
+    rows = up_ref.shape[0]
+    value = up_ref[...].astype(jnp.float32)
     first, second = lanes_split(value[:, :128], value[:, 128:])
-    out_ref[0] = first.astype(out_ref.dtype)
-    out_ref[1] = second.astype(out_ref.dtype)
-
-
-def cut_up(w_up, group):
-    rows = w_up.shape[0]
+    out_ref[:rows, :128] = first.astype(out_ref.dtype)
+    out_ref[rows:, :128] = second.astype(out_ref.dtype)
+    out_ref[:, 128:] = down_ref[...]
+
+
+def cut(w_up, w_down, group, y):
+    up_rows, down_rows = w_up.shape[0], w_down.shape[0]
     return pl.pallas_call(
         cut_kernel,
         grid_spec=pltpu.PrefetchScalarGridSpec(
             num_scalar_prefetch=1,
             grid=(1,),
-            in_specs=[pl.BlockSpec((rows, 256), lambda i, g: (0, g[0]))],
-            out_specs=pl.BlockSpec((2, rows, 128), lambda i, g: (0, 0, 0)),
-        ),
-        out_shape=jax.ShapeDtypeStruct((2, rows, 128), w_up.dtype),
-        name="cut_up",
-    )(group.reshape(1), w_up)
+            in_specs=[
+                pl.BlockSpec((up_rows, 256), lambda i, at: (0, at[0])),
+                pl.BlockSpec((down_rows, 256), lambda i, at: (0, at[1])),
+            ],
+            out_specs=pl.BlockSpec((down_rows, 384), lambda i, at: (0, 0)),
+        ),
+        out_shape=jax.ShapeDtypeStruct((down_rows, 384), w_up.dtype),
+        name="cut",
+    )(jnp.stack([group, y]), w_up, w_down)
+
+
+def spread_kernel(p0, p1, p2, p3, spread_ref, down_ref):
+    rows = spread_ref.shape[3]
+    for j, part in enumerate((p0, p1, p2, p3)):
+        down_ref[j] = part[:, 128:]
+        for c in range(N_C):
+            value = part[c * rows : (c + 1) * rows, :128]
+            for n in range(spread_ref.shape[0]):
+                spread_ref[n, c, j] = value
+
+
+def spread(parts):
+    down_rows = parts[0].shape[0]
+    rows = down_rows // N_C
+    return pl.pallas_call(
+        spread_kernel,
+        grid=(N_GRP,),
+        in_specs=[whole(part) for part in parts],
+        out_specs=[
+            pl.BlockSpec((N_X, N_C, N_ZH, rows, 128), lambda i: (i, 0, 0, 0, 0)),
+            pl.BlockSpec((N_ZH, down_rows, 256), lambda i: (0, 0, 0)),
+        ],
+        out_shape=(
+            jax.ShapeDtypeStruct((N_GRP * N_X, N_C, N_ZH, rows, 128), parts[0].dtype),
+            jax.ShapeDtypeStruct((N_ZH, down_rows, 256), parts[0].dtype),
+        ),
+        name="spread",
+    )(*parts)
 
 
 def final_kernel(both_ref, down_ref, up_ref):
@@ -120,10 +163,6 @@
             term_ref[g, x, 0] = term[x * 64 : (x + 1) * 64, g * 128 : (g + 1) * 128]
 
 
-def whole(array):
-    return pl.BlockSpec(array.shape, lambda *i: (0,) * array.ndim)
-
-
 def forward(zh, own, partner, cots, got_up):
     rows, width = own.shape
     half = N_GRP * 128
@@ -160,17 +199,21 @@
     )(zh.reshape(1), own, partner, *cots, got_up)
 
 
-def backward_kernel(own_ref, partner_ref, c0, c1, c2, c3, w_ref, pre_ref, cdf_ref, term_ref, pre_grad, cot):
+def backward_kernel(at_ref, own_ref, partner_ref, c0, c1, c2, c3, w0, w1, w2, w3, pre_ref, cdf_ref, term_ref, w, pre_grad, cot):
     @pl.when(pl.program_id(0) == 0)
     def _():
         join_cot((c0, c1, c2, c3), cot)
 
     rows, width = own_ref.shape
     step = rows // 2
-    w = w_ref[:, :64, :].reshape(256, width)
+    for j, ref in enumerate((w0, w1, w2, w3)):
+        column = pl.multiple_of((at_ref[1] + j) % SIZE["y"] * 256, 256)
+        for i in range(N_X):
+            row = pl.multiple_of((at_ref[2] + i) % N_X * 64, 64)
+            w[pl.ds(row, 64), pl.ds(column, 256)] = ref[i, 0]
     for at in range(0, 2 * rows, step):
         back = lax.dot_general(
-            cot[at : at + step, :], w, (((1,), (1,)), ((), ())), preferred_element_type=jnp.float32
+            cot[at : at + step, :], w[...], (((1,), (1,)), ((), ())), preferred_element_type=jnp.float32
         )
         pre = pre_ref[at : at + step, :]
         density = jnp.exp(-0.5 * pre * pre) * 0.3989422804014327
@@ -188,39 +231,45 @@
                     term_ref[g, x, c, z] = term[at : at + 32, g * 128 : (g + 1) * 128]
 
 
-def backward(own, partner, cots, down_all, pre, cdf_value):
+def backward(at, own, partner, cots, downs, pre, cdf_value):
     rows, width = own.shape
     half = N_GRP * 128
     return pl.pallas_call(
         backward_kernel,
         grid_spec=pltpu.PrefetchScalarGridSpec(
-            num_scalar_prefetch=0,
+            num_scalar_prefetch=1,
             grid=(N_ZH,),
             in_specs=[
                 whole(own),
                 whole(partner),
                 *[whole(c) for c in cots],
-                pl.BlockSpec((None, N_X) + down_all.shape[2:], lambda q: (q, 0, 0, 0)),
-                pl.BlockSpec((2 * rows, 256), lambda q: (0, q)),
-                pl.BlockSpec((2 * rows, 256), lambda q: (0, q)),
-            ],
-            out_specs=pl.BlockSpec((2, N_X, N_C, N_ZH, 32, 128), lambda q: (q, 0, 0, 0, 0, 0)),
+                *[pl.BlockSpec((N_X, 1, 64, 256), lambda q, at: (0, (q - at[0] + N_ZH) % N_ZH, 0, 0)) for _ in downs],
+                pl.BlockSpec((2 * rows, 256), lambda q, at: (0, q)),
+                pl.BlockSpec((2 * rows, 256), lambda q, at: (0, q)),
+            ],
+            out_specs=[
+                pl.BlockSpec((2, N_X, N_C, N_ZH, 32, 128), lambda q, at: (q, 0, 0, 0, 0, 0)),
+                pl.BlockSpec((256, width), lambda q, at: (q, 0)),
+            ],
             scratch_shapes=[pltpu.VMEM((2 * rows, 256), jnp.bfloat16), pltpu.VMEM((2 * rows, width), jnp.bfloat16)],
         ),
-        out_shape=jax.ShapeDtypeStruct((N_GRP, N_X, N_C, N_ZH, 32, 128), jnp.bfloat16),
+        out_shape=(
+            jax.ShapeDtypeStruct((N_GRP, N_X, N_C, N_ZH, 32, 128), jnp.bfloat16),
+            jax.ShapeDtypeStruct((half, width), jnp.bfloat16),
+        ),
         compiler_params=pltpu.CompilerParams(vmem_limit_bytes=VMEM_BYTES),
         cost_estimate=pl.CostEstimate(
             flops=8 * rows * width * half, bytes_accessed=20 * 1024 * 1024, transcendentals=0
         ),
         name="backward",
-    )(own, partner, *cots, down_all, pre, cdf_value)
+    )(at, own, partner, *cots, *downs, pre, cdf_value)
 
 
 def sum_zh(part, zh):
     total = lax.dynamic_index_in_dim(part, zh, 0, keepdims=False).astype(jnp.float32)
     for step in range(1, N_ZH):
         block = lax.dynamic_index_in_dim(part, (zh + step) % N_ZH, 0, keepdims=False)
-        total += shift_zh(block, step).astype(jnp.float32)
+        total += shift(block, "zh", step).astype(jnp.float32)
     return total.astype(jnp.bfloat16)
 
 
@@ -229,9 +278,6 @@
     fresh_count, width = new_rows.shape
     up_rows, hid = w_up.shape
     group, zh = lax.axis_index(GRP), lax.axis_index("zh")
-
-    down_all = lax.all_gather(jnp.pad(w_down, ((0, 16), (0, 0))), ("zh", "x"), axis=0, tiled=True)
-    down_all = down_all.reshape(N_ZH, N_X, -1, width)
 
     n_y, n_zl = SIZE["y"], SIZE["zl"]
     y, zl = lax.axis_index("y"), lax.axis_index("zl")
@@ -248,13 +294,13 @@
         order += [(y - dy) % n_y * n_zl + zl, (y - dy) % n_y * n_zl + 1 - zl]
     order = jnp.stack(order)
 
-    mine = cut_up(w_up, group)
-    column = jnp.stack([mine] + [shift_zh(mine, -step) for step in range(1, N_ZH)], axis=1)
-    column, *old_cot = lax.optimization_barrier((column, *old_cot))
-    old_cot = jnp.concatenate(old_cot, axis=0)
-    spread_up = jnp.broadcast_to(column[None], (N_GRP * N_X,) + column.shape)
+    parts = along(cut(w_up, w_down, group, y), "zh")
+    both = lax.optimization_barrier((*parts, *old_cot))
+    parts, old_cot = both[: len(parts)], jnp.concatenate(both[len(parts) :], axis=0)
+    spread_up, down_zh = spread(parts)
     spread_up = spread_up.reshape(N_GRP * N_X * N_C, N_ZH, up_rows, 128)
     got_up = exchange(spread_up, ("y", "zl", "x", "c")).reshape(N_GRP, N_X, N_C, N_ZH, up_rows, 128)
+    downs = along(jnp.stack(along(down_zh, "x")), "y")
 
     picks, counts = send_rows[0][order], send_count[0][order]
     live = (lax.broadcasted_iota(jnp.int32, (N_GRP, slots), 1) < counts[:, None]).astype(jnp.bfloat16)
@@ -266,17 +312,18 @@
     rows = normed.shape[0]
 
     hidden, pre, cdf_value, term_down = forward(zh, normed, partner, cots, got_up)
+    term_down, *downs = lax.optimization_barrier((term_down, *downs))
     part_down = exchange(term_down.reshape(N_GRP * N_X, N_ZH, 64, 128), ("y", "zl", "x"))
     part_down = jnp.sum(part_down.astype(jnp.float32), axis=0).astype(jnp.bfloat16)
     sum_down = sum_zh(part_down, zh)
 
-    term_up = backward(normed, partner, cots, down_all, pre, cdf_value)
+    at = jnp.stack([zh, y, lax.axis_index("x")])
+    term_up, down_half = backward(at, normed, partner, cots, downs, pre, cdf_value)
     part_up = exchange(term_up.reshape(N_GRP * N_X * N_C, N_ZH, up_rows, 128), ("y", "zl", "x", "c"))
     part_up = part_up.reshape(N_GRP * N_X, N_C, N_ZH, up_rows, 128)
     part_up = jnp.sum(part_up.astype(jnp.float32), axis=0).astype(jnp.bfloat16)
     sum_up = sum_zh(part_up.transpose(1, 0, 2, 3).reshape(N_ZH, N_C * up_rows, 128), zh)
 
-    down_half = down_all[:, :, :64].reshape(-1, width)
     other = jnp.dot(hidden[rows : rows + fresh_count], down_half, preferred_element_type=jnp.float32)
     mixed = jnp.dot(hidden[:fresh_count], down_half, preferred_element_type=jnp.float32)
     returned = swap(other.astype(jnp.bfloat16)).astype(jnp.float32)

time: 201 us -> 198 us (0.985)
  between operations: 14.4 us -> 1.03 us
  starting transfers between devices: 52.3 us -> 61.2 us
  Pallas kernels: 25.7 us -> 31.1 us
  waiting for transfers between devices: 80.2 us -> 74.9 us
    ppermute x9 -> x15, waiting for transfers between devices: 4.74 us -> 40.4 us  [shift(): return lax.ppermute(value, axis, [(i, (i + step) % n) for i in range(n)])]
    all_gather x1 -> x0, waiting for transfers between devices: 28.6 us -> none  [body(): lax.all_gather(jnp.pad(w_down, ((0, 16), (0, 0))), ('zh', 'x'), axis=0, t...]
    ppermute x9 -> x15, starting transfers between devices: 20.1 us -> 30.3 us  [shift(): return lax.ppermute(value, axis, [(i, (i + step) % n) for i in range(n)])]
    all_to_all x4, waiting for transfers between devices: 42.6 us -> 33.7 us  [exchange(): return lax.all_to_all(value, axes, split_axis=0, concat_axis=0, tiled=True)]
    pallas_call x1 -> x2, Pallas kernels: 1.4 us -> 6.16 us  [the longest x1 4.03 us: spread(): pl.pallas_call(spread_kernel, grid=(N_GRP,), in_specs=[whole(part) for pa...]
    unnamed x31 -> x39, local copies, waits for them, and re-layouts: 3.62 us -> 7.73 us
    ppermute x3, waiting for transfers between devices: 2.17 us -> 0.01 us  [body(): block = lax.ppermute(block, 'y', [(i, (i + dy) % n_y) for i in range(n_y)])]
    ppermute x4, waiting for transfers between devices: 2.1 us -> 0.01 us  [swap(): return lax.ppermute(value, 'c', [(0, 1), (1, 0)])]
  transfers between devices with their start and end apart: 22 -> 27, of which waited for: 9 -> 12; matrix products, arithmetic and copies ran while one was open for 11% -> 10% of each run, Pallas kernels for 12% -> 13%
where the time goes in v6:
time: 198 us; the launch traced here: 196 us
  waiting for transfers between devices  74.9 us (38%)
  starting transfers between devices  61.2 us (31%)
  Pallas kernels  31.1 us (16%)
  local copies, waits for them, and re-layouts  12.8 us (6%)
  matrix products  8.61 us (4%)
  other arithmetic  6.83 us (3%)
    ppermute x15, waiting for transfers between devices, shift(): return lax.ppermute(value, axis, [(i, (i + step) % n) for i in range(n)])  40.4 us
    all_to_all x4, waiting for transfers between devices, exchange(): return lax.all_to_all(value, axes, split_axis=0, concat_axis=0, tiled=True)  33.7 us
    ppermute x15, starting transfers between devices, shift(): return lax.ppermute(value, axis, [(i, (i + step) % n) for i in range(n)])  30.3 us
    all_to_all x4, starting transfers between devices, exchange(): return lax.all_to_all(value, axes, split_axis=0, concat_axis=0, tiled=True)  22.4 us
    pallas_call x1, Pallas kernels, backward(): pl.pallas_call(backward_kernel, grid_spec=pltpu.PrefetchScalarGridSpec(nu...  12.5 us
    pallas_call x1, Pallas kernels, forward(): pl.pallas_call(forward_kernel, grid_spec=pltpu.PrefetchScalarGridSpec(num...  10.7 us
    unnamed x39, local copies, waits for them, and re-layouts  7.73 us
    ppermute x3, starting transfers between devices, body(): block = lax.ppermute(block, 'y', [(i, (i + dy) % n_y) for i in range(n_y)])  5.9 us
  transfers between devices with their start and end apart: 27, of which 12 were waited for; matrix products, arithmetic and copies ran while one was open for 10% of the time, Pallas kernels for 13%

profile of v6, /device:TPU:64, one launch (start us, length us, event | category | flops | bytes accessed | tf_op | source)
XLA Modules:
  0.0 196.5 jit_solution(14226959810309063792)
XLA Ops:
  1.8 2.0 %collective-permute-start.4 = (bf16[4,16,1024]{2,1,0:T(8,128)(2,1)S(1)}, bf16[4,16,1024]{2,1,0:T(8,128)(2,1)S(1)}, u32[]{:S(2)}, u32[]{:S(2)}) collective-permute-start(bf16[4,16,1024]{2,1,0:T(8,128)(2,1)S(1)} %get-tuple-element.53), channel_id=1, source_target_pairs={{0,32},{32,0},{1,33},{33,1},{2,34},{34,2},{3,35},{35,3},{4,36},{36... | collective-permute-start | bytes 393224 | tf_op jit(solution)/shard_map/ppermute | solution.py:287
  4.4 2.1 %cut.1.p0 = bf16[64,384]{1,0:T(8,128)(2,1)} custom-call(s32[2]{0:T(128)} %pad_add_fusion.at_ref, bf16[32,2048]{1,0:T(8,128)(2,1)} %up_ref.1, bf16[64,1024]{1,0:T(8,128)(2,1)} %down_ref.1), custom_call_target="tpu_custom_call" | custom-call | tf_op jit(solution)/shard_map/cut/pallas_call | solution.py:65
  9.0 2.9 %collective-permute-start.6 = (bf16[2,16,1024]{2,1,0:T(8,128)(2,1)S(1)}, bf16[2,16,1024]{2,1,0:T(8,128)(2,1)}, u32[]{:S(2)}, u32[]{:S(2)}) collective-permute-start(bf16[2,16,1024]{2,1,0:T(8,128)(2,1)S(1)} %get-tuple-element.52), channel_id=1, source_target_pairs={{0,128},{64,192},{128,0},{192,64},{1,129},{65,193},{129,1},{193,65... | collective-permute-start | bytes 196616 | tf_op jit(solution)/shard_map/ppermute | solution.py:292
  13.2 5.2 %collective-permute-start.2 = (bf16[64,384]{1,0:T(8,128)(2,1)}, bf16[64,384]{1,0:T(8,128)(2,1)S(1)}, u32[]{:S(2)}, u32[]{:S(2)}) collective-permute-start(bf16[64,384]{1,0:T(8,128)(2,1)} %cut.1.p0), channel_id=1, source_target_pairs={{0,16},{8,24},{16,0},{24,8},{1,17},{9,25},{17,1},{25,9},{2,18},{10... | collective-permute-start | bytes 147464 | tf_op jit(solution)/shard_map/ppermute | solution.py:36
  18.5 2.6 %collective-permute-start.3 = (bf16[64,384]{1,0:T(8,128)(2,1)}, bf16[64,384]{1,0:T(8,128)(2,1)S(1)}, u32[]{:S(2)}, u32[]{:S(2)}) collective-permute-start(bf16[64,384]{1,0:T(8,128)(2,1)} %cut.1.p0), channel_id=1, source_target_pairs={{0,8},{8,16},{16,24},{24,0},{1,9},{9,17},{17,25},{25,1},{2,10},{10... | collective-permute-start | bytes 147464 | tf_op jit(solution)/shard_map/ppermute | solution.py:36
  21.4 2.2 %collective-permute-done.3.p3 = bf16[64,384]{1,0:T(8,128)(2,1)S(1)} collective-permute-done((bf16[64,384]{1,0:T(8,128)(2,1)}, bf16[64,384]{1,0:T(8,128)(2,1)S(1)}, u32[]{:S(2)}, u32[]{:S(2)}) %collective-permute-start.3) | collective-permute-done | bytes 49184 | tf_op jit(solution)/shard_map/ppermute | solution.py:36
  24.3 4.0 %spread.1 = (bf16[32,2,4,32,128]{4,3,2,1,0:T(8,128)(2,1)}, bf16[4,64,256]{2,1,0:T(8,128)(2,1)}) custom-call(bf16[64,384]{1,0:T(8,128)(2,1)} %cut.1.p0, bf16[64,384]{1,0:T(8,128)(2,1)} %copy-done.14, bf16[64,384]{1,0:T(8,128)(2,1)} %copy-done.15, bf16[64,384]{1,0:T(8,128)(2,1)} %copy-done.16), custom_call_target="tpu_custom_call" | custom-call | tf_op jit(solution)/shard_map/spread/pallas_call | solution.py:94
  28.3 6.9 %all-to-all-start = ((bf16[64,4,32,128]{3,2,1,0:T(8,128)(2,1)}), bf16[64,4,32,128]{3,2,1,0:T(8,128)(2,1)}, u32[]{:S(2)}, u32[]{:S(2)}) async-start(bf16[64,4,32,128]{3,2,1,0:T(8,128)(2,1)} %bitcast.68), calls=%async_computation | async-start | bytes 4194304 | tf_op jit(solution)/shard_map/all_to_all | solution.py:31
  40.1 2.7 %collective-permute-start.10 = (bf16[4,64,256]{2,1,0:T(8,128)(2,1)S(1)}, bf16[4,64,256]{2,1,0:T(8,128)(2,1)S(1)}, u32[]{:S(2)}, u32[]{:S(2)}) collective-permute-start(bf16[4,64,256]{2,1,0:T(8,128)(2,1)S(1)} %copy-done.13), channel_id=1, source_target_pairs={{0,6},{2,0},{4,2},{6,4},{1,7},{3,1},{5,3},{7,5},{8,14},{10,8},{12,... | collective-permute-start | bytes 393224 | tf_op jit(solution)/shard_map/ppermute | solution.py:36
  46.1 17.1 %collective-permute-done.10 = bf16[4,64,256]{2,1,0:T(8,128)(2,1)S(1)} collective-permute-done((bf16[4,64,256]{2,1,0:T(8,128)(2,1)S(1)}, bf16[4,64,256]{2,1,0:T(8,128)(2,1)S(1)}, u32[]{:S(2)}, u32[]{:S(2)}) %collective-permute-start.10) | collective-permute-done | bytes 131104 | tf_op jit(solution)/shard_map/ppermute | solution.py:36
  64.2 5.1 %collective-permute-done.12 = bf16[4,64,256]{2,1,0:T(8,128)(2,1)S(1)} collective-permute-done((bf16[4,64,256]{2,1,0:T(8,128)(2,1)S(1)}, bf16[4,64,256]{2,1,0:T(8,128)(2,1)S(1)}, u32[]{:S(2)}, u32[]{:S(2)}) %collective-permute-start.12) | collective-permute-done | bytes 131104 | tf_op jit(solution)/shard_map/ppermute | solution.py:36
  70.2 2.9 %collective-permute-start.13 = (bf16[4,4,64,256]{3,2,1,0:T(8,128)(2,1)}, bf16[4,4,64,256]{3,2,1,0:T(8,128)(2,1)}, u32[]{:S(2)}, u32[]{:S(2)}) collective-permute-start(bf16[4,4,64,256]{3,2,1,0:T(8,128)(2,1)} %pad_maximum_fusion.1.w0), channel_id=1, source_target_pairs={{0,192},{64,0},{128,64},{192,128},{1,193},{65,1},{129,65},{193,129... | collective-permute-start | bytes 1572872 | tf_op jit(solution)/shard_map/ppermute | solution.py:36
  77.3 10.7 %forward.1 = (bf16[1280,1024]{1,0:T(8,128)(2,1)}, f32[1280,1024]{1,0:T(8,128)}, bf16[1280,1024]{1,0:T(8,128)(2,1)}, bf16[8,4,4,64,128]{4,3,2,1,0:T(8,128)(2,1)}) custom-call(s32[1]{0:T(128)} %bitcast.zh_ref, bf16[640,1024]{1,0:T(8,128)(2,1)S(1)} %fusion.4.own_ref, bf16[640,1024]{1,0:T(8,128)(2,1)} %collective-permute-done.partner_ref, bf16[512,1024]{1,0:T(8,128)(2,1)} %c0.3, ...), custom_call_target="tpu_custom_call" | custom-call | bytes 1024 | tf_op jit(solution)/shard_map/forward/pallas_call | solution.py:169
  88.0 6.1 %collective-permute-done.13.w1 = bf16[4,4,64,256]{3,2,1,0:T(8,128)(2,1)} collective-permute-done((bf16[4,4,64,256]{3,2,1,0:T(8,128)(2,1)}, bf16[4,4,64,256]{3,2,1,0:T(8,128)(2,1)}, u32[]{:S(2)}, u32[]{:S(2)}) %collective-permute-start.13) | collective-permute-done | bytes 524320 | tf_op jit(solution)/shard_map/ppermute | solution.py:36
  94.0 3.7 %collective-permute-done.15.w3 = bf16[4,4,64,256]{3,2,1,0:T(8,128)(2,1)} collective-permute-done((bf16[4,4,64,256]{3,2,1,0:T(8,128)(2,1)}, bf16[4,4,64,256]{3,2,1,0:T(8,128)(2,1)}, u32[]{:S(2)}, u32[]{:S(2)}) %collective-permute-start.15) | collective-permute-done | bytes 524320 | tf_op jit(solution)/shard_map/ppermute | solution.py:36
  97.7 4.8 %all-to-all-start.1 = ((bf16[32,4,64,128]{3,2,1,0:T(8,128)(2,1)}), bf16[32,4,64,128]{3,2,1,0:T(8,128)(2,1)}, u32[]{:S(2)}, u32[]{:S(2)}) async-start(bf16[32,4,64,128]{3,2,1,0:T(8,128)(2,1)} %bitcast.70), calls=%async_computation.1 | async-start | bytes 4194304 | tf_op jit(solution)/shard_map/all_to_all | solution.py:31
  104.4 12.5 %backward.1 = (bf16[8,4,2,4,32,128]{5,4,3,2,1,0:T(8,128)(2,1)}, bf16[1024,1024]{1,0:T(8,128)(2,1)}) custom-call(s32[3]{0:T(128)S(1)} %pad_add_fusion.1.at_ref, bf16[640,1024]{1,0:T(8,128)(2,1)S(1)} %fusion.4.own_ref, bf16[640,1024]{1,0:T(8,128)(2,1)} %collective-permute-done.partner_ref, bf16[512,1024]{1,0:T(8,128)(2,1)} %c0.3, ...), custom_call_target="tpu_custom_call" | custom-call | flops 5368709120 | bytes 20971520 | tf_op jit(solution)/shard_map/backward/pallas_call | solution.py:237
  117.0 14.9 %all-to-all-done.1 = bf16[32,4,64,128]{3,2,1,0:T(8,128)(2,1)} async-done(((bf16[32,4,64,128]{3,2,1,0:T(8,128)(2,1)}), bf16[32,4,64,128]{3,2,1,0:T(8,128)(2,1)}, u32[]{:S(2)}, u32[]{:S(2)}) %all-to-all-start.1) | async-done | bytes 2097184 | tf_op jit(solution)/shard_map/all_to_all | solution.py:31
  131.8 6.8 %all-to-all-start.2 = ((bf16[64,4,32,128]{3,2,1,0:T(8,128)(2,1)}), bf16[64,4,32,128]{3,2,1,0:T(8,128)(2,1)}, u32[]{:S(2)}, u32[]{:S(2)}) async-start(bf16[64,4,32,128]{3,2,1,0:T(8,128)(2,1)} %bitcast.69), calls=%async_computation.2 | async-start | bytes 4194304 | tf_op jit(solution)/shard_map/all_to_all | solution.py:31
  138.6 4.1 %convolution_convert_fusion = bf16[512,1024]{1,0:T(8,128)(2,1)} fusion(bf16[1024,1024]{1,0:T(8,128)(2,1)} %get-tuple-element.44, bf16[1280,1024]{1,0:T(8,128)(2,1)} %get-tuple-element.35), kind=kOutput, calls=%fused_computation.11 | convolution fusion | flops 1074266112 | bytes 4194304 | tf_op jit(solution)/shard_map/dot_general | solution.py:327
  142.7 2.0 reduce_sum.44
  144.7 3.6 %collective-permute-start.17 = (bf16[64,128]{1,0:T(8,128)(2,1)S(1)}, bf16[64,128]{1,0:T(8,128)(2,1)S(1)}, u32[]{:S(2)}, u32[]{:S(2)}) collective-permute-start(bf16[64,128]{1,0:T(8,128)(2,1)S(1)} %get-tuple-element.55), channel_id=1, source_target_pairs={{0,8},{8,16},{16,24},{24,0},{1,9},{9,17},{17,25},{25,1},{2,10},{10... | collective-permute-start | bytes 49160 | tf_op jit(solution)/shard_map/ppermute | solution.py:36
  148.4 3.0 %collective-permute-start.18 = (bf16[64,128]{1,0:T(8,128)(2,1)S(1)}, bf16[64,128]{1,0:T(8,128)(2,1)S(1)}, u32[]{:S(2)}, u32[]{:S(2)}) collective-permute-start(bf16[64,128]{1,0:T(8,128)(2,1)S(1)} %get-tuple-element.57), channel_id=1, source_target_pairs={{0,16},{8,24},{16,0},{24,8},{1,17},{9,25},{17,1},{25,9},{2,18},{10... | collective-permute-start | bytes 49160 | tf_op jit(solution)/shard_map/ppermute | solution.py:36
  151.4 16.1 %all-to-all-done.2 = bf16[64,4,32,128]{3,2,1,0:T(8,128)(2,1)} async-done(((bf16[64,4,32,128]{3,2,1,0:T(8,128)(2,1)}), bf16[64,4,32,128]{3,2,1,0:T(8,128)(2,1)}, u32[]{:S(2)}, u32[]{:S(2)}) %all-to-all-start.2) | async-done | bytes 2097184 | tf_op jit(solution)/shard_map/all_to_all | solution.py:31
  167.5 1.9 reduce_sum.45
  169.4 3.8 %collective-permute-start.20 = (bf16[64,128]{1,0:T(8,128)(2,1)S(1)}, bf16[64,128]{1,0:T(8,128)(2,1)S(1)}, u32[]{:S(2)}, u32[]{:S(2)}) collective-permute-start(bf16[64,128]{1,0:T(8,128)(2,1)S(1)} %get-tuple-element.58), channel_id=1, source_target_pairs={{0,8},{8,16},{16,24},{24,0},{1,9},{9,17},{17,25},{25,1},{2,10},{10... | collective-permute-start | bytes 49160 | tf_op jit(solution)/shard_map/ppermute | solution.py:36
  173.3 2.9 %collective-permute-start.21 = (bf16[64,128]{1,0:T(8,128)(2,1)S(1)}, bf16[64,128]{1,0:T(8,128)(2,1)S(1)}, u32[]{:S(2)}, u32[]{:S(2)}) collective-permute-start(bf16[64,128]{1,0:T(8,128)(2,1)S(1)} %get-tuple-element.60), channel_id=1, source_target_pairs={{0,16},{8,24},{16,0},{24,8},{1,17},{9,25},{17,1},{25,9},{2,18},{10... | collective-permute-start | bytes 49160 | tf_op jit(solution)/shard_map/ppermute | solution.py:36
  176.2 4.8 %collective-permute-done.21 = bf16[64,128]{1,0:T(8,128)(2,1)S(1)} collective-permute-done((bf16[64,128]{1,0:T(8,128)(2,1)S(1)}, bf16[64,128]{1,0:T(8,128)(2,1)S(1)}, u32[]{:S(2)}, u32[]{:S(2)}) %collective-permute-start.21) | collective-permute-done | bytes 16416 | tf_op jit(solution)/shard_map/ppermute | solution.py:36
  182.7 3.9 %all-to-all-start.3 = ((bf16[8,2,64,128]{3,2,1,0:T(8,128)(2,1)}), bf16[8,2,64,128]{3,2,1,0:T(8,128)(2,1)S(1)}, u32[]{:S(2)}, u32[]{:S(2)}) async-start(bf16[8,2,64,128]{3,2,1,0:T(8,128)(2,1)} %broadcast_in_dim.2), calls=%async_computation.3 | async-start | bytes 524288 | tf_op jit(solution)/shard_map/all_to_all | solution.py:31
  186.7 4.5 %add_convert_fusion = bf16[512,1024]{1,0:T(8,128)(2,1)} fusion(bf16[512,1024]{1,0:T(8,128)(2,1)} %collective-permute-done.16, bf16[512,1024]{1,0:T(8,128)(2,1)S(1)} %copy-done.10, bf16[1024,1024]{1,0:T(8,128)(2,1)} %get-tuple-element.44, bf16[1280,1024]{1,0:T(8,128)(2,1)} %get-tuple-element.35), kind=kOutput, calls=%fused_computation.10 | convolution fusion | flops 1076363264 | bytes 6291456 | tf_op jit(solution)/shard_map/dot_general | solution.py:328
  191.2 2.8 %all-to-all-done.3.both_ref = bf16[8,2,64,128]{3,2,1,0:T(8,128)(2,1)S(1)} async-done(((bf16[8,2,64,128]{3,2,1,0:T(8,128)(2,1)}), bf16[8,2,64,128]{3,2,1,0:T(8,128)(2,1)S(1)}, u32[]{:S(2)}, u32[]{:S(2)}) %all-to-all-start.3) | async-done | bytes 262176 | tf_op jit(solution)/shard_map/all_to_all | solution.py:31
  194.7 1.8 finish.1
  (101 shorter events, 25.1 us)
Async XLA Ops:
  0.6 36.3 %copy-start = (bf16[1024,1024]{1,0:T(8,128)(2,1)S(1)}, bf16[1024,1024]{1,0:T(8,128)(2,1)}, u32[]{:S(2)}) copy-start(bf16[1024,1024]{1,0:T(8,128)(2,1)} %param.9) | copy-start | bytes 6291460
  1.8 5.5 %collective-permute-start.4 = (bf16[4,16,1024]{2,1,0:T(8,128)(2,1)S(1)}, bf16[4,16,1024]{2,1,0:T(8,128)(2,1)S(1)}, u32[]{:S(2)}, u32[]{:S(2)}) collective-permute-start(bf16[4,16,1024]{2,1,0:T(8,128)(2,1)S(1)} %get-tuple-element.53), channel_id=1, source_target_pairs={{0,32},{32,0},{1,33},{33,1},{2,34},{34,2},{3,35},{35,3},{4,36},{36... | collective-permute-start | bytes 393224 | tf_op jit(solution)/shard_map/ppermute | solution.py:287
  6.5 11.9 %collective-permute-start.1 = (bf16[64,384]{1,0:T(8,128)(2,1)}, bf16[64,384]{1,0:T(8,128)(2,1)S(1)}, u32[]{:S(2)}, u32[]{:S(2)}) collective-permute-start(bf16[64,384]{1,0:T(8,128)(2,1)} %cut.1.p0), channel_id=1, source_target_pairs={{0,24},{8,0},{16,8},{24,16},{1,25},{9,1},{17,9},{25,17},{2,26},{10... | collective-permute-start | bytes 147464 | tf_op jit(solution)/shard_map/ppermute | solution.py:36
  7.3 16.3 %collective-permute-start.5 = (bf16[2,16,1024]{2,1,0:T(8,128)(2,1)S(1)}, bf16[2,16,1024]{2,1,0:T(8,128)(2,1)S(1)}, u32[]{:S(2)}, u32[]{:S(2)}) collective-permute-start(bf16[2,16,1024]{2,1,0:T(8,128)(2,1)S(1)} %get-tuple-element.51), channel_id=1, source_target_pairs={{0,64},{64,128},{128,192},{192,0},{1,65},{65,129},{129,193},{193,1... | collective-permute-start | bytes 196616 | tf_op jit(solution)/shard_map/ppermute | solution.py:292
  9.0 14.7 %collective-permute-start.6 = (bf16[2,16,1024]{2,1,0:T(8,128)(2,1)S(1)}, bf16[2,16,1024]{2,1,0:T(8,128)(2,1)}, u32[]{:S(2)}, u32[]{:S(2)}) collective-permute-start(bf16[2,16,1024]{2,1,0:T(8,128)(2,1)S(1)} %get-tuple-element.52), channel_id=1, source_target_pairs={{0,128},{64,192},{128,0},{192,64},{1,129},{65,193},{129,1},{193,65... | collective-permute-start | bytes 196616 | tf_op jit(solution)/shard_map/ppermute | solution.py:292
  11.9 11.8 %collective-permute-start.7 = (bf16[2,16,1024]{2,1,0:T(8,128)(2,1)S(1)}, bf16[2,16,1024]{2,1,0:T(8,128)(2,1)}, u32[]{:S(2)}, u32[]{:S(2)}) collective-permute-start(bf16[2,16,1024]{2,1,0:T(8,128)(2,1)S(1)} %get-tuple-element.49), channel_id=1, source_target_pairs={{0,192},{64,0},{128,64},{192,128},{1,193},{65,1},{129,65},{193,129... | collective-permute-start | bytes 196616 | tf_op jit(solution)/shard_map/ppermute | solution.py:292
  13.2 8.2 %collective-permute-start.2 = (bf16[64,384]{1,0:T(8,128)(2,1)}, bf16[64,384]{1,0:T(8,128)(2,1)S(1)}, u32[]{:S(2)}, u32[]{:S(2)}) collective-permute-start(bf16[64,384]{1,0:T(8,128)(2,1)} %cut.1.p0), channel_id=1, source_target_pairs={{0,16},{8,24},{16,0},{24,8},{1,17},{9,25},{17,1},{25,9},{2,18},{10... | collective-permute-start | bytes 147464 | tf_op jit(solution)/shard_map/ppermute | solution.py:36
  18.5 5.2 %collective-permute-start.3 = (bf16[64,384]{1,0:T(8,128)(2,1)}, bf16[64,384]{1,0:T(8,128)(2,1)S(1)}, u32[]{:S(2)}, u32[]{:S(2)}) collective-permute-start(bf16[64,384]{1,0:T(8,128)(2,1)} %cut.1.p0), channel_id=1, source_target_pairs={{0,8},{8,16},{16,24},{24,0},{1,9},{9,17},{17,25},{25,1},{2,10},{10... | collective-permute-start | bytes 147464 | tf_op jit(solution)/shard_map/ppermute | solution.py:36
  28.3 7.1 %copy-start.12 = (s32[1,8,16]{2,1,0:T(8,128)S(1)}, s32[1,8,16]{2,1,0:T(8,128)}, u32[]{:S(2)}) copy-start(s32[1,8,16]{2,1,0:T(8,128)} %param.10) | copy-start | bytes 1540
  28.3 7.8 %copy-start.7 = (s32[1,8]{1,0:T(1,128)S(1)}, s32[1,8]{1,0:T(1,128)}, u32[]{:S(2)}) copy-start(s32[1,8]{1,0:T(1,128)} %param.11) | copy-start | bytes 100
  28.3 8.6 %copy-start.17 = (bf16[1024]{0:T(1024)(128)(2,1)S(1)}, bf16[1024]{0:T(1024)(128)(2,1)}, u32[]{:S(2)}) copy-start(bf16[1024]{0:T(1024)(128)(2,1)} %param.15) | copy-start | bytes 6148
  28.3 47.1 %all-to-all-start = ((bf16[64,4,32,128]{3,2,1,0:T(8,128)(2,1)}), bf16[64,4,32,128]{3,2,1,0:T(8,128)(2,1)}, u32[]{:S(2)}, u32[]{:S(2)}) async-start(bf16[64,4,32,128]{3,2,1,0:T(8,128)(2,1)} %bitcast.68), calls=%async_computation | async-start | bytes 4194304 | tf_op jit(solution)/shard_map/all_to_all | solution.py:31
  39.5 35.9 %collective-permute-start = (bf16[640,1024]{1,0:T(8,128)(2,1)S(1)}, bf16[640,1024]{1,0:T(8,128)(2,1)}, u32[]{:S(2)}, u32[]{:S(2)}) collective-permute-start(bf16[640,1024]{1,0:T(8,128)(2,1)S(1)} %fusion.4.own_ref), channel_id=1, source_target_pairs={{0,1},{1,0},{2,3},{3,2},{4,5},{5,4},{6,7},{7,6},{8,9},{9,8},{10,11... | collective-permute-start | bytes 3932168 | tf_op jit(solution)/shard_map/ppermute | solution.py:27
  39.6 35.8 %collective-permute-start.8 = (bf16[512,1024]{1,0:T(8,128)(2,1)}, bf16[512,1024]{1,0:T(8,128)(2,1)}, u32[]{:S(2)}, u32[]{:S(2)}) collective-permute-start(bf16[512,1024]{1,0:T(8,128)(2,1)} %c0.3), channel_id=1, source_target_pairs={{0,1},{1,0},{2,3},{3,2},{4,5},{5,4},{6,7},{7,6},{8,9},{9,8},{10,11... | collective-permute-start | bytes 3145736 | tf_op jit(solution)/shard_map/ppermute | solution.py:27
  40.1 23.0 %collective-permute-start.10 = (bf16[4,64,256]{2,1,0:T(8,128)(2,1)S(1)}, bf16[4,64,256]{2,1,0:T(8,128)(2,1)S(1)}, u32[]{:S(2)}, u32[]{:S(2)}) collective-permute-start(bf16[4,64,256]{2,1,0:T(8,128)(2,1)S(1)} %copy-done.13), channel_id=1, source_target_pairs={{0,6},{2,0},{4,2},{6,4},{1,7},{3,1},{5,3},{7,5},{8,14},{10,8},{12,... | collective-permute-start | bytes 393224 | tf_op jit(solution)/shard_map/ppermute | solution.py:36
  44.5 29.2 %collective-permute-start.9 = (bf16[128,1024]{1,0:T(8,128)(2,1)S(1)}, bf16[128,1024]{1,0:T(8,128)(2,1)S(1)}, u32[]{:S(2)}, u32[]{:S(2)}) collective-permute-start(bf16[128,1024]{1,0:T(8,128)(2,1)S(1)} %constant_dynamic-update-slice_fusion.c1), channel_id=1, source_target_pairs={{0,1},{1,0},{2,3},{3,2},{4,5},{5,4},{6,7},{7,6},{8,9},{9,8},{10,11... | collective-permute-start | bytes 786440 | tf_op jit(solution)/shard_map/ppermute | solution.py:27
  45.2 19.0 %collective-permute-start.11 = (bf16[4,64,256]{2,1,0:T(8,128)(2,1)S(1)}, bf16[4,64,256]{2,1,0:T(8,128)(2,1)S(1)}, u32[]{:S(2)}, u32[]{:S(2)}) collective-permute-start(bf16[4,64,256]{2,1,0:T(8,128)(2,1)S(1)} %copy-done.13), channel_id=1, source_target_pairs={{0,4},{2,6},{4,0},{6,2},{1,5},{3,7},{5,1},{7,3},{8,12},{10,14},{12... | collective-permute-start | bytes 393224 | tf_op jit(solution)/shard_map/ppermute | solution.py:36
  63.1 6.2 %collective-permute-start.12 = (bf16[4,64,256]{2,1,0:T(8,128)(2,1)S(1)}, bf16[4,64,256]{2,1,0:T(8,128)(2,1)S(1)}, u32[]{:S(2)}, u32[]{:S(2)}) collective-permute-start(bf16[4,64,256]{2,1,0:T(8,128)(2,1)S(1)} %copy-done.13), channel_id=1, source_target_pairs={{0,2},{2,4},{4,6},{6,0},{1,3},{3,5},{5,7},{7,1},{8,10},{10,12},{12... | collective-permute-start | bytes 393224 | tf_op jit(solution)/shard_map/ppermute | solution.py:36
  70.2 23.8 %collective-permute-start.13 = (bf16[4,4,64,256]{3,2,1,0:T(8,128)(2,1)}, bf16[4,4,64,256]{3,2,1,0:T(8,128)(2,1)}, u32[]{:S(2)}, u32[]{:S(2)}) collective-permute-start(bf16[4,4,64,256]{3,2,1,0:T(8,128)(2,1)} %pad_maximum_fusion.1.w0), channel_id=1, source_target_pairs={{0,192},{64,0},{128,64},{192,128},{1,193},{65,1},{129,65},{193,129... | collective-permute-start | bytes 1572872 | tf_op jit(solution)/shard_map/ppermute | solution.py:36
  73.1 21.0 %collective-permute-start.14 = (bf16[4,4,64,256]{3,2,1,0:T(8,128)(2,1)}, bf16[4,4,64,256]{3,2,1,0:T(8,128)(2,1)}, u32[]{:S(2)}, u32[]{:S(2)}) collective-permute-start(bf16[4,4,64,256]{3,2,1,0:T(8,128)(2,1)} %pad_maximum_fusion.1.w0), channel_id=1, source_target_pairs={{0,128},{64,192},{128,0},{192,64},{1,129},{65,193},{129,1},{193,65... | collective-permute-start | bytes 1572872 | tf_op jit(solution)/shard_map/ppermute | solution.py:36
  74.4 23.3 %collective-permute-start.15 = (bf16[4,4,64,256]{3,2,1,0:T(8,128)(2,1)}, bf16[4,4,64,256]{3,2,1,0:T(8,128)(2,1)}, u32[]{:S(2)}, u32[]{:S(2)}) collective-permute-start(bf16[4,4,64,256]{3,2,1,0:T(8,128)(2,1)} %pad_maximum_fusion.1.w0), channel_id=1, source_target_pairs={{0,64},{64,128},{128,192},{192,0},{1,65},{65,129},{129,193},{193,1... | collective-permute-start | bytes 1572872 | tf_op jit(solution)/shard_map/ppermute | solution.py:36
  97.7 34.1 %all-to-all-start.1 = ((bf16[32,4,64,128]{3,2,1,0:T(8,128)(2,1)}), bf16[32,4,64,128]{3,2,1,0:T(8,128)(2,1)}, u32[]{:S(2)}, u32[]{:S(2)}) async-start(bf16[32,4,64,128]{3,2,1,0:T(8,128)(2,1)} %bitcast.70), calls=%async_computation.1 | async-start | bytes 4194304 | tf_op jit(solution)/shard_map/all_to_all | solution.py:31
  131.8 35.6 %all-to-all-start.2 = ((bf16[64,4,32,128]{3,2,1,0:T(8,128)(2,1)}), bf16[64,4,32,128]{3,2,1,0:T(8,128)(2,1)}, u32[]{:S(2)}, u32[]{:S(2)}) async-start(bf16[64,4,32,128]{3,2,1,0:T(8,128)(2,1)} %bitcast.69), calls=%async_computation.2 | async-start | bytes 4194304 | tf_op jit(solution)/shard_map/all_to_all | solution.py:31
  142.7 44.0 %collective-permute-start.16 = (bf16[512,1024]{1,0:T(8,128)(2,1)}, bf16[512,1024]{1,0:T(8,128)(2,1)}, u32[]{:S(2)}, u32[]{:S(2)}) collective-permute-start(bf16[512,1024]{1,0:T(8,128)(2,1)} %convolution_convert_fusion), channel_id=1, source_target_pairs={{0,1},{1,0},{2,3},{3,2},{4,5},{5,4},{6,7},{7,6},{8,9},{9,8},{10,11... | collective-permute-start | bytes 3145736 | tf_op jit(solution)/shard_map/ppermute | solution.py:27
  144.7 42.0 %copy-start.10 = (bf16[512,1024]{1,0:T(8,128)(2,1)S(1)}, bf16[512,1024]{1,0:T(8,128)(2,1)}, u32[]{:S(2)}) copy-start(bf16[512,1024]{1,0:T(8,128)(2,1)} %param.12) | copy-start | bytes 3145732
  144.7 28.5 %collective-permute-start.17 = (bf16[64,128]{1,0:T(8,128)(2,1)S(1)}, bf16[64,128]{1,0:T(8,128)(2,1)S(1)}, u32[]{:S(2)}, u32[]{:S(2)}) collective-permute-start(bf16[64,128]{1,0:T(8,128)(2,1)S(1)} %get-tuple-element.55), channel_id=1, source_target_pairs={{0,8},{8,16},{16,24},{24,0},{1,9},{9,17},{17,25},{25,1},{2,10},{10... | collective-permute-start | bytes 49160 | tf_op jit(solution)/shard_map/ppermute | solution.py:36
  148.4 27.7 %collective-permute-start.18 = (bf16[64,128]{1,0:T(8,128)(2,1)S(1)}, bf16[64,128]{1,0:T(8,128)(2,1)S(1)}, u32[]{:S(2)}, u32[]{:S(2)}) collective-permute-start(bf16[64,128]{1,0:T(8,128)(2,1)S(1)} %get-tuple-element.57), channel_id=1, source_target_pairs={{0,16},{8,24},{16,0},{24,8},{1,17},{9,25},{17,1},{25,9},{2,18},{10... | collective-permute-start | bytes 49160 | tf_op jit(solution)/shard_map/ppermute | solution.py:36
  151.4 24.7 %collective-permute-start.19 = (bf16[64,128]{1,0:T(8,128)(2,1)S(1)}, bf16[64,128]{1,0:T(8,128)(2,1)S(1)}, u32[]{:S(2)}, u32[]{:S(2)}) collective-permute-start(bf16[64,128]{1,0:T(8,128)(2,1)S(1)} %get-tuple-element.56), channel_id=1, source_target_pairs={{0,24},{8,0},{16,8},{24,16},{1,25},{9,1},{17,9},{25,17},{2,26},{10... | collective-permute-start | bytes 49160 | tf_op jit(solution)/shard_map/ppermute | solution.py:36
  169.4 6.7 %collective-permute-start.20 = (bf16[64,128]{1,0:T(8,128)(2,1)S(1)}, bf16[64,128]{1,0:T(8,128)(2,1)S(1)}, u32[]{:S(2)}, u32[]{:S(2)}) collective-permute-start(bf16[64,128]{1,0:T(8,128)(2,1)S(1)} %get-tuple-element.58), channel_id=1, source_target_pairs={{0,8},{8,16},{16,24},{24,0},{1,9},{9,17},{17,25},{25,1},{2,10},{10... | collective-permute-start | bytes 49160 | tf_op jit(solution)/shard_map/ppermute | solution.py:36
  173.3 7.7 %collective-permute-start.21 = (bf16[64,128]{1,0:T(8,128)(2,1)S(1)}, bf16[64,128]{1,0:T(8,128)(2,1)S(1)}, u32[]{:S(2)}, u32[]{:S(2)}) collective-permute-start(bf16[64,128]{1,0:T(8,128)(2,1)S(1)} %get-tuple-element.60), channel_id=1, source_target_pairs={{0,16},{8,24},{16,0},{24,8},{1,17},{9,25},{17,1},{25,9},{2,18},{10... | collective-permute-start | bytes 49160 | tf_op jit(solution)/shard_map/ppermute | solution.py:36
  176.1 5.8 %collective-permute-start.22 = (bf16[64,128]{1,0:T(8,128)(2,1)S(1)}, bf16[64,128]{1,0:T(8,128)(2,1)S(1)}, u32[]{:S(2)}, u32[]{:S(2)}) collective-permute-start(bf16[64,128]{1,0:T(8,128)(2,1)S(1)} %get-tuple-element.59), channel_id=1, source_target_pairs={{0,24},{8,0},{16,8},{24,16},{1,25},{9,1},{17,9},{25,17},{2,26},{10... | collective-permute-start | bytes 49160 | tf_op jit(solution)/shard_map/ppermute | solution.py:36
  182.7 11.2 %all-to-all-start.3 = ((bf16[8,2,64,128]{3,2,1,0:T(8,128)(2,1)}), bf16[8,2,64,128]{3,2,1,0:T(8,128)(2,1)S(1)}, u32[]{:S(2)}, u32[]{:S(2)}) async-start(bf16[8,2,64,128]{3,2,1,0:T(8,128)(2,1)} %broadcast_in_dim.2), calls=%async_computation.3 | async-start | bytes 524288 | tf_op jit(solution)/shard_map/all_to_all | solution.py:31
  (13 other events, 19.8 us)

commit v7 on v6

--- a/solution.py
+++ b/solution.py
@@ -93,10 +93,10 @@
     rows = down_rows // N_C
     return pl.pallas_call(
         spread_kernel,
-        grid=(N_GRP,),
+        grid=(2,),
         in_specs=[whole(part) for part in parts],
         out_specs=[
-            pl.BlockSpec((N_X, N_C, N_ZH, rows, 128), lambda i: (i, 0, 0, 0, 0)),
+            pl.BlockSpec((N_GRP * N_X // 2, N_C, N_ZH, rows, 128), lambda i: (i, 0, 0, 0, 0)),
             pl.BlockSpec((N_ZH, down_rows, 256), lambda i: (0, 0, 0)),
         ],
         out_shape=(
@@ -137,10 +137,10 @@
         at += part.shape[0]
 
 
-def forward_kernel(zh_ref, own_ref, partner_ref, c0, c1, c2, c3, w_ref, hidden_ref, pre_ref, cdf_ref, term_ref, w, cot):
+def forward_kernel(zh_ref, own_ref, partner_ref, c0, c1, w_ref, hidden_ref, pre_ref, cdf_ref, term_ref, w, cot):
     @pl.when(pl.program_id(0) == 0)
     def _():
-        join_cot((c0, c1, c2, c3), cot)
+        join_cot((c0, c1), cot)
 
     for j in range(N_ZH):
         at = pl.multiple_of(((zh_ref[0] + j) % N_ZH) * 256, 256)
@@ -199,10 +199,10 @@
     )(zh.reshape(1), own, partner, *cots, got_up)
 
 
-def backward_kernel(at_ref, own_ref, partner_ref, c0, c1, c2, c3, w0, w1, w2, w3, pre_ref, cdf_ref, term_ref, w, pre_grad, cot):
+def backward_kernel(at_ref, own_ref, partner_ref, c0, c1, w0, w1, w2, w3, pre_ref, cdf_ref, term_ref, w, pre_grad, cot):
     @pl.when(pl.program_id(0) == 0)
     def _():
-        join_cot((c0, c1, c2, c3), cot)
+        join_cot((c0, c1), cot)
 
     rows, width = own_ref.shape
     step = rows // 2
@@ -259,7 +259,7 @@
         ),
         compiler_params=pltpu.CompilerParams(vmem_limit_bytes=VMEM_BYTES),
         cost_estimate=pl.CostEstimate(
-            flops=8 * rows * width * half, bytes_accessed=20 * 1024 * 1024, transcendentals=0
+            flops=400 * rows * width * half, bytes_accessed=20 * 1024 * 1024, transcendentals=0
         ),
         name="backward",
     )(at, own, partner, *cots, *downs, pre, cdf_value)
@@ -285,6 +285,8 @@
     kept = lax.dynamic_index_in_dim(blocks, zl, 1, keepdims=False)
     sent = lax.dynamic_index_in_dim(blocks, 1 - zl, 1, keepdims=False)
     pair = jnp.stack([kept, lax.ppermute(sent, "zl", [(0, 1), (1, 0)])], axis=1)
+    parts = along(cut(w_up, w_down, group, y), "zh")
+    pair, *parts = lax.optimization_barrier((pair, *parts))
     order, old_cot = [], []
     for dy in range(n_y):
         block = lax.dynamic_index_in_dim(pair, (y + dy) % n_y, 0, keepdims=False)
@@ -294,10 +296,9 @@
         order += [(y - dy) % n_y * n_zl + zl, (y - dy) % n_y * n_zl + 1 - zl]
     order = jnp.stack(order)
 
-    parts = along(cut(w_up, w_down, group, y), "zh")
-    both = lax.optimization_barrier((*parts, *old_cot))
-    parts, old_cot = both[: len(parts)], jnp.concatenate(both[len(parts) :], axis=0)
     spread_up, down_zh = spread(parts)
+    spread_up, *old_cot = lax.optimization_barrier((spread_up, *old_cot))
+    cot = jnp.concatenate([grad_new, *old_cot], axis=0)
     spread_up = spread_up.reshape(N_GRP * N_X * N_C, N_ZH, up_rows, 128)
     got_up = exchange(spread_up, ("y", "zl", "x", "c")).reshape(N_GRP, N_X, N_C, N_ZH, up_rows, 128)
     downs = along(jnp.stack(along(down_zh, "x")), "y")
@@ -308,11 +309,10 @@
 
     normed = normalize(jnp.concatenate([new_rows, picked], axis=0), ln_gain)
     partner = swap(normed)
-    cots = (grad_new, old_cot, swap(grad_new), swap(old_cot))
+    cots = (cot, swap(cot))
     rows = normed.shape[0]
 
     hidden, pre, cdf_value, term_down = forward(zh, normed, partner, cots, got_up)
-    term_down, *downs = lax.optimization_barrier((term_down, *downs))
     part_down = exchange(term_down.reshape(N_GRP * N_X, N_ZH, 64, 128), ("y", "zl", "x"))
     part_down = jnp.sum(part_down.astype(jnp.float32), axis=0).astype(jnp.bfloat16)
     sum_down = sum_zh(part_down, zh)

time: 198 us -> 194 us (0.980)
  starting transfers between devices: 61.2 us -> 65.1 us
  local copies, waits for them, and re-layouts: 12.8 us -> 9.59 us
  waiting for transfers between devices: 74.9 us -> 72.4 us
    all_to_all x4, waiting for transfers between devices: 33.7 us -> 18.2 us  [exchange(): return lax.all_to_all(value, axes, split_axis=0, concat_axis=0, tiled=True)]
    ppermute x15, waiting for transfers between devices: 40.4 us -> 53.7 us  [shift(): return lax.ppermute(value, axis, [(i, (i + step) % n) for i in range(n)])]
    unnamed x39 -> x38, local copies, waits for them, and re-layouts: 7.73 us -> 4.68 us
    ppermute x15, starting transfers between devices: 30.3 us -> 32.3 us  [shift(): return lax.ppermute(value, axis, [(i, (i + step) % n) for i in range(n)])]
  transfers between devices with their start and end apart: 27 -> 26, of which waited for: 12 -> 11; matrix products, arithmetic and copies ran while one was open for 10% -> 11% of each run, Pallas kernels for 13% -> 15%
where the time goes in v7:
time: 194 us; the launch traced here: 193 us
  waiting for transfers between devices  72.4 us (37%)
  starting transfers between devices  65.1 us (34%)
  Pallas kernels  29.8 us (15%)
  local copies, waits for them, and re-layouts  9.59 us (5%)
  matrix products  8.61 us (4%)
  other arithmetic  6.82 us (4%)
    ppermute x15, waiting for transfers between devices, shift(): return lax.ppermute(value, axis, [(i, (i + step) % n) for i in range(n)])  53.7 us
    ppermute x15, starting transfers between devices, shift(): return lax.ppermute(value, axis, [(i, (i + step) % n) for i in range(n)])  32.3 us
    all_to_all x4, starting transfers between devices, exchange(): return lax.all_to_all(value, axes, split_axis=0, concat_axis=0, tiled=True)  24.3 us
    all_to_all x4, waiting for transfers between devices, exchange(): return lax.all_to_all(value, axes, split_axis=0, concat_axis=0, tiled=True)  18.2 us
    pallas_call x1, Pallas kernels, backward(): pl.pallas_call(backward_kernel, grid_spec=pltpu.PrefetchScalarGridSpec(nu...  12.7 us
    pallas_call x1, Pallas kernels, forward(): pl.pallas_call(forward_kernel, grid_spec=pltpu.PrefetchScalarGridSpec(num...  10.8 us
    ppermute x3, starting transfers between devices, body(): block = lax.ppermute(block, 'y', [(i, (i + dy) % n_y) for i in range(n_y)])  5.9 us
    unnamed x38, local copies, waits for them, and re-layouts  4.68 us
  transfers between devices with their start and end apart: 26, of which 11 were waited for; matrix products, arithmetic and copies ran while one was open for 11% of the time, Pallas kernels for 15%

profile of v7, /device:TPU:64, one launch (start us, length us, event | category | flops | bytes accessed | tf_op | source)
XLA Modules:
  0.0 193.3 jit_solution(10086023264232982216)
XLA Ops:
  1.8 2.0 %collective-permute-start.1 = (bf16[4,16,1024]{2,1,0:T(8,128)(2,1)S(1)}, bf16[4,16,1024]{2,1,0:T(8,128)(2,1)S(1)}, u32[]{:S(2)}, u32[]{:S(2)}) collective-permute-start(bf16[4,16,1024]{2,1,0:T(8,128)(2,1)S(1)} %get-tuple-element.48), channel_id=1, source_target_pairs={{0,32},{32,0},{1,33},{33,1},{2,34},{34,2},{3,35},{35,3},{4,36},{36... | collective-permute-start | bytes 393224 | tf_op jit(solution)/shard_map/ppermute | solution.py:287
  4.4 2.1 %cut.1.p0 = bf16[64,384]{1,0:T(8,128)(2,1)} custom-call(s32[2]{0:T(128)} %pad_add_fusion.at_ref, bf16[32,2048]{1,0:T(8,128)(2,1)} %up_ref.1, bf16[64,1024]{1,0:T(8,128)(2,1)} %down_ref.1), custom_call_target="tpu_custom_call" | custom-call | tf_op jit(solution)/shard_map/cut/pallas_call | solution.py:65
  6.5 5.9 %collective-permute-start.3 = (bf16[64,384]{1,0:T(8,128)(2,1)}, bf16[64,384]{1,0:T(8,128)(2,1)S(1)}, u32[]{:S(2)}, u32[]{:S(2)}) collective-permute-start(bf16[64,384]{1,0:T(8,128)(2,1)} %cut.1.p0), channel_id=1, source_target_pairs={{0,16},{8,24},{16,0},{24,8},{1,17},{9,25},{17,1},{25,9},{2,18},{10... | collective-permute-start | bytes 147464 | tf_op jit(solution)/shard_map/ppermute | solution.py:36
  12.5 2.7 %collective-permute-start.4 = (bf16[64,384]{1,0:T(8,128)(2,1)}, bf16[64,384]{1,0:T(8,128)(2,1)S(1)}, u32[]{:S(2)}, u32[]{:S(2)}) collective-permute-start(bf16[64,384]{1,0:T(8,128)(2,1)} %cut.1.p0), channel_id=1, source_target_pairs={{0,8},{8,16},{16,24},{24,0},{1,9},{9,17},{17,25},{25,1},{2,10},{10... | collective-permute-start | bytes 147464 | tf_op jit(solution)/shard_map/ppermute | solution.py:36
  15.7 2.1 %collective-permute-done.4.p3 = bf16[64,384]{1,0:T(8,128)(2,1)S(1)} collective-permute-done((bf16[64,384]{1,0:T(8,128)(2,1)}, bf16[64,384]{1,0:T(8,128)(2,1)S(1)}, u32[]{:S(2)}, u32[]{:S(2)}) %collective-permute-start.4) | collective-permute-done | bytes 49184 | tf_op jit(solution)/shard_map/ppermute | solution.py:36
  17.8 1.7 collective-permute-start.5
  19.4 2.9 %collective-permute-start.6 = (bf16[2,16,1024]{2,1,0:T(8,128)(2,1)S(1)}, bf16[2,16,1024]{2,1,0:T(8,128)(2,1)S(1)}, u32[]{:S(2)}, u32[]{:S(2)}) collective-permute-start(bf16[2,16,1024]{2,1,0:T(8,128)(2,1)S(1)} %get-tuple-element.44), channel_id=1, source_target_pairs={{0,128},{64,192},{128,0},{192,64},{1,129},{65,193},{129,1},{193,65... | collective-permute-start | bytes 196616 | tf_op jit(solution)/shard_map/ppermute | solution.py:294
  23.7 2.5 %spread.1 = (bf16[32,2,4,32,128]{4,3,2,1,0:T(8,128)(2,1)}, bf16[4,64,256]{2,1,0:T(8,128)(2,1)}) custom-call(bf16[64,384]{1,0:T(8,128)(2,1)} %cut.1.p0, bf16[64,384]{1,0:T(8,128)(2,1)} %copy-done.13, bf16[64,384]{1,0:T(8,128)(2,1)} %copy-done.14, bf16[64,384]{1,0:T(8,128)(2,1)} %copy-done.15), custom_call_target="tpu_custom_call" | custom-call | tf_op jit(solution)/shard_map/spread/pallas_call | solution.py:94
  27.2 8.1 %all-to-all-start = ((bf16[64,4,32,128]{3,2,1,0:T(8,128)(2,1)}), bf16[64,4,32,128]{3,2,1,0:T(8,128)(2,1)}, u32[]{:S(2)}, u32[]{:S(2)}) async-start(bf16[64,4,32,128]{3,2,1,0:T(8,128)(2,1)} %bitcast.68), calls=%async_computation | async-start | bytes 4194304 | tf_op jit(solution)/shard_map/all_to_all | solution.py:31
  43.8 2.7 %collective-permute-start.9 = (bf16[4,64,256]{2,1,0:T(8,128)(2,1)S(1)}, bf16[4,64,256]{2,1,0:T(8,128)(2,1)S(1)}, u32[]{:S(2)}, u32[]{:S(2)}) collective-permute-start(bf16[4,64,256]{2,1,0:T(8,128)(2,1)S(1)} %copy-done.8), channel_id=1, source_target_pairs={{0,6},{2,0},{4,2},{6,4},{1,7},{3,1},{5,3},{7,5},{8,14},{10,8},{12,... | collective-permute-start | bytes 393224 | tf_op jit(solution)/shard_map/ppermute | solution.py:36
  48.2 15.0 %collective-permute-done.9 = bf16[4,64,256]{2,1,0:T(8,128)(2,1)S(1)} collective-permute-done((bf16[4,64,256]{2,1,0:T(8,128)(2,1)S(1)}, bf16[4,64,256]{2,1,0:T(8,128)(2,1)S(1)}, u32[]{:S(2)}, u32[]{:S(2)}) %collective-permute-start.9) | collective-permute-done | bytes 131104 | tf_op jit(solution)/shard_map/ppermute | solution.py:36
  64.7 2.0 %collective-permute-done.11 = bf16[4,64,256]{2,1,0:T(8,128)(2,1)S(1)} collective-permute-done((bf16[4,64,256]{2,1,0:T(8,128)(2,1)S(1)}, bf16[4,64,256]{2,1,0:T(8,128)(2,1)S(1)}, u32[]{:S(2)}, u32[]{:S(2)}) %collective-permute-start.11) | collective-permute-done | bytes 131104 | tf_op jit(solution)/shard_map/ppermute | solution.py:36
  67.6 2.9 %collective-permute-start.12 = (bf16[4,4,64,256]{3,2,1,0:T(8,128)(2,1)}, bf16[4,4,64,256]{3,2,1,0:T(8,128)(2,1)}, u32[]{:S(2)}, u32[]{:S(2)}) collective-permute-start(bf16[4,4,64,256]{3,2,1,0:T(8,128)(2,1)} %pad_maximum_fusion.1.w0), channel_id=1, source_target_pairs={{0,192},{64,0},{128,64},{192,128},{1,193},{65,1},{129,65},{193,129... | collective-permute-start | bytes 1572872 | tf_op jit(solution)/shard_map/ppermute | solution.py:36
  72.3 10.8 %forward.1 = (bf16[1280,1024]{1,0:T(8,128)(2,1)}, f32[1280,1024]{1,0:T(8,128)}, bf16[1280,1024]{1,0:T(8,128)(2,1)}, bf16[8,4,4,64,128]{4,3,2,1,0:T(8,128)(2,1)}) custom-call(s32[1]{0:T(128)} %bitcast.zh_ref, bf16[640,1024]{1,0:T(8,128)(2,1)S(1)} %fusion.4.own_ref, bf16[640,1024]{1,0:T(8,128)(2,1)} %collective-permute-done.partner_ref, ...), custom_call_target="tpu_custom_call" | custom-call | bytes 1024 | tf_op jit(solution)/shard_map/forward/pallas_call | solution.py:169
  83.0 6.1 %all-to-all-start.1 = ((bf16[32,4,64,128]{3,2,1,0:T(8,128)(2,1)}), bf16[32,4,64,128]{3,2,1,0:T(8,128)(2,1)}, u32[]{:S(2)}, u32[]{:S(2)}) async-start(bf16[32,4,64,128]{3,2,1,0:T(8,128)(2,1)} %bitcast.70), calls=%async_computation.1 | async-start | bytes 4194304 | tf_op jit(solution)/shard_map/all_to_all | solution.py:31
  89.1 25.8 %collective-permute-done.12.w1 = bf16[4,4,64,256]{3,2,1,0:T(8,128)(2,1)} collective-permute-done((bf16[4,4,64,256]{3,2,1,0:T(8,128)(2,1)}, bf16[4,4,64,256]{3,2,1,0:T(8,128)(2,1)}, u32[]{:S(2)}, u32[]{:S(2)}) %collective-permute-start.12) | collective-permute-done | bytes 524320 | tf_op jit(solution)/shard_map/ppermute | solution.py:36
  114.9 2.0 %collective-permute-done.14.w3 = bf16[4,4,64,256]{3,2,1,0:T(8,128)(2,1)} collective-permute-done((bf16[4,4,64,256]{3,2,1,0:T(8,128)(2,1)}, bf16[4,4,64,256]{3,2,1,0:T(8,128)(2,1)}, u32[]{:S(2)}, u32[]{:S(2)}) %collective-permute-start.14) | collective-permute-done | bytes 524320 | tf_op jit(solution)/shard_map/ppermute | solution.py:36
  116.9 12.7 %backward.1 = (bf16[8,4,2,4,32,128]{5,4,3,2,1,0:T(8,128)(2,1)}, bf16[1024,1024]{1,0:T(8,128)(2,1)}) custom-call(s32[3]{0:T(128)S(1)} %pad_add_fusion.1.at_ref, bf16[640,1024]{1,0:T(8,128)(2,1)S(1)} %fusion.4.own_ref, bf16[640,1024]{1,0:T(8,128)(2,1)} %collective-permute-done.partner_ref, bf16[640,1024]{1,0:T(8,128)(2,1)} %constant_dynamic-update-slice_fusion.c0, ...), custom_call_target="tpu_custom_call" | custom-call | flops 268435456000 | bytes 20971520 | tf_op jit(solution)/shard_map/backward/pallas_call | solution.py:237
  129.5 6.2 %all-to-all-start.2 = ((bf16[64,4,32,128]{3,2,1,0:T(8,128)(2,1)}), bf16[64,4,32,128]{3,2,1,0:T(8,128)(2,1)}, u32[]{:S(2)}, u32[]{:S(2)}) async-start(bf16[64,4,32,128]{3,2,1,0:T(8,128)(2,1)} %bitcast.69), calls=%async_computation.2 | async-start | bytes 4194304 | tf_op jit(solution)/shard_map/all_to_all | solution.py:31
  135.7 4.1 %convolution_convert_fusion = bf16[512,1024]{1,0:T(8,128)(2,1)} fusion(bf16[1024,1024]{1,0:T(8,128)(2,1)} %get-tuple-element.38, bf16[1280,1024]{1,0:T(8,128)(2,1)} %get-tuple-element.34), kind=kOutput, calls=%fused_computation.11 | convolution fusion | flops 1074266112 | bytes 4194304 | tf_op jit(solution)/shard_map/dot_general | solution.py:327
  139.9 2.0 %reduce_sum.44 = bf16[4,64,128]{2,1,0:T(8,128)(2,1)S(1)} reduce(bf16[32,4,64,128]{3,2,1,0:T(8,128)(2,1)} %all-to-all-done.1, bf16[]{:T(256)} %constant.144.clone.1), dimensions={0}, to_apply=%region_2.3 | reduce | flops 1015808 | bytes 2162690 | tf_op jit(solution)/shard_map/reduce_sum | solution.py:317
  141.9 4.5 %collective-permute-start.16 = (bf16[64,128]{1,0:T(8,128)(2,1)S(1)}, bf16[64,128]{1,0:T(8,128)(2,1)S(1)}, u32[]{:S(2)}, u32[]{:S(2)}) collective-permute-start(bf16[64,128]{1,0:T(8,128)(2,1)S(1)} %get-tuple-element.49), channel_id=1, source_target_pairs={{0,8},{8,16},{16,24},{24,0},{1,9},{9,17},{17,25},{25,1},{2,10},{10... | collective-permute-start | bytes 49160 | tf_op jit(solution)/shard_map/ppermute | solution.py:36
  147.5 1.7 collective-permute-start.18
  149.2 15.4 %all-to-all-done.2 = bf16[64,4,32,128]{3,2,1,0:T(8,128)(2,1)} async-done(((bf16[64,4,32,128]{3,2,1,0:T(8,128)(2,1)}), bf16[64,4,32,128]{3,2,1,0:T(8,128)(2,1)}, u32[]{:S(2)}, u32[]{:S(2)}) %all-to-all-start.2) | async-done | bytes 2097184 | tf_op jit(solution)/shard_map/all_to_all | solution.py:31
  164.6 1.9 reduce_sum.45
  166.6 4.5 %collective-permute-start.19 = (bf16[64,128]{1,0:T(8,128)(2,1)S(1)}, bf16[64,128]{1,0:T(8,128)(2,1)S(1)}, u32[]{:S(2)}, u32[]{:S(2)}) collective-permute-start(bf16[64,128]{1,0:T(8,128)(2,1)S(1)} %get-tuple-element.52), channel_id=1, source_target_pairs={{0,8},{8,16},{16,24},{24,0},{1,9},{9,17},{17,25},{25,1},{2,10},{10... | collective-permute-start | bytes 49160 | tf_op jit(solution)/shard_map/ppermute | solution.py:36
  172.2 1.7 collective-permute-start.21
  174.0 4.8 %collective-permute-done.20 = bf16[64,128]{1,0:T(8,128)(2,1)S(1)} collective-permute-done((bf16[64,128]{1,0:T(8,128)(2,1)S(1)}, bf16[64,128]{1,0:T(8,128)(2,1)S(1)}, u32[]{:S(2)}, u32[]{:S(2)}) %collective-permute-start.20) | collective-permute-done | bytes 16416 | tf_op jit(solution)/shard_map/ppermute | solution.py:36
  179.6 4.0 %all-to-all-start.3 = ((bf16[8,2,64,128]{3,2,1,0:T(8,128)(2,1)}), bf16[8,2,64,128]{3,2,1,0:T(8,128)(2,1)S(1)}, u32[]{:S(2)}, u32[]{:S(2)}) async-start(bf16[8,2,64,128]{3,2,1,0:T(8,128)(2,1)} %broadcast_in_dim.2), calls=%async_computation.3 | async-start | bytes 524288 | tf_op jit(solution)/shard_map/all_to_all | solution.py:31
  183.6 4.5 %add_convert_fusion = bf16[512,1024]{1,0:T(8,128)(2,1)} fusion(bf16[512,1024]{1,0:T(8,128)(2,1)} %collective-permute-done.15, bf16[512,1024]{1,0:T(8,128)(2,1)S(1)} %copy-done.4, bf16[1024,1024]{1,0:T(8,128)(2,1)} %get-tuple-element.38, bf16[1280,1024]{1,0:T(8,128)(2,1)} %get-tuple-element.34), kind=kOutput, calls=%fused_computation.10 | convolution fusion | flops 1076363264 | bytes 6291456 | tf_op jit(solution)/shard_map/dot_general | solution.py:328
  188.0 2.8 %all-to-all-done.3.both_ref = bf16[8,2,64,128]{3,2,1,0:T(8,128)(2,1)S(1)} async-done(((bf16[8,2,64,128]{3,2,1,0:T(8,128)(2,1)}), bf16[8,2,64,128]{3,2,1,0:T(8,128)(2,1)S(1)}, u32[]{:S(2)}, u32[]{:S(2)}) %all-to-all-start.3) | async-done | bytes 262176 | tf_op jit(solution)/shard_map/all_to_all | solution.py:31
  191.5 1.8 finish.1
  (99 shorter events, 22.4 us)
Async XLA Ops:
  0.6 36.4 %copy-start = (bf16[1024,1024]{1,0:T(8,128)(2,1)S(1)}, bf16[1024,1024]{1,0:T(8,128)(2,1)}, u32[]{:S(2)}) copy-start(bf16[1024,1024]{1,0:T(8,128)(2,1)} %param.9) | copy-start | bytes 6291460
  1.8 13.4 %collective-permute-start.1 = (bf16[4,16,1024]{2,1,0:T(8,128)(2,1)S(1)}, bf16[4,16,1024]{2,1,0:T(8,128)(2,1)S(1)}, u32[]{:S(2)}, u32[]{:S(2)}) collective-permute-start(bf16[4,16,1024]{2,1,0:T(8,128)(2,1)S(1)} %get-tuple-element.48), channel_id=1, source_target_pairs={{0,32},{32,0},{1,33},{33,1},{2,34},{34,2},{3,35},{35,3},{4,36},{36... | collective-permute-start | bytes 393224 | tf_op jit(solution)/shard_map/ppermute | solution.py:287
  6.5 8.7 %collective-permute-start.2 = (bf16[64,384]{1,0:T(8,128)(2,1)}, bf16[64,384]{1,0:T(8,128)(2,1)S(1)}, u32[]{:S(2)}, u32[]{:S(2)}) collective-permute-start(bf16[64,384]{1,0:T(8,128)(2,1)} %cut.1.p0), channel_id=1, source_target_pairs={{0,24},{8,0},{16,8},{24,16},{1,25},{9,1},{17,9},{25,17},{2,26},{10... | collective-permute-start | bytes 147464 | tf_op jit(solution)/shard_map/ppermute | solution.py:36
  6.5 9.1 %collective-permute-start.3 = (bf16[64,384]{1,0:T(8,128)(2,1)}, bf16[64,384]{1,0:T(8,128)(2,1)S(1)}, u32[]{:S(2)}, u32[]{:S(2)}) collective-permute-start(bf16[64,384]{1,0:T(8,128)(2,1)} %cut.1.p0), channel_id=1, source_target_pairs={{0,16},{8,24},{16,0},{24,8},{1,17},{9,25},{17,1},{25,9},{2,18},{10... | collective-permute-start | bytes 147464 | tf_op jit(solution)/shard_map/ppermute | solution.py:36
  12.5 5.3 %collective-permute-start.4 = (bf16[64,384]{1,0:T(8,128)(2,1)}, bf16[64,384]{1,0:T(8,128)(2,1)S(1)}, u32[]{:S(2)}, u32[]{:S(2)}) collective-permute-start(bf16[64,384]{1,0:T(8,128)(2,1)} %cut.1.p0), channel_id=1, source_target_pairs={{0,8},{8,16},{16,24},{24,0},{1,9},{9,17},{17,25},{25,1},{2,10},{10... | collective-permute-start | bytes 147464 | tf_op jit(solution)/shard_map/ppermute | solution.py:36
  15.2 8.5 %copy-start.13 = (bf16[64,384]{1,0:T(8,128)(2,1)}, bf16[64,384]{1,0:T(8,128)(2,1)S(1)}, u32[]{:S(2)}) copy-start(bf16[64,384]{1,0:T(8,128)(2,1)S(1)} %collective-permute-done.2.p1) | copy-start | bytes 147460
  17.8 8.4 %collective-permute-start.5 = (bf16[2,16,1024]{2,1,0:T(8,128)(2,1)S(1)}, bf16[2,16,1024]{2,1,0:T(8,128)(2,1)S(1)}, u32[]{:S(2)}, u32[]{:S(2)}) collective-permute-start(bf16[2,16,1024]{2,1,0:T(8,128)(2,1)S(1)} %get-tuple-element.45), channel_id=1, source_target_pairs={{0,64},{64,128},{128,192},{192,0},{1,65},{65,129},{129,193},{193,1... | collective-permute-start | bytes 196616 | tf_op jit(solution)/shard_map/ppermute | solution.py:294
  19.4 6.7 %collective-permute-start.6 = (bf16[2,16,1024]{2,1,0:T(8,128)(2,1)S(1)}, bf16[2,16,1024]{2,1,0:T(8,128)(2,1)S(1)}, u32[]{:S(2)}, u32[]{:S(2)}) collective-permute-start(bf16[2,16,1024]{2,1,0:T(8,128)(2,1)S(1)} %get-tuple-element.44), channel_id=1, source_target_pairs={{0,128},{64,192},{128,0},{192,64},{1,129},{65,193},{129,1},{193,65... | collective-permute-start | bytes 196616 | tf_op jit(solution)/shard_map/ppermute | solution.py:294
  22.3 4.3 %collective-permute-start.7 = (bf16[2,16,1024]{2,1,0:T(8,128)(2,1)S(1)}, bf16[2,16,1024]{2,1,0:T(8,128)(2,1)S(1)}, u32[]{:S(2)}, u32[]{:S(2)}) collective-permute-start(bf16[2,16,1024]{2,1,0:T(8,128)(2,1)S(1)} %get-tuple-element.43), channel_id=1, source_target_pairs={{0,192},{64,0},{128,64},{192,128},{1,193},{65,1},{129,65},{193,129... | collective-permute-start | bytes 196616 | tf_op jit(solution)/shard_map/ppermute | solution.py:294
  26.6 8.9 %copy-start.7 = (s32[1,8,16]{2,1,0:T(8,128)S(1)}, s32[1,8,16]{2,1,0:T(8,128)}, u32[]{:S(2)}) copy-start(s32[1,8,16]{2,1,0:T(8,128)} %param.10) | copy-start | bytes 1540
  26.6 9.6 %copy-start.1 = (s32[1,8]{1,0:T(1,128)S(1)}, s32[1,8]{1,0:T(1,128)}, u32[]{:S(2)}) copy-start(s32[1,8]{1,0:T(1,128)} %param.11) | copy-start | bytes 100
  26.6 10.4 %copy-start.16 = (bf16[1024]{0:T(1024)(128)(2,1)S(1)}, bf16[1024]{0:T(1024)(128)(2,1)}, u32[]{:S(2)}) copy-start(bf16[1024]{0:T(1024)(128)(2,1)} %param.15) | copy-start | bytes 6148
  27.2 45.0 %all-to-all-start = ((bf16[64,4,32,128]{3,2,1,0:T(8,128)(2,1)}), bf16[64,4,32,128]{3,2,1,0:T(8,128)(2,1)}, u32[]{:S(2)}, u32[]{:S(2)}) async-start(bf16[64,4,32,128]{3,2,1,0:T(8,128)(2,1)} %bitcast.68), calls=%async_computation | async-start | bytes 4194304 | tf_op jit(solution)/shard_map/all_to_all | solution.py:31
  39.6 32.7 %collective-permute-start = (bf16[640,1024]{1,0:T(8,128)(2,1)S(1)}, bf16[640,1024]{1,0:T(8,128)(2,1)}, u32[]{:S(2)}, u32[]{:S(2)}) collective-permute-start(bf16[640,1024]{1,0:T(8,128)(2,1)S(1)} %fusion.4.own_ref), channel_id=1, source_target_pairs={{0,1},{1,0},{2,3},{3,2},{4,5},{5,4},{6,7},{7,6},{8,9},{9,8},{10,11... | collective-permute-start | bytes 3932168 | tf_op jit(solution)/shard_map/ppermute | solution.py:27
  43.3 29.0 %collective-permute-start.8 = (bf16[640,1024]{1,0:T(8,128)(2,1)}, bf16[640,1024]{1,0:T(8,128)(2,1)}, u32[]{:S(2)}, u32[]{:S(2)}) collective-permute-start(bf16[640,1024]{1,0:T(8,128)(2,1)} %constant_dynamic-update-slice_fusion.c0), channel_id=1, source_target_pairs={{0,1},{1,0},{2,3},{3,2},{4,5},{5,4},{6,7},{7,6},{8,9},{9,8},{10,11... | collective-permute-start | bytes 3932168 | tf_op jit(solution)/shard_map/ppermute | solution.py:27
  43.8 19.5 %collective-permute-start.9 = (bf16[4,64,256]{2,1,0:T(8,128)(2,1)S(1)}, bf16[4,64,256]{2,1,0:T(8,128)(2,1)S(1)}, u32[]{:S(2)}, u32[]{:S(2)}) collective-permute-start(bf16[4,64,256]{2,1,0:T(8,128)(2,1)S(1)} %copy-done.8), channel_id=1, source_target_pairs={{0,6},{2,0},{4,2},{6,4},{1,7},{3,1},{5,3},{7,5},{8,14},{10,8},{12,... | collective-permute-start | bytes 393224 | tf_op jit(solution)/shard_map/ppermute | solution.py:36
  46.5 18.3 %collective-permute-start.10 = (bf16[4,64,256]{2,1,0:T(8,128)(2,1)S(1)}, bf16[4,64,256]{2,1,0:T(8,128)(2,1)S(1)}, u32[]{:S(2)}, u32[]{:S(2)}) collective-permute-start(bf16[4,64,256]{2,1,0:T(8,128)(2,1)S(1)} %copy-done.8), channel_id=1, source_target_pairs={{0,4},{2,6},{4,0},{6,2},{1,5},{3,7},{5,1},{7,3},{8,12},{10,14},{12... | collective-permute-start | bytes 393224 | tf_op jit(solution)/shard_map/ppermute | solution.py:36
  47.3 19.5 %collective-permute-start.11 = (bf16[4,64,256]{2,1,0:T(8,128)(2,1)S(1)}, bf16[4,64,256]{2,1,0:T(8,128)(2,1)S(1)}, u32[]{:S(2)}, u32[]{:S(2)}) collective-permute-start(bf16[4,64,256]{2,1,0:T(8,128)(2,1)S(1)} %copy-done.8), channel_id=1, source_target_pairs={{0,2},{2,4},{4,6},{6,0},{1,3},{3,5},{5,7},{7,1},{8,10},{10,12},{12... | collective-permute-start | bytes 393224 | tf_op jit(solution)/shard_map/ppermute | solution.py:36
  67.6 47.3 %collective-permute-start.12 = (bf16[4,4,64,256]{3,2,1,0:T(8,128)(2,1)}, bf16[4,4,64,256]{3,2,1,0:T(8,128)(2,1)}, u32[]{:S(2)}, u32[]{:S(2)}) collective-permute-start(bf16[4,4,64,256]{3,2,1,0:T(8,128)(2,1)} %pad_maximum_fusion.1.w0), channel_id=1, source_target_pairs={{0,192},{64,0},{128,64},{192,128},{1,193},{65,1},{129,65},{193,129... | collective-permute-start | bytes 1572872 | tf_op jit(solution)/shard_map/ppermute | solution.py:36
  70.6 44.3 %collective-permute-start.13 = (bf16[4,4,64,256]{3,2,1,0:T(8,128)(2,1)}, bf16[4,4,64,256]{3,2,1,0:T(8,128)(2,1)}, u32[]{:S(2)}, u32[]{:S(2)}) collective-permute-start(bf16[4,4,64,256]{3,2,1,0:T(8,128)(2,1)} %pad_maximum_fusion.1.w0), channel_id=1, source_target_pairs={{0,128},{64,192},{128,0},{192,64},{1,129},{65,193},{129,1},{193,65... | collective-permute-start | bytes 1572872 | tf_op jit(solution)/shard_map/ppermute | solution.py:36
  71.2 45.7 %collective-permute-start.14 = (bf16[4,4,64,256]{3,2,1,0:T(8,128)(2,1)}, bf16[4,4,64,256]{3,2,1,0:T(8,128)(2,1)}, u32[]{:S(2)}, u32[]{:S(2)}) collective-permute-start(bf16[4,4,64,256]{3,2,1,0:T(8,128)(2,1)} %pad_maximum_fusion.1.w0), channel_id=1, source_target_pairs={{0,64},{64,128},{128,192},{192,0},{1,65},{65,129},{129,193},{193,1... | collective-permute-start | bytes 1572872 | tf_op jit(solution)/shard_map/ppermute | solution.py:36
  83.0 46.5 %all-to-all-start.1 = ((bf16[32,4,64,128]{3,2,1,0:T(8,128)(2,1)}), bf16[32,4,64,128]{3,2,1,0:T(8,128)(2,1)}, u32[]{:S(2)}, u32[]{:S(2)}) async-start(bf16[32,4,64,128]{3,2,1,0:T(8,128)(2,1)} %bitcast.70), calls=%async_computation.1 | async-start | bytes 4194304 | tf_op jit(solution)/shard_map/all_to_all | solution.py:31
  129.5 35.1 %all-to-all-start.2 = ((bf16[64,4,32,128]{3,2,1,0:T(8,128)(2,1)}), bf16[64,4,32,128]{3,2,1,0:T(8,128)(2,1)}, u32[]{:S(2)}, u32[]{:S(2)}) async-start(bf16[64,4,32,128]{3,2,1,0:T(8,128)(2,1)} %bitcast.69), calls=%async_computation.2 | async-start | bytes 4194304 | tf_op jit(solution)/shard_map/all_to_all | solution.py:31
  139.9 43.7 %collective-permute-start.15 = (bf16[512,1024]{1,0:T(8,128)(2,1)}, bf16[512,1024]{1,0:T(8,128)(2,1)}, u32[]{:S(2)}, u32[]{:S(2)}) collective-permute-start(bf16[512,1024]{1,0:T(8,128)(2,1)} %convolution_convert_fusion), channel_id=1, source_target_pairs={{0,1},{1,0},{2,3},{3,2},{4,5},{5,4},{6,7},{7,6},{8,9},{9,8},{10,11... | collective-permute-start | bytes 3145736 | tf_op jit(solution)/shard_map/ppermute | solution.py:27
  141.8 41.7 %copy-start.4 = (bf16[512,1024]{1,0:T(8,128)(2,1)S(1)}, bf16[512,1024]{1,0:T(8,128)(2,1)}, u32[]{:S(2)}) copy-start(bf16[512,1024]{1,0:T(8,128)(2,1)} %param.12) | copy-start | bytes 3145732
  141.9 29.2 %collective-permute-start.16 = (bf16[64,128]{1,0:T(8,128)(2,1)S(1)}, bf16[64,128]{1,0:T(8,128)(2,1)S(1)}, u32[]{:S(2)}, u32[]{:S(2)}) collective-permute-start(bf16[64,128]{1,0:T(8,128)(2,1)S(1)} %get-tuple-element.49), channel_id=1, source_target_pairs={{0,8},{8,16},{16,24},{24,0},{1,9},{9,17},{17,25},{25,1},{2,10},{10... | collective-permute-start | bytes 49160 | tf_op jit(solution)/shard_map/ppermute | solution.py:36
  146.4 25.8 %collective-permute-start.17 = (bf16[64,128]{1,0:T(8,128)(2,1)S(1)}, bf16[64,128]{1,0:T(8,128)(2,1)S(1)}, u32[]{:S(2)}, u32[]{:S(2)}) collective-permute-start(bf16[64,128]{1,0:T(8,128)(2,1)S(1)} %get-tuple-element.51), channel_id=1, source_target_pairs={{0,16},{8,24},{16,0},{24,8},{1,17},{9,25},{17,1},{25,9},{2,18},{10... | collective-permute-start | bytes 49160 | tf_op jit(solution)/shard_map/ppermute | solution.py:36
  147.5 26.4 %collective-permute-start.18 = (bf16[64,128]{1,0:T(8,128)(2,1)S(1)}, bf16[64,128]{1,0:T(8,128)(2,1)S(1)}, u32[]{:S(2)}, u32[]{:S(2)}) collective-permute-start(bf16[64,128]{1,0:T(8,128)(2,1)S(1)} %get-tuple-element.50), channel_id=1, source_target_pairs={{0,24},{8,0},{16,8},{24,16},{1,25},{9,1},{17,9},{25,17},{2,26},{10... | collective-permute-start | bytes 49160 | tf_op jit(solution)/shard_map/ppermute | solution.py:36
  166.6 7.4 %collective-permute-start.19 = (bf16[64,128]{1,0:T(8,128)(2,1)S(1)}, bf16[64,128]{1,0:T(8,128)(2,1)S(1)}, u32[]{:S(2)}, u32[]{:S(2)}) collective-permute-start(bf16[64,128]{1,0:T(8,128)(2,1)S(1)} %get-tuple-element.52), channel_id=1, source_target_pairs={{0,8},{8,16},{16,24},{24,0},{1,9},{9,17},{17,25},{25,1},{2,10},{10... | collective-permute-start | bytes 49160 | tf_op jit(solution)/shard_map/ppermute | solution.py:36
  171.1 7.7 %collective-permute-start.20 = (bf16[64,128]{1,0:T(8,128)(2,1)S(1)}, bf16[64,128]{1,0:T(8,128)(2,1)S(1)}, u32[]{:S(2)}, u32[]{:S(2)}) collective-permute-start(bf16[64,128]{1,0:T(8,128)(2,1)S(1)} %get-tuple-element.54), channel_id=1, source_target_pairs={{0,16},{8,24},{16,0},{24,8},{1,17},{9,25},{17,1},{25,9},{2,18},{10... | collective-permute-start | bytes 49160 | tf_op jit(solution)/shard_map/ppermute | solution.py:36
  172.2 6.6 %collective-permute-start.21 = (bf16[64,128]{1,0:T(8,128)(2,1)S(1)}, bf16[64,128]{1,0:T(8,128)(2,1)S(1)}, u32[]{:S(2)}, u32[]{:S(2)}) collective-permute-start(bf16[64,128]{1,0:T(8,128)(2,1)S(1)} %get-tuple-element.53), channel_id=1, source_target_pairs={{0,24},{8,0},{16,8},{24,16},{1,25},{9,1},{17,9},{25,17},{2,26},{10... | collective-permute-start | bytes 49160 | tf_op jit(solution)/shard_map/ppermute | solution.py:36
  179.6 11.3 %all-to-all-start.3 = ((bf16[8,2,64,128]{3,2,1,0:T(8,128)(2,1)}), bf16[8,2,64,128]{3,2,1,0:T(8,128)(2,1)S(1)}, u32[]{:S(2)}, u32[]{:S(2)}) async-start(bf16[8,2,64,128]{3,2,1,0:T(8,128)(2,1)} %broadcast_in_dim.2), calls=%async_computation.3 | async-start | bytes 524288 | tf_op jit(solution)/shard_map/all_to_all | solution.py:31
  (11 other events, 32.3 us)

commit v8 on v7

--- a/solution.py
+++ b/solution.py
@@ -160,7 +160,7 @@
     term = term.astype(jnp.bfloat16)
     for x in range(N_X):
         for g in range(N_GRP):
-            term_ref[g, x, 0] = term[x * 64 : (x + 1) * 64, g * 128 : (g + 1) * 128]
+            term_ref[g % 2, x, g // 2, 0] = term[x * 64 : (x + 1) * 64, g * 128 : (g + 1) * 128]
 
 
 def forward(zh, own, partner, cots, got_up):
@@ -181,7 +181,7 @@
                 pl.BlockSpec((2 * rows, 256), lambda q, z: (0, q)),
                 pl.BlockSpec((2 * rows, 256), lambda q, z: (0, q)),
                 pl.BlockSpec((2 * rows, 256), lambda q, z: (0, q)),
-                pl.BlockSpec((N_GRP, N_X, 1, 64, 128), lambda q, z: (0, 0, q, 0, 0)),
+                pl.BlockSpec((SIZE["zl"], N_X, SIZE["y"], 1, 64, 128), lambda q, z: (0, 0, 0, q, 0, 0)),
             ],
             scratch_shapes=[pltpu.VMEM((width, 256), jnp.bfloat16), pltpu.VMEM((2 * rows, width), jnp.bfloat16)],
         ),
@@ -189,7 +189,7 @@
             jax.ShapeDtypeStruct((2 * rows, half), jnp.bfloat16),
             jax.ShapeDtypeStruct((2 * rows, half), jnp.float32),
             jax.ShapeDtypeStruct((2 * rows, half), jnp.bfloat16),
-            jax.ShapeDtypeStruct((N_GRP, N_X, N_ZH, 64, 128), jnp.bfloat16),
+            jax.ShapeDtypeStruct((SIZE["zl"], N_X, SIZE["y"], N_ZH, 64, 128), jnp.bfloat16),
         ),
         compiler_params=pltpu.CompilerParams(vmem_limit_bytes=VMEM_BYTES),
         cost_estimate=pl.CostEstimate(
@@ -265,11 +265,12 @@
     )(at, own, partner, *cots, *downs, pre, cdf_value)
 
 
-def sum_zh(part, zh):
-    total = lax.dynamic_index_in_dim(part, zh, 0, keepdims=False).astype(jnp.float32)
-    for step in range(1, N_ZH):
-        block = lax.dynamic_index_in_dim(part, (zh + step) % N_ZH, 0, keepdims=False)
-        total += shift(block, "zh", step).astype(jnp.float32)
+def sum_along(part, axis):
+    n, me = SIZE[axis], lax.axis_index(axis)
+    total = lax.dynamic_index_in_dim(part, me, 0, keepdims=False).astype(jnp.float32)
+    for step in range(1, n):
+        block = lax.dynamic_index_in_dim(part, (me + step) % n, 0, keepdims=False)
+        total += shift(block, axis, step).astype(jnp.float32)
     return total.astype(jnp.bfloat16)
 
 
@@ -313,23 +314,22 @@
     rows = normed.shape[0]
 
     hidden, pre, cdf_value, term_down = forward(zh, normed, partner, cots, got_up)
-    part_down = exchange(term_down.reshape(N_GRP * N_X, N_ZH, 64, 128), ("y", "zl", "x"))
-    part_down = jnp.sum(part_down.astype(jnp.float32), axis=0).astype(jnp.bfloat16)
-    sum_down = sum_zh(part_down, zh)
+    part_down = exchange(term_down.reshape((n_zl * N_X,) + term_down.shape[2:]), ("zl", "x"))
+    part_down = sum_along(jnp.sum(part_down.astype(jnp.float32), axis=0).astype(jnp.bfloat16), "y")
 
     at = jnp.stack([zh, y, lax.axis_index("x")])
     term_up, down_half = backward(at, normed, partner, cots, downs, pre, cdf_value)
     part_up = exchange(term_up.reshape(N_GRP * N_X * N_C, N_ZH, up_rows, 128), ("y", "zl", "x", "c"))
     part_up = part_up.reshape(N_GRP * N_X, N_C, N_ZH, up_rows, 128)
     part_up = jnp.sum(part_up.astype(jnp.float32), axis=0).astype(jnp.bfloat16)
-    sum_up = sum_zh(part_up.transpose(1, 0, 2, 3).reshape(N_ZH, N_C * up_rows, 128), zh)
+    part_up = part_up.transpose(1, 0, 2, 3).reshape(part_down.shape)
 
     other = jnp.dot(hidden[rows : rows + fresh_count], down_half, preferred_element_type=jnp.float32)
     mixed = jnp.dot(hidden[:fresh_count], down_half, preferred_element_type=jnp.float32)
     returned = swap(other.astype(jnp.bfloat16)).astype(jnp.float32)
     block_out = (new_rows.astype(jnp.float32) + (mixed + returned)).astype(jnp.bfloat16)
 
-    both = jnp.stack([sum_down, sum_up])
+    both = sum_along(jnp.stack([part_down, part_up], axis=1), "zh")
     both = exchange(jnp.broadcast_to(both[None], (N_GRP,) + both.shape), GRP)
     grad_down, grad_up = finish(both, width, hid)
     return (block_out, grad_up, grad_down)

time: 194 us -> 182 us (0.938)
  waiting for transfers between devices: 72.4 us -> 58.5 us
    all_to_all x4, waiting for transfers between devices: 18.2 us -> 6.07 us  [exchange(): return lax.all_to_all(value, axes, split_axis=0, concat_axis=0, tiled=True)]
    unnamed x38 -> x40, local copies, waits for them, and re-layouts: 4.68 us -> 5.31 us
  transfers between devices with their start and end apart: 26 -> 26, of which waited for: 11 -> 13; matrix products, arithmetic and copies ran while one was open for 11% -> 13% of each run, Pallas kernels for 15% -> 16%
where the time goes in v8:
time: 182 us; the launch traced here: 181 us
  starting transfers between devices  64 us (35%)
  waiting for transfers between devices  58.5 us (32%)
  Pallas kernels  29.9 us (16%)
  local copies, waits for them, and re-layouts  10.9 us (6%)
  matrix products  8.61 us (5%)
  other arithmetic  7.76 us (4%)
    ppermute x15, waiting for transfers between devices, shift(): return lax.ppermute(value, axis, [(i, (i + step) % n) for i in range(n)])  52.1 us
    ppermute x15, starting transfers between devices, shift(): return lax.ppermute(value, axis, [(i, (i + step) % n) for i in range(n)])  30.8 us
    all_to_all x4, starting transfers between devices, exchange(): return lax.all_to_all(value, axes, split_axis=0, concat_axis=0, tiled=True)  24.7 us
    pallas_call x1, Pallas kernels, backward(): pl.pallas_call(backward_kernel, grid_spec=pltpu.PrefetchScalarGridSpec(nu...  12.7 us
    pallas_call x1, Pallas kernels, forward(): pl.pallas_call(forward_kernel, grid_spec=pltpu.PrefetchScalarGridSpec(num...  10.8 us
    all_to_all x4, waiting for transfers between devices, exchange(): return lax.all_to_all(value, axes, split_axis=0, concat_axis=0, tiled=True)  6.07 us
    ppermute x3, starting transfers between devices, body(): block = lax.ppermute(block, 'y', [(i, (i + dy) % n_y) for i in range(n_y)])  5.9 us
    unnamed x40, local copies, waits for them, and re-layouts  5.31 us
  transfers between devices with their start and end apart: 26, of which 13 were waited for; matrix products, arithmetic and copies ran while one was open for 13% of the time, Pallas kernels for 16%

profile of v8, /device:TPU:64, one launch (start us, length us, event | category | flops | bytes accessed | tf_op | source)
XLA Modules:
  0.0 180.7 jit_solution(13597391444375020929)
XLA Ops:
  1.8 2.0 %collective-permute-start.1 = (bf16[4,16,1024]{2,1,0:T(8,128)(2,1)S(1)}, bf16[4,16,1024]{2,1,0:T(8,128)(2,1)S(1)}, u32[]{:S(2)}, u32[]{:S(2)}) collective-permute-start(bf16[4,16,1024]{2,1,0:T(8,128)(2,1)S(1)} %get-tuple-element.51), channel_id=1, source_target_pairs={{0,32},{32,0},{1,33},{33,1},{2,34},{34,2},{3,35},{35,3},{4,36},{36... | collective-permute-start | bytes 393224 | tf_op jit(solution)/shard_map/ppermute | solution.py:288
  4.4 2.1 %cut.1.p0 = bf16[64,384]{1,0:T(8,128)(2,1)} custom-call(s32[2]{0:T(128)} %pad_add_fusion.at_ref, bf16[32,2048]{1,0:T(8,128)(2,1)} %up_ref.1, bf16[64,1024]{1,0:T(8,128)(2,1)} %down_ref.1), custom_call_target="tpu_custom_call" | custom-call | tf_op jit(solution)/shard_map/cut/pallas_call | solution.py:65
  6.5 5.9 %collective-permute-start.3 = (bf16[64,384]{1,0:T(8,128)(2,1)}, bf16[64,384]{1,0:T(8,128)(2,1)S(1)}, u32[]{:S(2)}, u32[]{:S(2)}) collective-permute-start(bf16[64,384]{1,0:T(8,128)(2,1)} %cut.1.p0), channel_id=1, source_target_pairs={{0,16},{8,24},{16,0},{24,8},{1,17},{9,25},{17,1},{25,9},{2,18},{10... | collective-permute-start | bytes 147464 | tf_op jit(solution)/shard_map/ppermute | solution.py:36
  12.5 2.7 %collective-permute-start.4 = (bf16[64,384]{1,0:T(8,128)(2,1)}, bf16[64,384]{1,0:T(8,128)(2,1)S(1)}, u32[]{:S(2)}, u32[]{:S(2)}) collective-permute-start(bf16[64,384]{1,0:T(8,128)(2,1)} %cut.1.p0), channel_id=1, source_target_pairs={{0,8},{8,16},{16,24},{24,0},{1,9},{9,17},{17,25},{25,1},{2,10},{10... | collective-permute-start | bytes 147464 | tf_op jit(solution)/shard_map/ppermute | solution.py:36
  15.7 2.1 %collective-permute-done.4.p3 = bf16[64,384]{1,0:T(8,128)(2,1)S(1)} collective-permute-done((bf16[64,384]{1,0:T(8,128)(2,1)}, bf16[64,384]{1,0:T(8,128)(2,1)S(1)}, u32[]{:S(2)}, u32[]{:S(2)}) %collective-permute-start.4) | collective-permute-done | bytes 49184 | tf_op jit(solution)/shard_map/ppermute | solution.py:36
  19.4 2.9 %collective-permute-start.6 = (bf16[2,16,1024]{2,1,0:T(8,128)(2,1)S(1)}, bf16[2,16,1024]{2,1,0:T(8,128)(2,1)S(1)}, u32[]{:S(2)}, u32[]{:S(2)}) collective-permute-start(bf16[2,16,1024]{2,1,0:T(8,128)(2,1)S(1)} %get-tuple-element.47), channel_id=1, source_target_pairs={{0,128},{64,192},{128,0},{192,64},{1,129},{65,193},{129,1},{193,65... | collective-permute-start | bytes 196616 | tf_op jit(solution)/shard_map/ppermute | solution.py:295
  23.7 2.5 %spread.1 = (bf16[32,2,4,32,128]{4,3,2,1,0:T(8,128)(2,1)}, bf16[4,64,256]{2,1,0:T(8,128)(2,1)}) custom-call(bf16[64,384]{1,0:T(8,128)(2,1)} %cut.1.p0, bf16[64,384]{1,0:T(8,128)(2,1)} %copy-done.14, bf16[64,384]{1,0:T(8,128)(2,1)} %copy-done.15, bf16[64,384]{1,0:T(8,128)(2,1)} %copy-done.16), custom_call_target="tpu_custom_call" | custom-call | tf_op jit(solution)/shard_map/spread/pallas_call | solution.py:94
  27.2 8.1 %all-to-all-start = ((bf16[64,4,32,128]{3,2,1,0:T(8,128)(2,1)}), bf16[64,4,32,128]{3,2,1,0:T(8,128)(2,1)}, u32[]{:S(2)}, u32[]{:S(2)}) async-start(bf16[64,4,32,128]{3,2,1,0:T(8,128)(2,1)} %bitcast.68), calls=%async_computation | async-start | bytes 4194304 | tf_op jit(solution)/shard_map/all_to_all | solution.py:31
  43.8 2.7 %collective-permute-start.9 = (bf16[4,64,256]{2,1,0:T(8,128)(2,1)S(1)}, bf16[4,64,256]{2,1,0:T(8,128)(2,1)S(1)}, u32[]{:S(2)}, u32[]{:S(2)}) collective-permute-start(bf16[4,64,256]{2,1,0:T(8,128)(2,1)S(1)} %copy-done.8), channel_id=1, source_target_pairs={{0,6},{2,0},{4,2},{6,4},{1,7},{3,1},{5,3},{7,5},{8,14},{10,8},{12,... | collective-permute-start | bytes 393224 | tf_op jit(solution)/shard_map/ppermute | solution.py:36
  48.2 15.0 %collective-permute-done.9 = bf16[4,64,256]{2,1,0:T(8,128)(2,1)S(1)} collective-permute-done((bf16[4,64,256]{2,1,0:T(8,128)(2,1)S(1)}, bf16[4,64,256]{2,1,0:T(8,128)(2,1)S(1)}, u32[]{:S(2)}, u32[]{:S(2)}) %collective-permute-start.9) | collective-permute-done | bytes 131104 | tf_op jit(solution)/shard_map/ppermute | solution.py:36
  64.7 2.0 %collective-permute-done.11 = bf16[4,64,256]{2,1,0:T(8,128)(2,1)S(1)} collective-permute-done((bf16[4,64,256]{2,1,0:T(8,128)(2,1)S(1)}, bf16[4,64,256]{2,1,0:T(8,128)(2,1)S(1)}, u32[]{:S(2)}, u32[]{:S(2)}) %collective-permute-start.11) | collective-permute-done | bytes 131104 | tf_op jit(solution)/shard_map/ppermute | solution.py:36
  67.6 2.9 %collective-permute-start.12 = (bf16[4,4,64,256]{3,2,1,0:T(8,128)(2,1)}, bf16[4,4,64,256]{3,2,1,0:T(8,128)(2,1)}, u32[]{:S(2)}, u32[]{:S(2)}) collective-permute-start(bf16[4,4,64,256]{3,2,1,0:T(8,128)(2,1)} %pad_maximum_fusion.1.w0), channel_id=1, source_target_pairs={{0,192},{64,0},{128,64},{192,128},{1,193},{65,1},{129,65},{193,129... | collective-permute-start | bytes 1572872 | tf_op jit(solution)/shard_map/ppermute | solution.py:36
  72.3 10.8 %forward.1 = (bf16[1280,1024]{1,0:T(8,128)(2,1)}, f32[1280,1024]{1,0:T(8,128)}, bf16[1280,1024]{1,0:T(8,128)(2,1)}, bf16[2,4,4,4,64,128]{5,4,3,2,1,0:T(8,128)(2,1)}) custom-call(s32[1]{0:T(128)} %bitcast.zh_ref, bf16[640,1024]{1,0:T(8,128)(2,1)S(1)} %fusion.4.own_ref, bf16[640,1024]{1,0:T(8,128)(2,1)} %collective-permute-done.partner_ref, ...), custom_call_target="tpu_custom_call" | custom-call | bytes 1024 | tf_op jit(solution)/shard_map/forward/pallas_call | solution.py:169
  83.1 4.4 %all-to-all-start.1 = ((bf16[8,4,4,64,128]{4,3,2,1,0:T(8,128)(2,1)}), bf16[8,4,4,64,128]{4,3,2,1,0:T(8,128)(2,1)}, u32[]{:S(2)}, u32[]{:S(2)}) async-start(bf16[8,4,4,64,128]{4,3,2,1,0:T(8,128)(2,1)} %bitcast.70), calls=%async_computation.1 | async-start | bytes 4194304 | tf_op jit(solution)/shard_map/all_to_all | solution.py:31
  87.5 5.6 %collective-permute-done.12.w1 = bf16[4,4,64,256]{3,2,1,0:T(8,128)(2,1)} collective-permute-done((bf16[4,4,64,256]{3,2,1,0:T(8,128)(2,1)}, bf16[4,4,64,256]{3,2,1,0:T(8,128)(2,1)}, u32[]{:S(2)}, u32[]{:S(2)}) %collective-permute-start.12) | collective-permute-done | bytes 524320 | tf_op jit(solution)/shard_map/ppermute | solution.py:36
  93.1 3.7 %collective-permute-done.14.w3 = bf16[4,4,64,256]{3,2,1,0:T(8,128)(2,1)} collective-permute-done((bf16[4,4,64,256]{3,2,1,0:T(8,128)(2,1)}, bf16[4,4,64,256]{3,2,1,0:T(8,128)(2,1)}, u32[]{:S(2)}, u32[]{:S(2)}) %collective-permute-start.14) | collective-permute-done | bytes 524320 | tf_op jit(solution)/shard_map/ppermute | solution.py:36
  96.8 12.7 %backward.1 = (bf16[8,4,2,4,32,128]{5,4,3,2,1,0:T(8,128)(2,1)}, bf16[1024,1024]{1,0:T(8,128)(2,1)}) custom-call(s32[3]{0:T(128)S(1)} %pad_add_fusion.1.at_ref, bf16[640,1024]{1,0:T(8,128)(2,1)S(1)} %fusion.4.own_ref, bf16[640,1024]{1,0:T(8,128)(2,1)} %collective-permute-done.partner_ref, bf16[640,1024]{1,0:T(8,128)(2,1)} %constant_dynamic-update-slice_fusion.c0, ...), custom_call_target="tpu_custom_call" | custom-call | flops 268435456000 | bytes 20971520 | tf_op jit(solution)/shard_map/backward/pallas_call | solution.py:237
  109.5 3.3 %all-to-all-done.1 = bf16[8,4,4,64,128]{4,3,2,1,0:T(8,128)(2,1)} async-done(((bf16[8,4,4,64,128]{4,3,2,1,0:T(8,128)(2,1)}), bf16[8,4,4,64,128]{4,3,2,1,0:T(8,128)(2,1)}, u32[]{:S(2)}, u32[]{:S(2)}) %all-to-all-start.1) | async-done | bytes 2097184 | tf_op jit(solution)/shard_map/all_to_all | solution.py:31
  112.7 6.6 %all-to-all-start.2 = ((bf16[64,4,32,128]{3,2,1,0:T(8,128)(2,1)}), bf16[64,4,32,128]{3,2,1,0:T(8,128)(2,1)}, u32[]{:S(2)}, u32[]{:S(2)}) async-start(bf16[64,4,32,128]{3,2,1,0:T(8,128)(2,1)} %bitcast.69), calls=%async_computation.2 | async-start | bytes 4194304 | tf_op jit(solution)/shard_map/all_to_all | solution.py:31
  119.3 4.1 %convolution_convert_fusion = bf16[512,1024]{1,0:T(8,128)(2,1)} fusion(bf16[1024,1024]{1,0:T(8,128)(2,1)} %get-tuple-element.38, bf16[1280,1024]{1,0:T(8,128)(2,1)} %get-tuple-element.34), kind=kOutput, calls=%fused_computation.11 | convolution fusion | flops 1074266112 | bytes 4194304 | tf_op jit(solution)/shard_map/dot_general | solution.py:327
  123.5 2.0 %reduce_sum.44 = bf16[4,4,64,128]{3,2,1,0:T(8,128)(2,1)S(1)} reduce(bf16[8,4,4,64,128]{4,3,2,1,0:T(8,128)(2,1)} %all-to-all-done.1, bf16[]{:T(256)} %constant.146.clone.1), dimensions={0}, to_apply=%region_2.3 | reduce | flops 917504 | bytes 2359298 | tf_op jit(solution)/shard_map/reduce_sum | solution.py:318
  127.8 2.9 %collective-permute-start.17 = (bf16[4,64,128]{2,1,0:T(8,128)(2,1)}, bf16[4,64,128]{2,1,0:T(8,128)(2,1)S(1)}, u32[]{:S(2)}, u32[]{:S(2)}) collective-permute-start(bf16[4,64,128]{2,1,0:T(8,128)(2,1)} %get-tuple-element.45), channel_id=1, source_target_pairs={{0,128},{64,192},{128,0},{192,64},{1,129},{65,193},{129,1},{193,65... | collective-permute-start | bytes 196616 | tf_op jit(solution)/shard_map/ppermute | solution.py:36
  132.0 12.7 %collective-permute-done.16 = bf16[4,64,128]{2,1,0:T(8,128)(2,1)S(1)} collective-permute-done((bf16[4,64,128]{2,1,0:T(8,128)(2,1)}, bf16[4,64,128]{2,1,0:T(8,128)(2,1)S(1)}, u32[]{:S(2)}, u32[]{:S(2)}) %collective-permute-start.16) | collective-permute-done | bytes 65568 | tf_op jit(solution)/shard_map/ppermute | solution.py:36
  144.7 3.9 %collective-permute-done.17 = bf16[4,64,128]{2,1,0:T(8,128)(2,1)S(1)} collective-permute-done((bf16[4,64,128]{2,1,0:T(8,128)(2,1)}, bf16[4,64,128]{2,1,0:T(8,128)(2,1)S(1)}, u32[]{:S(2)}, u32[]{:S(2)}) %collective-permute-start.17) | collective-permute-done | bytes 65568 | tf_op jit(solution)/shard_map/ppermute | solution.py:36
  150.2 1.9 %reduce_sum.45 = bf16[2,4,32,128]{3,2,1,0:T(8,128)(2,1)S(1)} reduce(bf16[32,2,4,32,128]{4,3,2,1,0:T(8,128)(2,1)} %bitcast.39, bf16[]{:T(256)} %constant.146.clone.1), dimensions={0}, to_apply=%region_3.4 | reduce | flops 1015808 | bytes 2162690 | tf_op jit(solution)/shard_map/reduce_sum | solution.py:324
  152.2 4.5 %collective-permute-start.19 = (bf16[2,64,128]{2,1,0:T(8,128)(2,1)S(1)}, bf16[2,64,128]{2,1,0:T(8,128)(2,1)S(1)}, u32[]{:S(2)}, u32[]{:S(2)}) collective-permute-start(bf16[2,64,128]{2,1,0:T(8,128)(2,1)S(1)} %get-tuple-element.52), channel_id=1, source_target_pairs={{0,8},{8,16},{16,24},{24,0},{1,9},{9,17},{17,25},{25,1},{2,10},{10... | collective-permute-start | bytes 98312 | tf_op jit(solution)/shard_map/ppermute | solution.py:36
  157.8 1.7 collective-permute-start.21
  159.5 5.0 %collective-permute-done.20 = bf16[2,64,128]{2,1,0:T(8,128)(2,1)S(1)} collective-permute-done((bf16[2,64,128]{2,1,0:T(8,128)(2,1)S(1)}, bf16[2,64,128]{2,1,0:T(8,128)(2,1)S(1)}, u32[]{:S(2)}, u32[]{:S(2)}) %collective-permute-start.20) | collective-permute-done | bytes 32800 | tf_op jit(solution)/shard_map/ppermute | solution.py:36
  165.3 5.6 %all-to-all-start.3 = ((bf16[8,2,64,128]{3,2,1,0:T(8,128)(2,1)}), bf16[8,2,64,128]{3,2,1,0:T(8,128)(2,1)S(1)}, u32[]{:S(2)}, u32[]{:S(2)}) async-start(bf16[8,2,64,128]{3,2,1,0:T(8,128)(2,1)} %broadcast_in_dim.2), calls=%async_computation.3 | async-start | bytes 524288 | tf_op jit(solution)/shard_map/all_to_all | solution.py:31
  170.9 4.5 %add_convert_fusion = bf16[512,1024]{1,0:T(8,128)(2,1)} fusion(bf16[512,1024]{1,0:T(8,128)(2,1)} %collective-permute-done.15, bf16[512,1024]{1,0:T(8,128)(2,1)S(1)} %copy-done.4, bf16[1024,1024]{1,0:T(8,128)(2,1)} %get-tuple-element.38, bf16[1280,1024]{1,0:T(8,128)(2,1)} %get-tuple-element.34), kind=kOutput, calls=%fused_computation.10 | convolution fusion | flops 1076363264 | bytes 6291456 | tf_op jit(solution)/shard_map/dot_general | solution.py:328
  175.4 2.8 %all-to-all-done.3.both_ref = bf16[8,2,64,128]{3,2,1,0:T(8,128)(2,1)S(1)} async-done(((bf16[8,2,64,128]{3,2,1,0:T(8,128)(2,1)}), bf16[8,2,64,128]{3,2,1,0:T(8,128)(2,1)S(1)}, u32[]{:S(2)}, u32[]{:S(2)}) %all-to-all-start.3) | async-done | bytes 262176 | tf_op jit(solution)/shard_map/all_to_all | solution.py:31
  178.9 1.8 finish.1
  (100 shorter events, 28.2 us)
Async XLA Ops:
  0.6 36.4 %copy-start = (bf16[1024,1024]{1,0:T(8,128)(2,1)S(1)}, bf16[1024,1024]{1,0:T(8,128)(2,1)}, u32[]{:S(2)}) copy-start(bf16[1024,1024]{1,0:T(8,128)(2,1)} %param.9) | copy-start | bytes 6291460
  1.8 13.4 %collective-permute-start.1 = (bf16[4,16,1024]{2,1,0:T(8,128)(2,1)S(1)}, bf16[4,16,1024]{2,1,0:T(8,128)(2,1)S(1)}, u32[]{:S(2)}, u32[]{:S(2)}) collective-permute-start(bf16[4,16,1024]{2,1,0:T(8,128)(2,1)S(1)} %get-tuple-element.51), channel_id=1, source_target_pairs={{0,32},{32,0},{1,33},{33,1},{2,34},{34,2},{3,35},{35,3},{4,36},{36... | collective-permute-start | bytes 393224 | tf_op jit(solution)/shard_map/ppermute | solution.py:288
  6.5 8.7 %collective-permute-start.2 = (bf16[64,384]{1,0:T(8,128)(2,1)}, bf16[64,384]{1,0:T(8,128)(2,1)S(1)}, u32[]{:S(2)}, u32[]{:S(2)}) collective-permute-start(bf16[64,384]{1,0:T(8,128)(2,1)} %cut.1.p0), channel_id=1, source_target_pairs={{0,24},{8,0},{16,8},{24,16},{1,25},{9,1},{17,9},{25,17},{2,26},{10... | collective-permute-start | bytes 147464 | tf_op jit(solution)/shard_map/ppermute | solution.py:36
  6.5 9.1 %collective-permute-start.3 = (bf16[64,384]{1,0:T(8,128)(2,1)}, bf16[64,384]{1,0:T(8,128)(2,1)S(1)}, u32[]{:S(2)}, u32[]{:S(2)}) collective-permute-start(bf16[64,384]{1,0:T(8,128)(2,1)} %cut.1.p0), channel_id=1, source_target_pairs={{0,16},{8,24},{16,0},{24,8},{1,17},{9,25},{17,1},{25,9},{2,18},{10... | collective-permute-start | bytes 147464 | tf_op jit(solution)/shard_map/ppermute | solution.py:36
  12.5 5.3 %collective-permute-start.4 = (bf16[64,384]{1,0:T(8,128)(2,1)}, bf16[64,384]{1,0:T(8,128)(2,1)S(1)}, u32[]{:S(2)}, u32[]{:S(2)}) collective-permute-start(bf16[64,384]{1,0:T(8,128)(2,1)} %cut.1.p0), channel_id=1, source_target_pairs={{0,8},{8,16},{16,24},{24,0},{1,9},{9,17},{17,25},{25,1},{2,10},{10... | collective-permute-start | bytes 147464 | tf_op jit(solution)/shard_map/ppermute | solution.py:36
  15.2 8.5 %copy-start.14 = (bf16[64,384]{1,0:T(8,128)(2,1)}, bf16[64,384]{1,0:T(8,128)(2,1)S(1)}, u32[]{:S(2)}) copy-start(bf16[64,384]{1,0:T(8,128)(2,1)S(1)} %collective-permute-done.2.p1) | copy-start | bytes 147460
  17.8 8.4 %collective-permute-start.5 = (bf16[2,16,1024]{2,1,0:T(8,128)(2,1)S(1)}, bf16[2,16,1024]{2,1,0:T(8,128)(2,1)S(1)}, u32[]{:S(2)}, u32[]{:S(2)}) collective-permute-start(bf16[2,16,1024]{2,1,0:T(8,128)(2,1)S(1)} %get-tuple-element.48), channel_id=1, source_target_pairs={{0,64},{64,128},{128,192},{192,0},{1,65},{65,129},{129,193},{193,1... | collective-permute-start | bytes 196616 | tf_op jit(solution)/shard_map/ppermute | solution.py:295
  19.4 6.7 %collective-permute-start.6 = (bf16[2,16,1024]{2,1,0:T(8,128)(2,1)S(1)}, bf16[2,16,1024]{2,1,0:T(8,128)(2,1)S(1)}, u32[]{:S(2)}, u32[]{:S(2)}) collective-permute-start(bf16[2,16,1024]{2,1,0:T(8,128)(2,1)S(1)} %get-tuple-element.47), channel_id=1, source_target_pairs={{0,128},{64,192},{128,0},{192,64},{1,129},{65,193},{129,1},{193,65... | collective-permute-start | bytes 196616 | tf_op jit(solution)/shard_map/ppermute | solution.py:295
  22.3 4.3 %collective-permute-start.7 = (bf16[2,16,1024]{2,1,0:T(8,128)(2,1)S(1)}, bf16[2,16,1024]{2,1,0:T(8,128)(2,1)S(1)}, u32[]{:S(2)}, u32[]{:S(2)}) collective-permute-start(bf16[2,16,1024]{2,1,0:T(8,128)(2,1)S(1)} %get-tuple-element.46), channel_id=1, source_target_pairs={{0,192},{64,0},{128,64},{192,128},{1,193},{65,1},{129,65},{193,129... | collective-permute-start | bytes 196616 | tf_op jit(solution)/shard_map/ppermute | solution.py:295
  26.6 8.9 %copy-start.7 = (s32[1,8,16]{2,1,0:T(8,128)S(1)}, s32[1,8,16]{2,1,0:T(8,128)}, u32[]{:S(2)}) copy-start(s32[1,8,16]{2,1,0:T(8,128)} %param.10) | copy-start | bytes 1540
  26.6 9.6 %copy-start.1 = (s32[1,8]{1,0:T(1,128)S(1)}, s32[1,8]{1,0:T(1,128)}, u32[]{:S(2)}) copy-start(s32[1,8]{1,0:T(1,128)} %param.11) | copy-start | bytes 100
  26.6 10.4 %copy-start.17 = (bf16[1024]{0:T(1024)(128)(2,1)S(1)}, bf16[1024]{0:T(1024)(128)(2,1)}, u32[]{:S(2)}) copy-start(bf16[1024]{0:T(1024)(128)(2,1)} %param.15) | copy-start | bytes 6148
  27.2 45.0 %all-to-all-start = ((bf16[64,4,32,128]{3,2,1,0:T(8,128)(2,1)}), bf16[64,4,32,128]{3,2,1,0:T(8,128)(2,1)}, u32[]{:S(2)}, u32[]{:S(2)}) async-start(bf16[64,4,32,128]{3,2,1,0:T(8,128)(2,1)} %bitcast.68), calls=%async_computation | async-start | bytes 4194304 | tf_op jit(solution)/shard_map/all_to_all | solution.py:31
  39.6 32.7 %collective-permute-start = (bf16[640,1024]{1,0:T(8,128)(2,1)S(1)}, bf16[640,1024]{1,0:T(8,128)(2,1)}, u32[]{:S(2)}, u32[]{:S(2)}) collective-permute-start(bf16[640,1024]{1,0:T(8,128)(2,1)S(1)} %fusion.4.own_ref), channel_id=1, source_target_pairs={{0,1},{1,0},{2,3},{3,2},{4,5},{5,4},{6,7},{7,6},{8,9},{9,8},{10,11... | collective-permute-start | bytes 3932168 | tf_op jit(solution)/shard_map/ppermute | solution.py:27
  43.3 29.0 %collective-permute-start.8 = (bf16[640,1024]{1,0:T(8,128)(2,1)}, bf16[640,1024]{1,0:T(8,128)(2,1)}, u32[]{:S(2)}, u32[]{:S(2)}) collective-permute-start(bf16[640,1024]{1,0:T(8,128)(2,1)} %constant_dynamic-update-slice_fusion.c0), channel_id=1, source_target_pairs={{0,1},{1,0},{2,3},{3,2},{4,5},{5,4},{6,7},{7,6},{8,9},{9,8},{10,11... | collective-permute-start | bytes 3932168 | tf_op jit(solution)/shard_map/ppermute | solution.py:27
  43.8 19.4 %collective-permute-start.9 = (bf16[4,64,256]{2,1,0:T(8,128)(2,1)S(1)}, bf16[4,64,256]{2,1,0:T(8,128)(2,1)S(1)}, u32[]{:S(2)}, u32[]{:S(2)}) collective-permute-start(bf16[4,64,256]{2,1,0:T(8,128)(2,1)S(1)} %copy-done.8), channel_id=1, source_target_pairs={{0,6},{2,0},{4,2},{6,4},{1,7},{3,1},{5,3},{7,5},{8,14},{10,8},{12,... | collective-permute-start | bytes 393224 | tf_op jit(solution)/shard_map/ppermute | solution.py:36
  46.5 18.2 %collective-permute-start.10 = (bf16[4,64,256]{2,1,0:T(8,128)(2,1)S(1)}, bf16[4,64,256]{2,1,0:T(8,128)(2,1)S(1)}, u32[]{:S(2)}, u32[]{:S(2)}) collective-permute-start(bf16[4,64,256]{2,1,0:T(8,128)(2,1)S(1)} %copy-done.8), channel_id=1, source_target_pairs={{0,4},{2,6},{4,0},{6,2},{1,5},{3,7},{5,1},{7,3},{8,12},{10,14},{12... | collective-permute-start | bytes 393224 | tf_op jit(solution)/shard_map/ppermute | solution.py:36
  47.3 19.4 %collective-permute-start.11 = (bf16[4,64,256]{2,1,0:T(8,128)(2,1)S(1)}, bf16[4,64,256]{2,1,0:T(8,128)(2,1)S(1)}, u32[]{:S(2)}, u32[]{:S(2)}) collective-permute-start(bf16[4,64,256]{2,1,0:T(8,128)(2,1)S(1)} %copy-done.8), channel_id=1, source_target_pairs={{0,2},{2,4},{4,6},{6,0},{1,3},{3,5},{5,7},{7,1},{8,10},{10,12},{12... | collective-permute-start | bytes 393224 | tf_op jit(solution)/shard_map/ppermute | solution.py:36
  67.6 25.5 %collective-permute-start.12 = (bf16[4,4,64,256]{3,2,1,0:T(8,128)(2,1)}, bf16[4,4,64,256]{3,2,1,0:T(8,128)(2,1)}, u32[]{:S(2)}, u32[]{:S(2)}) collective-permute-start(bf16[4,4,64,256]{3,2,1,0:T(8,128)(2,1)} %pad_maximum_fusion.1.w0), channel_id=1, source_target_pairs={{0,192},{64,0},{128,64},{192,128},{1,193},{65,1},{129,65},{193,129... | collective-permute-start | bytes 1572872 | tf_op jit(solution)/shard_map/ppermute | solution.py:36
  70.6 22.5 %collective-permute-start.13 = (bf16[4,4,64,256]{3,2,1,0:T(8,128)(2,1)}, bf16[4,4,64,256]{3,2,1,0:T(8,128)(2,1)}, u32[]{:S(2)}, u32[]{:S(2)}) collective-permute-start(bf16[4,4,64,256]{3,2,1,0:T(8,128)(2,1)} %pad_maximum_fusion.1.w0), channel_id=1, source_target_pairs={{0,128},{64,192},{128,0},{192,64},{1,129},{65,193},{129,1},{193,65... | collective-permute-start | bytes 1572872 | tf_op jit(solution)/shard_map/ppermute | solution.py:36
  71.2 25.6 %collective-permute-start.14 = (bf16[4,4,64,256]{3,2,1,0:T(8,128)(2,1)}, bf16[4,4,64,256]{3,2,1,0:T(8,128)(2,1)}, u32[]{:S(2)}, u32[]{:S(2)}) collective-permute-start(bf16[4,4,64,256]{3,2,1,0:T(8,128)(2,1)} %pad_maximum_fusion.1.w0), channel_id=1, source_target_pairs={{0,64},{64,128},{128,192},{192,0},{1,65},{65,129},{129,193},{193,1... | collective-permute-start | bytes 1572872 | tf_op jit(solution)/shard_map/ppermute | solution.py:36
  83.1 29.6 %all-to-all-start.1 = ((bf16[8,4,4,64,128]{4,3,2,1,0:T(8,128)(2,1)}), bf16[8,4,4,64,128]{4,3,2,1,0:T(8,128)(2,1)}, u32[]{:S(2)}, u32[]{:S(2)}) async-start(bf16[8,4,4,64,128]{4,3,2,1,0:T(8,128)(2,1)} %bitcast.70), calls=%async_computation.1 | async-start | bytes 4194304 | tf_op jit(solution)/shard_map/all_to_all | solution.py:31
  112.7 37.5 %all-to-all-start.2 = ((bf16[64,4,32,128]{3,2,1,0:T(8,128)(2,1)}), bf16[64,4,32,128]{3,2,1,0:T(8,128)(2,1)}, u32[]{:S(2)}, u32[]{:S(2)}) async-start(bf16[64,4,32,128]{3,2,1,0:T(8,128)(2,1)} %bitcast.69), calls=%async_computation.2 | async-start | bytes 4194304 | tf_op jit(solution)/shard_map/all_to_all | solution.py:31
  123.5 47.5 %collective-permute-start.15 = (bf16[512,1024]{1,0:T(8,128)(2,1)}, bf16[512,1024]{1,0:T(8,128)(2,1)}, u32[]{:S(2)}, u32[]{:S(2)}) collective-permute-start(bf16[512,1024]{1,0:T(8,128)(2,1)} %convolution_convert_fusion), channel_id=1, source_target_pairs={{0,1},{1,0},{2,3},{3,2},{4,5},{5,4},{6,7},{7,6},{8,9},{9,8},{10,11... | collective-permute-start | bytes 3145736 | tf_op jit(solution)/shard_map/ppermute | solution.py:27
  126.1 44.8 %copy-start.4 = (bf16[512,1024]{1,0:T(8,128)(2,1)S(1)}, bf16[512,1024]{1,0:T(8,128)(2,1)}, u32[]{:S(2)}) copy-start(bf16[512,1024]{1,0:T(8,128)(2,1)} %param.12) | copy-start | bytes 3145732
  126.1 18.6 %collective-permute-start.16 = (bf16[4,64,128]{2,1,0:T(8,128)(2,1)}, bf16[4,64,128]{2,1,0:T(8,128)(2,1)S(1)}, u32[]{:S(2)}, u32[]{:S(2)}) collective-permute-start(bf16[4,64,128]{2,1,0:T(8,128)(2,1)} %get-tuple-element.43), channel_id=1, source_target_pairs={{0,64},{64,128},{128,192},{192,0},{1,65},{65,129},{129,193},{193,1... | collective-permute-start | bytes 196616 | tf_op jit(solution)/shard_map/ppermute | solution.py:36
  127.8 20.8 %collective-permute-start.17 = (bf16[4,64,128]{2,1,0:T(8,128)(2,1)}, bf16[4,64,128]{2,1,0:T(8,128)(2,1)S(1)}, u32[]{:S(2)}, u32[]{:S(2)}) collective-permute-start(bf16[4,64,128]{2,1,0:T(8,128)(2,1)} %get-tuple-element.45), channel_id=1, source_target_pairs={{0,128},{64,192},{128,0},{192,64},{1,129},{65,193},{129,1},{193,65... | collective-permute-start | bytes 196616 | tf_op jit(solution)/shard_map/ppermute | solution.py:36
  130.7 18.6 %collective-permute-start.18 = (bf16[4,64,128]{2,1,0:T(8,128)(2,1)}, bf16[4,64,128]{2,1,0:T(8,128)(2,1)}, u32[]{:S(2)}, u32[]{:S(2)}) collective-permute-start(bf16[4,64,128]{2,1,0:T(8,128)(2,1)} %get-tuple-element.44), channel_id=1, source_target_pairs={{0,192},{64,0},{128,64},{192,128},{1,193},{65,1},{129,65},{193,129... | collective-permute-start | bytes 196616 | tf_op jit(solution)/shard_map/ppermute | solution.py:36
  152.2 7.3 %collective-permute-start.19 = (bf16[2,64,128]{2,1,0:T(8,128)(2,1)S(1)}, bf16[2,64,128]{2,1,0:T(8,128)(2,1)S(1)}, u32[]{:S(2)}, u32[]{:S(2)}) collective-permute-start(bf16[2,64,128]{2,1,0:T(8,128)(2,1)S(1)} %get-tuple-element.52), channel_id=1, source_target_pairs={{0,8},{8,16},{16,24},{24,0},{1,9},{9,17},{17,25},{25,1},{2,10},{10... | collective-permute-start | bytes 98312 | tf_op jit(solution)/shard_map/ppermute | solution.py:36
  156.7 7.8 %collective-permute-start.20 = (bf16[2,64,128]{2,1,0:T(8,128)(2,1)S(1)}, bf16[2,64,128]{2,1,0:T(8,128)(2,1)S(1)}, u32[]{:S(2)}, u32[]{:S(2)}) collective-permute-start(bf16[2,64,128]{2,1,0:T(8,128)(2,1)S(1)} %get-tuple-element.53), channel_id=1, source_target_pairs={{0,16},{8,24},{16,0},{24,8},{1,17},{9,25},{17,1},{25,9},{2,18},{10... | collective-permute-start | bytes 98312 | tf_op jit(solution)/shard_map/ppermute | solution.py:36
  157.8 6.7 %collective-permute-start.21 = (bf16[2,64,128]{2,1,0:T(8,128)(2,1)S(1)}, bf16[2,64,128]{2,1,0:T(8,128)(2,1)S(1)}, u32[]{:S(2)}, u32[]{:S(2)}) collective-permute-start(bf16[2,64,128]{2,1,0:T(8,128)(2,1)S(1)} %get-tuple-element.54), channel_id=1, source_target_pairs={{0,24},{8,0},{16,8},{24,16},{1,25},{9,1},{17,9},{25,17},{2,26},{10... | collective-permute-start | bytes 98312 | tf_op jit(solution)/shard_map/ppermute | solution.py:36
  165.3 12.9 %all-to-all-start.3 = ((bf16[8,2,64,128]{3,2,1,0:T(8,128)(2,1)}), bf16[8,2,64,128]{3,2,1,0:T(8,128)(2,1)S(1)}, u32[]{:S(2)}, u32[]{:S(2)}) async-start(bf16[8,2,64,128]{3,2,1,0:T(8,128)(2,1)} %broadcast_in_dim.2), calls=%async_computation.3 | async-start | bytes 524288 | tf_op jit(solution)/shard_map/all_to_all | solution.py:31
  (12 other events, 33.0 us)

commit v9 on v8

--- a/solution.py
+++ b/solution.py
@@ -81,7 +81,7 @@
 def spread_kernel(p0, p1, p2, p3, spread_ref, down_ref):
     rows = spread_ref.shape[3]
     for j, part in enumerate((p0, p1, p2, p3)):
-        down_ref[j] = part[:, 128:]
+        down_ref[:, j * 256 : (j + 1) * 256] = part[:, 128:]
         for c in range(N_C):
             value = part[c * rows : (c + 1) * rows, :128]
             for n in range(spread_ref.shape[0]):
@@ -97,11 +97,11 @@
         in_specs=[whole(part) for part in parts],
         out_specs=[
             pl.BlockSpec((N_GRP * N_X // 2, N_C, N_ZH, rows, 128), lambda i: (i, 0, 0, 0, 0)),
-            pl.BlockSpec((N_ZH, down_rows, 256), lambda i: (0, 0, 0)),
+            pl.BlockSpec((down_rows, N_ZH * 256), lambda i: (0, 0)),
         ],
         out_shape=(
             jax.ShapeDtypeStruct((N_GRP * N_X, N_C, N_ZH, rows, 128), parts[0].dtype),
-            jax.ShapeDtypeStruct((N_ZH, down_rows, 256), parts[0].dtype),
+            jax.ShapeDtypeStruct((down_rows, N_ZH * 256), parts[0].dtype),
         ),
         name="spread",
     )(*parts)
@@ -160,7 +160,7 @@
     term = term.astype(jnp.bfloat16)
     for x in range(N_X):
         for g in range(N_GRP):
-            term_ref[g % 2, x, g // 2, 0] = term[x * 64 : (x + 1) * 64, g * 128 : (g + 1) * 128]
+            term_ref[g, x, 0] = term[x * 64 : (x + 1) * 64, g * 128 : (g + 1) * 128]
 
 
 def forward(zh, own, partner, cots, got_up):
@@ -181,7 +181,7 @@
                 pl.BlockSpec((2 * rows, 256), lambda q, z: (0, q)),
                 pl.BlockSpec((2 * rows, 256), lambda q, z: (0, q)),
                 pl.BlockSpec((2 * rows, 256), lambda q, z: (0, q)),
-                pl.BlockSpec((SIZE["zl"], N_X, SIZE["y"], 1, 64, 128), lambda q, z: (0, 0, 0, q, 0, 0)),
+                pl.BlockSpec((N_GRP, N_X, 1, 64, 128), lambda q, z: (0, 0, q, 0, 0)),
             ],
             scratch_shapes=[pltpu.VMEM((width, 256), jnp.bfloat16), pltpu.VMEM((2 * rows, width), jnp.bfloat16)],
         ),
@@ -189,7 +189,7 @@
             jax.ShapeDtypeStruct((2 * rows, half), jnp.bfloat16),
             jax.ShapeDtypeStruct((2 * rows, half), jnp.float32),
             jax.ShapeDtypeStruct((2 * rows, half), jnp.bfloat16),
-            jax.ShapeDtypeStruct((SIZE["zl"], N_X, SIZE["y"], N_ZH, 64, 128), jnp.bfloat16),
+            jax.ShapeDtypeStruct((N_GRP, N_X, N_ZH, 64, 128), jnp.bfloat16),
         ),
         compiler_params=pltpu.CompilerParams(vmem_limit_bytes=VMEM_BYTES),
         cost_estimate=pl.CostEstimate(
@@ -207,10 +207,10 @@
     rows, width = own_ref.shape
     step = rows // 2
     for j, ref in enumerate((w0, w1, w2, w3)):
-        column = pl.multiple_of((at_ref[1] + j) % SIZE["y"] * 256, 256)
-        for i in range(N_X):
-            row = pl.multiple_of((at_ref[2] + i) % N_X * 64, 64)
-            w[pl.ds(row, 64), pl.ds(column, 256)] = ref[i, 0]
+        row = pl.multiple_of((at_ref[2] + j) % N_X * 64, 64)
+        for i in range(SIZE["y"]):
+            column = pl.multiple_of((at_ref[1] + SIZE["y"] - i) % SIZE["y"] * 256, 256)
+            w[pl.ds(row, 64), pl.ds(column, 256)] = ref[i]
     for at in range(0, 2 * rows, step):
         back = lax.dot_general(
             cot[at : at + step, :], w[...], (((1,), (1,)), ((), ())), preferred_element_type=jnp.float32
@@ -243,7 +243,7 @@
                 whole(own),
                 whole(partner),
                 *[whole(c) for c in cots],
-                *[pl.BlockSpec((N_X, 1, 64, 256), lambda q, at: (0, (q - at[0] + N_ZH) % N_ZH, 0, 0)) for _ in downs],
+                *[pl.BlockSpec((SIZE["y"], 64, 256), lambda q, at: (0, 0, (q - at[0] + N_ZH) % N_ZH)) for _ in downs],
                 pl.BlockSpec((2 * rows, 256), lambda q, at: (0, q)),
                 pl.BlockSpec((2 * rows, 256), lambda q, at: (0, q)),
             ],
@@ -288,21 +288,22 @@
     pair = jnp.stack([kept, lax.ppermute(sent, "zl", [(0, 1), (1, 0)])], axis=1)
     parts = along(cut(w_up, w_down, group, y), "zh")
     pair, *parts = lax.optimization_barrier((pair, *parts))
-    order, old_cot = [], []
+    spread_up, down_zh = spread(parts)
+    spread_up = spread_up.reshape(N_GRP * N_X * N_C, N_ZH, up_rows, 128)
+    old_rows = n_zl * slots
+    order, old_cot, down_y = [], [], []
     for dy in range(n_y):
-        block = lax.dynamic_index_in_dim(pair, (y + dy) % n_y, 0, keepdims=False)
+        block = lax.dynamic_index_in_dim(pair, (y + dy) % n_y, 0, keepdims=False).reshape(old_rows, width)
         if dy:
-            block = lax.ppermute(block, "y", [(i, (i + dy) % n_y) for i in range(n_y)])
-        old_cot.append(block.reshape(n_zl * slots, width))
+            block = shift(jnp.concatenate([block, down_zh], axis=0), "y", dy)
+        old_cot.append(block[:old_rows])
+        down_y.append(block[old_rows:] if dy else down_zh)
         order += [(y - dy) % n_y * n_zl + zl, (y - dy) % n_y * n_zl + 1 - zl]
     order = jnp.stack(order)
-
-    spread_up, down_zh = spread(parts)
     spread_up, *old_cot = lax.optimization_barrier((spread_up, *old_cot))
     cot = jnp.concatenate([grad_new, *old_cot], axis=0)
-    spread_up = spread_up.reshape(N_GRP * N_X * N_C, N_ZH, up_rows, 128)
     got_up = exchange(spread_up, ("y", "zl", "x", "c")).reshape(N_GRP, N_X, N_C, N_ZH, up_rows, 128)
-    downs = along(jnp.stack(along(down_zh, "x")), "y")
+    downs = along(jnp.stack(down_y), "x")
 
     picks, counts = send_rows[0][order], send_count[0][order]
     live = (lax.broadcasted_iota(jnp.int32, (N_GRP, slots), 1) < counts[:, None]).astype(jnp.bfloat16)
@@ -314,8 +315,8 @@
     rows = normed.shape[0]
 
     hidden, pre, cdf_value, term_down = forward(zh, normed, partner, cots, got_up)
-    part_down = exchange(term_down.reshape((n_zl * N_X,) + term_down.shape[2:]), ("zl", "x"))
-    part_down = sum_along(jnp.sum(part_down.astype(jnp.float32), axis=0).astype(jnp.bfloat16), "y")
+    part_down = exchange(term_down, GRP)
+    part_down = sum_along(jnp.sum(part_down.astype(jnp.float32), axis=0).astype(jnp.bfloat16), "x")
 
     at = jnp.stack([zh, y, lax.axis_index("x")])
     term_up, down_half = backward(at, normed, partner, cots, downs, pre, cdf_value)

time: 182 us -> 181 us (level)
  waiting for transfers between devices: 58.5 us -> 53.2 us
  starting transfers between devices: 64 us -> 67 us
    ppermute x15, waiting for transfers between devices: 52.1 us -> 35.7 us  [shift(): return lax.ppermute(value, axis, [(i, (i + step) % n) for i in range(n)])]
    all_to_all x4, waiting for transfers between devices: 6.07 us -> 17.5 us  [exchange(): return lax.all_to_all(value, axes, split_axis=0, concat_axis=0, tiled=True)]
    all_to_all x4, starting transfers between devices: 24.7 us -> 31.3 us  [exchange(): return lax.all_to_all(value, axes, split_axis=0, concat_axis=0, tiled=True)]
    ppermute x3 -> x0, starting transfers between devices: 5.9 us -> none  [body(): block = lax.ppermute(block, 'y', [(i, (i + dy) % n_y) for i in range(n_y)])]
    unnamed x40 -> x44, local copies, waits for them, and re-layouts: 5.31 us -> 6.06 us
  transfers between devices with their start and end apart: 26 -> 23, of which waited for: 13 -> 12; matrix products, arithmetic and copies ran while one was open for 13% -> 13% of each run, Pallas kernels for 16% -> 14%
where the time goes in v9:
time: 181 us; the launch traced here: 180 us
  starting transfers between devices  67 us (37%)
  waiting for transfers between devices  53.2 us (29%)
  Pallas kernels  29.8 us (16%)
  local copies, waits for them, and re-layouts  11.7 us (6%)
  other arithmetic  8.72 us (5%)
  matrix products  8.61 us (5%)
    ppermute x15, waiting for transfers between devices, shift(): return lax.ppermute(value, axis, [(i, (i + step) % n) for i in range(n)])  35.7 us
    ppermute x15, starting transfers between devices, shift(): return lax.ppermute(value, axis, [(i, (i + step) % n) for i in range(n)])  32.2 us
    all_to_all x4, starting transfers between devices, exchange(): return lax.all_to_all(value, axes, split_axis=0, concat_axis=0, tiled=True)  31.3 us
    all_to_all x4, waiting for transfers between devices, exchange(): return lax.all_to_all(value, axes, split_axis=0, concat_axis=0, tiled=True)  17.5 us
    pallas_call x1, Pallas kernels, backward(): pl.pallas_call(backward_kernel, grid_spec=pltpu.PrefetchScalarGridSpec(nu...  12.6 us
    pallas_call x1, Pallas kernels, forward(): pl.pallas_call(forward_kernel, grid_spec=pltpu.PrefetchScalarGridSpec(num...  10.8 us
    unnamed x44, local copies, waits for them, and re-layouts  6.06 us
    dot_general x1, matrix products, body(): jnp.dot(hidden[:fresh_count], down_half, preferred_element_type=jnp.float32)  4.47 us
  transfers between devices with their start and end apart: 23, of which 12 were waited for; matrix products, arithmetic and copies ran while one was open for 13% of the time, Pallas kernels for 14%

profile of v9, /device:TPU:64, one launch (start us, length us, event | category | flops | bytes accessed | tf_op | source)
XLA Modules:
  0.0 180.1 jit_solution(14129983758896030213)
XLA Ops:
  1.8 2.0 %collective-permute-start.1 = (bf16[4,16,1024]{2,1,0:T(8,128)(2,1)S(1)}, bf16[4,16,1024]{2,1,0:T(8,128)(2,1)S(1)}, u32[]{:S(2)}, u32[]{:S(2)}) collective-permute-start(bf16[4,16,1024]{2,1,0:T(8,128)(2,1)S(1)} %get-tuple-element.51), channel_id=1, source_target_pairs={{0,32},{32,0},{1,33},{33,1},{2,34},{34,2},{3,35},{35,3},{4,36},{36... | collective-permute-start | bytes 393224 | tf_op jit(solution)/shard_map/ppermute | solution.py:288
  4.4 2.1 %cut.1.p0 = bf16[64,384]{1,0:T(8,128)(2,1)} custom-call(s32[2]{0:T(128)} %pad_add_fusion.at_ref, bf16[32,2048]{1,0:T(8,128)(2,1)} %up_ref.1, bf16[64,1024]{1,0:T(8,128)(2,1)} %down_ref.1), custom_call_target="tpu_custom_call" | custom-call | tf_op jit(solution)/shard_map/cut/pallas_call | solution.py:65
  6.5 5.9 %collective-permute-start.3 = (bf16[64,384]{1,0:T(8,128)(2,1)}, bf16[64,384]{1,0:T(8,128)(2,1)S(1)}, u32[]{:S(2)}, u32[]{:S(2)}) collective-permute-start(bf16[64,384]{1,0:T(8,128)(2,1)} %cut.1.p0), channel_id=1, source_target_pairs={{0,16},{8,24},{16,0},{24,8},{1,17},{9,25},{17,1},{25,9},{2,18},{10... | collective-permute-start | bytes 147464 | tf_op jit(solution)/shard_map/ppermute | solution.py:36
  12.5 2.7 %collective-permute-start.4 = (bf16[64,384]{1,0:T(8,128)(2,1)}, bf16[64,384]{1,0:T(8,128)(2,1)S(1)}, u32[]{:S(2)}, u32[]{:S(2)}) collective-permute-start(bf16[64,384]{1,0:T(8,128)(2,1)} %cut.1.p0), channel_id=1, source_target_pairs={{0,8},{8,16},{16,24},{24,0},{1,9},{9,17},{17,25},{25,1},{2,10},{10... | collective-permute-start | bytes 147464 | tf_op jit(solution)/shard_map/ppermute | solution.py:36
  15.7 2.1 %collective-permute-done.4.p3 = bf16[64,384]{1,0:T(8,128)(2,1)S(1)} collective-permute-done((bf16[64,384]{1,0:T(8,128)(2,1)}, bf16[64,384]{1,0:T(8,128)(2,1)S(1)}, u32[]{:S(2)}, u32[]{:S(2)}) %collective-permute-start.4) | collective-permute-done | bytes 49184 | tf_op jit(solution)/shard_map/ppermute | solution.py:36
  18.4 2.5 %spread.1 = (bf16[32,2,4,32,128]{4,3,2,1,0:T(8,128)(2,1)}, bf16[64,1024]{1,0:T(8,128)(2,1)}) custom-call(bf16[64,384]{1,0:T(8,128)(2,1)} %cut.1.p0, bf16[64,384]{1,0:T(8,128)(2,1)} %copy-done.16, bf16[64,384]{1,0:T(8,128)(2,1)} %copy-done.17, bf16[64,384]{1,0:T(8,128)(2,1)} %copy-done.18), custom_call_target="tpu_custom_call" | custom-call | tf_op jit(solution)/shard_map/spread/pallas_call | solution.py:94
  21.8 1.7 collective-permute-start.5
  23.5 2.9 %collective-permute-start.6 = (bf16[96,1024]{1,0:T(8,128)(2,1)S(1)}, bf16[96,1024]{1,0:T(8,128)(2,1)S(1)}, u32[]{:S(2)}, u32[]{:S(2)}) collective-permute-start(bf16[96,1024]{1,0:T(8,128)(2,1)S(1)} %get-tuple-element.56), channel_id=1, source_target_pairs={{0,128},{64,192},{128,0},{192,64},{1,129},{65,193},{129,1},{193,65... | collective-permute-start | bytes 589832 | tf_op jit(solution)/shard_map/ppermute | solution.py:36
  27.7 2.1 %collective-permute-done.5 = bf16[96,1024]{1,0:T(8,128)(2,1)S(1)} collective-permute-done((bf16[96,1024]{1,0:T(8,128)(2,1)S(1)}, bf16[96,1024]{1,0:T(8,128)(2,1)S(1)}, u32[]{:S(2)}, u32[]{:S(2)}) %collective-permute-start.5) | collective-permute-done | bytes 196640 | tf_op jit(solution)/shard_map/ppermute | solution.py:36
  29.8 4.4 %collective-permute-done.6 = bf16[96,1024]{1,0:T(8,128)(2,1)S(1)} collective-permute-done((bf16[96,1024]{1,0:T(8,128)(2,1)S(1)}, bf16[96,1024]{1,0:T(8,128)(2,1)S(1)}, u32[]{:S(2)}, u32[]{:S(2)}) %collective-permute-start.6) | collective-permute-done | bytes 196640 | tf_op jit(solution)/shard_map/ppermute | solution.py:36
  35.0 8.0 %all-to-all-start = ((bf16[64,4,32,128]{3,2,1,0:T(8,128)(2,1)}), bf16[64,4,32,128]{3,2,1,0:T(8,128)(2,1)}, u32[]{:S(2)}, u32[]{:S(2)}) async-start(bf16[64,4,32,128]{3,2,1,0:T(8,128)(2,1)} %bitcast.64), calls=%async_computation | async-start | bytes 4194304 | tf_op jit(solution)/shard_map/all_to_all | solution.py:31
  52.5 3.0 %collective-permute-start.10 = (bf16[4,64,1024]{2,1,0:T(8,128)(2,1)}, bf16[4,64,1024]{2,1,0:T(8,128)(2,1)}, u32[]{:S(2)}, u32[]{:S(2)}) collective-permute-start(bf16[4,64,1024]{2,1,0:T(8,128)(2,1)} %pad_maximum_fusion.1.w0), channel_id=1, source_target_pairs={{0,4},{2,6},{4,0},{6,2},{1,5},{3,7},{5,1},{7,3},{8,12},{10,14},{12... | collective-permute-start | bytes 1572872 | tf_op jit(solution)/shard_map/ppermute | solution.py:36
  56.0 2.7 %collective-permute-start.9 = (bf16[4,64,1024]{2,1,0:T(8,128)(2,1)}, bf16[4,64,1024]{2,1,0:T(8,128)(2,1)}, u32[]{:S(2)}, u32[]{:S(2)}) collective-permute-start(bf16[4,64,1024]{2,1,0:T(8,128)(2,1)} %pad_maximum_fusion.1.w0), channel_id=1, source_target_pairs={{0,6},{2,0},{4,2},{6,4},{1,7},{3,1},{5,3},{7,5},{8,14},{10,8},{12,... | collective-permute-start | bytes 1572872 | tf_op jit(solution)/shard_map/ppermute | solution.py:36
  58.8 12.8 %all-to-all-done = bf16[64,4,32,128]{3,2,1,0:T(8,128)(2,1)} async-done(((bf16[64,4,32,128]{3,2,1,0:T(8,128)(2,1)}), bf16[64,4,32,128]{3,2,1,0:T(8,128)(2,1)}, u32[]{:S(2)}, u32[]{:S(2)}) %all-to-all-start) | async-done | bytes 2097184 | tf_op jit(solution)/shard_map/all_to_all | solution.py:31
  71.6 10.8 %forward.1 = (bf16[1280,1024]{1,0:T(8,128)(2,1)}, f32[1280,1024]{1,0:T(8,128)}, bf16[1280,1024]{1,0:T(8,128)(2,1)}, bf16[8,4,4,64,128]{4,3,2,1,0:T(8,128)(2,1)}) custom-call(s32[1]{0:T(128)} %bitcast.zh_ref, bf16[640,1024]{1,0:T(8,128)(2,1)S(1)} %fusion.4.own_ref, bf16[640,1024]{1,0:T(8,128)(2,1)} %collective-permute-done.partner_ref, ...), custom_call_target="tpu_custom_call" | custom-call | bytes 1024 | tf_op jit(solution)/shard_map/forward/pallas_call | solution.py:169
  82.4 4.4 %all-to-all-start.1 = ((bf16[8,4,4,64,128]{4,3,2,1,0:T(8,128)(2,1)}), bf16[8,4,4,64,128]{4,3,2,1,0:T(8,128)(2,1)}, u32[]{:S(2)}, u32[]{:S(2)}) async-start(bf16[8,4,4,64,128]{4,3,2,1,0:T(8,128)(2,1)} %get-tuple-element.39), calls=%async_computation.1 | async-start | bytes 4194304 | tf_op jit(solution)/shard_map/all_to_all | solution.py:31
  86.8 4.6 %collective-permute-done.11.w3 = bf16[4,64,1024]{2,1,0:T(8,128)(2,1)} collective-permute-done((bf16[4,64,1024]{2,1,0:T(8,128)(2,1)}, bf16[4,64,1024]{2,1,0:T(8,128)(2,1)}, u32[]{:S(2)}, u32[]{:S(2)}) %collective-permute-start.11) | collective-permute-done | bytes 524320 | tf_op jit(solution)/shard_map/ppermute | solution.py:36
  91.4 12.6 %backward.1 = (bf16[8,4,2,4,32,128]{5,4,3,2,1,0:T(8,128)(2,1)}, bf16[1024,1024]{1,0:T(8,128)(2,1)}) custom-call(s32[3]{0:T(128)S(1)} %pad_add_fusion.1.at_ref, bf16[640,1024]{1,0:T(8,128)(2,1)S(1)} %fusion.4.own_ref, bf16[640,1024]{1,0:T(8,128)(2,1)} %collective-permute-done.partner_ref, bf16[640,1024]{1,0:T(8,128)(2,1)} %constant_dynamic-update-slice_fusion.c0, ...), custom_call_target="tpu_custom_call" | custom-call | flops 268435456000 | bytes 20971520 | tf_op jit(solution)/shard_map/backward/pallas_call | solution.py:237
  104.0 1.9 %all-to-all-done.1 = bf16[8,4,4,64,128]{4,3,2,1,0:T(8,128)(2,1)} async-done(((bf16[8,4,4,64,128]{4,3,2,1,0:T(8,128)(2,1)}), bf16[8,4,4,64,128]{4,3,2,1,0:T(8,128)(2,1)}, u32[]{:S(2)}, u32[]{:S(2)}) %all-to-all-start.1) | async-done | bytes 2097184 | tf_op jit(solution)/shard_map/all_to_all | solution.py:31
  105.9 13.5 %all-to-all-start.2 = ((bf16[64,4,32,128]{3,2,1,0:T(8,128)(2,1)}), bf16[64,4,32,128]{3,2,1,0:T(8,128)(2,1)}, u32[]{:S(2)}, u32[]{:S(2)}) async-start(bf16[64,4,32,128]{3,2,1,0:T(8,128)(2,1)} %bitcast.65), calls=%async_computation.2 | async-start | bytes 4194304 | tf_op jit(solution)/shard_map/all_to_all | solution.py:31
  119.4 4.1 %convolution_convert_fusion = bf16[512,1024]{1,0:T(8,128)(2,1)} fusion(bf16[1024,1024]{1,0:T(8,128)(2,1)} %get-tuple-element.38, bf16[1280,1024]{1,0:T(8,128)(2,1)} %get-tuple-element.35), kind=kOutput, calls=%fused_computation.11 | convolution fusion | flops 1074266112 | bytes 4194304 | tf_op jit(solution)/shard_map/dot_general | solution.py:328
  124.5 2.0 %reduce_sum.44 = bf16[4,4,64,128]{3,2,1,0:T(8,128)(2,1)S(1)} reduce(bf16[8,4,4,64,128]{4,3,2,1,0:T(8,128)(2,1)} %all-to-all-done.1, bf16[]{:T(256)} %constant.152.clone.1), dimensions={0}, to_apply=%region_2.3 | reduce | flops 917504 | bytes 2359298 | tf_op jit(solution)/shard_map/reduce_sum | solution.py:319
  128.3 2.3 %collective-permute-start.14 = (bf16[4,64,128]{2,1,0:T(8,128)(2,1)}, bf16[4,64,128]{2,1,0:T(8,128)(2,1)S(1)}, u32[]{:S(2)}, u32[]{:S(2)}) collective-permute-start(bf16[4,64,128]{2,1,0:T(8,128)(2,1)} %get-tuple-element.45), channel_id=1, source_target_pairs={{0,4},{2,6},{4,0},{6,2},{1,5},{3,7},{5,1},{7,3},{8,12},{10,14},{12... | collective-permute-start | bytes 196616 | tf_op jit(solution)/shard_map/ppermute | solution.py:36
  132.0 14.8 %collective-permute-done.13 = bf16[4,64,128]{2,1,0:T(8,128)(2,1)S(1)} collective-permute-done((bf16[4,64,128]{2,1,0:T(8,128)(2,1)}, bf16[4,64,128]{2,1,0:T(8,128)(2,1)S(1)}, u32[]{:S(2)}, u32[]{:S(2)}) %collective-permute-start.13) | collective-permute-done | bytes 65568 | tf_op jit(solution)/shard_map/ppermute | solution.py:36
  149.9 1.9 %reduce_sum.45 = bf16[2,4,32,128]{3,2,1,0:T(8,128)(2,1)S(1)} reduce(bf16[32,2,4,32,128]{4,3,2,1,0:T(8,128)(2,1)} %bitcast.35, bf16[]{:T(256)} %constant.152.clone.1), dimensions={0}, to_apply=%region_3.4 | reduce | flops 1015808 | bytes 2162690 | tf_op jit(solution)/shard_map/reduce_sum | solution.py:325
  151.9 4.1 %collective-permute-start.16 = (bf16[2,64,128]{2,1,0:T(8,128)(2,1)S(1)}, bf16[2,64,128]{2,1,0:T(8,128)(2,1)S(1)}, u32[]{:S(2)}, u32[]{:S(2)}) collective-permute-start(bf16[2,64,128]{2,1,0:T(8,128)(2,1)S(1)} %get-tuple-element.52), channel_id=1, source_target_pairs={{0,8},{8,16},{16,24},{24,0},{1,9},{9,17},{17,25},{25,1},{2,10},{10... | collective-permute-start | bytes 98312 | tf_op jit(solution)/shard_map/ppermute | solution.py:36
  156.0 2.1 %collective-permute-start.17 = (bf16[2,64,128]{2,1,0:T(8,128)(2,1)S(1)}, bf16[2,64,128]{2,1,0:T(8,128)(2,1)S(1)}, u32[]{:S(2)}, u32[]{:S(2)}) collective-permute-start(bf16[2,64,128]{2,1,0:T(8,128)(2,1)S(1)} %get-tuple-element.53), channel_id=1, source_target_pairs={{0,16},{8,24},{16,0},{24,8},{1,17},{9,25},{17,1},{25,9},{2,18},{10... | collective-permute-start | bytes 98312 | tf_op jit(solution)/shard_map/ppermute | solution.py:36
  158.4 5.4 %collective-permute-done.17 = bf16[2,64,128]{2,1,0:T(8,128)(2,1)S(1)} collective-permute-done((bf16[2,64,128]{2,1,0:T(8,128)(2,1)S(1)}, bf16[2,64,128]{2,1,0:T(8,128)(2,1)S(1)}, u32[]{:S(2)}, u32[]{:S(2)}) %collective-permute-start.17) | collective-permute-done | bytes 32800 | tf_op jit(solution)/shard_map/ppermute | solution.py:36
  164.8 5.4 %all-to-all-start.3 = ((bf16[8,2,64,128]{3,2,1,0:T(8,128)(2,1)}), bf16[8,2,64,128]{3,2,1,0:T(8,128)(2,1)S(1)}, u32[]{:S(2)}, u32[]{:S(2)}) async-start(bf16[8,2,64,128]{3,2,1,0:T(8,128)(2,1)} %broadcast_in_dim.2), calls=%async_computation.3 | async-start | bytes 524288 | tf_op jit(solution)/shard_map/all_to_all | solution.py:31
  170.3 4.5 %add_convert_fusion = bf16[512,1024]{1,0:T(8,128)(2,1)} fusion(bf16[512,1024]{1,0:T(8,128)(2,1)} %collective-permute-done.12, bf16[512,1024]{1,0:T(8,128)(2,1)S(1)} %copy-done.4, bf16[1024,1024]{1,0:T(8,128)(2,1)} %get-tuple-element.38, bf16[1280,1024]{1,0:T(8,128)(2,1)} %get-tuple-element.35), kind=kOutput, calls=%fused_computation.10 | convolution fusion | flops 1076363264 | bytes 6291456 | tf_op jit(solution)/shard_map/dot_general | solution.py:329
  174.8 2.8 %all-to-all-done.3.both_ref = bf16[8,2,64,128]{3,2,1,0:T(8,128)(2,1)S(1)} async-done(((bf16[8,2,64,128]{3,2,1,0:T(8,128)(2,1)}), bf16[8,2,64,128]{3,2,1,0:T(8,128)(2,1)S(1)}, u32[]{:S(2)}, u32[]{:S(2)}) %all-to-all-start.3) | async-done | bytes 262176 | tf_op jit(solution)/shard_map/all_to_all | solution.py:31
  178.3 1.8 finish.1
  (107 shorter events, 25.2 us)
Async XLA Ops:
  0.6 44.1 %copy-start = (bf16[1024,1024]{1,0:T(8,128)(2,1)S(1)}, bf16[1024,1024]{1,0:T(8,128)(2,1)}, u32[]{:S(2)}) copy-start(bf16[1024,1024]{1,0:T(8,128)(2,1)} %param.9) | copy-start | bytes 6291460
  1.8 13.4 %collective-permute-start.1 = (bf16[4,16,1024]{2,1,0:T(8,128)(2,1)S(1)}, bf16[4,16,1024]{2,1,0:T(8,128)(2,1)S(1)}, u32[]{:S(2)}, u32[]{:S(2)}) collective-permute-start(bf16[4,16,1024]{2,1,0:T(8,128)(2,1)S(1)} %get-tuple-element.51), channel_id=1, source_target_pairs={{0,32},{32,0},{1,33},{33,1},{2,34},{34,2},{3,35},{35,3},{4,36},{36... | collective-permute-start | bytes 393224 | tf_op jit(solution)/shard_map/ppermute | solution.py:288
  6.5 8.7 %collective-permute-start.2 = (bf16[64,384]{1,0:T(8,128)(2,1)}, bf16[64,384]{1,0:T(8,128)(2,1)S(1)}, u32[]{:S(2)}, u32[]{:S(2)}) collective-permute-start(bf16[64,384]{1,0:T(8,128)(2,1)} %cut.1.p0), channel_id=1, source_target_pairs={{0,24},{8,0},{16,8},{24,16},{1,25},{9,1},{17,9},{25,17},{2,26},{10... | collective-permute-start | bytes 147464 | tf_op jit(solution)/shard_map/ppermute | solution.py:36
  6.5 9.1 %collective-permute-start.3 = (bf16[64,384]{1,0:T(8,128)(2,1)}, bf16[64,384]{1,0:T(8,128)(2,1)S(1)}, u32[]{:S(2)}, u32[]{:S(2)}) collective-permute-start(bf16[64,384]{1,0:T(8,128)(2,1)} %cut.1.p0), channel_id=1, source_target_pairs={{0,16},{8,24},{16,0},{24,8},{1,17},{9,25},{17,1},{25,9},{2,18},{10... | collective-permute-start | bytes 147464 | tf_op jit(solution)/shard_map/ppermute | solution.py:36
  12.5 5.3 %collective-permute-start.4 = (bf16[64,384]{1,0:T(8,128)(2,1)}, bf16[64,384]{1,0:T(8,128)(2,1)S(1)}, u32[]{:S(2)}, u32[]{:S(2)}) collective-permute-start(bf16[64,384]{1,0:T(8,128)(2,1)} %cut.1.p0), channel_id=1, source_target_pairs={{0,8},{8,16},{16,24},{24,0},{1,9},{9,17},{17,25},{25,1},{2,10},{10... | collective-permute-start | bytes 147464 | tf_op jit(solution)/shard_map/ppermute | solution.py:36
  21.8 8.0 %collective-permute-start.5 = (bf16[96,1024]{1,0:T(8,128)(2,1)S(1)}, bf16[96,1024]{1,0:T(8,128)(2,1)S(1)}, u32[]{:S(2)}, u32[]{:S(2)}) collective-permute-start(bf16[96,1024]{1,0:T(8,128)(2,1)S(1)} %get-tuple-element.57), channel_id=1, source_target_pairs={{0,64},{64,128},{128,192},{192,0},{1,65},{65,129},{129,193},{193,1... | collective-permute-start | bytes 589832 | tf_op jit(solution)/shard_map/ppermute | solution.py:36
  23.5 10.8 %collective-permute-start.6 = (bf16[96,1024]{1,0:T(8,128)(2,1)S(1)}, bf16[96,1024]{1,0:T(8,128)(2,1)S(1)}, u32[]{:S(2)}, u32[]{:S(2)}) collective-permute-start(bf16[96,1024]{1,0:T(8,128)(2,1)S(1)} %get-tuple-element.56), channel_id=1, source_target_pairs={{0,128},{64,192},{128,0},{192,64},{1,129},{65,193},{129,1},{193,65... | collective-permute-start | bytes 589832 | tf_op jit(solution)/shard_map/ppermute | solution.py:36
  26.4 7.9 %collective-permute-start.7 = (bf16[96,1024]{1,0:T(8,128)(2,1)S(1)}, bf16[96,1024]{1,0:T(8,128)(2,1)S(1)}, u32[]{:S(2)}, u32[]{:S(2)}) collective-permute-start(bf16[96,1024]{1,0:T(8,128)(2,1)S(1)} %get-tuple-element.55), channel_id=1, source_target_pairs={{0,192},{64,0},{128,64},{192,128},{1,193},{65,1},{129,65},{193,129... | collective-permute-start | bytes 589832 | tf_op jit(solution)/shard_map/ppermute | solution.py:36
  29.8 4.5 %copy-start.9 = (bf16[96,1024]{1,0:T(8,128)(2,1)}, bf16[96,1024]{1,0:T(8,128)(2,1)S(1)}, u32[]{:S(2)}) copy-start(bf16[96,1024]{1,0:T(8,128)(2,1)S(1)} %collective-permute-done.5) | copy-start | bytes 589828
  35.0 8.2 %copy-start.8 = (s32[1,8,16]{2,1,0:T(8,128)S(1)}, s32[1,8,16]{2,1,0:T(8,128)}, u32[]{:S(2)}) copy-start(s32[1,8,16]{2,1,0:T(8,128)} %param.10) | copy-start | bytes 1540
  35.0 8.9 %copy-start.1 = (s32[1,8]{1,0:T(1,128)S(1)}, s32[1,8]{1,0:T(1,128)}, u32[]{:S(2)}) copy-start(s32[1,8]{1,0:T(1,128)} %param.11) | copy-start | bytes 100
  35.0 9.7 %copy-start.19 = (bf16[1024]{0:T(1024)(128)(2,1)S(1)}, bf16[1024]{0:T(1024)(128)(2,1)}, u32[]{:S(2)}) copy-start(bf16[1024]{0:T(1024)(128)(2,1)} %param.15) | copy-start | bytes 6148
  35.0 36.6 %all-to-all-start = ((bf16[64,4,32,128]{3,2,1,0:T(8,128)(2,1)}), bf16[64,4,32,128]{3,2,1,0:T(8,128)(2,1)}, u32[]{:S(2)}, u32[]{:S(2)}) async-start(bf16[64,4,32,128]{3,2,1,0:T(8,128)(2,1)} %bitcast.64), calls=%async_computation | async-start | bytes 4194304 | tf_op jit(solution)/shard_map/all_to_all | solution.py:31
  46.8 4.7 %copy-start.14 = (bf16[96,1024]{1,0:T(8,128)(2,1)S(1)}, bf16[96,1024]{1,0:T(8,128)(2,1)}, u32[]{:S(2)}) copy-start(bf16[96,1024]{1,0:T(8,128)(2,1)} %copy-done.13) | copy-start | bytes 589828
  47.3 4.3 %copy-start.10 = (bf16[96,1024]{1,0:T(8,128)(2,1)S(1)}, bf16[96,1024]{1,0:T(8,128)(2,1)}, u32[]{:S(2)}) copy-start(bf16[96,1024]{1,0:T(8,128)(2,1)} %copy-done.9) | copy-start | bytes 589828
  47.3 4.3 %copy-start.7 = (bf16[64,1024]{1,0:T(8,128)(2,1)S(1)}, bf16[64,1024]{1,0:T(8,128)(2,1)}, u32[]{:S(2)}) copy-start(bf16[64,1024]{1,0:T(8,128)(2,1)} %get-tuple-element.29) | copy-start | bytes 393220
  47.3 11.5 %collective-permute-start = (bf16[640,1024]{1,0:T(8,128)(2,1)S(1)}, bf16[640,1024]{1,0:T(8,128)(2,1)}, u32[]{:S(2)}, u32[]{:S(2)}) collective-permute-start(bf16[640,1024]{1,0:T(8,128)(2,1)S(1)} %fusion.4.own_ref), channel_id=1, source_target_pairs={{0,1},{1,0},{2,3},{3,2},{4,5},{5,4},{6,7},{7,6},{8,9},{9,8},{10,11... | collective-permute-start | bytes 3932168 | tf_op jit(solution)/shard_map/ppermute | solution.py:27
  51.0 7.8 %collective-permute-start.8 = (bf16[640,1024]{1,0:T(8,128)(2,1)}, bf16[640,1024]{1,0:T(8,128)(2,1)}, u32[]{:S(2)}, u32[]{:S(2)}) collective-permute-start(bf16[640,1024]{1,0:T(8,128)(2,1)} %constant_dynamic-update-slice_fusion.c0), channel_id=1, source_target_pairs={{0,1},{1,0},{2,3},{3,2},{4,5},{5,4},{6,7},{7,6},{8,9},{9,8},{10,11... | collective-permute-start | bytes 3932168 | tf_op jit(solution)/shard_map/ppermute | solution.py:27
  52.5 34.3 %collective-permute-start.10 = (bf16[4,64,1024]{2,1,0:T(8,128)(2,1)}, bf16[4,64,1024]{2,1,0:T(8,128)(2,1)}, u32[]{:S(2)}, u32[]{:S(2)}) collective-permute-start(bf16[4,64,1024]{2,1,0:T(8,128)(2,1)} %pad_maximum_fusion.1.w0), channel_id=1, source_target_pairs={{0,4},{2,6},{4,0},{6,2},{1,5},{3,7},{5,1},{7,3},{8,12},{10,14},{12... | collective-permute-start | bytes 1572872 | tf_op jit(solution)/shard_map/ppermute | solution.py:36
  55.5 35.9 %collective-permute-start.11 = (bf16[4,64,1024]{2,1,0:T(8,128)(2,1)}, bf16[4,64,1024]{2,1,0:T(8,128)(2,1)}, u32[]{:S(2)}, u32[]{:S(2)}) collective-permute-start(bf16[4,64,1024]{2,1,0:T(8,128)(2,1)} %pad_maximum_fusion.1.w0), channel_id=1, source_target_pairs={{0,2},{2,4},{4,6},{6,0},{1,3},{3,5},{5,7},{7,1},{8,10},{10,12},{12... | collective-permute-start | bytes 1572872 | tf_op jit(solution)/shard_map/ppermute | solution.py:36
  56.0 35.4 %collective-permute-start.9 = (bf16[4,64,1024]{2,1,0:T(8,128)(2,1)}, bf16[4,64,1024]{2,1,0:T(8,128)(2,1)}, u32[]{:S(2)}, u32[]{:S(2)}) collective-permute-start(bf16[4,64,1024]{2,1,0:T(8,128)(2,1)} %pad_maximum_fusion.1.w0), channel_id=1, source_target_pairs={{0,6},{2,0},{4,2},{6,4},{1,7},{3,1},{5,3},{7,5},{8,14},{10,8},{12,... | collective-permute-start | bytes 1572872 | tf_op jit(solution)/shard_map/ppermute | solution.py:36
  82.4 23.5 %all-to-all-start.1 = ((bf16[8,4,4,64,128]{4,3,2,1,0:T(8,128)(2,1)}), bf16[8,4,4,64,128]{4,3,2,1,0:T(8,128)(2,1)}, u32[]{:S(2)}, u32[]{:S(2)}) async-start(bf16[8,4,4,64,128]{4,3,2,1,0:T(8,128)(2,1)} %get-tuple-element.39), calls=%async_computation.1 | async-start | bytes 4194304 | tf_op jit(solution)/shard_map/all_to_all | solution.py:31
  105.9 44.0 %all-to-all-start.2 = ((bf16[64,4,32,128]{3,2,1,0:T(8,128)(2,1)}), bf16[64,4,32,128]{3,2,1,0:T(8,128)(2,1)}, u32[]{:S(2)}, u32[]{:S(2)}) async-start(bf16[64,4,32,128]{3,2,1,0:T(8,128)(2,1)} %bitcast.65), calls=%async_computation.2 | async-start | bytes 4194304 | tf_op jit(solution)/shard_map/all_to_all | solution.py:31
  123.6 46.7 %collective-permute-start.12 = (bf16[512,1024]{1,0:T(8,128)(2,1)}, bf16[512,1024]{1,0:T(8,128)(2,1)}, u32[]{:S(2)}, u32[]{:S(2)}) collective-permute-start(bf16[512,1024]{1,0:T(8,128)(2,1)} %convolution_convert_fusion), channel_id=1, source_target_pairs={{0,1},{1,0},{2,3},{3,2},{4,5},{5,4},{6,7},{7,6},{8,9},{9,8},{10,11... | collective-permute-start | bytes 3145736 | tf_op jit(solution)/shard_map/ppermute | solution.py:27
  127.2 43.1 %copy-start.4 = (bf16[512,1024]{1,0:T(8,128)(2,1)S(1)}, bf16[512,1024]{1,0:T(8,128)(2,1)}, u32[]{:S(2)}) copy-start(bf16[512,1024]{1,0:T(8,128)(2,1)} %param.12) | copy-start | bytes 3145732
  127.2 19.7 %collective-permute-start.13 = (bf16[4,64,128]{2,1,0:T(8,128)(2,1)}, bf16[4,64,128]{2,1,0:T(8,128)(2,1)S(1)}, u32[]{:S(2)}, u32[]{:S(2)}) collective-permute-start(bf16[4,64,128]{2,1,0:T(8,128)(2,1)} %get-tuple-element.43), channel_id=1, source_target_pairs={{0,2},{2,4},{4,6},{6,0},{1,3},{3,5},{5,7},{7,1},{8,10},{10,12},{12... | collective-permute-start | bytes 196616 | tf_op jit(solution)/shard_map/ppermute | solution.py:36
  128.3 20.1 %collective-permute-start.14 = (bf16[4,64,128]{2,1,0:T(8,128)(2,1)}, bf16[4,64,128]{2,1,0:T(8,128)(2,1)S(1)}, u32[]{:S(2)}, u32[]{:S(2)}) collective-permute-start(bf16[4,64,128]{2,1,0:T(8,128)(2,1)} %get-tuple-element.45), channel_id=1, source_target_pairs={{0,4},{2,6},{4,0},{6,2},{1,5},{3,7},{5,1},{7,3},{8,12},{10,14},{12... | collective-permute-start | bytes 196616 | tf_op jit(solution)/shard_map/ppermute | solution.py:36
  130.6 18.4 %collective-permute-start.15 = (bf16[4,64,128]{2,1,0:T(8,128)(2,1)}, bf16[4,64,128]{2,1,0:T(8,128)(2,1)}, u32[]{:S(2)}, u32[]{:S(2)}) collective-permute-start(bf16[4,64,128]{2,1,0:T(8,128)(2,1)} %get-tuple-element.44), channel_id=1, source_target_pairs={{0,6},{2,0},{4,2},{6,4},{1,7},{3,1},{5,3},{7,5},{8,14},{10,8},{12,... | collective-permute-start | bytes 196616 | tf_op jit(solution)/shard_map/ppermute | solution.py:36
  151.9 6.5 %collective-permute-start.16 = (bf16[2,64,128]{2,1,0:T(8,128)(2,1)S(1)}, bf16[2,64,128]{2,1,0:T(8,128)(2,1)S(1)}, u32[]{:S(2)}, u32[]{:S(2)}) collective-permute-start(bf16[2,64,128]{2,1,0:T(8,128)(2,1)S(1)} %get-tuple-element.52), channel_id=1, source_target_pairs={{0,8},{8,16},{16,24},{24,0},{1,9},{9,17},{17,25},{25,1},{2,10},{10... | collective-permute-start | bytes 98312 | tf_op jit(solution)/shard_map/ppermute | solution.py:36
  156.0 7.8 %collective-permute-start.17 = (bf16[2,64,128]{2,1,0:T(8,128)(2,1)S(1)}, bf16[2,64,128]{2,1,0:T(8,128)(2,1)S(1)}, u32[]{:S(2)}, u32[]{:S(2)}) collective-permute-start(bf16[2,64,128]{2,1,0:T(8,128)(2,1)S(1)} %get-tuple-element.53), channel_id=1, source_target_pairs={{0,16},{8,24},{16,0},{24,8},{1,17},{9,25},{17,1},{25,9},{2,18},{10... | collective-permute-start | bytes 98312 | tf_op jit(solution)/shard_map/ppermute | solution.py:36
  158.0 6.0 %collective-permute-start.18 = (bf16[2,64,128]{2,1,0:T(8,128)(2,1)S(1)}, bf16[2,64,128]{2,1,0:T(8,128)(2,1)S(1)}, u32[]{:S(2)}, u32[]{:S(2)}) collective-permute-start(bf16[2,64,128]{2,1,0:T(8,128)(2,1)S(1)} %get-tuple-element.54), channel_id=1, source_target_pairs={{0,24},{8,0},{16,8},{24,16},{1,25},{9,1},{17,9},{25,17},{2,26},{10... | collective-permute-start | bytes 98312 | tf_op jit(solution)/shard_map/ppermute | solution.py:36
  164.8 12.7 %all-to-all-start.3 = ((bf16[8,2,64,128]{3,2,1,0:T(8,128)(2,1)}), bf16[8,2,64,128]{3,2,1,0:T(8,128)(2,1)S(1)}, u32[]{:S(2)}, u32[]{:S(2)}) async-start(bf16[8,2,64,128]{3,2,1,0:T(8,128)(2,1)} %broadcast_in_dim.2), calls=%async_computation.3 | async-start | bytes 524288 | tf_op jit(solution)/shard_map/all_to_all | solution.py:31
  (13 other events, 22.9 us)

commit v10 on v9

--- a/solution.py
+++ b/solution.py
@@ -300,7 +300,6 @@
         down_y.append(block[old_rows:] if dy else down_zh)
         order += [(y - dy) % n_y * n_zl + zl, (y - dy) % n_y * n_zl + 1 - zl]
     order = jnp.stack(order)
-    spread_up, *old_cot = lax.optimization_barrier((spread_up, *old_cot))
     cot = jnp.concatenate([grad_new, *old_cot], axis=0)
     got_up = exchange(spread_up, ("y", "zl", "x", "c")).reshape(N_GRP, N_X, N_C, N_ZH, up_rows, 128)
     downs = along(jnp.stack(down_y), "x")

time: 181 us -> 183 us (1.011)
  waiting for transfers between devices: 53.2 us -> 63.6 us
  starting transfers between devices: 67 us -> 57.9 us
    ppermute x15, waiting for transfers between devices: 35.7 us -> 49.9 us  [shift(): return lax.ppermute(value, axis, [(i, (i + step) % n) for i in range(n)])]
    all_to_all x4, starting transfers between devices: 31.3 us -> 24.4 us  [exchange(): return lax.all_to_all(value, axes, split_axis=0, concat_axis=0, tiled=True)]
    all_to_all x4, waiting for transfers between devices: 17.5 us -> 11.1 us  [exchange(): return lax.all_to_all(value, axes, split_axis=0, concat_axis=0, tiled=True)]
    ppermute x1, waiting for transfers between devices: 0.01 us -> 2.53 us  [body(): pair = jnp.stack([kept, lax.ppermute(sent, 'zl', [(0, 1), (1, 0)])], axis=1)]
    unnamed x44 -> x30, local copies, waits for them, and re-layouts: 6.06 us -> 5.9 us
  transfers between devices with their start and end apart: 23 -> 23, of which waited for: 12 -> 10; matrix products, arithmetic and copies ran while one was open for 13% -> 15% of each run, Pallas kernels for 14% -> 13%
where the time goes in v10:
time: 183 us
  waiting for transfers between devices  63.6 us (35%)
  starting transfers between devices  57.9 us (32%)
  Pallas kernels  29.8 us (16%)
  local copies, waits for them, and re-layouts  13 us (7%)
  matrix products  8.62 us (5%)
  other arithmetic  8.52 us (5%)
    ppermute x15, waiting for transfers between devices, shift(): return lax.ppermute(value, axis, [(i, (i + step) % n) for i in range(n)])  49.9 us
    ppermute x15, starting transfers between devices, shift(): return lax.ppermute(value, axis, [(i, (i + step) % n) for i in range(n)])  32.3 us
    all_to_all x4, starting transfers between devices, exchange(): return lax.all_to_all(value, axes, split_axis=0, concat_axis=0, tiled=True)  24.4 us
    pallas_call x1, Pallas kernels, backward(): pl.pallas_call(backward_kernel, grid_spec=pltpu.PrefetchScalarGridSpec(nu...  12.6 us
    all_to_all x4, waiting for transfers between devices, exchange(): return lax.all_to_all(value, axes, split_axis=0, concat_axis=0, tiled=True)  11.1 us
    pallas_call x1, Pallas kernels, forward(): pl.pallas_call(forward_kernel, grid_spec=pltpu.PrefetchScalarGridSpec(num...  10.8 us
    unnamed x30, local copies, waits for them, and re-layouts  5.9 us
    dot_general x1, matrix products, body(): jnp.dot(hidden[:fresh_count], down_half, preferred_element_type=jnp.float32)  4.47 us
  transfers between devices with their start and end apart: 23, of which 10 were waited for; matrix products, arithmetic and copies ran while one was open for 15% of the time, Pallas kernels for 13%

profile of v10, /device:TPU:64, one launch (start us, length us, event | category | flops | bytes accessed | tf_op | source)
XLA Modules:
  0.0 182.5 jit_solution(11901548020354609642)
XLA Ops:
  1.2 2.3 %cut.1.p0 = bf16[64,384]{1,0:T(8,128)(2,1)} custom-call(s32[2]{0:T(128)} %pad_add_fusion.at_ref, bf16[32,2048]{1,0:T(8,128)(2,1)} %up_ref.1, bf16[64,1024]{1,0:T(8,128)(2,1)} %down_ref.1), custom_call_target="tpu_custom_call" | custom-call | tf_op jit(solution)/shard_map/cut/pallas_call | solution.py:65
  4.9 5.5 %collective-permute-start.3 = (bf16[64,384]{1,0:T(8,128)(2,1)}, bf16[64,384]{1,0:T(8,128)(2,1)S(1)}, u32[]{:S(2)}, u32[]{:S(2)}) collective-permute-start(bf16[64,384]{1,0:T(8,128)(2,1)} %cut.1.p0), channel_id=1, source_target_pairs={{0,16},{8,24},{16,0},{24,8},{1,17},{9,25},{17,1},{25,9},{2,18},{10... | collective-permute-start | bytes 147464 | tf_op jit(solution)/shard_map/ppermute | solution.py:36
  10.3 2.7 %collective-permute-start.4 = (bf16[64,384]{1,0:T(8,128)(2,1)}, bf16[64,384]{1,0:T(8,128)(2,1)S(1)}, u32[]{:S(2)}, u32[]{:S(2)}) collective-permute-start(bf16[64,384]{1,0:T(8,128)(2,1)} %cut.1.p0), channel_id=1, source_target_pairs={{0,8},{8,16},{16,24},{24,0},{1,9},{9,17},{17,25},{25,1},{2,10},{10... | collective-permute-start | bytes 147464 | tf_op jit(solution)/shard_map/ppermute | solution.py:36
  16.5 2.5 %collective-permute-done.1 = bf16[4,16,1024]{2,1,0:T(8,128)(2,1)S(1)} collective-permute-done((bf16[4,16,1024]{2,1,0:T(8,128)(2,1)S(1)}, bf16[4,16,1024]{2,1,0:T(8,128)(2,1)S(1)}, u32[]{:S(2)}, u32[]{:S(2)}) %collective-permute-start.1) | collective-permute-done | bytes 131104 | tf_op jit(solution)/shard_map/ppermute | solution.py:288
  21.1 2.4 %spread.1 = (bf16[32,2,4,32,128]{4,3,2,1,0:T(8,128)(2,1)}, bf16[64,1024]{1,0:T(8,128)(2,1)}) custom-call(bf16[64,384]{1,0:T(8,128)(2,1)} %cut.1.p0, bf16[64,384]{1,0:T(8,128)(2,1)} %copy-done.9, bf16[64,384]{1,0:T(8,128)(2,1)} %copy-done.10, bf16[64,384]{1,0:T(8,128)(2,1)} %copy-done.11), custom_call_target="tpu_custom_call" | custom-call | tf_op jit(solution)/shard_map/spread/pallas_call | solution.py:94
  23.5 8.8 %all-to-all-start = ((bf16[64,4,32,128]{3,2,1,0:T(8,128)(2,1)}), bf16[64,4,32,128]{3,2,1,0:T(8,128)(2,1)}, u32[]{:S(2)}, u32[]{:S(2)}) async-start(bf16[64,4,32,128]{3,2,1,0:T(8,128)(2,1)} %bitcast.65), calls=%async_computation | async-start | bytes 4194304 | tf_op jit(solution)/shard_map/all_to_all | solution.py:31
  37.0 1.7 collective-permute-start.5
  39.8 2.9 %collective-permute-start.6 = (bf16[96,1024]{1,0:T(8,128)(2,1)S(1)}, bf16[96,1024]{1,0:T(8,128)(2,1)S(1)}, u32[]{:S(2)}, u32[]{:S(2)}) collective-permute-start(bf16[96,1024]{1,0:T(8,128)(2,1)S(1)} %get-tuple-element.46), channel_id=1, source_target_pairs={{0,128},{64,192},{128,0},{192,64},{1,129},{65,193},{129,1},{193,65... | collective-permute-start | bytes 589832 | tf_op jit(solution)/shard_map/ppermute | solution.py:36
  44.6 18.3 %collective-permute-done.5 = bf16[96,1024]{1,0:T(8,128)(2,1)S(1)} collective-permute-done((bf16[96,1024]{1,0:T(8,128)(2,1)S(1)}, bf16[96,1024]{1,0:T(8,128)(2,1)S(1)}, u32[]{:S(2)}, u32[]{:S(2)}) %collective-permute-start.5) | collective-permute-done | bytes 196640 | tf_op jit(solution)/shard_map/ppermute | solution.py:36
  63.5 3.7 %collective-permute-done.6 = bf16[96,1024]{1,0:T(8,128)(2,1)S(1)} collective-permute-done((bf16[96,1024]{1,0:T(8,128)(2,1)S(1)}, bf16[96,1024]{1,0:T(8,128)(2,1)S(1)}, u32[]{:S(2)}, u32[]{:S(2)}) %collective-permute-start.6) | collective-permute-done | bytes 196640 | tf_op jit(solution)/shard_map/ppermute | solution.py:36
  69.4 2.8 %collective-permute-start.10 = (bf16[4,64,1024]{2,1,0:T(8,128)(2,1)}, bf16[4,64,1024]{2,1,0:T(8,128)(2,1)}, u32[]{:S(2)}, u32[]{:S(2)}) collective-permute-start(bf16[4,64,1024]{2,1,0:T(8,128)(2,1)} %pad_maximum_fusion.1.w0), channel_id=1, source_target_pairs={{0,4},{2,6},{4,0},{6,2},{1,5},{3,7},{5,1},{7,3},{8,12},{10,14},{12... | collective-permute-start | bytes 1572872 | tf_op jit(solution)/shard_map/ppermute | solution.py:36
  72.8 2.7 %collective-permute-start.9 = (bf16[4,64,1024]{2,1,0:T(8,128)(2,1)}, bf16[4,64,1024]{2,1,0:T(8,128)(2,1)}, u32[]{:S(2)}, u32[]{:S(2)}) collective-permute-start(bf16[4,64,1024]{2,1,0:T(8,128)(2,1)} %pad_maximum_fusion.1.w0), channel_id=1, source_target_pairs={{0,6},{2,0},{4,2},{6,4},{1,7},{3,1},{5,3},{7,5},{8,14},{10,8},{12,... | collective-permute-start | bytes 1572872 | tf_op jit(solution)/shard_map/ppermute | solution.py:36
  75.5 10.8 %forward.1 = (bf16[1280,1024]{1,0:T(8,128)(2,1)}, f32[1280,1024]{1,0:T(8,128)}, bf16[1280,1024]{1,0:T(8,128)(2,1)}, bf16[8,4,4,64,128]{4,3,2,1,0:T(8,128)(2,1)}) custom-call(s32[1]{0:T(128)} %bitcast.zh_ref, bf16[640,1024]{1,0:T(8,128)(2,1)S(1)} %fusion.4.own_ref, bf16[640,1024]{1,0:T(8,128)(2,1)} %collective-permute-done.partner_ref, ...), custom_call_target="tpu_custom_call" | custom-call | bytes 1024 | tf_op jit(solution)/shard_map/forward/pallas_call | solution.py:169
  86.3 4.4 %all-to-all-start.1 = ((bf16[8,4,4,64,128]{4,3,2,1,0:T(8,128)(2,1)}), bf16[8,4,4,64,128]{4,3,2,1,0:T(8,128)(2,1)}, u32[]{:S(2)}, u32[]{:S(2)}) async-start(bf16[8,4,4,64,128]{4,3,2,1,0:T(8,128)(2,1)} %get-tuple-element.29), calls=%async_computation.1 | async-start | bytes 4194304 | tf_op jit(solution)/shard_map/all_to_all | solution.py:31
  90.7 6.1 %collective-permute-done.11.w3 = bf16[4,64,1024]{2,1,0:T(8,128)(2,1)} collective-permute-done((bf16[4,64,1024]{2,1,0:T(8,128)(2,1)}, bf16[4,64,1024]{2,1,0:T(8,128)(2,1)}, u32[]{:S(2)}, u32[]{:S(2)}) %collective-permute-start.11) | collective-permute-done | bytes 524320 | tf_op jit(solution)/shard_map/ppermute | solution.py:36
  96.8 12.6 %backward.1 = (bf16[8,4,2,4,32,128]{5,4,3,2,1,0:T(8,128)(2,1)}, bf16[1024,1024]{1,0:T(8,128)(2,1)}) custom-call(s32[3]{0:T(128)S(1)} %pad_add_fusion.1.at_ref, bf16[640,1024]{1,0:T(8,128)(2,1)S(1)} %fusion.4.own_ref, bf16[640,1024]{1,0:T(8,128)(2,1)} %collective-permute-done.partner_ref, bf16[640,1024]{1,0:T(8,128)(2,1)} %slice_dynamic-update-slice_fusion.c0, ...), custom_call_target="tpu_custom_call" | custom-call | flops 268435456000 | bytes 20971520 | tf_op jit(solution)/shard_map/backward/pallas_call | solution.py:237
  109.4 8.3 %all-to-all-done.1 = bf16[8,4,4,64,128]{4,3,2,1,0:T(8,128)(2,1)} async-done(((bf16[8,4,4,64,128]{4,3,2,1,0:T(8,128)(2,1)}), bf16[8,4,4,64,128]{4,3,2,1,0:T(8,128)(2,1)}, u32[]{:S(2)}, u32[]{:S(2)}) %all-to-all-start.1) | async-done | bytes 2097184 | tf_op jit(solution)/shard_map/all_to_all | solution.py:31
  117.7 5.6 %all-to-all-start.2 = ((bf16[64,4,32,128]{3,2,1,0:T(8,128)(2,1)}), bf16[64,4,32,128]{3,2,1,0:T(8,128)(2,1)}, u32[]{:S(2)}, u32[]{:S(2)}) async-start(bf16[64,4,32,128]{3,2,1,0:T(8,128)(2,1)} %bitcast.64), calls=%async_computation.2 | async-start | bytes 4194304 | tf_op jit(solution)/shard_map/all_to_all | solution.py:31
  123.3 4.1 %convolution_convert_fusion = bf16[512,1024]{1,0:T(8,128)(2,1)} fusion(bf16[1024,1024]{1,0:T(8,128)(2,1)} %get-tuple-element.28, bf16[1280,1024]{1,0:T(8,128)(2,1)} %get-tuple-element.25), kind=kOutput, calls=%fused_computation.11 | convolution fusion | flops 1074266112 | bytes 4194304 | tf_op jit(solution)/shard_map/dot_general | solution.py:327
  127.4 2.0 %reduce_sum.44 = bf16[4,4,64,128]{3,2,1,0:T(8,128)(2,1)S(1)} reduce(bf16[8,4,4,64,128]{4,3,2,1,0:T(8,128)(2,1)} %all-to-all-done.1, bf16[]{:T(256)} %constant.152.clone.1), dimensions={0}, to_apply=%region_2.3 | reduce | flops 917504 | bytes 2359298 | tf_op jit(solution)/shard_map/reduce_sum | solution.py:318
  130.1 1.6 collective-permute-start.13
  131.6 2.7 %collective-permute-start.14 = (bf16[4,64,128]{2,1,0:T(8,128)(2,1)}, bf16[4,64,128]{2,1,0:T(8,128)(2,1)S(1)}, u32[]{:S(2)}, u32[]{:S(2)}) collective-permute-start(bf16[4,64,128]{2,1,0:T(8,128)(2,1)} %get-tuple-element.35), channel_id=1, source_target_pairs={{0,4},{2,6},{4,0},{6,2},{1,5},{3,7},{5,1},{7,3},{8,12},{10,14},{12... | collective-permute-start | bytes 196616 | tf_op jit(solution)/shard_map/ppermute | solution.py:36
  135.8 14.8 %collective-permute-done.13 = bf16[4,64,128]{2,1,0:T(8,128)(2,1)S(1)} collective-permute-done((bf16[4,64,128]{2,1,0:T(8,128)(2,1)}, bf16[4,64,128]{2,1,0:T(8,128)(2,1)S(1)}, u32[]{:S(2)}, u32[]{:S(2)}) %collective-permute-start.13) | collective-permute-done | bytes 65568 | tf_op jit(solution)/shard_map/ppermute | solution.py:36
  150.6 1.5 collective-permute-done.14
  153.7 1.9 %reduce_sum.45 = bf16[2,4,32,128]{3,2,1,0:T(8,128)(2,1)S(1)} reduce(bf16[32,2,4,32,128]{4,3,2,1,0:T(8,128)(2,1)} %bitcast.35, bf16[]{:T(256)} %constant.152.clone.1), dimensions={0}, to_apply=%region_3.4 | reduce | flops 1015808 | bytes 2162690 | tf_op jit(solution)/shard_map/reduce_sum | solution.py:324
  155.6 2.4 %collective-permute-start.16 = (bf16[2,64,128]{2,1,0:T(8,128)(2,1)S(1)}, bf16[2,64,128]{2,1,0:T(8,128)(2,1)S(1)}, u32[]{:S(2)}, u32[]{:S(2)}) collective-permute-start(bf16[2,64,128]{2,1,0:T(8,128)(2,1)S(1)} %get-tuple-element.42), channel_id=1, source_target_pairs={{0,8},{8,16},{16,24},{24,0},{1,9},{9,17},{17,25},{25,1},{2,10},{10... | collective-permute-start | bytes 98312 | tf_op jit(solution)/shard_map/ppermute | solution.py:36
  158.0 2.2 %collective-permute-start.17 = (bf16[2,64,128]{2,1,0:T(8,128)(2,1)S(1)}, bf16[2,64,128]{2,1,0:T(8,128)(2,1)S(1)}, u32[]{:S(2)}, u32[]{:S(2)}) collective-permute-start(bf16[2,64,128]{2,1,0:T(8,128)(2,1)S(1)} %get-tuple-element.43), channel_id=1, source_target_pairs={{0,16},{8,24},{16,0},{24,8},{1,17},{9,25},{17,1},{25,9},{2,18},{10... | collective-permute-start | bytes 98312 | tf_op jit(solution)/shard_map/ppermute | solution.py:36
  160.8 5.3 %collective-permute-done.17 = bf16[2,64,128]{2,1,0:T(8,128)(2,1)S(1)} collective-permute-done((bf16[2,64,128]{2,1,0:T(8,128)(2,1)S(1)}, bf16[2,64,128]{2,1,0:T(8,128)(2,1)S(1)}, u32[]{:S(2)}, u32[]{:S(2)}) %collective-permute-start.17) | collective-permute-done | bytes 32800 | tf_op jit(solution)/shard_map/ppermute | solution.py:36
  167.0 5.7 %all-to-all-start.3 = ((bf16[8,2,64,128]{3,2,1,0:T(8,128)(2,1)}), bf16[8,2,64,128]{3,2,1,0:T(8,128)(2,1)S(1)}, u32[]{:S(2)}, u32[]{:S(2)}) async-start(bf16[8,2,64,128]{3,2,1,0:T(8,128)(2,1)} %broadcast_in_dim.2), calls=%async_computation.3 | async-start | bytes 524288 | tf_op jit(solution)/shard_map/all_to_all | solution.py:31
  172.8 4.5 %add_convert_fusion = bf16[512,1024]{1,0:T(8,128)(2,1)} fusion(bf16[512,1024]{1,0:T(8,128)(2,1)} %collective-permute-done.12, bf16[512,1024]{1,0:T(8,128)(2,1)S(1)} %copy-done.3, bf16[1024,1024]{1,0:T(8,128)(2,1)} %get-tuple-element.28, bf16[1280,1024]{1,0:T(8,128)(2,1)} %get-tuple-element.25), kind=kOutput, calls=%fused_computation.10 | convolution fusion | flops 1076363264 | bytes 6291456 | tf_op jit(solution)/shard_map/dot_general | solution.py:328
  177.2 2.8 %all-to-all-done.3.both_ref = bf16[8,2,64,128]{3,2,1,0:T(8,128)(2,1)S(1)} async-done(((bf16[8,2,64,128]{3,2,1,0:T(8,128)(2,1)}), bf16[8,2,64,128]{3,2,1,0:T(8,128)(2,1)S(1)}, u32[]{:S(2)}, u32[]{:S(2)}) %all-to-all-start.3) | async-done | bytes 262176 | tf_op jit(solution)/shard_map/all_to_all | solution.py:31
  180.7 1.8 finish.1
  (88 shorter events, 24.4 us)
Async XLA Ops:
  0.6 32.6 %copy-start = (bf16[1024,1024]{1,0:T(8,128)(2,1)S(1)}, bf16[1024,1024]{1,0:T(8,128)(2,1)}, u32[]{:S(2)}) copy-start(bf16[1024,1024]{1,0:T(8,128)(2,1)} %param.9) | copy-start | bytes 6291460
  3.5 16.3 %collective-permute-start.2 = (bf16[64,384]{1,0:T(8,128)(2,1)}, bf16[64,384]{1,0:T(8,128)(2,1)S(1)}, u32[]{:S(2)}, u32[]{:S(2)}) collective-permute-start(bf16[64,384]{1,0:T(8,128)(2,1)} %cut.1.p0), channel_id=1, source_target_pairs={{0,24},{8,0},{16,8},{24,16},{1,25},{9,1},{17,9},{25,17},{2,26},{10... | collective-permute-start | bytes 147464 | tf_op jit(solution)/shard_map/ppermute | solution.py:36
  4.9 14.9 %collective-permute-start.3 = (bf16[64,384]{1,0:T(8,128)(2,1)}, bf16[64,384]{1,0:T(8,128)(2,1)S(1)}, u32[]{:S(2)}, u32[]{:S(2)}) collective-permute-start(bf16[64,384]{1,0:T(8,128)(2,1)} %cut.1.p0), channel_id=1, source_target_pairs={{0,16},{8,24},{16,0},{24,8},{1,17},{9,25},{17,1},{25,9},{2,18},{10... | collective-permute-start | bytes 147464 | tf_op jit(solution)/shard_map/ppermute | solution.py:36
  10.3 9.5 %collective-permute-start.4 = (bf16[64,384]{1,0:T(8,128)(2,1)}, bf16[64,384]{1,0:T(8,128)(2,1)S(1)}, u32[]{:S(2)}, u32[]{:S(2)}) collective-permute-start(bf16[64,384]{1,0:T(8,128)(2,1)} %cut.1.p0), channel_id=1, source_target_pairs={{0,8},{8,16},{16,24},{24,0},{1,9},{9,17},{17,25},{25,1},{2,10},{10... | collective-permute-start | bytes 147464 | tf_op jit(solution)/shard_map/ppermute | solution.py:36
  14.0 5.1 %collective-permute-start.1 = (bf16[4,16,1024]{2,1,0:T(8,128)(2,1)S(1)}, bf16[4,16,1024]{2,1,0:T(8,128)(2,1)S(1)}, u32[]{:S(2)}, u32[]{:S(2)}) collective-permute-start(bf16[4,16,1024]{2,1,0:T(8,128)(2,1)S(1)} %get-tuple-element.41), channel_id=1, source_target_pairs={{0,32},{32,0},{1,33},{33,1},{2,34},{34,2},{3,35},{35,3},{4,36},{36... | collective-permute-start | bytes 393224 | tf_op jit(solution)/shard_map/ppermute | solution.py:288
  23.5 8.9 %copy-start.7 = (s32[1,8,16]{2,1,0:T(8,128)S(1)}, s32[1,8,16]{2,1,0:T(8,128)}, u32[]{:S(2)}) copy-start(s32[1,8,16]{2,1,0:T(8,128)} %param.10) | copy-start | bytes 1540
  23.5 9.6 %copy-start.12 = (bf16[1024]{0:T(1024)(128)(2,1)S(1)}, bf16[1024]{0:T(1024)(128)(2,1)}, u32[]{:S(2)}) copy-start(bf16[1024]{0:T(1024)(128)(2,1)} %param.15) | copy-start | bytes 6148
  23.5 52.0 %all-to-all-start = ((bf16[64,4,32,128]{3,2,1,0:T(8,128)(2,1)}), bf16[64,4,32,128]{3,2,1,0:T(8,128)(2,1)}, u32[]{:S(2)}, u32[]{:S(2)}) async-start(bf16[64,4,32,128]{3,2,1,0:T(8,128)(2,1)} %bitcast.65), calls=%async_computation | async-start | bytes 4194304 | tf_op jit(solution)/shard_map/all_to_all | solution.py:31
  32.3 1.8 %copy-start.1 = (bf16[512,1024]{1,0:T(8,128)(2,1)S(1)}, bf16[512,1024]{1,0:T(8,128)(2,1)}, u32[]{:S(2)}) copy-start(bf16[512,1024]{1,0:T(8,128)(2,1)} %param.12) | copy-start | bytes 3145732
  34.0 1.2 copy-start.2
  34.4 2.5 %copy-start.6 = (bf16[64,1024]{1,0:T(8,128)(2,1)S(1)}, bf16[64,1024]{1,0:T(8,128)(2,1)}, u32[]{:S(2)}) copy-start(bf16[64,1024]{1,0:T(8,128)(2,1)} %get-tuple-element.23) | copy-start | bytes 393220
  35.7 39.8 %collective-permute-start = (bf16[640,1024]{1,0:T(8,128)(2,1)S(1)}, bf16[640,1024]{1,0:T(8,128)(2,1)}, u32[]{:S(2)}, u32[]{:S(2)}) collective-permute-start(bf16[640,1024]{1,0:T(8,128)(2,1)S(1)} %fusion.4.own_ref), channel_id=1, source_target_pairs={{0,1},{1,0},{2,3},{3,2},{4,5},{5,4},{6,7},{7,6},{8,9},{9,8},{10,11... | collective-permute-start | bytes 3932168 | tf_op jit(solution)/shard_map/ppermute | solution.py:27
  35.9 2.8 %copy-start.4 = (bf16[512,1024]{1,0:T(8,128)(2,1)S(1)}, bf16[512,1024]{1,0:T(8,128)(2,1)}, u32[]{:S(2)}) copy-start(bf16[512,1024]{1,0:T(8,128)(2,1)} %param.16) | copy-start | bytes 3145732
  37.0 25.9 %collective-permute-start.5 = (bf16[96,1024]{1,0:T(8,128)(2,1)S(1)}, bf16[96,1024]{1,0:T(8,128)(2,1)S(1)}, u32[]{:S(2)}, u32[]{:S(2)}) collective-permute-start(bf16[96,1024]{1,0:T(8,128)(2,1)S(1)} %get-tuple-element.47), channel_id=1, source_target_pairs={{0,64},{64,128},{128,192},{192,0},{1,65},{65,129},{129,193},{193,1... | collective-permute-start | bytes 589832 | tf_op jit(solution)/shard_map/ppermute | solution.py:36
  39.8 27.5 %collective-permute-start.6 = (bf16[96,1024]{1,0:T(8,128)(2,1)S(1)}, bf16[96,1024]{1,0:T(8,128)(2,1)S(1)}, u32[]{:S(2)}, u32[]{:S(2)}) collective-permute-start(bf16[96,1024]{1,0:T(8,128)(2,1)S(1)} %get-tuple-element.46), channel_id=1, source_target_pairs={{0,128},{64,192},{128,0},{192,64},{1,129},{65,193},{129,1},{193,65... | collective-permute-start | bytes 589832 | tf_op jit(solution)/shard_map/ppermute | solution.py:36
  42.6 25.2 %collective-permute-start.7 = (bf16[96,1024]{1,0:T(8,128)(2,1)S(1)}, bf16[96,1024]{1,0:T(8,128)(2,1)S(1)}, u32[]{:S(2)}, u32[]{:S(2)}) collective-permute-start(bf16[96,1024]{1,0:T(8,128)(2,1)S(1)} %get-tuple-element.45), channel_id=1, source_target_pairs={{0,192},{64,0},{128,64},{192,128},{1,193},{65,1},{129,65},{193,129... | collective-permute-start | bytes 589832 | tf_op jit(solution)/shard_map/ppermute | solution.py:36
  68.5 7.0 %collective-permute-start.8 = (bf16[640,1024]{1,0:T(8,128)(2,1)}, bf16[640,1024]{1,0:T(8,128)(2,1)}, u32[]{:S(2)}, u32[]{:S(2)}) collective-permute-start(bf16[640,1024]{1,0:T(8,128)(2,1)} %slice_dynamic-update-slice_fusion.c0), channel_id=1, source_target_pairs={{0,1},{1,0},{2,3},{3,2},{4,5},{5,4},{6,7},{7,6},{8,9},{9,8},{10,11... | collective-permute-start | bytes 3932168 | tf_op jit(solution)/shard_map/ppermute | solution.py:27
  69.4 21.3 %collective-permute-start.10 = (bf16[4,64,1024]{2,1,0:T(8,128)(2,1)}, bf16[4,64,1024]{2,1,0:T(8,128)(2,1)}, u32[]{:S(2)}, u32[]{:S(2)}) collective-permute-start(bf16[4,64,1024]{2,1,0:T(8,128)(2,1)} %pad_maximum_fusion.1.w0), channel_id=1, source_target_pairs={{0,4},{2,6},{4,0},{6,2},{1,5},{3,7},{5,1},{7,3},{8,12},{10,14},{12... | collective-permute-start | bytes 1572872 | tf_op jit(solution)/shard_map/ppermute | solution.py:36
  72.2 24.6 %collective-permute-start.11 = (bf16[4,64,1024]{2,1,0:T(8,128)(2,1)}, bf16[4,64,1024]{2,1,0:T(8,128)(2,1)}, u32[]{:S(2)}, u32[]{:S(2)}) collective-permute-start(bf16[4,64,1024]{2,1,0:T(8,128)(2,1)} %pad_maximum_fusion.1.w0), channel_id=1, source_target_pairs={{0,2},{2,4},{4,6},{6,0},{1,3},{3,5},{5,7},{7,1},{8,10},{10,12},{12... | collective-permute-start | bytes 1572872 | tf_op jit(solution)/shard_map/ppermute | solution.py:36
  72.8 24.1 %collective-permute-start.9 = (bf16[4,64,1024]{2,1,0:T(8,128)(2,1)}, bf16[4,64,1024]{2,1,0:T(8,128)(2,1)}, u32[]{:S(2)}, u32[]{:S(2)}) collective-permute-start(bf16[4,64,1024]{2,1,0:T(8,128)(2,1)} %pad_maximum_fusion.1.w0), channel_id=1, source_target_pairs={{0,6},{2,0},{4,2},{6,4},{1,7},{3,1},{5,3},{7,5},{8,14},{10,8},{12,... | collective-permute-start | bytes 1572872 | tf_op jit(solution)/shard_map/ppermute | solution.py:36
  86.3 31.4 %all-to-all-start.1 = ((bf16[8,4,4,64,128]{4,3,2,1,0:T(8,128)(2,1)}), bf16[8,4,4,64,128]{4,3,2,1,0:T(8,128)(2,1)}, u32[]{:S(2)}, u32[]{:S(2)}) async-start(bf16[8,4,4,64,128]{4,3,2,1,0:T(8,128)(2,1)} %get-tuple-element.29), calls=%async_computation.1 | async-start | bytes 4194304 | tf_op jit(solution)/shard_map/all_to_all | solution.py:31
  117.7 36.0 %all-to-all-start.2 = ((bf16[64,4,32,128]{3,2,1,0:T(8,128)(2,1)}), bf16[64,4,32,128]{3,2,1,0:T(8,128)(2,1)}, u32[]{:S(2)}, u32[]{:S(2)}) async-start(bf16[64,4,32,128]{3,2,1,0:T(8,128)(2,1)} %bitcast.64), calls=%async_computation.2 | async-start | bytes 4194304 | tf_op jit(solution)/shard_map/all_to_all | solution.py:31
  127.4 45.3 %collective-permute-start.12 = (bf16[512,1024]{1,0:T(8,128)(2,1)}, bf16[512,1024]{1,0:T(8,128)(2,1)}, u32[]{:S(2)}, u32[]{:S(2)}) collective-permute-start(bf16[512,1024]{1,0:T(8,128)(2,1)} %convolution_convert_fusion), channel_id=1, source_target_pairs={{0,1},{1,0},{2,3},{3,2},{4,5},{5,4},{6,7},{7,6},{8,9},{9,8},{10,11... | collective-permute-start | bytes 3145736 | tf_op jit(solution)/shard_map/ppermute | solution.py:27
  130.1 42.7 %copy-start.3 = (bf16[512,1024]{1,0:T(8,128)(2,1)S(1)}, bf16[512,1024]{1,0:T(8,128)(2,1)}, u32[]{:S(2)}) copy-start(bf16[512,1024]{1,0:T(8,128)(2,1)} %param.12) | copy-start | bytes 3145732
  130.1 20.5 %collective-permute-start.13 = (bf16[4,64,128]{2,1,0:T(8,128)(2,1)}, bf16[4,64,128]{2,1,0:T(8,128)(2,1)S(1)}, u32[]{:S(2)}, u32[]{:S(2)}) collective-permute-start(bf16[4,64,128]{2,1,0:T(8,128)(2,1)} %get-tuple-element.33), channel_id=1, source_target_pairs={{0,2},{2,4},{4,6},{6,0},{1,3},{3,5},{5,7},{7,1},{8,10},{10,12},{12... | collective-permute-start | bytes 196616 | tf_op jit(solution)/shard_map/ppermute | solution.py:36
  131.6 20.5 %collective-permute-start.14 = (bf16[4,64,128]{2,1,0:T(8,128)(2,1)}, bf16[4,64,128]{2,1,0:T(8,128)(2,1)S(1)}, u32[]{:S(2)}, u32[]{:S(2)}) collective-permute-start(bf16[4,64,128]{2,1,0:T(8,128)(2,1)} %get-tuple-element.35), channel_id=1, source_target_pairs={{0,4},{2,6},{4,0},{6,2},{1,5},{3,7},{5,1},{7,3},{8,12},{10,14},{12... | collective-permute-start | bytes 196616 | tf_op jit(solution)/shard_map/ppermute | solution.py:36
  134.3 18.4 %collective-permute-start.15 = (bf16[4,64,128]{2,1,0:T(8,128)(2,1)}, bf16[4,64,128]{2,1,0:T(8,128)(2,1)}, u32[]{:S(2)}, u32[]{:S(2)}) collective-permute-start(bf16[4,64,128]{2,1,0:T(8,128)(2,1)} %get-tuple-element.34), channel_id=1, source_target_pairs={{0,6},{2,0},{4,2},{6,4},{1,7},{3,1},{5,3},{7,5},{8,14},{10,8},{12,... | collective-permute-start | bytes 196616 | tf_op jit(solution)/shard_map/ppermute | solution.py:36
  155.6 5.2 %collective-permute-start.16 = (bf16[2,64,128]{2,1,0:T(8,128)(2,1)S(1)}, bf16[2,64,128]{2,1,0:T(8,128)(2,1)S(1)}, u32[]{:S(2)}, u32[]{:S(2)}) collective-permute-start(bf16[2,64,128]{2,1,0:T(8,128)(2,1)S(1)} %get-tuple-element.42), channel_id=1, source_target_pairs={{0,8},{8,16},{16,24},{24,0},{1,9},{9,17},{17,25},{25,1},{2,10},{10... | collective-permute-start | bytes 98312 | tf_op jit(solution)/shard_map/ppermute | solution.py:36
  158.0 8.0 %collective-permute-start.17 = (bf16[2,64,128]{2,1,0:T(8,128)(2,1)S(1)}, bf16[2,64,128]{2,1,0:T(8,128)(2,1)S(1)}, u32[]{:S(2)}, u32[]{:S(2)}) collective-permute-start(bf16[2,64,128]{2,1,0:T(8,128)(2,1)S(1)} %get-tuple-element.43), channel_id=1, source_target_pairs={{0,16},{8,24},{16,0},{24,8},{1,17},{9,25},{17,1},{25,9},{2,18},{10... | collective-permute-start | bytes 98312 | tf_op jit(solution)/shard_map/ppermute | solution.py:36
  160.2 6.0 %collective-permute-start.18 = (bf16[2,64,128]{2,1,0:T(8,128)(2,1)S(1)}, bf16[2,64,128]{2,1,0:T(8,128)(2,1)S(1)}, u32[]{:S(2)}, u32[]{:S(2)}) collective-permute-start(bf16[2,64,128]{2,1,0:T(8,128)(2,1)S(1)} %get-tuple-element.44), channel_id=1, source_target_pairs={{0,24},{8,0},{16,8},{24,16},{1,25},{9,1},{17,9},{25,17},{2,26},{10... | collective-permute-start | bytes 98312 | tf_op jit(solution)/shard_map/ppermute | solution.py:36
  167.0 13.0 %all-to-all-start.3 = ((bf16[8,2,64,128]{3,2,1,0:T(8,128)(2,1)}), bf16[8,2,64,128]{3,2,1,0:T(8,128)(2,1)S(1)}, u32[]{:S(2)}, u32[]{:S(2)}) async-start(bf16[8,2,64,128]{3,2,1,0:T(8,128)(2,1)} %broadcast_in_dim.2), calls=%async_computation.3 | async-start | bytes 524288 | tf_op jit(solution)/shard_map/all_to_all | solution.py:31
  180.0 0.7 copy-start.5
  (4 other events, 2.5 us)
